TPU v7x, 256 devices: a whole 4x4x8 slice. The times are simulated.
256 devices in a mesh: rows: 16 (over y, z_hi, core), cols: 16 (over z_lo, x).
Axes of the slice: x: 4, y: 4, z: 8 (z_hi: 2, z_lo: 4; z = z_hi * 4 + z_lo), core: 2. Of those that a mesh axis runs over, the one named last changes fastest.
Arguments:
- eigvecs: float32 [8192, 2048], P('rows', 'cols'), may hold values from -6 to 6
- wy_packed: float32 [256, 128, 128], P(('rows', 'cols')), may hold values from -6 to 6
- slot_block: int32 [16, 8, 2], P('rows'), may hold values from 0 to 1, each once within a row
Outputs:
- transformed: float32 [8192, 2048], P('rows', 'cols')
Inputs may be any that keep to these rules, and one draw needn't show every extreme that they name: `slot_block`: for every group and level the 2 entries name each of 0 .. 1 once.
All inputs are finite; a program needn't handle non-finite values.
Results may differ from a plain program's by a relative error of at most 0.0003.
Values sent between devices are 32-bit elements; how exact they have to be, the bound alone decides.
No kernel may reach another device: no remote copies, remote signals or barrier semaphores. Data moves between devices by JAX's collectives and lax.ppermute only.
A program may use at most 64 MiB of HBM per device.

v0:
```python
import jax
import jax.numpy as jnp
from jax import lax
from jax.sharding import PartitionSpec as P

LEVELS = 8


highest = lax.Precision.HIGHEST


def from_everyone(array, axis):
    copies = jnp.broadcast_to(array, (lax.axis_size(axis), *array.shape))
    return lax.all_to_all(copies, axis, split_axis=0, concat_axis=0, tiled=True)


def joined_along(tiles, dim):
    tiles = jnp.moveaxis(tiles, 0, dim)
    shape = tiles.shape
    return tiles.reshape(*shape[:dim], shape[dim] * shape[dim + 1], *shape[dim + 2 :])


def collect(array, axis, dim):
    tiles = from_everyone(array, axis)
    return joined_along(tiles, dim)


def passed_along(value, axis, steps):
    count = lax.axis_size(axis)
    first, last = (max(0, -steps), min(count, count - steps))
    return lax.ppermute(value, axis, [(source, source + steps) for source in range(first, last)])


def unpack(packed):
    blocks, band_width = (packed.shape[0], packed.shape[1])
    flipped = jnp.swapaxes(packed, 1, 2)
    padded = jnp.pad(flipped, ((0, 0), (0, 0), (0, band_width + 1)))
    flattened = padded.reshape(blocks, band_width * (2 * band_width + 1))[
        :, : 2 * band_width * band_width
    ]
    return flattened.reshape(blocks, band_width, 2 * band_width)


def upper_inverse(upper):
    band_width = upper.shape[1]
    index_row = jnp.arange(band_width, dtype=jnp.int32)
    diag_values = jnp.diagonal(upper, axis1=1, axis2=2)
    identity = jnp.eye(band_width, dtype=upper.dtype)
    inverted = identity[None] * (1.0 / diag_values)[:, None, :]
    width = 1
    while width < band_width:
        same_new = index_row[:, None] // (2 * width) == index_row[None, :] // (2 * width)
        same_old = index_row[:, None] // width == index_row[None, :] // width
        selector = jnp.logical_and(same_new, jnp.logical_not(same_old)).astype(upper.dtype)
        corner = upper * selector[None]
        partial_block = jnp.einsum("nij,njk->nik", corner, inverted, precision=highest)
        inverted = inverted - jnp.einsum("nij,njk->nik", inverted, partial_block, precision=highest)
        width = 2 * width
    return inverted


def wy_factor(reflectors):
    band_width = reflectors.shape[1]
    gram_matrix = jnp.einsum("njr,nkr->njk", reflectors, reflectors, precision=highest)
    identity = jnp.eye(band_width, dtype=gram_matrix.dtype)
    triangle = jnp.triu(gram_matrix, 1) + 0.5 * gram_matrix * identity
    return upper_inverse(triangle)


def reflect(reflectors, factors, windows):
    projected = jnp.einsum("njr,nrc->njc", reflectors, windows, precision=highest)
    scaled = jnp.einsum("njk,nkc->njc", factors, projected, precision=highest)
    return windows - jnp.einsum("njr,njc->nrc", reflectors, scaled, precision=highest)


def per_device(eigvecs, wy_packed, slot_block):
    band_width = wy_packed.shape[1]
    row_count, col_count = eigvecs.shape
    per_level = row_count // (2 * band_width)
    orders = slot_block[0]
    payload = jnp.stack([wy_packed, wy_factor(unpack(wy_packed))], axis=1)
    gathered = collect(payload, "cols", 0)
    current = eigvecs
    first_owner = lax.axis_index("rows") == 0
    positions = jnp.arange(per_level, dtype=jnp.int32)
    for level_index in range(LEVELS):
        pieces = gathered[level_index * per_level : (level_index + 1) * per_level]
        selector = (orders[level_index][:, None] == positions[None, :]).astype(jnp.float32)
        chosen = jnp.einsum("hp,pkij->hkij", selector, pieces, precision=highest)
        reflectors = unpack(chosen[:, 0])
        factors = chosen[:, 1]
        if level_index % 2 == 0:
            windows = current.reshape(per_level, 2 * band_width, col_count)
            current = reflect(reflectors, factors, windows).reshape(row_count, col_count)
        else:
            below = passed_along(current[:band_width], "rows", -1)
            extended = jnp.concatenate([current[band_width:], below], axis=0)
            windows = extended.reshape(per_level, 2 * band_width, col_count)
            result = reflect(reflectors, factors, windows).reshape(row_count, col_count)
            above = passed_along(result[row_count - band_width :], "rows", 1)
            middle = result[: row_count - band_width]
            top_rows = jnp.where(first_owner, current[:band_width], above)
            current = jnp.concatenate([top_rows, middle], axis=0)
    return current


def solution(mesh):
    placed = (P("rows", "cols"), P(("rows", "cols"), None, None), P("rows", None, None))
    return jax.shard_map(
        per_device, mesh=mesh, in_specs=placed, out_specs=P("rows", "cols"), check_vma=False
    )
```

profile of v0, /device:TPU:56, one launch (start us, length us, event | category | flops | bytes accessed | tf_op | source)
XLA Modules:
  0.0 143.3 jit_solution(8370941051078306720)
XLA Ops:
  0.1 0.9 copy.78
  1.0 0.5 reshape.750
  1.5 0.4 slice_reduce_fusion
  1.9 0.3 select_add_fusion
  2.2 1.2 gather_fusion
  6.8 1.6 %broadcast_in_dim.13 = f32[16,1,2,128,128]{4,3,2,1,0:T(8,128)} broadcast(f32[2,128,128]{2,1,0:T(8,128)S(1)} %maximum_bitcast_fusion), dimensions={2,3,4} | broadcast | bytes 2228224 | tf_op jit(solution)/shard_map/broadcast_in_dim | solution.py:13
  8.4 8.6 %all-to-all-start = ((f32[16,1,2,128,128]{4,3,2,1,0:T(8,128)}), f32[16,1,2,128,128]{4,3,2,1,0:T(8,128)S(1)}, u32[]{:S(2)}, u32[]{:S(2)}) async-start(f32[16,1,2,128,128]{4,3,2,1,0:T(8,128)} %broadcast_in_dim.13), calls=%async_computation | async-start | bytes 4194304 | tf_op jit(solution)/shard_map/all_to_all | solution.py:14
  17.0 0.8 slice_reduce_fusion.1
  17.9 46.4 %all-to-all-done = f32[16,1,2,128,128]{4,3,2,1,0:T(8,128)S(1)} async-done(((f32[16,1,2,128,128]{4,3,2,1,0:T(8,128)}), f32[16,1,2,128,128]{4,3,2,1,0:T(8,128)S(1)}, u32[]{:S(2)}, u32[]{:S(2)}) %all-to-all-start) | async-done | bytes 2097184 | tf_op jit(solution)/shard_map/all_to_all | solution.py:14
  64.3 1.0 fusion.162
  65.3 0.7 fusion.25
  66.2 0.5 reshape.752
  66.8 0.4 fusion.23
  67.2 0.3 fusion.63
  67.4 0.6 convolution_subtract_fusion.7
  68.0 4.3 %collective-permute-start = (f32[128,128]{1,0:T(8,128)S(1)}, f32[128,128]{1,0:T(8,128)S(1)}, u32[]{:S(2)}, u32[]{:S(2)}) collective-permute-start(f32[128,128]{1,0:T(8,128)S(1)} %slice.279), channel_id=1, source_target_pairs={{16,0},{32,16},{48,32},{64,48},{80,64},{96,80},{112,96},{128,112},... | collective-permute-start | bytes 196616 | tf_op jit(solution)/shard_map/ppermute | solution.py:31
  72.4 0.7 fusion.26
  73.1 1.4 fusion.27
  74.5 1.4 fusion.28
  76.0 0.7 fusion.29
  76.7 0.7 fusion.30
  77.4 0.7 fusion.31
  78.1 0.7 fusion.32
  79.0 0.5 reshape.756
  79.6 0.4 fusion.20
  80.0 0.3 fusion.61
  80.3 0.6 convolution_subtract_fusion.6
  80.9 1.9 %collective-permute-start.1 = (f32[128,128]{1,0:T(8,128)S(1)}, f32[128,128]{1,0:T(8,128)S(1)}, u32[]{:S(2)}, u32[]{:S(2)}) collective-permute-start(f32[128,128]{1,0:T(8,128)S(1)} %slice.285), channel_id=1, source_target_pairs={{0,16},{16,32},{32,48},{48,64},{64,80},{80,96},{96,112},{112,128},... | collective-permute-start | bytes 196616 | tf_op jit(solution)/shard_map/ppermute | solution.py:31
  83.0 0.5 reshape.760
  83.6 7.7 %collective-permute-done.1 = f32[128,128]{1,0:T(8,128)S(1)} collective-permute-done((f32[128,128]{1,0:T(8,128)S(1)}, f32[128,128]{1,0:T(8,128)S(1)}, u32[]{:S(2)}, u32[]{:S(2)}) %collective-permute-start.1) | collective-permute-done | bytes 65568 | tf_op jit(solution)/shard_map/ppermute | solution.py:31
  91.3 0.4 fusion.17
  91.7 0.3 fusion.59
  92.0 0.6 convolution_subtract_fusion.5
  92.6 1.9 %collective-permute-start.2 = (f32[128,128]{1,0:T(8,128)S(1)}, f32[128,128]{1,0:T(8,128)S(1)}, u32[]{:S(2)}, u32[]{:S(2)}) collective-permute-start(f32[128,128]{1,0:T(8,128)S(1)} %slice.291), channel_id=1, source_target_pairs={{16,0},{32,16},{48,32},{64,48},{80,64},{96,80},{112,96},{128,112},... | collective-permute-start | bytes 196616 | tf_op jit(solution)/shard_map/ppermute | solution.py:31
  94.7 0.5 reshape.764
  95.3 1.2 collective-permute-done.2
  96.4 0.4 fusion.14
  97.1 0.6 convolution_subtract_fusion.4
  97.7 4.3 %collective-permute-start.3 = (f32[128,128]{1,0:T(8,128)S(1)}, f32[128,128]{1,0:T(8,128)S(1)}, u32[]{:S(2)}, u32[]{:S(2)}) collective-permute-start(f32[128,128]{1,0:T(8,128)S(1)} %slice.297), channel_id=1, source_target_pairs={{0,16},{16,32},{32,48},{48,64},{64,80},{80,96},{96,112},{112,128},... | collective-permute-start | bytes 196616 | tf_op jit(solution)/shard_map/ppermute | solution.py:31
  102.2 0.5 reshape.768
  102.7 5.4 %collective-permute-done.3 = f32[128,128]{1,0:T(8,128)S(1)} collective-permute-done((f32[128,128]{1,0:T(8,128)S(1)}, f32[128,128]{1,0:T(8,128)S(1)}, u32[]{:S(2)}, u32[]{:S(2)}) %collective-permute-start.3) | collective-permute-done | bytes 65568 | tf_op jit(solution)/shard_map/ppermute | solution.py:31
  108.2 0.4 fusion.11
  108.6 0.3 fusion.55
  108.9 0.6 convolution_subtract_fusion.3
  109.5 1.9 %collective-permute-start.4 = (f32[128,128]{1,0:T(8,128)S(1)}, f32[128,128]{1,0:T(8,128)S(1)}, u32[]{:S(2)}, u32[]{:S(2)}) collective-permute-start(f32[128,128]{1,0:T(8,128)S(1)} %slice.303), channel_id=1, source_target_pairs={{16,0},{32,16},{48,32},{64,48},{80,64},{96,80},{112,96},{128,112},... | collective-permute-start | bytes 196616 | tf_op jit(solution)/shard_map/ppermute | solution.py:31
  111.6 0.5 reshape.772
  112.1 1.2 collective-permute-done.4
  113.3 0.4 fusion.8
  113.7 0.3 fusion.53
  114.0 0.6 convolution_subtract_fusion.2
  114.6 3.2 %collective-permute-start.5 = (f32[128,128]{1,0:T(8,128)S(1)}, f32[128,128]{1,0:T(8,128)S(1)}, u32[]{:S(2)}, u32[]{:S(2)}) collective-permute-start(f32[128,128]{1,0:T(8,128)S(1)} %slice.309), channel_id=1, source_target_pairs={{0,16},{16,32},{32,48},{48,64},{64,80},{80,96},{96,112},{112,128},... | collective-permute-start | bytes 196616 | tf_op jit(solution)/shard_map/ppermute | solution.py:31
  118.0 0.5 reshape.776
  118.5 6.5 %collective-permute-done.5 = f32[128,128]{1,0:T(8,128)S(1)} collective-permute-done((f32[128,128]{1,0:T(8,128)S(1)}, f32[128,128]{1,0:T(8,128)S(1)}, u32[]{:S(2)}, u32[]{:S(2)}) %collective-permute-start.5) | collective-permute-done | bytes 65568 | tf_op jit(solution)/shard_map/ppermute | solution.py:31
  125.1 0.4 fusion.5
  125.5 0.3 fusion.51
  125.7 0.6 convolution_subtract_fusion.1
  126.4 1.9 %collective-permute-start.6 = (f32[128,128]{1,0:T(8,128)S(1)}, f32[128,128]{1,0:T(8,128)S(1)}, u32[]{:S(2)}, u32[]{:S(2)}) collective-permute-start(f32[128,128]{1,0:T(8,128)S(1)} %slice.315), channel_id=1, source_target_pairs={{16,0},{32,16},{48,32},{64,48},{80,64},{96,80},{112,96},{128,112},... | collective-permute-start | bytes 196616 | tf_op jit(solution)/shard_map/ppermute | solution.py:31
  128.4 0.5 reshape.780
  129.0 1.2 collective-permute-done.6
  130.2 0.4 fusion.2
  130.9 0.6 convolution_subtract_fusion
  131.5 2.4 %collective-permute-start.7 = (f32[128,128]{1,0:T(8,128)S(1)}, f32[128,128]{1,0:T(8,128)S(1)}, u32[]{:S(2)}, u32[]{:S(2)}) collective-permute-start(f32[128,128]{1,0:T(8,128)S(1)} %slice.321), channel_id=1, source_target_pairs={{0,16},{16,32},{32,48},{48,64},{64,80},{80,96},{96,112},{112,128},... | collective-permute-start | bytes 196616 | tf_op jit(solution)/shard_map/ppermute | solution.py:31
  133.9 8.7 %collective-permute-done.7 = f32[128,128]{1,0:T(8,128)S(1)} collective-permute-done((f32[128,128]{1,0:T(8,128)S(1)}, f32[128,128]{1,0:T(8,128)S(1)}, u32[]{:S(2)}, u32[]{:S(2)}) %collective-permute-start.7) | collective-permute-done | bytes 65568 | tf_op jit(solution)/shard_map/ppermute | solution.py:31
  142.6 0.7 pad_maximum_fusion.7
  (105 shorter events, 5.6 us)
Async XLA Ops:
  1.9 4.9 %copy-start.5 = (f32[1,128,128]{2,1,0:T(8,128)S(1)}, f32[1,128,128]{2,1,0:T(8,128)}, u32[]{:S(2)}) copy-start(f32[1,128,128]{2,1,0:T(8,128)} %param.4) | copy-start | bytes 196612
  8.4 8.6 %copy-start.6 = (s32[1,8,2]{1,2,0:T(2,128)S(1)}, s32[1,8,2]{1,2,0:T(2,128)}, u32[]{:S(2)}) copy-start(s32[1,8,2]{1,2,0:T(2,128)} %param.5) | copy-start | bytes 196
  8.4 55.9 %all-to-all-start = ((f32[16,1,2,128,128]{4,3,2,1,0:T(8,128)}), f32[16,1,2,128,128]{4,3,2,1,0:T(8,128)S(1)}, u32[]{:S(2)}, u32[]{:S(2)}) async-start(f32[16,1,2,128,128]{4,3,2,1,0:T(8,128)} %broadcast_in_dim.13), calls=%async_computation | async-start | bytes 4194304 | tf_op jit(solution)/shard_map/all_to_all | solution.py:14
  65.3 1.5 %copy-start = (f32[512,128]{1,0:T(8,128)S(1)}, f32[512,128]{1,0:T(8,128)}, u32[]{:S(2)}) copy-start(f32[512,128]{1,0:T(8,128)} %param.3) | copy-start | bytes 786436
  66.0 6.3 %copy-start.2 = (f32[2,1,2,128,128]{4,3,2,1,0:T(8,128)S(1)}, f32[2,1,2,128,128]{4,3,2,1,0:T(8,128)}, u32[]{:S(2)}) copy-start(f32[2,1,2,128,128]{4,3,2,1,0:T(8,128)} %get-tuple-element.19) | copy-start | bytes 786436
  66.0 6.3 %copy-start.9 = (s32[2]{0:T(128)S(1)}, s32[2]{0:T(128)}, u32[]{:S(2)}) copy-start(s32[2]{0:T(128)} %get-tuple-element.10) | copy-start | bytes 28
  66.1 7.0 %copy-start.1 = (f32[2,1,2,128,128]{4,3,2,1,0:T(8,128)S(1)}, f32[2,1,2,128,128]{4,3,2,1,0:T(8,128)}, u32[]{:S(2)}) copy-start(f32[2,1,2,128,128]{4,3,2,1,0:T(8,128)} %get-tuple-element.18) | copy-start | bytes 786436
  66.2 7.0 %copy-start.8 = (s32[2]{0:T(128)S(1)}, s32[2]{0:T(128)}, u32[]{:S(2)}) copy-start(s32[2]{0:T(128)} %get-tuple-element.9) | copy-start | bytes 28
  66.2 8.3 %copy-start.7 = (s32[2]{0:T(128)S(1)}, s32[2]{0:T(128)}, u32[]{:S(2)}) copy-start(s32[2]{0:T(128)} %get-tuple-element.8) | copy-start | bytes 28
  68.0 11.5 %collective-permute-start = (f32[128,128]{1,0:T(8,128)S(1)}, f32[128,128]{1,0:T(8,128)S(1)}, u32[]{:S(2)}, u32[]{:S(2)}) collective-permute-start(f32[128,128]{1,0:T(8,128)S(1)} %slice.279), channel_id=1, source_target_pairs={{16,0},{32,16},{48,32},{64,48},{80,64},{96,80},{112,96},{128,112},... | collective-permute-start | bytes 196616 | tf_op jit(solution)/shard_map/ppermute | solution.py:31
  79.0 3.8 %copy-start.4 = (f32[2,2,128,128]{3,0,2,1:T(2,128)S(1)}, f32[2,2,128,128]{3,0,2,1:T(2,128)}, u32[]{:S(2)}) copy-start(f32[2,2,128,128]{3,0,2,1:T(2,128)} %fusion.27) | copy-start | bytes 786436
  80.9 10.4 %collective-permute-start.1 = (f32[128,128]{1,0:T(8,128)S(1)}, f32[128,128]{1,0:T(8,128)S(1)}, u32[]{:S(2)}, u32[]{:S(2)}) collective-permute-start(f32[128,128]{1,0:T(8,128)S(1)} %slice.285), channel_id=1, source_target_pairs={{0,16},{16,32},{32,48},{48,64},{64,80},{80,96},{96,112},{112,128},... | collective-permute-start | bytes 196616 | tf_op jit(solution)/shard_map/ppermute | solution.py:31
  83.0 11.5 %copy-start.3 = (f32[2,2,128,128]{3,0,2,1:T(2,128)S(1)}, f32[2,2,128,128]{3,0,2,1:T(2,128)}, u32[]{:S(2)}) copy-start(f32[2,2,128,128]{3,0,2,1:T(2,128)} %fusion.28) | copy-start | bytes 786436
  92.6 3.8 %collective-permute-start.2 = (f32[128,128]{1,0:T(8,128)S(1)}, f32[128,128]{1,0:T(8,128)S(1)}, u32[]{:S(2)}, u32[]{:S(2)}) collective-permute-start(f32[128,128]{1,0:T(8,128)S(1)} %slice.291), channel_id=1, source_target_pairs={{16,0},{32,16},{48,32},{64,48},{80,64},{96,80},{112,96},{128,112},... | collective-permute-start | bytes 196616 | tf_op jit(solution)/shard_map/ppermute | solution.py:31
  97.7 10.4 %collective-permute-start.3 = (f32[128,128]{1,0:T(8,128)S(1)}, f32[128,128]{1,0:T(8,128)S(1)}, u32[]{:S(2)}, u32[]{:S(2)}) collective-permute-start(f32[128,128]{1,0:T(8,128)S(1)} %slice.297), channel_id=1, source_target_pairs={{0,16},{16,32},{32,48},{48,64},{64,80},{80,96},{96,112},{112,128},... | collective-permute-start | bytes 196616 | tf_op jit(solution)/shard_map/ppermute | solution.py:31
  109.5 3.8 %collective-permute-start.4 = (f32[128,128]{1,0:T(8,128)S(1)}, f32[128,128]{1,0:T(8,128)S(1)}, u32[]{:S(2)}, u32[]{:S(2)}) collective-permute-start(f32[128,128]{1,0:T(8,128)S(1)} %slice.303), channel_id=1, source_target_pairs={{16,0},{32,16},{48,32},{64,48},{80,64},{96,80},{112,96},{128,112},... | collective-permute-start | bytes 196616 | tf_op jit(solution)/shard_map/ppermute | solution.py:31
  114.6 10.4 %collective-permute-start.5 = (f32[128,128]{1,0:T(8,128)S(1)}, f32[128,128]{1,0:T(8,128)S(1)}, u32[]{:S(2)}, u32[]{:S(2)}) collective-permute-start(f32[128,128]{1,0:T(8,128)S(1)} %slice.309), channel_id=1, source_target_pairs={{0,16},{16,32},{32,48},{48,64},{64,80},{80,96},{96,112},{112,128},... | collective-permute-start | bytes 196616 | tf_op jit(solution)/shard_map/ppermute | solution.py:31
  126.4 3.8 %collective-permute-start.6 = (f32[128,128]{1,0:T(8,128)S(1)}, f32[128,128]{1,0:T(8,128)S(1)}, u32[]{:S(2)}, u32[]{:S(2)}) collective-permute-start(f32[128,128]{1,0:T(8,128)S(1)} %slice.315), channel_id=1, source_target_pairs={{16,0},{32,16},{48,32},{64,48},{80,64},{96,80},{112,96},{128,112},... | collective-permute-start | bytes 196616 | tf_op jit(solution)/shard_map/ppermute | solution.py:31
  131.5 11.1 %collective-permute-start.7 = (f32[128,128]{1,0:T(8,128)S(1)}, f32[128,128]{1,0:T(8,128)S(1)}, u32[]{:S(2)}, u32[]{:S(2)}) collective-permute-start(f32[128,128]{1,0:T(8,128)S(1)} %slice.321), channel_id=1, source_target_pairs={{0,16},{16,32},{32,48},{48,64},{64,80},{80,96},{96,112},{112,128},... | collective-permute-start | bytes 196616 | tf_op jit(solution)/shard_map/ppermute | solution.py:31
where the time goes:
time: 146 us; the launch traced here: 143 us
  waiting for transfers between devices  78.3 us (54%)
  starting transfers between devices  30.5 us (21%)
  matrix products  20.6 us (14%)
  local copies, waits for them, and re-layouts  12 us (8%)
    all_to_all x1, waiting for transfers between devices, from_everyone(): return lax.all_to_all(copies, axis, split_axis=0, concat_axis=0, tiled=True)  46.4 us
    ppermute x8, waiting for transfers between devices, passed_along(): lax.ppermute(value, axis, [(source, source + steps) for source in range(f...  31.8 us
    ppermute x8, starting transfers between devices, passed_along(): lax.ppermute(value, axis, [(source, source + steps) for source in range(f...  21.9 us
    all_to_all x1, starting transfers between devices, from_everyone(): return lax.all_to_all(copies, axis, split_axis=0, concat_axis=0, tiled=True)  8.61 us
    dot_general x8, matrix products, per_device(): chosen = jnp.einsum('hp,pkij->hkij', selector, pieces, precision=highest)  7.09 us
    dot_general x8, matrix products, reflect(): jnp.einsum('njr,njc->nrc', reflectors, scaled, precision=highest)  4.72 us
    reshape x9, local copies, waits for them, and re-layouts, unpack(): padded.reshape(blocks, band_width * (2 * band_width + 1))  4.47 us
    dot_general x8, matrix products, reflect(): jnp.einsum('njr,nrc->njc', reflectors, windows, precision=highest)  3.1 us
  transfers between devices with their start and end apart: 9, of which 8 were waited for; matrix products, arithmetic and copies ran while one was open for 8% of the time, Pallas kernels for 0%

commit v1 on v0

v1 whole, which is shorter than its diff:
```python
import jax
import jax.numpy as jnp
from jax import lax
from jax.experimental import pallas as pl
from jax.experimental.pallas import tpu as pltpu
from jax.sharding import PartitionSpec as P

F32 = jnp.float32
BF16 = jnp.bfloat16
W = 128
SUB = 32
VMEM = pltpu.VMEM
SMEM = pltpu.SMEM


def split(x):
    high = x.astype(BF16)
    low = (x - high.astype(F32)).astype(BF16)
    return high, low


def mm(a, b, dims=((1,), (0,))):
    return lax.dot_general(a, b, (dims, ((), ())), preferred_element_type=F32)


def dot3(a, b):
    ah, al = a
    bh, bl = b
    return mm(ah, bh) + (mm(ah, bl) + mm(al, bh))


def unpacked(packed):
    wide = jnp.concatenate([packed.T, jnp.zeros((W, W), F32)], axis=1)
    return pltpu.roll(wide, 0, axis=1, stride=1, stride_axis=0)


def diagonal_inverses(gram):
    row = lax.broadcasted_iota(jnp.int32, (SUB, W), 0)
    lane = lax.broadcasted_iota(jnp.int32, (SUB, W), 1)
    group = lane // SUB
    place = lane % SUB
    compact = gram[0:SUB]
    for d in range(1, 4):
        compact = jnp.where(group == d, gram[d * SUB : (d + 1) * SUB], compact)
    diagonal = jnp.sum(jnp.where(row == place, compact, 0.0), axis=0, keepdims=True)
    inverse_diagonal = jnp.broadcast_to(2.0 / diagonal, (SUB, W))
    scaled = compact * inverse_diagonal
    scaled = jnp.where(row < place, scaled, 0.0)
    rows = [jnp.where(row == place, 1.0, 0.0)[8 * i : 8 * i + 8] for i in range(4)]
    base = group * SUB
    for k in range(SUB - 1, 0, -1):
        tile, at = k // 8, k % 8
        pivot = jnp.broadcast_to(rows[tile][at : at + 1], (8, W))
        for i in range(tile + 1):
            if i * 8 >= k:
                continue
            factor = jnp.take_along_axis(
                scaled[8 * i : 8 * i + 8], base[8 * i : 8 * i + 8] + k, axis=1, mode="promise_in_bounds"
            )
            rows[i] = rows[i] - factor * pivot
    unit = jnp.concatenate(rows, axis=0)
    row_scale = jnp.take_along_axis(inverse_diagonal, base + row, axis=1, mode="promise_in_bounds")
    return unit * row_scale


def triangle_inverse(gram):
    small = diagonal_inverses(gram)
    lane = lax.broadcasted_iota(jnp.int32, (SUB, W), 1)
    group = lane // SUB
    parts = [jnp.where(group == d, small, 0.0) for d in range(4)]
    base = jnp.concatenate(parts, axis=0)
    base_parts = split(base)
    zero = jnp.zeros((SUB, W), F32)
    corner = jnp.concatenate(
        [jnp.where(group == 1, gram[0:SUB], 0.0), jnp.where(group == 3, gram[2 * SUB : 3 * SUB], 0.0)], axis=0
    )
    product = dot3(split(corner), base_parts)
    full = jnp.concatenate([product[0:SUB], zero, product[SUB:], zero], axis=0)
    left = jnp.concatenate([parts[0], parts[2]], axis=0)
    change = dot3(split(left), split(full))
    upper = jnp.concatenate([parts[0] - change[0:SUB], parts[1]], axis=0)
    lower = jnp.concatenate([parts[2] - change[SUB:], parts[3]], axis=0)
    half = 2 * SUB
    lane2 = lax.broadcasted_iota(jnp.int32, (half, W), 1)
    corner2 = jnp.where(lane2 >= half, gram[0:half], 0.0)
    stacked = jnp.concatenate([jnp.zeros((half, W), F32), lower], axis=0)
    product2 = dot3(split(corner2), split(stacked))
    stacked2 = jnp.concatenate([product2, jnp.zeros((half, W), F32)], axis=0)
    change2 = dot3(split(upper), split(stacked2))
    return jnp.concatenate([upper - change2, lower], axis=0)


def factor_block(packed, a_ref, v_ref, at):
    reflectors = unpacked(packed)
    rh, rl = split(reflectors)
    nt = ((1,), (1,))
    cross = mm(rh, rl, nt)
    gram = mm(rh, rh, nt) + (cross + mm(rl, rh, nt))
    inverse = triangle_inverse(gram)
    ah, al = split(dot3(split(inverse), (rh, rl)))
    a_ref[at, :, : 2 * W] = ah
    a_ref[at, :, 2 * W :] = al
    vh, vl = split(reflectors.T)
    v_ref[at, :, :W] = vh
    v_ref[at, :, W:] = vl


def factor_kernel(picks, foreign, scalars, *refs):
    pieces = refs[:4]
    rest = refs[4:]
    if foreign:
        other, rest = rest[0], rest[1:]
    a_ref, v_ref, held = rest
    for k in range(4):
        held[(scalars[0] + 4 - k) % 4] = pieces[k][...]
    for at, pick in enumerate(picks):
        packed = other[...] if pick is None else held[scalars[pick]]
        factor_block(packed, a_ref, v_ref, at)


def factor_call(scalars, pieces, picks, other=None):
    count = len(picks)
    args = [scalars, *pieces] + ([] if other is None else [other])
    return pl.pallas_call(
        lambda *refs: factor_kernel(picks, other is not None, *refs),
        out_shape=(
            jax.ShapeDtypeStruct((count, W, 4 * W), BF16),
            jax.ShapeDtypeStruct((count, 2 * W, 2 * W), BF16),
        ),
        in_specs=[pl.BlockSpec(memory_space=SMEM)] + [pl.BlockSpec(memory_space=VMEM)] * (len(args) - 1),
        out_specs=(pl.BlockSpec(memory_space=VMEM),) * 2,
        scratch_shapes=[pltpu.VMEM((4, W, W), F32)],
        compiler_params=pltpu.CompilerParams(vmem_limit_bytes=24 * 1024 * 1024),
        cost_estimate=pl.CostEstimate(flops=count * 100_000_000, bytes_accessed=count * 400_000, transcendentals=0),
        name="factors",
    )(*args)


def applied(x, a_ref, v_ref, at):
    xh, xl = split(x)
    a = a_ref[at]
    z = mm(a[:, : 2 * W], xl) + (mm(a[:, 2 * W :], xh) + mm(a[:, : 2 * W], xh))
    zh, zl = split(z)
    v = v_ref[at]
    return x - (mm(v[:, :W], zl) + (mm(v[:, W:], zh) + mm(v[:, :W], zh)))


def inner(top, low, a_ref, v_ref, at):
    middle = applied(jnp.concatenate([top[W:], low[:W]], axis=0), a_ref, v_ref, at)
    return jnp.concatenate([top[:W], middle[:W]], axis=0), jnp.concatenate([middle[W:], low[W:]], axis=0)


def first_kernel(x_ref, a0, v0, top_ref, low_ref):
    top = applied(x_ref[: 2 * W], a0, v0, 0)
    low = applied(x_ref[2 * W :], a0, v0, 1)
    top, low = inner(top, low, a0, v0, 2)
    top_ref[...] = top
    low_ref[...] = low


def boundary(last, low, below, a_ref, v_ref, at):
    seen = jnp.where(last, 0.0, below[:W])
    middle = applied(jnp.concatenate([low[W:], seen], axis=0), a_ref, v_ref, at)
    low = jnp.concatenate([low[:W], middle[:W]], axis=0)
    return low, jnp.concatenate([jnp.where(last, below[:W], middle[W:]), below[W:]], axis=0)


def boundary_kernel(scalars, low_ref, below_ref, a0, v0, a1, v1, low_out, below_out):
    last = scalars[1] == 1
    low, below = boundary(last, low_ref[...], below_ref[...], a0, v0, 3)
    low = applied(low, a1, v1, 0)
    below = applied(below, a1, v1, 1)
    low, below = boundary(last, low, below, a1, v1, 3)
    low_out[...] = low
    below_out[...] = below


def middle_kernel(low_ref, top_ref, a1, v1, a2, v2, low_out, top_out):
    top, low = inner(top_ref[...], low_ref[...], a1, v1, 2)
    top = applied(top, a2, v2, 0)
    low = applied(low, a2, v2, 1)
    top, low = inner(top, low, a2, v2, 2)
    low_out[...] = low
    top_out[...] = top


def last_kernel(low_ref, top_ref, a3, v3, out_ref):
    top, low = inner(top_ref[...], low_ref[...], a3, v3, 2)
    out_ref[: 2 * W] = top
    out_ref[2 * W :] = low


def apply_call(kernel, args, shapes, smem=0, diamonds=4):
    return pl.pallas_call(
        kernel,
        out_shape=tuple(jax.ShapeDtypeStruct(s, F32) for s in shapes),
        in_specs=[pl.BlockSpec(memory_space=SMEM)] * smem + [pl.BlockSpec(memory_space=VMEM)] * (len(args) - smem),
        out_specs=(pl.BlockSpec(memory_space=VMEM),) * len(shapes),
        compiler_params=pltpu.CompilerParams(vmem_limit_bytes=24 * 1024 * 1024),
        cost_estimate=pl.CostEstimate(flops=diamonds * 100_000_000, bytes_accessed=2_000_000, transcendentals=0),
        name=kernel.__name__,
    )(*args)


def shifted(value, axis, steps):
    count = lax.axis_size(axis)
    return lax.ppermute(value, axis, [(i, (i + steps) % count) for i in range(count)])


def per_device(eigvecs, wy_packed, slot_block):
    slots = slot_block[0]
    column = lax.axis_index("cols")
    plane, place = column // 4, column % 4
    last = (lax.axis_index("rows") == lax.axis_size("rows") - 1).astype(jnp.int32)
    packed = wy_packed[0]

    def along_x(value, k):
        return lax.ppermute(value, "cols", [(i, (i // 4) * 4 + (i + k) % 4) for i in range(16)])

    planes = [packed] + [shifted(packed, "cols", 4 * k) for k in (1, 2, 3)]
    ordered = [lax.select_n((plane + 4 - j) % 4, *planes) for j in range(4)]
    part0 = [ordered[0]] + [along_x(ordered[0], k) for k in (1, 2, 3)]
    part1 = [ordered[1]] + [along_x(ordered[1], k) for k in (1, 2, 3)]
    pair = jnp.stack(ordered[2:])
    pairs = [pair] + [along_x(pair, k) for k in (1, 2, 3)]
    part2 = [p[0] for p in pairs]
    part3 = [p[1] for p in pairs]

    def scalars_of(z):
        own = slots[2 * z : 2 * z + 2] + jnp.array([[0], [2]], jnp.int32)
        return jnp.concatenate([jnp.stack([place, last]), own.reshape(4)])

    scalars = [scalars_of(z) for z in range(4)]

    def for_above(part, z):
        return shifted(lax.select_n((place + 4 - slots[2 * z, 0]) % 4, *part), "rows", -1)

    half = (2 * W, eigvecs.shape[1])
    a0, v0 = factor_call(scalars[0], part0, (2, 3, 4, 5))
    top, low = apply_call(first_kernel, (eigvecs, a0, v0), (half, half), diamonds=3)
    below = shifted(top, "rows", -1)
    a1, v1 = factor_call(scalars[1], part1, (3, None, 4, 5), for_above(part1, 1))
    low, below = apply_call(boundary_kernel, (scalars[0], low, below, a0, v0, a1, v1), (half, half), smem=1)
    top = shifted(below, "rows", 1)
    a2, v2 = factor_call(scalars[2], part2, (2, 3, 4, 5))
    low, top = apply_call(middle_kernel, (low, top, a1, v1, a2, v2), (half, half))
    below = shifted(top, "rows", -1)
    a3, v3 = factor_call(scalars[3], part3, (3, None, 4, 5), for_above(part3, 3))
    low, below = apply_call(boundary_kernel, (scalars[0], low, below, a2, v2, a3, v3), (half, half), smem=1)
    top = shifted(below, "rows", 1)
    return apply_call(last_kernel, (low, top, a3, v3), (eigvecs.shape,), diamonds=1)[0]


def solution(mesh):
    placed = (P("rows", "cols"), P(("rows", "cols"), None, None), P("rows", None, None))
    return jax.shard_map(
        per_device, mesh=mesh, in_specs=placed, out_specs=P("rows", "cols"), check_vma=False
    )
```

time: 146 us -> 86.9 us (0.60)
  the two profiles are of different devices: /device:TPU:56 before, /device:TPU:0 now
where the time goes in v1:
time: 86.9 us; the launch traced here: 86.7 us
  starting transfers between devices  33.8 us (39%)
  Pallas kernels  29.6 us (34%)
  waiting for transfers between devices  19.3 us (22%)
  local copies, waits for them, and re-layouts  2.3 us (3%)
  between operations  1.57 us (2%)
    pallas_call x4, Pallas kernels, factor_call(): pl.pallas_call(lambda *refs: factor_kernel(picks, other is not None, *ref...  22.2 us
    ppermute x9, waiting for transfers between devices, shifted(): lax.ppermute(value, axis, [(i, (i + steps) % count) for i in range(count)])  19.2 us
    ppermute x9, starting transfers between devices, shifted(): lax.ppermute(value, axis, [(i, (i + steps) % count) for i in range(count)])  19.1 us
    ppermute x9, starting transfers between devices, along_x(): lax.ppermute(value, 'cols', [(i, i // 4 * 4 + (i + k) % 4) for i in range...  14.7 us
    pallas_call x5, Pallas kernels, apply_call(): pl.pallas_call(kernel, out_shape=tuple((jax.ShapeDtypeStruct(s, F32) for...  7.43 us
  transfers between devices with their start and end apart: 18, of which 5 were waited for; matrix products, arithmetic and copies ran while one was open for 2% of the time, Pallas kernels for 29%

profile of v1, /device:TPU:0, one launch (start us, length us, event | category | flops | bytes accessed | tf_op | source)
XLA Modules:
  0.0 86.7 jit_solution(16006102238548332970)
XLA Ops:
  0.0 1.5 %collective-permute-start.1 = (f32[128,128]{1,0:T(8,128)}, f32[128,128]{1,0:T(8,128)S(1)}, u32[]{:S(2)}, u32[]{:S(2)}) collective-permute-start(f32[128,128]{1,0:T(8,128)} %bitcast.32), channel_id=1, source_target_pairs={{0,8},{1,9},{2,10},{3,11},{4,12},{5,13},{6,14},{7,15},{8,0},{9,1},... | collective-permute-start | bytes 196616 | tf_op jit(solution)/shard_map/ppermute | solution.py:207
  1.5 1.4 %collective-permute-start.2 = (f32[128,128]{1,0:T(8,128)}, f32[128,128]{1,0:T(8,128)S(1)}, u32[]{:S(2)}, u32[]{:S(2)}) collective-permute-start(f32[128,128]{1,0:T(8,128)} %bitcast.33), channel_id=1, source_target_pairs={{0,12},{1,13},{2,14},{3,15},{4,0},{5,1},{6,2},{7,3},{8,4},{9,5},{1... | collective-permute-start | bytes 196616 | tf_op jit(solution)/shard_map/ppermute | solution.py:207
  2.9 0.7 collective-permute-start
  3.6 0.0 copy-start.2
  3.6 0.7 copy-done.2
  4.2 0.1 fusion.1
  4.3 0.1 copy.10
  4.4 0.1 slice.54
  4.5 0.1 add.96
  4.6 0.0 copy-start.1
  4.6 0.1 add.97
  4.7 0.1 copy.11
  4.7 0.1 slice.59
  4.8 0.1 copy.9
  4.9 0.1 slice.51
  5.0 0.1 copy.8
  5.1 0.1 slice.49
  5.2 0.1 pad_add_fusion.4
  5.3 0.1 pad_add_fusion.3
  5.3 0.7 fusion
  7.4 0.0 collective-permute-done.1
  7.4 0.0 collective-permute-done.2
  7.4 1.8 %collective-permute-done = f32[128,128]{1,0:T(8,128)S(1)} collective-permute-done((f32[128,128]{1,0:T(8,128)}, f32[128,128]{1,0:T(8,128)S(1)}, u32[]{:S(2)}, u32[]{:S(2)}) %collective-permute-start) | collective-permute-done | bytes 65568 | tf_op jit(solution)/shard_map/ppermute | solution.py:207
  9.2 0.0 copy-done.1
  9.2 1.6 %collective-permute-start.3 = (f32[128,128]{1,0:T(8,128)S(1)}, f32[128,128]{1,0:T(8,128)S(1)}, u32[]{:S(2)}, u32[]{:S(2)}) collective-permute-start(f32[128,128]{1,0:T(8,128)S(1)} %get-tuple-element.42.refs_1_), channel_id=1, source_target_pairs={{0,1},{1,2},{2,3},{3,0},{4,5},{5,6},{6,7},{7,4},{8,9},{9,10},{10,1... | collective-permute-start | bytes 196616 | tf_op jit(solution)/shard_map/ppermute | solution.py:218
  10.8 2.7 %collective-permute-start.4 = (f32[128,128]{1,0:T(8,128)S(1)}, f32[128,128]{1,0:T(8,128)S(1)}, u32[]{:S(2)}, u32[]{:S(2)}) collective-permute-start(f32[128,128]{1,0:T(8,128)S(1)} %get-tuple-element.42.refs_1_), channel_id=1, source_target_pairs={{0,2},{1,3},{2,0},{3,1},{4,6},{5,7},{6,4},{7,5},{8,10},{9,11},{10,... | collective-permute-start | bytes 196616 | tf_op jit(solution)/shard_map/ppermute | solution.py:218
  13.5 1.4 %collective-permute-start.5 = (f32[128,128]{1,0:T(8,128)S(1)}, f32[128,128]{1,0:T(8,128)S(1)}, u32[]{:S(2)}, u32[]{:S(2)}) collective-permute-start(f32[128,128]{1,0:T(8,128)S(1)} %get-tuple-element.42.refs_1_), channel_id=1, source_target_pairs={{0,3},{1,0},{2,1},{3,2},{4,7},{5,4},{6,5},{7,6},{8,11},{9,8},{10,9... | collective-permute-start | bytes 196616 | tf_op jit(solution)/shard_map/ppermute | solution.py:218
  14.9 0.6 collective-permute-start.7
  15.6 0.8 collective-permute-start.8
  16.4 0.0 collective-permute-done.3.refs_2_
  16.4 1.9 %collective-permute-start.9 = (f32[128,128]{1,0:T(8,128)S(1)}, f32[128,128]{1,0:T(8,128)S(1)}, u32[]{:S(2)}, u32[]{:S(2)}) collective-permute-start(f32[128,128]{1,0:T(8,128)S(1)} %get-tuple-element.41.refs_1_), channel_id=1, source_target_pairs={{0,3},{1,0},{2,1},{3,2},{4,7},{5,4},{6,5},{7,6},{8,11},{9,8},{10,9... | collective-permute-start | bytes 196616 | tf_op jit(solution)/shard_map/ppermute | solution.py:218
  18.3 0.0 collective-permute-done.4.refs_3_
  18.3 0.9 %collective-permute-start.12 = (f32[2,128,128]{2,1,0:T(8,128)S(1)}, f32[2,128,128]{2,1,0:T(8,128)S(1)}, u32[]{:S(2)}, u32[]{:S(2)}) collective-permute-start(f32[2,128,128]{2,1,0:T(8,128)S(1)} %pad_maximum_fusion), channel_id=1, source_target_pairs={{0,1},{1,2},{2,3},{3,0},{4,5},{5,6},{6,7},{7,4},{8,9},{9,10},{10,1... | collective-permute-start | bytes 393224 | tf_op jit(solution)/shard_map/ppermute | solution.py:218
  19.2 0.0 collective-permute-done.5.refs_4_
  19.2 2.1 %collective-permute-start.13 = (f32[2,128,128]{2,1,0:T(8,128)S(1)}, f32[2,128,128]{2,1,0:T(8,128)S(1)}, u32[]{:S(2)}, u32[]{:S(2)}) collective-permute-start(f32[2,128,128]{2,1,0:T(8,128)S(1)} %pad_maximum_fusion), channel_id=1, source_target_pairs={{0,2},{1,3},{2,0},{3,1},{4,6},{5,7},{6,4},{7,5},{8,10},{9,11},{10,... | collective-permute-start | bytes 393224 | tf_op jit(solution)/shard_map/ppermute | solution.py:218
  21.3 5.5 %factors.4 = (bf16[4,128,512]{2,1,0:T(8,128)(2,1)S(1)}, bf16[4,256,256]{2,1,0:T(8,128)(2,1)S(1)}) custom-call(s32[6]{0:T(128)S(1)} %get-tuple-element.57.refs_0_.scalars, f32[128,128]{1,0:T(8,128)S(1)} %get-tuple-element.42.refs_1_, f32[128,128]{1,0:T(8,128)S(1)} %collective-permute-done.3.refs_2_, f32[128,128]{1,0:T(8,128)S(1)} %collective-permute-done.4.refs_3_, ...), custom_call_target="tpu_custom_call" | custom-call | flops 400000000 | bytes 1600000 | tf_op jit(solution)/shard_map/factors/pallas_call | solution.py:124
  26.9 0.0 copy-done
  26.9 1.0 %first_kernel.1 = (f32[256,128]{1,0:T(8,128)S(1)}, f32[256,128]{1,0:T(8,128)S(1)}) custom-call(f32[512,128]{1,0:T(8,128)S(1)} %copy-done, bf16[4,128,512]{2,1,0:T(8,128)(2,1)S(1)} %get-tuple-element.21.a0, bf16[4,256,256]{2,1,0:T(8,128)(2,1)S(1)} %get-tuple-element.22.v0), custom_call_target="tpu_custom_call" | custom-call | flops 300000000 | bytes 2000000 | tf_op jit(solution)/shard_map/first_kernel/pallas_call | solution.py:194
  27.9 0.0 collective-permute-done.7.refs_2_
  27.9 2.6 %collective-permute-start.14 = (f32[2,128,128]{2,1,0:T(8,128)S(1)}, f32[2,128,128]{2,1,0:T(8,128)S(1)}, u32[]{:S(2)}, u32[]{:S(2)}) collective-permute-start(f32[2,128,128]{2,1,0:T(8,128)S(1)} %pad_maximum_fusion), channel_id=1, source_target_pairs={{0,3},{1,0},{2,1},{3,2},{4,7},{5,4},{6,5},{7,6},{8,11},{9,8},{10,9... | collective-permute-start | bytes 393224 | tf_op jit(solution)/shard_map/ppermute | solution.py:218
  30.5 0.0 collective-permute-done.8.refs_3_
  30.5 3.7 %collective-permute-start.6 = (f32[256,128]{1,0:T(8,128)S(1)}, f32[256,128]{1,0:T(8,128)S(1)}, u32[]{:S(2)}, u32[]{:S(2)}) collective-permute-start(f32[256,128]{1,0:T(8,128)S(1)} %get-tuple-element.24), channel_id=1, source_target_pairs={{0,240},{16,0},{32,16},{48,32},{64,48},{80,64},{96,80},{112,96},{1... | collective-permute-start | bytes 393224 | tf_op jit(solution)/shard_map/ppermute | solution.py:207
  34.2 0.0 collective-permute-done.9.refs_4_
  34.2 4.9 %collective-permute-start.10 = (f32[128,128]{1,0:T(8,128)S(1)}, f32[128,128]{1,0:T(8,128)S(1)}, u32[]{:S(2)}, u32[]{:S(2)}) collective-permute-start(f32[128,128]{1,0:T(8,128)S(1)} %select_select_fusion.3), channel_id=1, source_target_pairs={{0,240},{16,0},{32,16},{48,32},{64,48},{80,64},{96,80},{112,96},{1... | collective-permute-start | bytes 196616 | tf_op jit(solution)/shard_map/ppermute | solution.py:207
  39.1 0.0 collective-permute-done.12
  39.1 0.0 collective-permute-done.13
  39.1 1.9 %collective-permute-done.10.refs_5_ = f32[128,128]{1,0:T(8,128)S(1)} collective-permute-done((f32[128,128]{1,0:T(8,128)S(1)}, f32[128,128]{1,0:T(8,128)S(1)}, u32[]{:S(2)}, u32[]{:S(2)}) %collective-permute-start.10) | collective-permute-done | bytes 65568 | tf_op jit(solution)/shard_map/ppermute | solution.py:207
  41.0 5.5 %factors.5 = (bf16[4,128,512]{2,1,0:T(8,128)(2,1)S(1)}, bf16[4,256,256]{2,1,0:T(8,128)(2,1)S(1)}) custom-call(s32[6]{0:T(128)S(1)} %get-tuple-element.56.refs_0_, f32[128,128]{1,0:T(8,128)S(1)} %get-tuple-element.41.refs_1_, f32[128,128]{1,0:T(8,128)S(1)} %collective-permute-done.7.refs_2_, f32[128,128]{1,0:T(8,128)S(1)} %collective-permute-done.8.refs_3_, ...), custom_call_target="tpu_custom_call" | custom-call | flops 400000000 | bytes 1600000 | tf_op jit(solution)/shard_map/factors/pallas_call | solution.py:124
  46.6 0.0 collective-permute-done.6.below_ref
  46.6 1.9 %boundary_kernel.2 = (f32[256,128]{1,0:T(8,128)S(1)}, f32[256,128]{1,0:T(8,128)S(1)}) custom-call(s32[6]{0:T(128)S(1)} %get-tuple-element.57.refs_0_.scalars, f32[256,128]{1,0:T(8,128)S(1)} %get-tuple-element.23.low_ref, f32[256,128]{1,0:T(8,128)S(1)} %collective-permute-done.6.below_ref, bf16[4,128,512]{2,1,0:T(8,128)(2,1)S(1)} %get-tuple-element.21.a0, ...), custom_call_target="tpu_custom_call" | custom-call | flops 400000000 | bytes 2000000 | tf_op jit(solution)/shard_map/boundary_kernel/pallas_call | solution.py:194
  48.5 0.1 collective-permute-start.11
  48.6 0.0 collective-permute-done.14
  48.6 5.6 %factors.6 = (bf16[4,128,512]{2,1,0:T(8,128)(2,1)S(1)}, bf16[4,256,256]{2,1,0:T(8,128)(2,1)S(1)}) custom-call(s32[6]{0:T(128)S(1)} %get-tuple-element.55.refs_0_, f32[128,128]{1,0:T(8,128)S(1)} %get-tuple-element.40.refs_1_, f32[128,128]{1,0:T(8,128)S(1)} %get-tuple-element.48.refs_2_, f32[128,128]{1,0:T(8,128)S(1)} %get-tuple-element.46.refs_3_, ...), custom_call_target="tpu_custom_call" | custom-call | flops 400000000 | bytes 1600000 | tf_op jit(solution)/shard_map/factors/pallas_call | solution.py:124
  54.2 4.8 %collective-permute-done.11.top_ref = f32[256,128]{1,0:T(8,128)S(1)} collective-permute-done((f32[256,128]{1,0:T(8,128)S(1)}, f32[256,128]{1,0:T(8,128)S(1)}, u32[]{:S(2)}, u32[]{:S(2)}) %collective-permute-start.11) | collective-permute-done | bytes 131104 | tf_op jit(solution)/shard_map/ppermute | solution.py:207
  59.1 1.4 %middle_kernel.1 = (f32[256,128]{1,0:T(8,128)S(1)}, f32[256,128]{1,0:T(8,128)S(1)}) custom-call(f32[256,128]{1,0:T(8,128)S(1)} %get-tuple-element.27.low_ref, f32[256,128]{1,0:T(8,128)S(1)} %collective-permute-done.11.top_ref, bf16[4,128,512]{2,1,0:T(8,128)(2,1)S(1)} %get-tuple-element.25.a1, bf16[4,256,256]{2,1,0:T(8,128)(2,1)S(1)} %get-tuple-element.26.v1, ...), custom_call_target="tpu_custom_call" | custom-call | flops 400000000 | bytes 2000000 | tf_op jit(solution)/shard_map/middle_kernel/pallas_call | solution.py:194
  60.5 3.0 %collective-permute-start.15 = (f32[256,128]{1,0:T(8,128)S(1)}, f32[256,128]{1,0:T(8,128)S(1)}, u32[]{:S(2)}, u32[]{:S(2)}) collective-permute-start(f32[256,128]{1,0:T(8,128)S(1)} %get-tuple-element.32), channel_id=1, source_target_pairs={{0,240},{16,0},{32,16},{48,32},{64,48},{80,64},{96,80},{112,96},{1... | collective-permute-start | bytes 393224 | tf_op jit(solution)/shard_map/ppermute | solution.py:207
  63.5 0.6 collective-permute-start.16
  64.1 3.3 %collective-permute-done.16.refs_5_ = f32[128,128]{1,0:T(8,128)S(1)} collective-permute-done((f32[128,128]{1,0:T(8,128)S(1)}, f32[128,128]{1,0:T(8,128)S(1)}, u32[]{:S(2)}, u32[]{:S(2)}) %collective-permute-start.16) | collective-permute-done | bytes 65568 | tf_op jit(solution)/shard_map/ppermute | solution.py:207
  67.4 5.5 %factors.7 = (bf16[4,128,512]{2,1,0:T(8,128)(2,1)S(1)}, bf16[4,256,256]{2,1,0:T(8,128)(2,1)S(1)}) custom-call(s32[6]{0:T(128)S(1)} %get-tuple-element.37.refs_0_, f32[128,128]{1,0:T(8,128)S(1)} %get-tuple-element.39.refs_1_, f32[128,128]{1,0:T(8,128)S(1)} %get-tuple-element.47.refs_2_, f32[128,128]{1,0:T(8,128)S(1)} %get-tuple-element.45.refs_3_, ...), custom_call_target="tpu_custom_call" | custom-call | flops 400000000 | bytes 1600000 | tf_op jit(solution)/shard_map/factors/pallas_call | solution.py:124
  72.9 0.0 collective-permute-done.15.below_ref
  72.9 1.9 %boundary_kernel.3 = (f32[256,128]{1,0:T(8,128)S(1)}, f32[256,128]{1,0:T(8,128)S(1)}) custom-call(s32[6]{0:T(128)S(1)} %get-tuple-element.57.refs_0_.scalars, f32[256,128]{1,0:T(8,128)S(1)} %get-tuple-element.31.low_ref, f32[256,128]{1,0:T(8,128)S(1)} %collective-permute-done.15.below_ref, bf16[4,128,512]{2,1,0:T(8,128)(2,1)S(1)} %get-tuple-element.29.a2.a0, ...), custom_call_target="tpu_custom_call" | custom-call | flops 400000000 | bytes 2000000 | tf_op jit(solution)/shard_map/boundary_kernel/pallas_call | solution.py:194
  74.9 3.3 %collective-permute-start.17 = (f32[256,128]{1,0:T(8,128)S(1)}, f32[256,128]{1,0:T(8,128)S(1)}, u32[]{:S(2)}, u32[]{:S(2)}) collective-permute-start(f32[256,128]{1,0:T(8,128)S(1)} %get-tuple-element.36), channel_id=1, source_target_pairs={{0,16},{16,32},{32,48},{48,64},{64,80},{80,96},{96,112},{112,128},... | collective-permute-start | bytes 393224 | tf_op jit(solution)/shard_map/ppermute | solution.py:207
  78.2 7.4 %collective-permute-done.17.top_ref = f32[256,128]{1,0:T(8,128)S(1)} collective-permute-done((f32[256,128]{1,0:T(8,128)S(1)}, f32[256,128]{1,0:T(8,128)S(1)}, u32[]{:S(2)}, u32[]{:S(2)}) %collective-permute-start.17) | collective-permute-done | bytes 131104 | tf_op jit(solution)/shard_map/ppermute | solution.py:207
  85.6 1.2 %last_kernel.1 = f32[512,128]{1,0:T(8,128)} custom-call(f32[256,128]{1,0:T(8,128)S(1)} %get-tuple-element.35.low_ref, f32[256,128]{1,0:T(8,128)S(1)} %collective-permute-done.17.top_ref, bf16[4,128,512]{2,1,0:T(8,128)(2,1)S(1)} %get-tuple-element.33.a1.a3, bf16[4,256,256]{2,1,0:T(8,128)(2,1)S(1)} %get-tuple-element.34.v1.v3), custom_call_target="tpu_custom_call" | custom-call | flops 100000000 | bytes 2000000 | tf_op jit(solution)/shard_map/last_kernel/pallas_call | solution.py:194
  (10 shorter events, 0.1 us)
Async XLA Ops:
  0.0 7.4 %collective-permute-start.1 = (f32[128,128]{1,0:T(8,128)}, f32[128,128]{1,0:T(8,128)S(1)}, u32[]{:S(2)}, u32[]{:S(2)}) collective-permute-start(f32[128,128]{1,0:T(8,128)} %bitcast.32), channel_id=1, source_target_pairs={{0,8},{1,9},{2,10},{3,11},{4,12},{5,13},{6,14},{7,15},{8,0},{9,1},... | collective-permute-start | bytes 196616 | tf_op jit(solution)/shard_map/ppermute | solution.py:207
  1.5 5.9 %collective-permute-start.2 = (f32[128,128]{1,0:T(8,128)}, f32[128,128]{1,0:T(8,128)S(1)}, u32[]{:S(2)}, u32[]{:S(2)}) collective-permute-start(f32[128,128]{1,0:T(8,128)} %bitcast.33), channel_id=1, source_target_pairs={{0,12},{1,13},{2,14},{3,15},{4,0},{5,1},{6,2},{7,3},{8,4},{9,5},{1... | collective-permute-start | bytes 196616 | tf_op jit(solution)/shard_map/ppermute | solution.py:207
  2.9 6.3 %collective-permute-start = (f32[128,128]{1,0:T(8,128)}, f32[128,128]{1,0:T(8,128)S(1)}, u32[]{:S(2)}, u32[]{:S(2)}) collective-permute-start(f32[128,128]{1,0:T(8,128)} %bitcast.34), channel_id=1, source_target_pairs={{0,4},{1,5},{2,6},{3,7},{4,8},{5,9},{6,10},{7,11},{8,12},{9,13},{1... | collective-permute-start | bytes 196616 | tf_op jit(solution)/shard_map/ppermute | solution.py:207
  3.6 0.7 copy-start.2
  4.6 4.6 %copy-start.1 = (f32[1,128,128]{2,1,0:T(8,128)S(1)}, f32[1,128,128]{2,1,0:T(8,128)}, u32[]{:S(2)}) copy-start(f32[1,128,128]{2,1,0:T(8,128)} %param.8) | copy-start | bytes 196612
  9.2 7.2 %collective-permute-start.3 = (f32[128,128]{1,0:T(8,128)S(1)}, f32[128,128]{1,0:T(8,128)S(1)}, u32[]{:S(2)}, u32[]{:S(2)}) collective-permute-start(f32[128,128]{1,0:T(8,128)S(1)} %get-tuple-element.42.refs_1_), channel_id=1, source_target_pairs={{0,1},{1,2},{2,3},{3,0},{4,5},{5,6},{6,7},{7,4},{8,9},{9,10},{10,1... | collective-permute-start | bytes 196616 | tf_op jit(solution)/shard_map/ppermute | solution.py:218
  10.8 7.6 %collective-permute-start.4 = (f32[128,128]{1,0:T(8,128)S(1)}, f32[128,128]{1,0:T(8,128)S(1)}, u32[]{:S(2)}, u32[]{:S(2)}) collective-permute-start(f32[128,128]{1,0:T(8,128)S(1)} %get-tuple-element.42.refs_1_), channel_id=1, source_target_pairs={{0,2},{1,3},{2,0},{3,1},{4,6},{5,7},{6,4},{7,5},{8,10},{9,11},{10,... | collective-permute-start | bytes 196616 | tf_op jit(solution)/shard_map/ppermute | solution.py:218
  13.5 5.7 %collective-permute-start.5 = (f32[128,128]{1,0:T(8,128)S(1)}, f32[128,128]{1,0:T(8,128)S(1)}, u32[]{:S(2)}, u32[]{:S(2)}) collective-permute-start(f32[128,128]{1,0:T(8,128)S(1)} %get-tuple-element.42.refs_1_), channel_id=1, source_target_pairs={{0,3},{1,0},{2,1},{3,2},{4,7},{5,4},{6,5},{7,6},{8,11},{9,8},{10,9... | collective-permute-start | bytes 196616 | tf_op jit(solution)/shard_map/ppermute | solution.py:218
  14.9 12.9 %collective-permute-start.7 = (f32[128,128]{1,0:T(8,128)S(1)}, f32[128,128]{1,0:T(8,128)S(1)}, u32[]{:S(2)}, u32[]{:S(2)}) collective-permute-start(f32[128,128]{1,0:T(8,128)S(1)} %get-tuple-element.41.refs_1_), channel_id=1, source_target_pairs={{0,1},{1,2},{2,3},{3,0},{4,5},{5,6},{6,7},{7,4},{8,9},{9,10},{10,1... | collective-permute-start | bytes 196616 | tf_op jit(solution)/shard_map/ppermute | solution.py:218
  15.6 14.9 %collective-permute-start.8 = (f32[128,128]{1,0:T(8,128)S(1)}, f32[128,128]{1,0:T(8,128)S(1)}, u32[]{:S(2)}, u32[]{:S(2)}) collective-permute-start(f32[128,128]{1,0:T(8,128)S(1)} %get-tuple-element.41.refs_1_), channel_id=1, source_target_pairs={{0,2},{1,3},{2,0},{3,1},{4,6},{5,7},{6,4},{7,5},{8,10},{9,11},{10,... | collective-permute-start | bytes 196616 | tf_op jit(solution)/shard_map/ppermute | solution.py:218
  16.4 17.8 %collective-permute-start.9 = (f32[128,128]{1,0:T(8,128)S(1)}, f32[128,128]{1,0:T(8,128)S(1)}, u32[]{:S(2)}, u32[]{:S(2)}) collective-permute-start(f32[128,128]{1,0:T(8,128)S(1)} %get-tuple-element.41.refs_1_), channel_id=1, source_target_pairs={{0,3},{1,0},{2,1},{3,2},{4,7},{5,4},{6,5},{7,6},{8,11},{9,8},{10,9... | collective-permute-start | bytes 196616 | tf_op jit(solution)/shard_map/ppermute | solution.py:218
  18.3 20.7 %collective-permute-start.12 = (f32[2,128,128]{2,1,0:T(8,128)S(1)}, f32[2,128,128]{2,1,0:T(8,128)S(1)}, u32[]{:S(2)}, u32[]{:S(2)}) collective-permute-start(f32[2,128,128]{2,1,0:T(8,128)S(1)} %pad_maximum_fusion), channel_id=1, source_target_pairs={{0,1},{1,2},{2,3},{3,0},{4,5},{5,6},{6,7},{7,4},{8,9},{9,10},{10,1... | collective-permute-start | bytes 393224 | tf_op jit(solution)/shard_map/ppermute | solution.py:218
  19.2 19.9 %collective-permute-start.13 = (f32[2,128,128]{2,1,0:T(8,128)S(1)}, f32[2,128,128]{2,1,0:T(8,128)S(1)}, u32[]{:S(2)}, u32[]{:S(2)}) collective-permute-start(f32[2,128,128]{2,1,0:T(8,128)S(1)} %pad_maximum_fusion), channel_id=1, source_target_pairs={{0,2},{1,3},{2,0},{3,1},{4,6},{5,7},{6,4},{7,5},{8,10},{9,11},{10,... | collective-permute-start | bytes 393224 | tf_op jit(solution)/shard_map/ppermute | solution.py:218
  21.3 5.6 %copy-start = (f32[512,128]{1,0:T(8,128)S(1)}, f32[512,128]{1,0:T(8,128)}, u32[]{:S(2)}) copy-start(f32[512,128]{1,0:T(8,128)} %x_ref.1) | copy-start | bytes 786436
  27.9 20.8 %collective-permute-start.14 = (f32[2,128,128]{2,1,0:T(8,128)S(1)}, f32[2,128,128]{2,1,0:T(8,128)S(1)}, u32[]{:S(2)}, u32[]{:S(2)}) collective-permute-start(f32[2,128,128]{2,1,0:T(8,128)S(1)} %pad_maximum_fusion), channel_id=1, source_target_pairs={{0,3},{1,0},{2,1},{3,2},{4,7},{5,4},{6,5},{7,6},{8,11},{9,8},{10,9... | collective-permute-start | bytes 393224 | tf_op jit(solution)/shard_map/ppermute | solution.py:218
  30.5 16.1 %collective-permute-start.6 = (f32[256,128]{1,0:T(8,128)S(1)}, f32[256,128]{1,0:T(8,128)S(1)}, u32[]{:S(2)}, u32[]{:S(2)}) collective-permute-start(f32[256,128]{1,0:T(8,128)S(1)} %get-tuple-element.24), channel_id=1, source_target_pairs={{0,240},{16,0},{32,16},{48,32},{64,48},{80,64},{96,80},{112,96},{1... | collective-permute-start | bytes 393224 | tf_op jit(solution)/shard_map/ppermute | solution.py:207
  34.2 6.8 %collective-permute-start.10 = (f32[128,128]{1,0:T(8,128)S(1)}, f32[128,128]{1,0:T(8,128)S(1)}, u32[]{:S(2)}, u32[]{:S(2)}) collective-permute-start(f32[128,128]{1,0:T(8,128)S(1)} %select_select_fusion.3), channel_id=1, source_target_pairs={{0,240},{16,0},{32,16},{48,32},{64,48},{80,64},{96,80},{112,96},{1... | collective-permute-start | bytes 196616 | tf_op jit(solution)/shard_map/ppermute | solution.py:207
  48.5 10.5 %collective-permute-start.11 = (f32[256,128]{1,0:T(8,128)S(1)}, f32[256,128]{1,0:T(8,128)S(1)}, u32[]{:S(2)}, u32[]{:S(2)}) collective-permute-start(f32[256,128]{1,0:T(8,128)S(1)} %get-tuple-element.28), channel_id=1, source_target_pairs={{0,16},{16,32},{32,48},{48,64},{64,80},{80,96},{96,112},{112,128},... | collective-permute-start | bytes 393224 | tf_op jit(solution)/shard_map/ppermute | solution.py:207
  60.5 12.5 %collective-permute-start.15 = (f32[256,128]{1,0:T(8,128)S(1)}, f32[256,128]{1,0:T(8,128)S(1)}, u32[]{:S(2)}, u32[]{:S(2)}) collective-permute-start(f32[256,128]{1,0:T(8,128)S(1)} %get-tuple-element.32), channel_id=1, source_target_pairs={{0,240},{16,0},{32,16},{48,32},{64,48},{80,64},{96,80},{112,96},{1... | collective-permute-start | bytes 393224 | tf_op jit(solution)/shard_map/ppermute | solution.py:207
  63.5 3.9 %collective-permute-start.16 = (f32[128,128]{1,0:T(8,128)S(1)}, f32[128,128]{1,0:T(8,128)S(1)}, u32[]{:S(2)}, u32[]{:S(2)}) collective-permute-start(f32[128,128]{1,0:T(8,128)S(1)} %select_select_fusion), channel_id=1, source_target_pairs={{0,240},{16,0},{32,16},{48,32},{64,48},{80,64},{96,80},{112,96},{1... | collective-permute-start | bytes 196616 | tf_op jit(solution)/shard_map/ppermute | solution.py:207
  74.9 10.7 %collective-permute-start.17 = (f32[256,128]{1,0:T(8,128)S(1)}, f32[256,128]{1,0:T(8,128)S(1)}, u32[]{:S(2)}, u32[]{:S(2)}) collective-permute-start(f32[256,128]{1,0:T(8,128)S(1)} %get-tuple-element.36), channel_id=1, source_target_pairs={{0,16},{16,32},{32,48},{48,64},{64,80},{80,96},{96,112},{112,128},... | collective-permute-start | bytes 393224 | tf_op jit(solution)/shard_map/ppermute | solution.py:207

commit v2 on v1

v2 whole, which is shorter than its diff:
```python
import jax
import jax.numpy as jnp
from jax import lax
from jax.experimental import pallas as pl
from jax.experimental.pallas import tpu as pltpu
from jax.sharding import PartitionSpec as P

F32 = jnp.float32
BF16 = jnp.bfloat16
W = 128
SUB = 32
VMEM = pltpu.VMEM
SMEM = pltpu.SMEM


def split(x):
    high = x.astype(BF16)
    low = (x - high.astype(F32)).astype(BF16)
    return high, low


def mm(a, b, dims=((1,), (0,))):
    return lax.dot_general(a, b, (dims, ((), ())), preferred_element_type=F32)


def dot3(a, b):
    ah, al = a
    bh, bl = b
    return mm(ah, bh) + (mm(ah, bl) + mm(al, bh))


def unpacked(packed):
    wide = jnp.concatenate([packed.T, jnp.zeros((W, W), F32)], axis=1)
    return pltpu.roll(wide, 0, axis=1, stride=1, stride_axis=0)


def diagonal_inverses(grams):
    row = lax.broadcasted_iota(jnp.int32, (SUB, W), 0)
    lane = lax.broadcasted_iota(jnp.int32, (SUB, W), 1)
    group = lane // SUB
    place = lane % SUB
    base = group * SUB

    def prepared(gram):
        compact = gram[0:SUB]
        for d in range(1, 4):
            compact = jnp.where(group == d, gram[d * SUB : (d + 1) * SUB], compact)
        diagonal = jnp.sum(jnp.where(row == place, compact, 0.0), axis=0, keepdims=True)
        scale = jnp.broadcast_to(2.0 / diagonal, (SUB, W))
        return jnp.where(row < place, compact * scale, 0.0), scale

    pairs = [prepared(gram) for gram in grams]
    start = [jnp.where(row == place, 1.0, 0.0)[8 * i : 8 * i + 8] for i in range(4)]
    rows = [list(start) for _ in grams]
    for k in range(SUB - 1, 0, -1):
        tile, at = k // 8, k % 8
        for n in range(len(grams)):
            pivot = jnp.broadcast_to(rows[n][tile][at : at + 1], (8, W))
            for i in range(tile + 1):
                if i * 8 < k:
                    factor = jnp.take_along_axis(
                        pairs[n][0][8 * i : 8 * i + 8], base[8 * i : 8 * i + 8] + k, axis=1, mode="promise_in_bounds"
                    )
                    rows[n][i] = rows[n][i] - factor * pivot
    row_scales = [jnp.take_along_axis(scale, base + row, axis=1, mode="promise_in_bounds") for _, scale in pairs]
    return [jnp.concatenate(r, axis=0) * s for r, s in zip(rows, row_scales)]


def dots3(lefts, rights):
    return [dot3(a, b) for a, b in zip(lefts, rights)]


def splits(values):
    return [split(v) for v in values]


def triangle_inverses(grams):
    small = diagonal_inverses(grams)
    lane = lax.broadcasted_iota(jnp.int32, (SUB, W), 1)
    group = lane // SUB
    half = 2 * SUB
    zero = jnp.zeros((SUB, W), F32)
    zeros = jnp.zeros((half, W), F32)
    parts = [[jnp.where(group == d, s, 0.0) for d in range(4)] for s in small]
    bases = splits([jnp.concatenate(p, axis=0) for p in parts])
    corners = splits(
        [
            jnp.concatenate(
                [jnp.where(group == 1, g[0:SUB], 0.0), jnp.where(group == 3, g[2 * SUB : 3 * SUB], 0.0)], axis=0
            )
            for g in grams
        ]
    )
    lane2 = lax.broadcasted_iota(jnp.int32, (half, W), 1)
    corners2 = splits([jnp.where(lane2 >= half, g[0:half], 0.0) for g in grams])
    products = dots3(corners, bases)
    fulls = splits([jnp.concatenate([p[0:SUB], zero, p[SUB:], zero], axis=0) for p in products])
    changes = dots3(splits([jnp.concatenate([p[0], p[2]], axis=0) for p in parts]), fulls)
    uppers = [jnp.concatenate([p[0] - c[0:SUB], p[1]], axis=0) for p, c in zip(parts, changes)]
    lowers = [jnp.concatenate([p[2] - c[SUB:], p[3]], axis=0) for p, c in zip(parts, changes)]
    products = dots3(corners2, splits([jnp.concatenate([zeros, low], axis=0) for low in lowers]))
    changes = dots3(splits(uppers), splits([jnp.concatenate([p, zeros], axis=0) for p in products]))
    return [jnp.concatenate([u - c, low], axis=0) for u, c, low in zip(uppers, changes, lowers)]


def factor_blocks(packed, a_ref, v_ref):
    reflectors = [unpacked(p) for p in packed]
    halves = splits(reflectors)
    nt = ((1,), (1,))
    grams = [mm(h, h, nt) + (mm(h, l, nt) + mm(l, h, nt)) for h, l in halves]
    for at, r in enumerate(reflectors):
        vh, vl = split(r.T)
        v_ref[at, :, :W] = vh
        v_ref[at, :, W:] = vl
    inverses = splits(triangle_inverses(grams))
    for at, a in enumerate(dots3(inverses, halves)):
        ah, al = split(a)
        a_ref[at, :, : 2 * W] = ah
        a_ref[at, :, 2 * W :] = al


def slot_of(scalars, level, half):
    return scalars[3 + 2 * level + half]


def gathered(scalars, pieces, held, at=None):
    for k in range(4):
        held[(scalars[0] + 4 - k) % 4] = pieces[k][...] if at is None else pieces[k][at]


def block_of(scalars, held, level, half):
    return held[2 * (level % 2) + slot_of(scalars, level, half)]


def applied(x, a_ref, v_ref, at):
    xh, xl = split(x)
    a = a_ref[at]
    z = mm(a[:, : 2 * W], xl) + (mm(a[:, 2 * W :], xh) + mm(a[:, : 2 * W], xh))
    zh, zl = split(z)
    v = v_ref[at]
    return x - (mm(v[:, :W], zl) + (mm(v[:, W:], zh) + mm(v[:, :W], zh)))


def across(top, low, a_ref, v_ref, at):
    middle = applied(jnp.concatenate([top[W:], low[:W]], axis=0), a_ref, v_ref, at)
    return jnp.concatenate([top[:W], middle[:W]], axis=0), jnp.concatenate([middle[W:], low[W:]], axis=0)


def across_below(last, low, below, a_ref, v_ref, at):
    new_low, new_below = across(low, jnp.where(last, 0.0, below), a_ref, v_ref, at)
    return new_low, jnp.where(last, below, new_below)


def across_above(first, above, top, a_ref, v_ref, at):
    new_above, new_top = across(above, top, a_ref, v_ref, at)
    return new_above, jnp.where(first, top, new_top)


def first_kernel(scalars, x_ref, p0, p1, p2, p3, q0, q1, q2, q3, message, low_ref, a0, v0, held):
    gathered(scalars, (q0, q1, q2, q3), held)
    message[2 * W :] = block_of(scalars, held, 2, 0)
    gathered(scalars, (p0, p1, p2, p3), held)
    factor_blocks([block_of(scalars, held, level, half) for level in (0, 1) for half in (0, 1)], a0, v0)
    top = applied(x_ref[: 2 * W], a0, v0, 0)
    low = applied(x_ref[2 * W :], a0, v0, 1)
    top, low = across(top, low, a0, v0, 2)
    message[: 2 * W] = top
    low_ref[...] = low


def factor1_kernel(scalars, after, p0, p1, p2, p3, o2, o3, a1, v1, pair, held):
    pair[0] = o2[...]
    pair[1] = o3[...]
    gathered(scalars, (p0, p1, p2, p3), held)
    factor_blocks([block_of(scalars, held, level, half) for level, half in ((2, 1), (3, 0), (3, 1))], a1, v1)


def second_kernel(scalars, low_ref, message, a0, v0, a1, v1, low_out, below_out, af, vf):
    last = scalars[1] == 1
    factor_blocks([message[2 * W :]], af, vf)
    low, below = across_below(last, low_ref[...], message[: 2 * W], a0, v0, 3)
    low = applied(low, a1, v1, 0)
    below = applied(below, af, vf, 0)
    low, below = across_below(last, low, below, a1, v1, 2)
    low_out[...] = low
    below_out[...] = below


def factor2_kernel(scalars, after, p0, p1, p2, p3, a2, v2, down, up, held):
    gathered(scalars, (p0, p1, p2, p3), held, 1)
    down[1] = block_of(scalars, held, 6, 1)
    down[2] = block_of(scalars, held, 7, 1)
    up[...] = block_of(scalars, held, 6, 0)
    gathered(scalars, (p0, p1, p2, p3), held, 0)
    down[0] = block_of(scalars, held, 5, 1)
    factor_blocks([block_of(scalars, held, level, half) for level in (4, 5) for half in (0, 1)], a2, v2)


def third_kernel(low_ref, top_ref, a1, v1, a2, v2, low_out, top_out):
    top, low = across(top_ref[...], low_ref[...], a1, v1, 1)
    top = applied(top, a2, v2, 0)
    low = applied(low, a2, v2, 1)
    top, low = across(top, low, a2, v2, 2)
    low_out[...] = low
    top_out[...] = top


def factor3_kernel(scalars, after, p0, p1, p2, p3, a3, v3, held):
    gathered(scalars, (p0, p1, p2, p3), held, 1)
    factor_blocks([block_of(scalars, held, level, half) for level in (6, 7) for half in (0, 1)], a3, v3)


def factor4_kernel(after, down, up, a4, v4):
    factor_blocks([down[0], down[1], down[2], up[...]], a4, v4)


def fourth_kernel(scalars, low_ref, top_ref, above_ref, below_ref, a2, v2, a3, v3, a4, v4, out_ref):
    last = scalars[1] == 1
    first = scalars[2] == 1
    low, below = across_below(last, low_ref[...], below_ref[...], a2, v2, 3)
    above, top = across_above(first, above_ref[...], top_ref[...], a4, v4, 0)
    above = applied(above, a4, v4, 1)
    top = applied(top, a3, v3, 0)
    low = applied(low, a3, v3, 1)
    below = applied(below, a4, v4, 3)
    _, top = across_above(first, above, top, a4, v4, 2)
    low, _ = across_below(last, low, below, a3, v3, 3)
    top, low = across(top, low, a3, v3, 2)
    out_ref[: 2 * W] = top
    out_ref[2 * W :] = low


def factor_shapes(count):
    return [jax.ShapeDtypeStruct((count, W, 4 * W), BF16), jax.ShapeDtypeStruct((count, 2 * W, 2 * W), BF16)]


def rows_shape(*shape):
    return jax.ShapeDtypeStruct(shape, F32)


HELD = [pltpu.VMEM((4, W, W), F32)]


def call(kernel, args, shapes, scratch=(), smem=1, flops=400_000_000):
    return pl.pallas_call(
        kernel,
        out_shape=tuple(shapes),
        in_specs=[pl.BlockSpec(memory_space=SMEM)] * smem + [pl.BlockSpec(memory_space=VMEM)] * (len(args) - smem),
        out_specs=(pl.BlockSpec(memory_space=VMEM),) * len(shapes),
        scratch_shapes=list(scratch),
        compiler_params=pltpu.CompilerParams(vmem_limit_bytes=24 * 1024 * 1024),
        cost_estimate=pl.CostEstimate(flops=flops, bytes_accessed=2_000_000, transcendentals=0),
        name=kernel.__name__,
    )(*args)


def shifted(value, axis, steps):
    count = lax.axis_size(axis)
    return lax.ppermute(value, axis, [(i, (i + steps) % count) for i in range(count)])


def along_x(value):
    return [value] + [lax.ppermute(value, "cols", [(i, (i // 4) * 4 + (i + k) % 4) for i in range(16)]) for k in (1, 2, 3)]


def per_device(eigvecs, wy_packed, slot_block):
    column = lax.axis_index("cols")
    row = lax.axis_index("rows")
    plane, place = column // 4, column % 4
    edges = jnp.stack([place, row == lax.axis_size("rows") - 1, row == 0]).astype(jnp.int32)
    scalars = jnp.concatenate([edges, slot_block.reshape(-1)])
    packed = wy_packed[0]
    half = rows_shape(2 * W, W)

    planes = [packed] + [shifted(packed, "cols", 4 * k) for k in (1, 2, 3)]
    ordered = [lax.select_n((plane + 4 - j) % 4, *planes) for j in range(4)]
    part0 = along_x(ordered[0])
    part1 = along_x(ordered[1])
    message, low, a0, v0 = call(
        first_kernel,
        (scalars, eigvecs, *part0, *part1),
        [rows_shape(3 * W, W), half, *factor_shapes(4)],
        HELD,
    )
    message = shifted(message, "rows", -1)
    a1, v1, pair = call(
        factor1_kernel,
        (scalars, low, *part1, ordered[2], ordered[3]),
        [*factor_shapes(3), rows_shape(2, W, W)],
        HELD,
    )
    pairs = along_x(pair)
    scratch = [pltpu.VMEM(s.shape, s.dtype) for s in factor_shapes(1)]
    low, below = call(second_kernel, (scalars, low, message, a0, v0, a1, v1), [half, half], scratch)
    top = shifted(below, "rows", 1)
    a2, v2, down, up = call(
        factor2_kernel,
        (scalars, low, *pairs),
        [*factor_shapes(4), rows_shape(3, W, W), rows_shape(W, W)],
        HELD,
    )
    down = shifted(down, "rows", 1)
    up = shifted(up, "rows", -1)
    low, top = call(third_kernel, (low, top, a1, v1, a2, v2), [half, half], smem=0)
    above = shifted(low, "rows", 1)
    below = shifted(top, "rows", -1)
    a3, v3 = call(factor3_kernel, (scalars, low, *pairs), factor_shapes(4), HELD)
    a4, v4 = call(factor4_kernel, (low, down, up), factor_shapes(4), smem=0)
    return call(
        fourth_kernel, (scalars, low, top, above, below, a2, v2, a3, v3, a4, v4), [rows_shape(*eigvecs.shape)]
    )[0]


def solution(mesh):
    placed = (P("rows", "cols"), P(("rows", "cols"), None, None), P("rows", None, None))
    return jax.shard_map(
        per_device, mesh=mesh, in_specs=placed, out_specs=P("rows", "cols"), check_vma=False
    )
```

time: 86.9 us -> 74.1 us (0.85)
  the two profiles are of different devices: /device:TPU:0 before, /device:TPU:25 now
where the time goes in v2:
time: 74.1 us; the launch traced here: 74 us
  starting transfers between devices  27.3 us (37%)
  waiting for transfers between devices  23.9 us (32%)
  Pallas kernels  21.8 us (29%)
  local copies, waits for them, and re-layouts  0.85 us (1%)
    pallas_call x8, Pallas kernels, call(): pl.pallas_call(kernel, out_shape=tuple(shapes), in_specs=[pl.BlockSpec(me...  21.8 us
    ppermute x9, waiting for transfers between devices, shifted(): lax.ppermute(value, axis, [(i, (i + steps) % count) for i in range(count)])  18.8 us
    ppermute x9, starting transfers between devices, shifted(): lax.ppermute(value, axis, [(i, (i + steps) % count) for i in range(count)])  18.6 us
    ppermute x9, starting transfers between devices, along_x(): lax.ppermute(value, 'cols', [(i, i // 4 * 4 + (i + k) % 4) for i in range...  8.67 us
    ppermute x9, waiting for transfers between devices, along_x(): lax.ppermute(value, 'cols', [(i, i // 4 * 4 + (i + k) % 4) for i in range...  5.05 us
  transfers between devices with their start and end apart: 18, of which 10 were waited for; matrix products, arithmetic and copies ran while one was open for 0% of the time, Pallas kernels for 20%

profile of v2, /device:TPU:25, one launch (start us, length us, event | category | flops | bytes accessed | tf_op | source)
XLA Modules:
  0.0 74.0 jit_solution(17947443278695540555)
XLA Ops:
  0.0 3.0 %collective-permute-start.1 = (f32[128,128]{1,0:T(8,128)}, f32[128,128]{1,0:T(8,128)S(1)}, u32[]{:S(2)}, u32[]{:S(2)}) collective-permute-start(f32[128,128]{1,0:T(8,128)} %bitcast.8), channel_id=1, source_target_pairs={{0,8},{1,9},{2,10},{3,11},{4,12},{5,13},{6,14},{7,15},{8,0},{9,1},... | collective-permute-start | bytes 196616 | tf_op jit(solution)/shard_map/ppermute | solution.py:259
  3.0 1.4 %collective-permute-start.2 = (f32[128,128]{1,0:T(8,128)}, f32[128,128]{1,0:T(8,128)S(1)}, u32[]{:S(2)}, u32[]{:S(2)}) collective-permute-start(f32[128,128]{1,0:T(8,128)} %bitcast.9), channel_id=1, source_target_pairs={{0,12},{1,13},{2,14},{3,15},{4,0},{5,1},{6,2},{7,3},{8,4},{9,5},{1... | collective-permute-start | bytes 196616 | tf_op jit(solution)/shard_map/ppermute | solution.py:259
  4.3 0.3 collective-permute-start
  4.6 0.0 copy-start.1
  4.6 0.0 copy-start
  4.6 0.2 collective-permute-done.1
  4.9 1.9 %collective-permute-done.2 = f32[128,128]{1,0:T(8,128)S(1)} collective-permute-done((f32[128,128]{1,0:T(8,128)}, f32[128,128]{1,0:T(8,128)S(1)}, u32[]{:S(2)}, u32[]{:S(2)}) %collective-permute-start.2) | collective-permute-done | bytes 65568 | tf_op jit(solution)/shard_map/ppermute | solution.py:259
  6.8 2.8 %collective-permute-done = f32[128,128]{1,0:T(8,128)S(1)} collective-permute-done((f32[128,128]{1,0:T(8,128)}, f32[128,128]{1,0:T(8,128)S(1)}, u32[]{:S(2)}, u32[]{:S(2)}) %collective-permute-start) | collective-permute-done | bytes 65568 | tf_op jit(solution)/shard_map/ppermute | solution.py:259
  9.6 0.0 copy-done.1
  9.6 2.6 %collective-permute-start.5 = (f32[128,128]{1,0:T(8,128)S(1)}, f32[128,128]{1,0:T(8,128)S(1)}, u32[]{:S(2)}, u32[]{:S(2)}) collective-permute-start(f32[128,128]{1,0:T(8,128)S(1)} %get-tuple-element.46.p0), channel_id=1, source_target_pairs={{0,3},{1,0},{2,1},{3,2},{4,7},{5,4},{6,5},{7,6},{8,11},{9,8},{10,9... | collective-permute-start | bytes 196616 | tf_op jit(solution)/shard_map/ppermute | solution.py:263
  12.2 0.0 copy-start.2
  12.2 0.7 copy-done.2
  12.9 0.1 copy.5
  12.9 0.1 reshape.3
  13.0 0.5 collective-permute-start.4
  13.6 0.6 collective-permute-start.3
  14.2 2.1 %collective-permute-start.8 = (f32[128,128]{1,0:T(8,128)S(1)}, f32[128,128]{1,0:T(8,128)S(1)}, u32[]{:S(2)}, u32[]{:S(2)}) collective-permute-start(f32[128,128]{1,0:T(8,128)S(1)} %get-tuple-element.45.q0.p0), channel_id=1, source_target_pairs={{0,3},{1,0},{2,1},{3,2},{4,7},{5,4},{6,5},{7,6},{8,11},{9,8},{10,9... | collective-permute-start | bytes 196616 | tf_op jit(solution)/shard_map/ppermute | solution.py:263
  16.2 1.2 %collective-permute-start.7 = (f32[128,128]{1,0:T(8,128)S(1)}, f32[128,128]{1,0:T(8,128)S(1)}, u32[]{:S(2)}, u32[]{:S(2)}) collective-permute-start(f32[128,128]{1,0:T(8,128)S(1)} %get-tuple-element.45.q0.p0), channel_id=1, source_target_pairs={{0,2},{1,3},{2,0},{3,1},{4,6},{5,7},{6,4},{7,5},{8,10},{9,11},{10,... | collective-permute-start | bytes 196616 | tf_op jit(solution)/shard_map/ppermute | solution.py:263
  17.5 0.0 collective-permute-done.5.p3
  17.5 0.0 collective-permute-start.6
  17.5 0.1 pad_add_fusion.scalars
  17.6 0.1 collective-permute-done.4.p2
  17.7 0.7 collective-permute-done.3.p1
  18.4 0.5 collective-permute-done.8.q3.p3
  18.9 2.6 %collective-permute-done.7.q2.p2 = f32[128,128]{1,0:T(8,128)S(1)} collective-permute-done((f32[128,128]{1,0:T(8,128)S(1)}, f32[128,128]{1,0:T(8,128)S(1)}, u32[]{:S(2)}, u32[]{:S(2)}) %collective-permute-start.7) | collective-permute-done | bytes 65568 | tf_op jit(solution)/shard_map/ppermute | solution.py:263
  21.5 1.1 %collective-permute-done.6.q1.p1 = f32[128,128]{1,0:T(8,128)S(1)} collective-permute-done((f32[128,128]{1,0:T(8,128)S(1)}, f32[128,128]{1,0:T(8,128)S(1)}, u32[]{:S(2)}, u32[]{:S(2)}) %collective-permute-start.6) | collective-permute-done | bytes 65568 | tf_op jit(solution)/shard_map/ppermute | solution.py:263
  22.6 0.0 copy-done
  22.6 3.7 %first_kernel.1 = (f32[384,128]{1,0:T(8,128)S(1)}, f32[256,128]{1,0:T(8,128)S(1)}, bf16[4,128,512]{2,1,0:T(8,128)(2,1)S(1)}, bf16[4,256,256]{2,1,0:T(8,128)(2,1)S(1)}) custom-call(s32[19]{0:T(128)S(1)} %pad_add_fusion.scalars, f32[512,128]{1,0:T(8,128)S(1)} %copy-done, f32[128,128]{1,0:T(8,128)S(1)} %get-tuple-element.46.p0, ...), custom_call_target="tpu_custom_call" | custom-call | flops 400000000 | bytes 2000000 | tf_op jit(solution)/shard_map/first_kernel/pallas_call | solution.py:245
  26.3 3.8 %collective-permute-start.9 = (f32[384,128]{1,0:T(8,128)S(1)}, f32[384,128]{1,0:T(8,128)S(1)}, u32[]{:S(2)}, u32[]{:S(2)}) collective-permute-start(f32[384,128]{1,0:T(8,128)S(1)} %get-tuple-element.25), channel_id=1, source_target_pairs={{0,240},{16,0},{32,16},{48,32},{64,48},{80,64},{96,80},{112,96},{1... | collective-permute-start | bytes 589832 | tf_op jit(solution)/shard_map/ppermute | solution.py:259
  30.1 2.6 %factor1_kernel.1 = (bf16[3,128,512]{2,1,0:T(8,128)(2,1)S(1)}, bf16[3,256,256]{2,1,0:T(8,128)(2,1)S(1)}, f32[2,128,128]{2,1,0:T(8,128)S(1)}) custom-call(s32[19]{0:T(128)S(1)} %pad_add_fusion.scalars, f32[256,128]{1,0:T(8,128)S(1)} %get-tuple-element.24.after.low_ref, f32[128,128]{1,0:T(8,128)S(1)} %get-tuple-element.45.q0.p0, ...), custom_call_target="tpu_custom_call" | custom-call | flops 400000000 | bytes 2000000 | tf_op jit(solution)/shard_map/factor1_kernel/pallas_call | solution.py:245
  32.7 0.1 collective-permute-start.13
  32.8 1.0 %collective-permute-start.12 = (f32[2,128,128]{2,1,0:T(8,128)S(1)}, f32[2,128,128]{2,1,0:T(8,128)S(1)}, u32[]{:S(2)}, u32[]{:S(2)}) collective-permute-start(f32[2,128,128]{2,1,0:T(8,128)S(1)} %get-tuple-element.32.p0), channel_id=1, source_target_pairs={{0,2},{1,3},{2,0},{3,1},{4,6},{5,7},{6,4},{7,5},{8,10},{9,11},{10,... | collective-permute-start | bytes 393224 | tf_op jit(solution)/shard_map/ppermute | solution.py:263
  33.8 0.6 collective-permute-start.11
  34.3 6.8 %collective-permute-done.9.message = f32[384,128]{1,0:T(8,128)S(1)} collective-permute-done((f32[384,128]{1,0:T(8,128)S(1)}, f32[384,128]{1,0:T(8,128)S(1)}, u32[]{:S(2)}, u32[]{:S(2)}) %collective-permute-start.9) | collective-permute-done | bytes 196640 | tf_op jit(solution)/shard_map/ppermute | solution.py:259
  41.1 3.3 %second_kernel.1 = (f32[256,128]{1,0:T(8,128)S(1)}, f32[256,128]{1,0:T(8,128)S(1)}) custom-call(s32[19]{0:T(128)S(1)} %pad_add_fusion.scalars, f32[256,128]{1,0:T(8,128)S(1)} %get-tuple-element.24.after.low_ref, f32[384,128]{1,0:T(8,128)S(1)} %collective-permute-done.9.message, bf16[4,128,512]{2,1,0:T(8,128)(2,1)S(1)} %get-tuple-element.26.a0, ...), custom_call_target="tpu_custom_call" | custom-call | flops 400000000 | bytes 2000000 | tf_op jit(solution)/shard_map/second_kernel/pallas_call | solution.py:245
  44.5 0.1 collective-permute-start.10
  44.5 0.0 collective-permute-done.13.p3
  44.6 0.0 collective-permute-done.12.p2
  44.6 0.0 collective-permute-done.11.p1
  44.6 2.8 %factor2_kernel.1 = (bf16[4,128,512]{2,1,0:T(8,128)(2,1)S(1)}, bf16[4,256,256]{2,1,0:T(8,128)(2,1)S(1)}, f32[3,128,128]{2,1,0:T(8,128)S(1)}, f32[128,128]{1,0:T(8,128)S(1)}) custom-call(s32[19]{0:T(128)S(1)} %pad_add_fusion.scalars, f32[256,128]{1,0:T(8,128)S(1)} %get-tuple-element.30.after.low_ref, f32[2,128,128]{2,1,0:T(8,128)S(1)} %get-tuple-element.32.p0, ...), custom_call_target="tpu_custom_call" | custom-call | flops 400000000 | bytes 2000000 | tf_op jit(solution)/shard_map/factor2_kernel/pallas_call | solution.py:245
  47.4 4.3 %collective-permute-start.16 = (f32[3,128,128]{2,1,0:T(8,128)S(1)}, f32[3,128,128]{2,1,0:T(8,128)S(1)}, u32[]{:S(2)}, u32[]{:S(2)}) collective-permute-start(f32[3,128,128]{2,1,0:T(8,128)S(1)} %get-tuple-element.39), channel_id=1, source_target_pairs={{0,16},{16,32},{32,48},{48,64},{64,80},{80,96},{96,112},{112,128},... | collective-permute-start | bytes 589832 | tf_op jit(solution)/shard_map/ppermute | solution.py:259
  51.7 0.0 collective-permute-done.10.top_ref
  51.7 1.4 %third_kernel.1 = (f32[256,128]{1,0:T(8,128)S(1)}, f32[256,128]{1,0:T(8,128)S(1)}) custom-call(f32[256,128]{1,0:T(8,128)S(1)} %get-tuple-element.30.after.low_ref, f32[256,128]{1,0:T(8,128)S(1)} %collective-permute-done.10.top_ref, bf16[3,128,512]{2,1,0:T(8,128)(2,1)S(1)} %get-tuple-element.28.a1, bf16[3,256,256]{2,1,0:T(8,128)(2,1)S(1)} %get-tuple-element.29.v1, ...), custom_call_target="tpu_custom_call" | custom-call | flops 400000000 | bytes 2000000 | tf_op jit(solution)/shard_map/third_kernel/pallas_call | solution.py:245
  53.1 0.4 collective-permute-start.15
  53.5 5.3 %collective-permute-start.14 = (f32[256,128]{1,0:T(8,128)S(1)}, f32[256,128]{1,0:T(8,128)S(1)}, u32[]{:S(2)}, u32[]{:S(2)}) collective-permute-start(f32[256,128]{1,0:T(8,128)S(1)} %get-tuple-element.35.after.low_ref), channel_id=1, source_target_pairs={{0,16},{16,32},{32,48},{48,64},{64,80},{80,96},{96,112},{112,128},... | collective-permute-start | bytes 393224 | tf_op jit(solution)/shard_map/ppermute | solution.py:259
  58.9 0.0 collective-permute-start.17
  58.9 2.8 %factor3_kernel.1 = (bf16[4,128,512]{2,1,0:T(8,128)(2,1)S(1)}, bf16[4,256,256]{2,1,0:T(8,128)(2,1)S(1)}) custom-call(s32[19]{0:T(128)S(1)} %pad_add_fusion.scalars, f32[256,128]{1,0:T(8,128)S(1)} %get-tuple-element.35.after.low_ref, f32[2,128,128]{2,1,0:T(8,128)S(1)} %get-tuple-element.32.p0, f32[2,128,128]{2,1,0:T(8,128)S(1)} %collective-permute-done.11.p1, ...), custom_call_target="tpu_custom_call" | custom-call | flops 400000000 | bytes 2000000 | tf_op jit(solution)/shard_map/factor3_kernel/pallas_call | solution.py:245
  61.6 7.1 %collective-permute-done.17.up = f32[128,128]{1,0:T(8,128)S(1)} collective-permute-done((f32[128,128]{1,0:T(8,128)S(1)}, f32[128,128]{1,0:T(8,128)S(1)}, u32[]{:S(2)}, u32[]{:S(2)}) %collective-permute-start.17) | collective-permute-done | bytes 65568 | tf_op jit(solution)/shard_map/ppermute | solution.py:259
  68.7 0.0 collective-permute-done.16.down
  68.7 2.2 %factor4_kernel.1 = (bf16[4,128,512]{2,1,0:T(8,128)(2,1)S(1)}, bf16[4,256,256]{2,1,0:T(8,128)(2,1)S(1)}) custom-call(f32[256,128]{1,0:T(8,128)S(1)} %get-tuple-element.35.after.low_ref, f32[3,128,128]{2,1,0:T(8,128)S(1)} %collective-permute-done.16.down, f32[128,128]{1,0:T(8,128)S(1)} %collective-permute-done.17.up), custom_call_target="tpu_custom_call" | custom-call | flops 400000000 | bytes 2000000 | tf_op jit(solution)/shard_map/factor4_kernel/pallas_call | solution.py:245
  70.9 0.0 collective-permute-done.15.below_ref
  70.9 0.0 collective-permute-done.14.above_ref
  70.9 3.1 %fourth_kernel.1 = f32[512,128]{1,0:T(8,128)} custom-call(s32[19]{0:T(128)S(1)} %pad_add_fusion.scalars, f32[256,128]{1,0:T(8,128)S(1)} %get-tuple-element.35.after.low_ref, f32[256,128]{1,0:T(8,128)S(1)} %get-tuple-element.36.top_ref, f32[256,128]{1,0:T(8,128)S(1)} %collective-permute-done.14.above_ref, f32[256,128]{1,0:T(8,128)S(1)} %collective-permute-done.15.below_ref, ...), custom_call_target="tpu_custom_call" | custom-call | flops 400000000 | bytes 2000000 | tf_op jit(solution)/shard_map/fourth_kernel/pallas_call | solution.py:245
  (1 shorter events, 0.0 us)
Async XLA Ops:
  0.0 4.9 %collective-permute-start.1 = (f32[128,128]{1,0:T(8,128)}, f32[128,128]{1,0:T(8,128)S(1)}, u32[]{:S(2)}, u32[]{:S(2)}) collective-permute-start(f32[128,128]{1,0:T(8,128)} %bitcast.8), channel_id=1, source_target_pairs={{0,8},{1,9},{2,10},{3,11},{4,12},{5,13},{6,14},{7,15},{8,0},{9,1},... | collective-permute-start | bytes 196616 | tf_op jit(solution)/shard_map/ppermute | solution.py:259
  3.0 3.8 %collective-permute-start.2 = (f32[128,128]{1,0:T(8,128)}, f32[128,128]{1,0:T(8,128)S(1)}, u32[]{:S(2)}, u32[]{:S(2)}) collective-permute-start(f32[128,128]{1,0:T(8,128)} %bitcast.9), channel_id=1, source_target_pairs={{0,12},{1,13},{2,14},{3,15},{4,0},{5,1},{6,2},{7,3},{8,4},{9,5},{1... | collective-permute-start | bytes 196616 | tf_op jit(solution)/shard_map/ppermute | solution.py:259
  4.3 5.2 %collective-permute-start = (f32[128,128]{1,0:T(8,128)}, f32[128,128]{1,0:T(8,128)S(1)}, u32[]{:S(2)}, u32[]{:S(2)}) collective-permute-start(f32[128,128]{1,0:T(8,128)} %bitcast.10), channel_id=1, source_target_pairs={{0,4},{1,5},{2,6},{3,7},{4,8},{5,9},{6,10},{7,11},{8,12},{9,13},{1... | collective-permute-start | bytes 196616 | tf_op jit(solution)/shard_map/ppermute | solution.py:259
  4.6 5.0 %copy-start.1 = (f32[1,128,128]{2,1,0:T(8,128)S(1)}, f32[1,128,128]{2,1,0:T(8,128)}, u32[]{:S(2)}) copy-start(f32[1,128,128]{2,1,0:T(8,128)} %param.4) | copy-start | bytes 196612
  4.6 18.0 %copy-start = (f32[512,128]{1,0:T(8,128)S(1)}, f32[512,128]{1,0:T(8,128)}, u32[]{:S(2)}) copy-start(f32[512,128]{1,0:T(8,128)} %x_ref.1) | copy-start | bytes 786436
  9.6 7.9 %collective-permute-start.5 = (f32[128,128]{1,0:T(8,128)S(1)}, f32[128,128]{1,0:T(8,128)S(1)}, u32[]{:S(2)}, u32[]{:S(2)}) collective-permute-start(f32[128,128]{1,0:T(8,128)S(1)} %get-tuple-element.46.p0), channel_id=1, source_target_pairs={{0,3},{1,0},{2,1},{3,2},{4,7},{5,4},{6,5},{7,6},{8,11},{9,8},{10,9... | collective-permute-start | bytes 196616 | tf_op jit(solution)/shard_map/ppermute | solution.py:263
  12.2 0.7 copy-start.2
  13.0 4.7 %collective-permute-start.4 = (f32[128,128]{1,0:T(8,128)S(1)}, f32[128,128]{1,0:T(8,128)S(1)}, u32[]{:S(2)}, u32[]{:S(2)}) collective-permute-start(f32[128,128]{1,0:T(8,128)S(1)} %get-tuple-element.46.p0), channel_id=1, source_target_pairs={{0,2},{1,3},{2,0},{3,1},{4,6},{5,7},{6,4},{7,5},{8,10},{9,11},{10,... | collective-permute-start | bytes 196616 | tf_op jit(solution)/shard_map/ppermute | solution.py:263
  13.6 4.8 %collective-permute-start.3 = (f32[128,128]{1,0:T(8,128)S(1)}, f32[128,128]{1,0:T(8,128)S(1)}, u32[]{:S(2)}, u32[]{:S(2)}) collective-permute-start(f32[128,128]{1,0:T(8,128)S(1)} %get-tuple-element.46.p0), channel_id=1, source_target_pairs={{0,1},{1,2},{2,3},{3,0},{4,5},{5,6},{6,7},{7,4},{8,9},{9,10},{10,1... | collective-permute-start | bytes 196616 | tf_op jit(solution)/shard_map/ppermute | solution.py:263
  14.2 4.7 %collective-permute-start.8 = (f32[128,128]{1,0:T(8,128)S(1)}, f32[128,128]{1,0:T(8,128)S(1)}, u32[]{:S(2)}, u32[]{:S(2)}) collective-permute-start(f32[128,128]{1,0:T(8,128)S(1)} %get-tuple-element.45.q0.p0), channel_id=1, source_target_pairs={{0,3},{1,0},{2,1},{3,2},{4,7},{5,4},{6,5},{7,6},{8,11},{9,8},{10,9... | collective-permute-start | bytes 196616 | tf_op jit(solution)/shard_map/ppermute | solution.py:263
  16.2 5.2 %collective-permute-start.7 = (f32[128,128]{1,0:T(8,128)S(1)}, f32[128,128]{1,0:T(8,128)S(1)}, u32[]{:S(2)}, u32[]{:S(2)}) collective-permute-start(f32[128,128]{1,0:T(8,128)S(1)} %get-tuple-element.45.q0.p0), channel_id=1, source_target_pairs={{0,2},{1,3},{2,0},{3,1},{4,6},{5,7},{6,4},{7,5},{8,10},{9,11},{10,... | collective-permute-start | bytes 196616 | tf_op jit(solution)/shard_map/ppermute | solution.py:263
  17.5 5.1 %collective-permute-start.6 = (f32[128,128]{1,0:T(8,128)S(1)}, f32[128,128]{1,0:T(8,128)S(1)}, u32[]{:S(2)}, u32[]{:S(2)}) collective-permute-start(f32[128,128]{1,0:T(8,128)S(1)} %get-tuple-element.45.q0.p0), channel_id=1, source_target_pairs={{0,1},{1,2},{2,3},{3,0},{4,5},{5,6},{6,7},{7,4},{8,9},{9,10},{10,1... | collective-permute-start | bytes 196616 | tf_op jit(solution)/shard_map/ppermute | solution.py:263
  26.3 14.8 %collective-permute-start.9 = (f32[384,128]{1,0:T(8,128)S(1)}, f32[384,128]{1,0:T(8,128)S(1)}, u32[]{:S(2)}, u32[]{:S(2)}) collective-permute-start(f32[384,128]{1,0:T(8,128)S(1)} %get-tuple-element.25), channel_id=1, source_target_pairs={{0,240},{16,0},{32,16},{48,32},{64,48},{80,64},{96,80},{112,96},{1... | collective-permute-start | bytes 589832 | tf_op jit(solution)/shard_map/ppermute | solution.py:259
  32.7 11.9 %collective-permute-start.13 = (f32[2,128,128]{2,1,0:T(8,128)S(1)}, f32[2,128,128]{2,1,0:T(8,128)S(1)}, u32[]{:S(2)}, u32[]{:S(2)}) collective-permute-start(f32[2,128,128]{2,1,0:T(8,128)S(1)} %get-tuple-element.32.p0), channel_id=1, source_target_pairs={{0,3},{1,0},{2,1},{3,2},{4,7},{5,4},{6,5},{7,6},{8,11},{9,8},{10,9... | collective-permute-start | bytes 393224 | tf_op jit(solution)/shard_map/ppermute | solution.py:263
  32.8 11.8 %collective-permute-start.12 = (f32[2,128,128]{2,1,0:T(8,128)S(1)}, f32[2,128,128]{2,1,0:T(8,128)S(1)}, u32[]{:S(2)}, u32[]{:S(2)}) collective-permute-start(f32[2,128,128]{2,1,0:T(8,128)S(1)} %get-tuple-element.32.p0), channel_id=1, source_target_pairs={{0,2},{1,3},{2,0},{3,1},{4,6},{5,7},{6,4},{7,5},{8,10},{9,11},{10,... | collective-permute-start | bytes 393224 | tf_op jit(solution)/shard_map/ppermute | solution.py:263
  33.8 10.8 %collective-permute-start.11 = (f32[2,128,128]{2,1,0:T(8,128)S(1)}, f32[2,128,128]{2,1,0:T(8,128)S(1)}, u32[]{:S(2)}, u32[]{:S(2)}) collective-permute-start(f32[2,128,128]{2,1,0:T(8,128)S(1)} %get-tuple-element.32.p0), channel_id=1, source_target_pairs={{0,1},{1,2},{2,3},{3,0},{4,5},{5,6},{6,7},{7,4},{8,9},{9,10},{10,1... | collective-permute-start | bytes 393224 | tf_op jit(solution)/shard_map/ppermute | solution.py:263
  44.5 7.3 %collective-permute-start.10 = (f32[256,128]{1,0:T(8,128)S(1)}, f32[256,128]{1,0:T(8,128)S(1)}, u32[]{:S(2)}, u32[]{:S(2)}) collective-permute-start(f32[256,128]{1,0:T(8,128)S(1)} %get-tuple-element.31), channel_id=1, source_target_pairs={{0,16},{16,32},{32,48},{48,64},{64,80},{80,96},{96,112},{112,128},... | collective-permute-start | bytes 393224 | tf_op jit(solution)/shard_map/ppermute | solution.py:259
  47.4 21.3 %collective-permute-start.16 = (f32[3,128,128]{2,1,0:T(8,128)S(1)}, f32[3,128,128]{2,1,0:T(8,128)S(1)}, u32[]{:S(2)}, u32[]{:S(2)}) collective-permute-start(f32[3,128,128]{2,1,0:T(8,128)S(1)} %get-tuple-element.39), channel_id=1, source_target_pairs={{0,16},{16,32},{32,48},{48,64},{64,80},{80,96},{96,112},{112,128},... | collective-permute-start | bytes 589832 | tf_op jit(solution)/shard_map/ppermute | solution.py:259
  53.1 17.8 %collective-permute-start.15 = (f32[256,128]{1,0:T(8,128)S(1)}, f32[256,128]{1,0:T(8,128)S(1)}, u32[]{:S(2)}, u32[]{:S(2)}) collective-permute-start(f32[256,128]{1,0:T(8,128)S(1)} %get-tuple-element.36.top_ref), channel_id=1, source_target_pairs={{0,240},{16,0},{32,16},{48,32},{64,48},{80,64},{96,80},{112,96},{1... | collective-permute-start | bytes 393224 | tf_op jit(solution)/shard_map/ppermute | solution.py:259
  53.5 17.4 %collective-permute-start.14 = (f32[256,128]{1,0:T(8,128)S(1)}, f32[256,128]{1,0:T(8,128)S(1)}, u32[]{:S(2)}, u32[]{:S(2)}) collective-permute-start(f32[256,128]{1,0:T(8,128)S(1)} %get-tuple-element.35.after.low_ref), channel_id=1, source_target_pairs={{0,16},{16,32},{32,48},{48,64},{64,80},{80,96},{96,112},{112,128},... | collective-permute-start | bytes 393224 | tf_op jit(solution)/shard_map/ppermute | solution.py:259
  58.9 9.8 %collective-permute-start.17 = (f32[128,128]{1,0:T(8,128)S(1)}, f32[128,128]{1,0:T(8,128)S(1)}, u32[]{:S(2)}, u32[]{:S(2)}) collective-permute-start(f32[128,128]{1,0:T(8,128)S(1)} %get-tuple-element.40), channel_id=1, source_target_pairs={{0,240},{16,0},{32,16},{48,32},{64,48},{80,64},{96,80},{112,96},{1... | collective-permute-start | bytes 196616 | tf_op jit(solution)/shard_map/ppermute | solution.py:259

commit v3 on v2

--- a/solution.py
+++ b/solution.py
@@ -103,129 +103,148 @@
     return [jnp.concatenate([u - c, low], axis=0) for u, c, low in zip(uppers, changes, lowers)]
 
 
-def factor_blocks(packed, a_ref, v_ref):
+def factors(packed):
     reflectors = [unpacked(p) for p in packed]
     halves = splits(reflectors)
     nt = ((1,), (1,))
     grams = [mm(h, h, nt) + (mm(h, l, nt) + mm(l, h, nt)) for h, l in halves]
-    for at, r in enumerate(reflectors):
-        vh, vl = split(r.T)
+    inverses = splits(triangle_inverses(grams))
+    products = splits(dots3(inverses, halves))
+    return [(*a, *split(r.T)) for a, r in zip(products, reflectors)]
+
+
+def stored_factors(packed, a_ref, v_ref):
+    for at, (ah, al, vh, vl) in enumerate(factors(packed)):
+        a_ref[at, :, : 2 * W] = ah
+        a_ref[at, :, 2 * W :] = al
         v_ref[at, :, :W] = vh
         v_ref[at, :, W:] = vl
-    inverses = splits(triangle_inverses(grams))
-    for at, a in enumerate(dots3(inverses, halves)):
-        ah, al = split(a)
-        a_ref[at, :, : 2 * W] = ah
-        a_ref[at, :, 2 * W :] = al
+
+
+def loaded(a_ref, v_ref, at):
+    a, v = a_ref[at], v_ref[at]
+    return a[:, : 2 * W], a[:, 2 * W :], v[:, :W], v[:, W:]
 
 
 def slot_of(scalars, level, half):
     return scalars[3 + 2 * level + half]
 
 
-def gathered(scalars, pieces, held, at=None):
+def gathered(scalars, pieces, held, at):
     for k in range(4):
-        held[(scalars[0] + 4 - k) % 4] = pieces[k][...] if at is None else pieces[k][at]
+        held[(scalars[0] + 4 - k) % 4] = pieces[k][at]
 
 
 def block_of(scalars, held, level, half):
     return held[2 * (level % 2) + slot_of(scalars, level, half)]
 
 
-def applied(x, a_ref, v_ref, at):
-    xh, xl = split(x)
-    a = a_ref[at]
-    z = mm(a[:, : 2 * W], xl) + (mm(a[:, 2 * W :], xh) + mm(a[:, : 2 * W], xh))
-    zh, zl = split(z)
-    v = v_ref[at]
-    return x - (mm(v[:, :W], zl) + (mm(v[:, W:], zh) + mm(v[:, :W], zh)))
-
-
-def across(top, low, a_ref, v_ref, at):
-    middle = applied(jnp.concatenate([top[W:], low[:W]], axis=0), a_ref, v_ref, at)
+def applied(x, factor):
+    ah, al, vh, vl = factor
+    x_parts = split(x)
+    z_parts = split(dot3((ah, al), x_parts))
+    return x - dot3((vh, vl), z_parts)
+
+
+def across(top, low, factor):
+    middle = applied(jnp.concatenate([top[W:], low[:W]], axis=0), factor)
     return jnp.concatenate([top[:W], middle[:W]], axis=0), jnp.concatenate([middle[W:], low[W:]], axis=0)
 
 
-def across_below(last, low, below, a_ref, v_ref, at):
-    new_low, new_below = across(low, jnp.where(last, 0.0, below), a_ref, v_ref, at)
+def across_below(last, low, below, factor):
+    new_low, new_below = across(low, jnp.where(last, 0.0, below), factor)
     return new_low, jnp.where(last, below, new_below)
 
 
-def across_above(first, above, top, a_ref, v_ref, at):
-    new_above, new_top = across(above, top, a_ref, v_ref, at)
+def across_above(first, above, top, factor):
+    new_above, new_top = across(above, top, factor)
     return new_above, jnp.where(first, top, new_top)
 
 
-def first_kernel(scalars, x_ref, p0, p1, p2, p3, q0, q1, q2, q3, message, low_ref, a0, v0, held):
-    gathered(scalars, (q0, q1, q2, q3), held)
+def order_kernel(plane, p0, p1, p2, p3, near, far, held):
+    for k, piece in enumerate((p0, p1, p2, p3)):
+        held[(plane[0] + 4 - k) % 4] = piece[...]
+    near[...] = held[0:2]
+    far[...] = held[2:4]
+
+
+def first_kernel(scalars, x_ref, p0, p1, p2, p3, message, low_ref, a0, v0, held):
+    pieces = (p0, p1, p2, p3)
+    gathered(scalars, pieces, held, 1)
     message[2 * W :] = block_of(scalars, held, 2, 0)
-    gathered(scalars, (p0, p1, p2, p3), held)
-    factor_blocks([block_of(scalars, held, level, half) for level in (0, 1) for half in (0, 1)], a0, v0)
-    top = applied(x_ref[: 2 * W], a0, v0, 0)
-    low = applied(x_ref[2 * W :], a0, v0, 1)
-    top, low = across(top, low, a0, v0, 2)
+    gathered(scalars, pieces, held, 0)
+    stored_factors([block_of(scalars, held, level, half) for level in (0, 1) for half in (0, 1)], a0, v0)
+    top = applied(x_ref[: 2 * W], loaded(a0, v0, 0))
+    low = applied(x_ref[2 * W :], loaded(a0, v0, 1))
+    top, low = across(top, low, loaded(a0, v0, 2))
     message[: 2 * W] = top
     low_ref[...] = low
 
 
-def factor1_kernel(scalars, after, p0, p1, p2, p3, o2, o3, a1, v1, pair, held):
-    pair[0] = o2[...]
-    pair[1] = o3[...]
-    gathered(scalars, (p0, p1, p2, p3), held)
-    factor_blocks([block_of(scalars, held, level, half) for level, half in ((2, 1), (3, 0), (3, 1))], a1, v1)
-
-
-def second_kernel(scalars, low_ref, message, a0, v0, a1, v1, low_out, below_out, af, vf):
+def factor1_kernel(scalars, after, p0, p1, p2, p3, far, a1, v1, sent, held):
+    sent[...] = far[...]
+    gathered(scalars, (p0, p1, p2, p3), held, 1)
+    stored_factors([block_of(scalars, held, level, half) for level, half in ((2, 1), (3, 0), (3, 1))], a1, v1)
+
+
+def second_kernel(scalars, low_ref, message, a0, v0, a1, v1, low_out, below_out):
     last = scalars[1] == 1
-    factor_blocks([message[2 * W :]], af, vf)
-    low, below = across_below(last, low_ref[...], message[: 2 * W], a0, v0, 3)
-    low = applied(low, a1, v1, 0)
-    below = applied(below, af, vf, 0)
-    low, below = across_below(last, low, below, a1, v1, 2)
+    (foreign,) = factors([message[2 * W :]])
+    low, below = across_below(last, low_ref[...], message[: 2 * W], loaded(a0, v0, 3))
+    low = applied(low, loaded(a1, v1, 0))
+    below = applied(below, foreign)
+    low, below = across_below(last, low, below, loaded(a1, v1, 2))
     low_out[...] = low
     below_out[...] = below
 
 
-def factor2_kernel(scalars, after, p0, p1, p2, p3, a2, v2, down, up, held):
-    gathered(scalars, (p0, p1, p2, p3), held, 1)
+def choose_kernel(scalars, after, p0, p1, p2, p3, down, up, held):
+    pieces = (p0, p1, p2, p3)
+    gathered(scalars, pieces, held, 1)
     down[1] = block_of(scalars, held, 6, 1)
     down[2] = block_of(scalars, held, 7, 1)
     up[...] = block_of(scalars, held, 6, 0)
+    gathered(scalars, pieces, held, 0)
+    down[0] = block_of(scalars, held, 5, 1)
+
+
+def factor2_kernel(scalars, after, p0, p1, p2, p3, a2, v2, held):
     gathered(scalars, (p0, p1, p2, p3), held, 0)
-    down[0] = block_of(scalars, held, 5, 1)
-    factor_blocks([block_of(scalars, held, level, half) for level in (4, 5) for half in (0, 1)], a2, v2)
-
-
-def third_kernel(low_ref, top_ref, a1, v1, a2, v2, low_out, top_out):
-    top, low = across(top_ref[...], low_ref[...], a1, v1, 1)
-    top = applied(top, a2, v2, 0)
-    low = applied(low, a2, v2, 1)
-    top, low = across(top, low, a2, v2, 2)
+    stored_factors([block_of(scalars, held, level, half) for level in (4, 5) for half in (0, 1)], a2, v2)
+
+
+def third_kernel(low_ref, top_ref, up, a1, v1, a2, v2, low_out, message):
+    message[2 * W :] = up[...]
+    top, low = across(top_ref[...], low_ref[...], loaded(a1, v1, 1))
+    top = applied(top, loaded(a2, v2, 0))
+    low = applied(low, loaded(a2, v2, 1))
+    top, low = across(top, low, loaded(a2, v2, 2))
     low_out[...] = low
-    top_out[...] = top
+    message[: 2 * W] = top
 
 
 def factor3_kernel(scalars, after, p0, p1, p2, p3, a3, v3, held):
     gathered(scalars, (p0, p1, p2, p3), held, 1)
-    factor_blocks([block_of(scalars, held, level, half) for level in (6, 7) for half in (0, 1)], a3, v3)
-
-
-def factor4_kernel(after, down, up, a4, v4):
-    factor_blocks([down[0], down[1], down[2], up[...]], a4, v4)
-
-
-def fourth_kernel(scalars, low_ref, top_ref, above_ref, below_ref, a2, v2, a3, v3, a4, v4, out_ref):
+    stored_factors([block_of(scalars, held, level, half) for level in (6, 7) for half in (0, 1)], a3, v3)
+
+
+def factor4_kernel(after, down, a4, v4):
+    stored_factors([down[0], down[1], down[2]], a4, v4)
+
+
+def fourth_kernel(scalars, low_ref, own, above_ref, message, a2, v2, a3, v3, a4, v4, out_ref):
     last = scalars[1] == 1
     first = scalars[2] == 1
-    low, below = across_below(last, low_ref[...], below_ref[...], a2, v2, 3)
-    above, top = across_above(first, above_ref[...], top_ref[...], a4, v4, 0)
-    above = applied(above, a4, v4, 1)
-    top = applied(top, a3, v3, 0)
-    low = applied(low, a3, v3, 1)
-    below = applied(below, a4, v4, 3)
-    _, top = across_above(first, above, top, a4, v4, 2)
-    low, _ = across_below(last, low, below, a3, v3, 3)
-    top, low = across(top, low, a3, v3, 2)
+    (foreign,) = factors([message[2 * W :]])
+    low, below = across_below(last, low_ref[...], message[: 2 * W], loaded(a2, v2, 3))
+    above, top = across_above(first, above_ref[...], own[: 2 * W], loaded(a4, v4, 0))
+    above = applied(above, loaded(a4, v4, 1))
+    top = applied(top, loaded(a3, v3, 0))
+    low = applied(low, loaded(a3, v3, 1))
+    below = applied(below, foreign)
+    _, top = across_above(first, above, top, loaded(a4, v4, 2))
+    low, _ = across_below(last, low, below, loaded(a3, v3, 3))
+    top, low = across(top, low, loaded(a3, v3, 2))
     out_ref[: 2 * W] = top
     out_ref[2 * W :] = low
 
@@ -273,41 +292,27 @@
     half = rows_shape(2 * W, W)
 
     planes = [packed] + [shifted(packed, "cols", 4 * k) for k in (1, 2, 3)]
-    ordered = [lax.select_n((plane + 4 - j) % 4, *planes) for j in range(4)]
-    part0 = along_x(ordered[0])
-    part1 = along_x(ordered[1])
+    pair = rows_shape(2, W, W)
+    near, far = call(order_kernel, (plane.reshape(1), *planes), [pair, pair], HELD)
+    near = along_x(near)
     message, low, a0, v0 = call(
-        first_kernel,
-        (scalars, eigvecs, *part0, *part1),
-        [rows_shape(3 * W, W), half, *factor_shapes(4)],
-        HELD,
+        first_kernel, (scalars, eigvecs, *near), [rows_shape(3 * W, W), half, *factor_shapes(4)], HELD
     )
     message = shifted(message, "rows", -1)
-    a1, v1, pair = call(
-        factor1_kernel,
-        (scalars, low, *part1, ordered[2], ordered[3]),
-        [*factor_shapes(3), rows_shape(2, W, W)],
-        HELD,
-    )
-    pairs = along_x(pair)
-    scratch = [pltpu.VMEM(s.shape, s.dtype) for s in factor_shapes(1)]
-    low, below = call(second_kernel, (scalars, low, message, a0, v0, a1, v1), [half, half], scratch)
+    a1, v1, far = call(factor1_kernel, (scalars, low, *near, far), [*factor_shapes(3), pair], HELD)
+    far = along_x(far)
+    low, below = call(second_kernel, (scalars, low, message, a0, v0, a1, v1), [half, half])
     top = shifted(below, "rows", 1)
-    a2, v2, down, up = call(
-        factor2_kernel,
-        (scalars, low, *pairs),
-        [*factor_shapes(4), rows_shape(3, W, W), rows_shape(W, W)],
-        HELD,
-    )
+    down, up = call(choose_kernel, (scalars, low, *far), [rows_shape(3, W, W), rows_shape(W, W)], HELD)
+    a2, v2 = call(factor2_kernel, (scalars, up, *far), factor_shapes(4), HELD)
     down = shifted(down, "rows", 1)
-    up = shifted(up, "rows", -1)
-    low, top = call(third_kernel, (low, top, a1, v1, a2, v2), [half, half], smem=0)
+    low, own = call(third_kernel, (low, top, up, a1, v1, a2, v2), [half, rows_shape(3 * W, W)], smem=0)
     above = shifted(low, "rows", 1)
-    below = shifted(top, "rows", -1)
-    a3, v3 = call(factor3_kernel, (scalars, low, *pairs), factor_shapes(4), HELD)
-    a4, v4 = call(factor4_kernel, (low, down, up), factor_shapes(4), smem=0)
+    message = shifted(own, "rows", -1)
+    a3, v3 = call(factor3_kernel, (scalars, low, *far), factor_shapes(4), HELD)
+    a4, v4 = call(factor4_kernel, (low, down), factor_shapes(3), smem=0)
     return call(
-        fourth_kernel, (scalars, low, top, above, below, a2, v2, a3, v3, a4, v4), [rows_shape(*eigvecs.shape)]
+        fourth_kernel, (scalars, low, own, above, message, a2, v2, a3, v3, a4, v4), [rows_shape(*eigvecs.shape)]
     )[0]
 
 

time: 74.1 us -> 72.7 us (0.981)
  the two profiles are of different devices: /device:TPU:25 before, /device:TPU:32 now
where the time goes in v3:
time: 72.7 us; the launch traced here: 72.6 us
  waiting for transfers between devices  25.7 us (35%)
  Pallas kernels  23.5 us (32%)
  starting transfers between devices  21.5 us (30%)
  local copies, waits for them, and re-layouts  1.68 us (2%)
    pallas_call x10, Pallas kernels, call(): pl.pallas_call(kernel, out_shape=tuple(shapes), in_specs=[pl.BlockSpec(me...  23.5 us
    ppermute x8, waiting for transfers between devices, shifted(): lax.ppermute(value, axis, [(i, (i + steps) % count) for i in range(count)])  17.7 us
    ppermute x8, starting transfers between devices, shifted(): lax.ppermute(value, axis, [(i, (i + steps) % count) for i in range(count)])  14.9 us
    ppermute x6, waiting for transfers between devices, along_x(): lax.ppermute(value, 'cols', [(i, i // 4 * 4 + (i + k) % 4) for i in range...  8 us
    ppermute x6, starting transfers between devices, along_x(): lax.ppermute(value, 'cols', [(i, i // 4 * 4 + (i + k) % 4) for i in range...  6.62 us
    unnamed x7, local copies, waits for them, and re-layouts  1.6 us
  transfers between devices with their start and end apart: 14, of which 10 were waited for; matrix products, arithmetic and copies ran while one was open for 0% of the time, Pallas kernels for 21%

profile of v3, /device:TPU:32, one launch (start us, length us, event | category | flops | bytes accessed | tf_op | source)
XLA Modules:
  0.0 72.6 jit_solution(2576684813541220754)
XLA Ops:
  0.0 1.8 %collective-permute-start.2 = (f32[128,128]{1,0:T(8,128)}, f32[128,128]{1,0:T(8,128)S(1)}, u32[]{:S(2)}, u32[]{:S(2)}) collective-permute-start(f32[128,128]{1,0:T(8,128)} %bitcast.5), channel_id=1, source_target_pairs={{0,12},{1,13},{2,14},{3,15},{4,0},{5,1},{6,2},{7,3},{8,4},{9,5},{1... | collective-permute-start | bytes 196616 | tf_op jit(solution)/shard_map/ppermute | solution.py:278
  1.8 1.5 %collective-permute-start.1 = (f32[128,128]{1,0:T(8,128)}, f32[128,128]{1,0:T(8,128)S(1)}, u32[]{:S(2)}, u32[]{:S(2)}) collective-permute-start(f32[128,128]{1,0:T(8,128)} %bitcast.6), channel_id=1, source_target_pairs={{0,8},{1,9},{2,10},{3,11},{4,12},{5,13},{6,14},{7,15},{8,0},{9,1},... | collective-permute-start | bytes 196616 | tf_op jit(solution)/shard_map/ppermute | solution.py:278
  3.4 2.8 %collective-permute-start = (f32[128,128]{1,0:T(8,128)}, f32[128,128]{1,0:T(8,128)S(1)}, u32[]{:S(2)}, u32[]{:S(2)}) collective-permute-start(f32[128,128]{1,0:T(8,128)} %bitcast.7), channel_id=1, source_target_pairs={{0,4},{1,5},{2,6},{3,7},{4,8},{5,9},{6,10},{7,11},{8,12},{9,13},{1... | collective-permute-start | bytes 196616 | tf_op jit(solution)/shard_map/ppermute | solution.py:278
  6.2 0.0 collective-permute-done.2.p3
  6.2 2.2 %collective-permute-done.1.p2 = f32[128,128]{1,0:T(8,128)S(1)} collective-permute-done((f32[128,128]{1,0:T(8,128)}, f32[128,128]{1,0:T(8,128)S(1)}, u32[]{:S(2)}, u32[]{:S(2)}) %collective-permute-start.1) | collective-permute-done | bytes 65568 | tf_op jit(solution)/shard_map/ppermute | solution.py:278
  8.4 1.2 %collective-permute-done.p1 = f32[128,128]{1,0:T(8,128)S(1)} collective-permute-done((f32[128,128]{1,0:T(8,128)}, f32[128,128]{1,0:T(8,128)S(1)}, u32[]{:S(2)}, u32[]{:S(2)}) %collective-permute-start) | collective-permute-done | bytes 65568 | tf_op jit(solution)/shard_map/ppermute | solution.py:278
  9.6 0.0 copy-start.1
  9.6 0.8 %copy-done.1 = f32[1,128,128]{2,1,0:T(8,128)S(1)} copy-done((f32[1,128,128]{2,1,0:T(8,128)S(1)}, f32[1,128,128]{2,1,0:T(8,128)}, u32[]{:S(2)}) %copy-start.1) | copy-done | bytes 65560
  10.4 0.0 copy-start
  10.4 2.8 %collective-permute-start.5 = (f32[2,128,128]{2,1,0:T(8,128)S(1)}, f32[2,128,128]{2,1,0:T(8,128)S(1)}, u32[]{:S(2)}, u32[]{:S(2)}) collective-permute-start(f32[2,128,128]{2,1,0:T(8,128)S(1)} %get-tuple-element.26.p0), channel_id=1, source_target_pairs={{0,3},{1,0},{2,1},{3,2},{4,7},{5,4},{6,5},{7,6},{8,11},{9,8},{10,9... | collective-permute-start | bytes 393224 | tf_op jit(solution)/shard_map/ppermute | solution.py:282
  13.3 0.8 %collective-permute-start.4 = (f32[2,128,128]{2,1,0:T(8,128)S(1)}, f32[2,128,128]{2,1,0:T(8,128)S(1)}, u32[]{:S(2)}, u32[]{:S(2)}) collective-permute-start(f32[2,128,128]{2,1,0:T(8,128)S(1)} %get-tuple-element.26.p0), channel_id=1, source_target_pairs={{0,2},{1,3},{2,0},{3,1},{4,6},{5,7},{6,4},{7,5},{8,10},{9,11},{10,... | collective-permute-start | bytes 393224 | tf_op jit(solution)/shard_map/ppermute | solution.py:282
  14.1 0.9 %collective-permute-start.3 = (f32[2,128,128]{2,1,0:T(8,128)S(1)}, f32[2,128,128]{2,1,0:T(8,128)S(1)}, u32[]{:S(2)}, u32[]{:S(2)}) collective-permute-start(f32[2,128,128]{2,1,0:T(8,128)S(1)} %get-tuple-element.26.p0), channel_id=1, source_target_pairs={{0,1},{1,2},{2,3},{3,0},{4,5},{5,6},{6,7},{7,4},{8,9},{9,10},{10,1... | collective-permute-start | bytes 393224 | tf_op jit(solution)/shard_map/ppermute | solution.py:282
  15.0 0.0 copy-start.2
  15.0 0.7 copy-done.2
  15.7 0.1 copy.5
  15.7 0.1 reshape.6
  15.8 0.1 pad_add_fusion.scalars
  15.9 2.4 %collective-permute-done.5.p3 = f32[2,128,128]{2,1,0:T(8,128)S(1)} collective-permute-done((f32[2,128,128]{2,1,0:T(8,128)S(1)}, f32[2,128,128]{2,1,0:T(8,128)S(1)}, u32[]{:S(2)}, u32[]{:S(2)}) %collective-permute-start.5) | collective-permute-done | bytes 131104 | tf_op jit(solution)/shard_map/ppermute | solution.py:282
  18.3 2.3 %collective-permute-done.4.p2 = f32[2,128,128]{2,1,0:T(8,128)S(1)} collective-permute-done((f32[2,128,128]{2,1,0:T(8,128)S(1)}, f32[2,128,128]{2,1,0:T(8,128)S(1)}, u32[]{:S(2)}, u32[]{:S(2)}) %collective-permute-start.4) | collective-permute-done | bytes 131104 | tf_op jit(solution)/shard_map/ppermute | solution.py:282
  20.7 1.3 %collective-permute-done.3.p1 = f32[2,128,128]{2,1,0:T(8,128)S(1)} collective-permute-done((f32[2,128,128]{2,1,0:T(8,128)S(1)}, f32[2,128,128]{2,1,0:T(8,128)S(1)}, u32[]{:S(2)}, u32[]{:S(2)}) %collective-permute-start.3) | collective-permute-done | bytes 131104 | tf_op jit(solution)/shard_map/ppermute | solution.py:282
  22.0 0.0 copy-done
  22.0 3.7 %first_kernel.1 = (f32[384,128]{1,0:T(8,128)S(1)}, f32[256,128]{1,0:T(8,128)S(1)}, bf16[4,128,512]{2,1,0:T(8,128)(2,1)S(1)}, bf16[4,256,256]{2,1,0:T(8,128)(2,1)S(1)}) custom-call(s32[19]{0:T(128)S(1)} %pad_add_fusion.scalars, f32[512,128]{1,0:T(8,128)S(1)} %copy-done, f32[2,128,128]{2,1,0:T(8,128)S(1)} %get-tuple-element.26.p0, ...), custom_call_target="tpu_custom_call" | custom-call | flops 400000000 | bytes 2000000 | tf_op jit(solution)/shard_map/first_kernel/pallas_call | solution.py:264
  25.7 7.3 %collective-permute-start.6 = (f32[384,128]{1,0:T(8,128)S(1)}, f32[384,128]{1,0:T(8,128)S(1)}, u32[]{:S(2)}, u32[]{:S(2)}) collective-permute-start(f32[384,128]{1,0:T(8,128)S(1)} %get-tuple-element.28), channel_id=1, source_target_pairs={{0,240},{16,0},{32,16},{48,32},{64,48},{80,64},{96,80},{112,96},{1... | collective-permute-start | bytes 589832 | tf_op jit(solution)/shard_map/ppermute | solution.py:278
  33.0 2.6 %factor1_kernel.1 = (bf16[3,128,512]{2,1,0:T(8,128)(2,1)S(1)}, bf16[3,256,256]{2,1,0:T(8,128)(2,1)S(1)}, f32[2,128,128]{2,1,0:T(8,128)S(1)}) custom-call(s32[19]{0:T(128)S(1)} %pad_add_fusion.scalars, f32[256,128]{1,0:T(8,128)S(1)} %get-tuple-element.27.after.low_ref, f32[2,128,128]{2,1,0:T(8,128)S(1)} %get-tuple-element.26.p0, ...), custom_call_target="tpu_custom_call" | custom-call | flops 400000000 | bytes 2000000 | tf_op jit(solution)/shard_map/factor1_kernel/pallas_call | solution.py:264
  35.6 0.1 collective-permute-start.10
  35.7 0.5 collective-permute-start.9
  36.1 1.6 %collective-permute-start.8 = (f32[2,128,128]{2,1,0:T(8,128)S(1)}, f32[2,128,128]{2,1,0:T(8,128)S(1)}, u32[]{:S(2)}, u32[]{:S(2)}) collective-permute-start(f32[2,128,128]{2,1,0:T(8,128)S(1)} %get-tuple-element.36.p0), channel_id=1, source_target_pairs={{0,1},{1,2},{2,3},{3,0},{4,5},{5,6},{6,7},{7,4},{8,9},{9,10},{10,1... | collective-permute-start | bytes 393224 | tf_op jit(solution)/shard_map/ppermute | solution.py:282
  37.7 0.7 collective-permute-done.6.message
  38.3 3.3 %second_kernel.1 = (f32[256,128]{1,0:T(8,128)S(1)}, f32[256,128]{1,0:T(8,128)S(1)}) custom-call(s32[19]{0:T(128)S(1)} %pad_add_fusion.scalars, f32[256,128]{1,0:T(8,128)S(1)} %get-tuple-element.27.after.low_ref, f32[384,128]{1,0:T(8,128)S(1)} %collective-permute-done.6.message, bf16[4,128,512]{2,1,0:T(8,128)(2,1)S(1)} %get-tuple-element.29.a0, ...), custom_call_target="tpu_custom_call" | custom-call | flops 400000000 | bytes 2000000 | tf_op jit(solution)/shard_map/second_kernel/pallas_call | solution.py:264
  41.7 0.1 collective-permute-start.7
  41.7 0.0 collective-permute-done.10.p3
  41.8 0.5 collective-permute-done.9.p2
  42.3 1.4 %collective-permute-done.8.p1 = f32[2,128,128]{2,1,0:T(8,128)S(1)} collective-permute-done((f32[2,128,128]{2,1,0:T(8,128)S(1)}, f32[2,128,128]{2,1,0:T(8,128)S(1)}, u32[]{:S(2)}, u32[]{:S(2)}) %collective-permute-start.8) | collective-permute-done | bytes 131104 | tf_op jit(solution)/shard_map/ppermute | solution.py:282
  43.6 0.6 choose_kernel.1
  44.3 0.1 collective-permute-start.13
  44.3 2.8 %factor2_kernel.1 = (bf16[4,128,512]{2,1,0:T(8,128)(2,1)S(1)}, bf16[4,256,256]{2,1,0:T(8,128)(2,1)S(1)}) custom-call(s32[19]{0:T(128)S(1)} %pad_add_fusion.scalars, f32[128,128]{1,0:T(8,128)S(1)} %get-tuple-element.37.after.up, f32[2,128,128]{2,1,0:T(8,128)S(1)} %get-tuple-element.36.p0, f32[2,128,128]{2,1,0:T(8,128)S(1)} %collective-permute-done.8.p1, ...), custom_call_target="tpu_custom_call" | custom-call | flops 400000000 | bytes 2000000 | tf_op jit(solution)/shard_map/factor2_kernel/pallas_call | solution.py:264
  47.1 6.7 %collective-permute-done.7.top_ref = f32[256,128]{1,0:T(8,128)S(1)} collective-permute-done((f32[256,128]{1,0:T(8,128)S(1)}, f32[256,128]{1,0:T(8,128)S(1)}, u32[]{:S(2)}, u32[]{:S(2)}) %collective-permute-start.7) | collective-permute-done | bytes 131104 | tf_op jit(solution)/shard_map/ppermute | solution.py:278
  53.8 1.4 %third_kernel.1 = (f32[256,128]{1,0:T(8,128)S(1)}, f32[384,128]{1,0:T(8,128)S(1)}) custom-call(f32[256,128]{1,0:T(8,128)S(1)} %get-tuple-element.34.after.low_ref, f32[256,128]{1,0:T(8,128)S(1)} %collective-permute-done.7.top_ref, f32[128,128]{1,0:T(8,128)S(1)} %get-tuple-element.37.after.up, bf16[3,128,512]{2,1,0:T(8,128)(2,1)S(1)} %get-tuple-element.32.a1, ...), custom_call_target="tpu_custom_call" | custom-call | flops 400000000 | bytes 2000000 | tf_op jit(solution)/shard_map/third_kernel/pallas_call | solution.py:264
  55.2 1.2 %collective-permute-start.12 = (f32[384,128]{1,0:T(8,128)S(1)}, f32[384,128]{1,0:T(8,128)S(1)}, u32[]{:S(2)}, u32[]{:S(2)}) collective-permute-start(f32[384,128]{1,0:T(8,128)S(1)} %get-tuple-element.41.own), channel_id=1, source_target_pairs={{0,240},{16,0},{32,16},{48,32},{64,48},{80,64},{96,80},{112,96},{1... | collective-permute-start | bytes 589832 | tf_op jit(solution)/shard_map/ppermute | solution.py:278
  56.4 0.0 collective-permute-start.11
  56.4 2.8 %factor3_kernel.1 = (bf16[4,128,512]{2,1,0:T(8,128)(2,1)S(1)}, bf16[4,256,256]{2,1,0:T(8,128)(2,1)S(1)}) custom-call(s32[19]{0:T(128)S(1)} %pad_add_fusion.scalars, f32[256,128]{1,0:T(8,128)S(1)} %get-tuple-element.40.after.low_ref, f32[2,128,128]{2,1,0:T(8,128)S(1)} %get-tuple-element.36.p0, f32[2,128,128]{2,1,0:T(8,128)S(1)} %collective-permute-done.8.p1, ...), custom_call_target="tpu_custom_call" | custom-call | flops 400000000 | bytes 2000000 | tf_op jit(solution)/shard_map/factor3_kernel/pallas_call | solution.py:264
  59.1 0.0 collective-permute-done.13.down
  59.1 2.0 %factor4_kernel.1 = (bf16[3,128,512]{2,1,0:T(8,128)(2,1)S(1)}, bf16[3,256,256]{2,1,0:T(8,128)(2,1)S(1)}) custom-call(f32[256,128]{1,0:T(8,128)S(1)} %get-tuple-element.40.after.low_ref, f32[3,128,128]{2,1,0:T(8,128)S(1)} %collective-permute-done.13.down), custom_call_target="tpu_custom_call" | custom-call | flops 400000000 | bytes 2000000 | tf_op jit(solution)/shard_map/factor4_kernel/pallas_call | solution.py:264
  61.1 7.0 %collective-permute-done.11.above_ref = f32[256,128]{1,0:T(8,128)S(1)} collective-permute-done((f32[256,128]{1,0:T(8,128)S(1)}, f32[256,128]{1,0:T(8,128)S(1)}, u32[]{:S(2)}, u32[]{:S(2)}) %collective-permute-start.11) | collective-permute-done | bytes 131104 | tf_op jit(solution)/shard_map/ppermute | solution.py:278
  68.1 0.0 collective-permute-done.12.message
  68.1 4.4 %fourth_kernel.1 = f32[512,128]{1,0:T(8,128)} custom-call(s32[19]{0:T(128)S(1)} %pad_add_fusion.scalars, f32[256,128]{1,0:T(8,128)S(1)} %get-tuple-element.40.after.low_ref, f32[384,128]{1,0:T(8,128)S(1)} %get-tuple-element.41.own, f32[256,128]{1,0:T(8,128)S(1)} %collective-permute-done.11.above_ref, f32[384,128]{1,0:T(8,128)S(1)} %collective-permute-done.12.message, ...), custom_call_target="tpu_custom_call" | custom-call | flops 400000000 | bytes 2000000 | tf_op jit(solution)/shard_map/fourth_kernel/pallas_call | solution.py:264
  (1 shorter events, 0.0 us)
Async XLA Ops:
  0.0 6.2 %collective-permute-start.2 = (f32[128,128]{1,0:T(8,128)}, f32[128,128]{1,0:T(8,128)S(1)}, u32[]{:S(2)}, u32[]{:S(2)}) collective-permute-start(f32[128,128]{1,0:T(8,128)} %bitcast.5), channel_id=1, source_target_pairs={{0,12},{1,13},{2,14},{3,15},{4,0},{5,1},{6,2},{7,3},{8,4},{9,5},{1... | collective-permute-start | bytes 196616 | tf_op jit(solution)/shard_map/ppermute | solution.py:278
  1.8 6.6 %collective-permute-start.1 = (f32[128,128]{1,0:T(8,128)}, f32[128,128]{1,0:T(8,128)S(1)}, u32[]{:S(2)}, u32[]{:S(2)}) collective-permute-start(f32[128,128]{1,0:T(8,128)} %bitcast.6), channel_id=1, source_target_pairs={{0,8},{1,9},{2,10},{3,11},{4,12},{5,13},{6,14},{7,15},{8,0},{9,1},... | collective-permute-start | bytes 196616 | tf_op jit(solution)/shard_map/ppermute | solution.py:278
  3.4 6.2 %collective-permute-start = (f32[128,128]{1,0:T(8,128)}, f32[128,128]{1,0:T(8,128)S(1)}, u32[]{:S(2)}, u32[]{:S(2)}) collective-permute-start(f32[128,128]{1,0:T(8,128)} %bitcast.7), channel_id=1, source_target_pairs={{0,4},{1,5},{2,6},{3,7},{4,8},{5,9},{6,10},{7,11},{8,12},{9,13},{1... | collective-permute-start | bytes 196616 | tf_op jit(solution)/shard_map/ppermute | solution.py:278
  9.6 0.8 %copy-start.1 = (f32[1,128,128]{2,1,0:T(8,128)S(1)}, f32[1,128,128]{2,1,0:T(8,128)}, u32[]{:S(2)}) copy-start(f32[1,128,128]{2,1,0:T(8,128)} %param.4) | copy-start | bytes 196612
  10.4 11.6 %copy-start = (f32[512,128]{1,0:T(8,128)S(1)}, f32[512,128]{1,0:T(8,128)}, u32[]{:S(2)}) copy-start(f32[512,128]{1,0:T(8,128)} %x_ref.1) | copy-start | bytes 786436
  10.4 7.9 %collective-permute-start.5 = (f32[2,128,128]{2,1,0:T(8,128)S(1)}, f32[2,128,128]{2,1,0:T(8,128)S(1)}, u32[]{:S(2)}, u32[]{:S(2)}) collective-permute-start(f32[2,128,128]{2,1,0:T(8,128)S(1)} %get-tuple-element.26.p0), channel_id=1, source_target_pairs={{0,3},{1,0},{2,1},{3,2},{4,7},{5,4},{6,5},{7,6},{8,11},{9,8},{10,9... | collective-permute-start | bytes 393224 | tf_op jit(solution)/shard_map/ppermute | solution.py:282
  13.3 7.4 %collective-permute-start.4 = (f32[2,128,128]{2,1,0:T(8,128)S(1)}, f32[2,128,128]{2,1,0:T(8,128)S(1)}, u32[]{:S(2)}, u32[]{:S(2)}) collective-permute-start(f32[2,128,128]{2,1,0:T(8,128)S(1)} %get-tuple-element.26.p0), channel_id=1, source_target_pairs={{0,2},{1,3},{2,0},{3,1},{4,6},{5,7},{6,4},{7,5},{8,10},{9,11},{10,... | collective-permute-start | bytes 393224 | tf_op jit(solution)/shard_map/ppermute | solution.py:282
  14.1 7.9 %collective-permute-start.3 = (f32[2,128,128]{2,1,0:T(8,128)S(1)}, f32[2,128,128]{2,1,0:T(8,128)S(1)}, u32[]{:S(2)}, u32[]{:S(2)}) collective-permute-start(f32[2,128,128]{2,1,0:T(8,128)S(1)} %get-tuple-element.26.p0), channel_id=1, source_target_pairs={{0,1},{1,2},{2,3},{3,0},{4,5},{5,6},{6,7},{7,4},{8,9},{9,10},{10,1... | collective-permute-start | bytes 393224 | tf_op jit(solution)/shard_map/ppermute | solution.py:282
  15.0 0.7 copy-start.2
  25.7 12.7 %collective-permute-start.6 = (f32[384,128]{1,0:T(8,128)S(1)}, f32[384,128]{1,0:T(8,128)S(1)}, u32[]{:S(2)}, u32[]{:S(2)}) collective-permute-start(f32[384,128]{1,0:T(8,128)S(1)} %get-tuple-element.28), channel_id=1, source_target_pairs={{0,240},{16,0},{32,16},{48,32},{64,48},{80,64},{96,80},{112,96},{1... | collective-permute-start | bytes 589832 | tf_op jit(solution)/shard_map/ppermute | solution.py:278
  35.6 6.2 %collective-permute-start.10 = (f32[2,128,128]{2,1,0:T(8,128)S(1)}, f32[2,128,128]{2,1,0:T(8,128)S(1)}, u32[]{:S(2)}, u32[]{:S(2)}) collective-permute-start(f32[2,128,128]{2,1,0:T(8,128)S(1)} %get-tuple-element.36.p0), channel_id=1, source_target_pairs={{0,3},{1,0},{2,1},{3,2},{4,7},{5,4},{6,5},{7,6},{8,11},{9,8},{10,9... | collective-permute-start | bytes 393224 | tf_op jit(solution)/shard_map/ppermute | solution.py:282
  35.7 6.6 %collective-permute-start.9 = (f32[2,128,128]{2,1,0:T(8,128)S(1)}, f32[2,128,128]{2,1,0:T(8,128)S(1)}, u32[]{:S(2)}, u32[]{:S(2)}) collective-permute-start(f32[2,128,128]{2,1,0:T(8,128)S(1)} %get-tuple-element.36.p0), channel_id=1, source_target_pairs={{0,2},{1,3},{2,0},{3,1},{4,6},{5,7},{6,4},{7,5},{8,10},{9,11},{10,... | collective-permute-start | bytes 393224 | tf_op jit(solution)/shard_map/ppermute | solution.py:282
  36.1 7.5 %collective-permute-start.8 = (f32[2,128,128]{2,1,0:T(8,128)S(1)}, f32[2,128,128]{2,1,0:T(8,128)S(1)}, u32[]{:S(2)}, u32[]{:S(2)}) collective-permute-start(f32[2,128,128]{2,1,0:T(8,128)S(1)} %get-tuple-element.36.p0), channel_id=1, source_target_pairs={{0,1},{1,2},{2,3},{3,0},{4,5},{5,6},{6,7},{7,4},{8,9},{9,10},{10,1... | collective-permute-start | bytes 393224 | tf_op jit(solution)/shard_map/ppermute | solution.py:282
  41.7 12.1 %collective-permute-start.7 = (f32[256,128]{1,0:T(8,128)S(1)}, f32[256,128]{1,0:T(8,128)S(1)}, u32[]{:S(2)}, u32[]{:S(2)}) collective-permute-start(f32[256,128]{1,0:T(8,128)S(1)} %get-tuple-element.35), channel_id=1, source_target_pairs={{0,16},{16,32},{32,48},{48,64},{64,80},{80,96},{96,112},{112,128},... | collective-permute-start | bytes 393224 | tf_op jit(solution)/shard_map/ppermute | solution.py:278
  44.3 14.9 %collective-permute-start.13 = (f32[3,128,128]{2,1,0:T(8,128)S(1)}, f32[3,128,128]{2,1,0:T(8,128)S(1)}, u32[]{:S(2)}, u32[]{:S(2)}) collective-permute-start(f32[3,128,128]{2,1,0:T(8,128)S(1)} %get-tuple-element.44), channel_id=1, source_target_pairs={{0,16},{16,32},{32,48},{48,64},{64,80},{80,96},{96,112},{112,128},... | collective-permute-start | bytes 589832 | tf_op jit(solution)/shard_map/ppermute | solution.py:278
  55.2 13.0 %collective-permute-start.12 = (f32[384,128]{1,0:T(8,128)S(1)}, f32[384,128]{1,0:T(8,128)S(1)}, u32[]{:S(2)}, u32[]{:S(2)}) collective-permute-start(f32[384,128]{1,0:T(8,128)S(1)} %get-tuple-element.41.own), channel_id=1, source_target_pairs={{0,240},{16,0},{32,16},{48,32},{64,48},{80,64},{96,80},{112,96},{1... | collective-permute-start | bytes 589832 | tf_op jit(solution)/shard_map/ppermute | solution.py:278
  56.4 11.8 %collective-permute-start.11 = (f32[256,128]{1,0:T(8,128)S(1)}, f32[256,128]{1,0:T(8,128)S(1)}, u32[]{:S(2)}, u32[]{:S(2)}) collective-permute-start(f32[256,128]{1,0:T(8,128)S(1)} %get-tuple-element.40.after.low_ref), channel_id=1, source_target_pairs={{0,16},{16,32},{32,48},{48,64},{64,80},{80,96},{96,112},{112,128},... | collective-permute-start | bytes 393224 | tf_op jit(solution)/shard_map/ppermute | solution.py:278

commit v4 on v3

--- a/solution.py
+++ b/solution.py
@@ -181,8 +181,7 @@
     low_ref[...] = low
 
 
-def factor1_kernel(scalars, after, p0, p1, p2, p3, far, a1, v1, sent, held):
-    sent[...] = far[...]
+def factor1_kernel(scalars, after, p0, p1, p2, p3, a1, v1, held):
     gathered(scalars, (p0, p1, p2, p3), held, 1)
     stored_factors([block_of(scalars, held, level, half) for level, half in ((2, 1), (3, 0), (3, 1))], a1, v1)
 
@@ -213,14 +212,13 @@
     stored_factors([block_of(scalars, held, level, half) for level in (4, 5) for half in (0, 1)], a2, v2)
 
 
-def third_kernel(low_ref, top_ref, up, a1, v1, a2, v2, low_out, message):
-    message[2 * W :] = up[...]
+def third_kernel(low_ref, top_ref, after1, after2, a1, v1, a2, v2, low_out, top_out):
     top, low = across(top_ref[...], low_ref[...], loaded(a1, v1, 1))
     top = applied(top, loaded(a2, v2, 0))
     low = applied(low, loaded(a2, v2, 1))
     top, low = across(top, low, loaded(a2, v2, 2))
     low_out[...] = low
-    message[: 2 * W] = top
+    top_out[...] = top
 
 
 def factor3_kernel(scalars, after, p0, p1, p2, p3, a3, v3, held):
@@ -228,20 +226,19 @@
     stored_factors([block_of(scalars, held, level, half) for level in (6, 7) for half in (0, 1)], a3, v3)
 
 
-def factor4_kernel(after, down, a4, v4):
-    stored_factors([down[0], down[1], down[2]], a4, v4)
-
-
-def fourth_kernel(scalars, low_ref, own, above_ref, message, a2, v2, a3, v3, a4, v4, out_ref):
+def factor4_kernel(after, down, up, a4, v4):
+    stored_factors([down[0], down[1], down[2], up[...]], a4, v4)
+
+
+def fourth_kernel(scalars, low_ref, top_ref, above_ref, below_ref, a2, v2, a3, v3, a4, v4, out_ref):
     last = scalars[1] == 1
     first = scalars[2] == 1
-    (foreign,) = factors([message[2 * W :]])
-    low, below = across_below(last, low_ref[...], message[: 2 * W], loaded(a2, v2, 3))
-    above, top = across_above(first, above_ref[...], own[: 2 * W], loaded(a4, v4, 0))
+    low, below = across_below(last, low_ref[...], below_ref[...], loaded(a2, v2, 3))
+    above, top = across_above(first, above_ref[...], top_ref[...], loaded(a4, v4, 0))
     above = applied(above, loaded(a4, v4, 1))
     top = applied(top, loaded(a3, v3, 0))
     low = applied(low, loaded(a3, v3, 1))
-    below = applied(below, foreign)
+    below = applied(below, loaded(a4, v4, 3))
     _, top = across_above(first, above, top, loaded(a4, v4, 2))
     low, _ = across_below(last, low, below, loaded(a3, v3, 3))
     top, low = across(top, low, loaded(a3, v3, 2))
@@ -295,24 +292,25 @@
     pair = rows_shape(2, W, W)
     near, far = call(order_kernel, (plane.reshape(1), *planes), [pair, pair], HELD)
     near = along_x(near)
+    far = along_x(far)
     message, low, a0, v0 = call(
         first_kernel, (scalars, eigvecs, *near), [rows_shape(3 * W, W), half, *factor_shapes(4)], HELD
     )
     message = shifted(message, "rows", -1)
-    a1, v1, far = call(factor1_kernel, (scalars, low, *near, far), [*factor_shapes(3), pair], HELD)
-    far = along_x(far)
+    a1, v1 = call(factor1_kernel, (scalars, low, *near), factor_shapes(3), HELD)
+    down, up = call(choose_kernel, (scalars, low, *far), [rows_shape(3, W, W), rows_shape(W, W)], HELD)
+    down = shifted(down, "rows", 1)
+    up = shifted(up, "rows", -1)
     low, below = call(second_kernel, (scalars, low, message, a0, v0, a1, v1), [half, half])
     top = shifted(below, "rows", 1)
-    down, up = call(choose_kernel, (scalars, low, *far), [rows_shape(3, W, W), rows_shape(W, W)], HELD)
-    a2, v2 = call(factor2_kernel, (scalars, up, *far), factor_shapes(4), HELD)
-    down = shifted(down, "rows", 1)
-    low, own = call(third_kernel, (low, top, up, a1, v1, a2, v2), [half, rows_shape(3 * W, W)], smem=0)
+    a2, v2 = call(factor2_kernel, (scalars, low, *far), factor_shapes(4), HELD)
+    low, own = call(third_kernel, (low, top, up, down, a1, v1, a2, v2), [half, half], smem=0)
     above = shifted(low, "rows", 1)
-    message = shifted(own, "rows", -1)
+    below = shifted(own, "rows", -1)
     a3, v3 = call(factor3_kernel, (scalars, low, *far), factor_shapes(4), HELD)
-    a4, v4 = call(factor4_kernel, (low, down), factor_shapes(3), smem=0)
+    a4, v4 = call(factor4_kernel, (low, down, up), factor_shapes(4), smem=0)
     return call(
-        fourth_kernel, (scalars, low, own, above, message, a2, v2, a3, v3, a4, v4), [rows_shape(*eigvecs.shape)]
+        fourth_kernel, (scalars, low, own, above, below, a2, v2, a3, v3, a4, v4), [rows_shape(*eigvecs.shape)]
     )[0]
 
 

time: 72.7 us -> 80.1 us (1.10)
  starting transfers between devices: 21.5 us -> 35 us
  waiting for transfers between devices: 25.7 us -> 20.7 us
  Pallas kernels: 23.5 us -> 22.4 us
    ppermute x8 -> x9, starting transfers between devices: 14.9 us -> 26.6 us  [shifted(): lax.ppermute(value, axis, [(i, (i + steps) % count) for i in range(count)])]
    ppermute x6, waiting for transfers between devices: 8 us -> 5.43 us  [along_x(): lax.ppermute(value, 'cols', [(i, i // 4 * 4 + (i + k) % 4) for i in range...]
    ppermute x8 -> x9, waiting for transfers between devices: 17.7 us -> 15.2 us  [shifted(): lax.ppermute(value, axis, [(i, (i + steps) % count) for i in range(count)])]
    ppermute x6, starting transfers between devices: 6.62 us -> 8.41 us  [along_x(): lax.ppermute(value, 'cols', [(i, i // 4 * 4 + (i + k) % 4) for i in range...]
    pallas_call x10, Pallas kernels: 23.5 us -> 22.4 us  [call(): pl.pallas_call(kernel, out_shape=tuple(shapes), in_specs=[pl.BlockSpec(me...]
  transfers between devices with their start and end apart: 14 -> 15, of which waited for: 10 -> 7; matrix products, arithmetic and copies ran while one was open for 0% -> 0% of each run, Pallas kernels for 21% -> 22%
where the time goes in v4:
time: 80.1 us; the launch traced here: 80 us
  starting transfers between devices  35 us (44%)
  Pallas kernels  22.4 us (28%)
  waiting for transfers between devices  20.7 us (26%)
  local copies, waits for them, and re-layouts  1.68 us (2%)
    ppermute x9, starting transfers between devices, shifted(): lax.ppermute(value, axis, [(i, (i + steps) % count) for i in range(count)])  26.6 us
    pallas_call x10, Pallas kernels, call(): pl.pallas_call(kernel, out_shape=tuple(shapes), in_specs=[pl.BlockSpec(me...  22.4 us
    ppermute x9, waiting for transfers between devices, shifted(): lax.ppermute(value, axis, [(i, (i + steps) % count) for i in range(count)])  15.2 us
    ppermute x6, starting transfers between devices, along_x(): lax.ppermute(value, 'cols', [(i, i // 4 * 4 + (i + k) % 4) for i in range...  8.41 us
    ppermute x6, waiting for transfers between devices, along_x(): lax.ppermute(value, 'cols', [(i, i // 4 * 4 + (i + k) % 4) for i in range...  5.43 us
    unnamed x7, local copies, waits for them, and re-layouts  1.6 us
  transfers between devices with their start and end apart: 15, of which 7 were waited for; matrix products, arithmetic and copies ran while one was open for 0% of the time, Pallas kernels for 22%

profile of v4, /device:TPU:32, one launch (start us, length us, event | category | flops | bytes accessed | tf_op | source)
XLA Modules:
  0.0 80.0 jit_solution(2874846677550018296)
XLA Ops:
  0.0 1.8 %collective-permute-start.2 = (f32[128,128]{1,0:T(8,128)}, f32[128,128]{1,0:T(8,128)S(1)}, u32[]{:S(2)}, u32[]{:S(2)}) collective-permute-start(f32[128,128]{1,0:T(8,128)} %bitcast.5), channel_id=1, source_target_pairs={{0,12},{1,13},{2,14},{3,15},{4,0},{5,1},{6,2},{7,3},{8,4},{9,5},{1... | collective-permute-start | bytes 196616 | tf_op jit(solution)/shard_map/ppermute | solution.py:275
  1.8 1.5 %collective-permute-start.1 = (f32[128,128]{1,0:T(8,128)}, f32[128,128]{1,0:T(8,128)S(1)}, u32[]{:S(2)}, u32[]{:S(2)}) collective-permute-start(f32[128,128]{1,0:T(8,128)} %bitcast.6), channel_id=1, source_target_pairs={{0,8},{1,9},{2,10},{3,11},{4,12},{5,13},{6,14},{7,15},{8,0},{9,1},... | collective-permute-start | bytes 196616 | tf_op jit(solution)/shard_map/ppermute | solution.py:275
  3.4 2.8 %collective-permute-start = (f32[128,128]{1,0:T(8,128)}, f32[128,128]{1,0:T(8,128)S(1)}, u32[]{:S(2)}, u32[]{:S(2)}) collective-permute-start(f32[128,128]{1,0:T(8,128)} %bitcast.7), channel_id=1, source_target_pairs={{0,4},{1,5},{2,6},{3,7},{4,8},{5,9},{6,10},{7,11},{8,12},{9,13},{1... | collective-permute-start | bytes 196616 | tf_op jit(solution)/shard_map/ppermute | solution.py:275
  6.2 0.0 collective-permute-done.2.p3
  6.2 2.2 %collective-permute-done.1.p2 = f32[128,128]{1,0:T(8,128)S(1)} collective-permute-done((f32[128,128]{1,0:T(8,128)}, f32[128,128]{1,0:T(8,128)S(1)}, u32[]{:S(2)}, u32[]{:S(2)}) %collective-permute-start.1) | collective-permute-done | bytes 65568 | tf_op jit(solution)/shard_map/ppermute | solution.py:275
  8.4 1.2 %collective-permute-done.p1 = f32[128,128]{1,0:T(8,128)S(1)} collective-permute-done((f32[128,128]{1,0:T(8,128)}, f32[128,128]{1,0:T(8,128)S(1)}, u32[]{:S(2)}, u32[]{:S(2)}) %collective-permute-start) | collective-permute-done | bytes 65568 | tf_op jit(solution)/shard_map/ppermute | solution.py:275
  9.6 0.0 copy-start.1
  9.6 0.8 %copy-done.1 = f32[1,128,128]{2,1,0:T(8,128)S(1)} copy-done((f32[1,128,128]{2,1,0:T(8,128)S(1)}, f32[1,128,128]{2,1,0:T(8,128)}, u32[]{:S(2)}) %copy-start.1) | copy-done | bytes 65560
  10.4 0.0 copy-start
  10.4 2.8 %collective-permute-start.5 = (f32[2,128,128]{2,1,0:T(8,128)S(1)}, f32[2,128,128]{2,1,0:T(8,128)S(1)}, u32[]{:S(2)}, u32[]{:S(2)}) collective-permute-start(f32[2,128,128]{2,1,0:T(8,128)S(1)} %get-tuple-element.25.p0), channel_id=1, source_target_pairs={{0,3},{1,0},{2,1},{3,2},{4,7},{5,4},{6,5},{7,6},{8,11},{9,8},{10,9... | collective-permute-start | bytes 393224 | tf_op jit(solution)/shard_map/ppermute | solution.py:279
  13.3 0.8 collective-permute-start.4
  14.1 0.9 %collective-permute-start.3 = (f32[2,128,128]{2,1,0:T(8,128)S(1)}, f32[2,128,128]{2,1,0:T(8,128)S(1)}, u32[]{:S(2)}, u32[]{:S(2)}) collective-permute-start(f32[2,128,128]{2,1,0:T(8,128)S(1)} %get-tuple-element.25.p0), channel_id=1, source_target_pairs={{0,1},{1,2},{2,3},{3,0},{4,5},{5,6},{6,7},{7,4},{8,9},{9,10},{10,1... | collective-permute-start | bytes 393224 | tf_op jit(solution)/shard_map/ppermute | solution.py:279
  15.0 0.0 copy-start.2
  15.0 0.7 copy-done.2
  15.7 0.1 copy.5
  15.7 0.1 reshape.6
  15.8 0.1 pad_add_fusion.scalars
  15.9 2.4 %collective-permute-start.10 = (f32[2,128,128]{2,1,0:T(8,128)S(1)}, f32[2,128,128]{2,1,0:T(8,128)S(1)}, u32[]{:S(2)}, u32[]{:S(2)}) collective-permute-start(f32[2,128,128]{2,1,0:T(8,128)S(1)} %get-tuple-element.34.p0), channel_id=1, source_target_pairs={{0,3},{1,0},{2,1},{3,2},{4,7},{5,4},{6,5},{7,6},{8,11},{9,8},{10,9... | collective-permute-start | bytes 393224 | tf_op jit(solution)/shard_map/ppermute | solution.py:279
  18.3 1.5 %collective-permute-start.9 = (f32[2,128,128]{2,1,0:T(8,128)S(1)}, f32[2,128,128]{2,1,0:T(8,128)S(1)}, u32[]{:S(2)}, u32[]{:S(2)}) collective-permute-start(f32[2,128,128]{2,1,0:T(8,128)S(1)} %get-tuple-element.34.p0), channel_id=1, source_target_pairs={{0,2},{1,3},{2,0},{3,1},{4,6},{5,7},{6,4},{7,5},{8,10},{9,11},{10,... | collective-permute-start | bytes 393224 | tf_op jit(solution)/shard_map/ppermute | solution.py:279
  19.8 0.0 collective-permute-done.5.p3
  19.8 0.0 collective-permute-start.8
  19.8 0.9 %collective-permute-done.4.p2 = f32[2,128,128]{2,1,0:T(8,128)S(1)} collective-permute-done((f32[2,128,128]{2,1,0:T(8,128)S(1)}, f32[2,128,128]{2,1,0:T(8,128)S(1)}, u32[]{:S(2)}, u32[]{:S(2)}) %collective-permute-start.4) | collective-permute-done | bytes 131104 | tf_op jit(solution)/shard_map/ppermute | solution.py:279
  20.7 4.5 %collective-permute-done.3.p1 = f32[2,128,128]{2,1,0:T(8,128)S(1)} collective-permute-done((f32[2,128,128]{2,1,0:T(8,128)S(1)}, f32[2,128,128]{2,1,0:T(8,128)S(1)}, u32[]{:S(2)}, u32[]{:S(2)}) %collective-permute-start.3) | collective-permute-done | bytes 131104 | tf_op jit(solution)/shard_map/ppermute | solution.py:279
  25.2 0.0 copy-done
  25.2 3.7 %first_kernel.1 = (f32[384,128]{1,0:T(8,128)S(1)}, f32[256,128]{1,0:T(8,128)S(1)}, bf16[4,128,512]{2,1,0:T(8,128)(2,1)S(1)}, bf16[4,256,256]{2,1,0:T(8,128)(2,1)S(1)}) custom-call(s32[19]{0:T(128)S(1)} %pad_add_fusion.scalars, f32[512,128]{1,0:T(8,128)S(1)} %copy-done, f32[2,128,128]{2,1,0:T(8,128)S(1)} %get-tuple-element.25.p0, ...), custom_call_target="tpu_custom_call" | custom-call | flops 400000000 | bytes 2000000 | tf_op jit(solution)/shard_map/first_kernel/pallas_call | solution.py:261
  28.9 5.3 %collective-permute-start.6 = (f32[384,128]{1,0:T(8,128)S(1)}, f32[384,128]{1,0:T(8,128)S(1)}, u32[]{:S(2)}, u32[]{:S(2)}) collective-permute-start(f32[384,128]{1,0:T(8,128)S(1)} %get-tuple-element.27), channel_id=1, source_target_pairs={{0,240},{16,0},{32,16},{48,32},{64,48},{80,64},{96,80},{112,96},{1... | collective-permute-start | bytes 589832 | tf_op jit(solution)/shard_map/ppermute | solution.py:275
  34.2 0.0 collective-permute-done.10.p3
  34.2 0.0 collective-permute-done.9.p2
  34.2 0.0 collective-permute-done.8.p1
  34.2 0.6 choose_kernel.1
  34.8 0.3 collective-permute-start.12
  35.1 2.6 %factor1_kernel.1 = (bf16[3,128,512]{2,1,0:T(8,128)(2,1)S(1)}, bf16[3,256,256]{2,1,0:T(8,128)(2,1)S(1)}) custom-call(s32[19]{0:T(128)S(1)} %pad_add_fusion.scalars, f32[256,128]{1,0:T(8,128)S(1)} %get-tuple-element.26.after.low_ref, f32[2,128,128]{2,1,0:T(8,128)S(1)} %get-tuple-element.25.p0, f32[2,128,128]{2,1,0:T(8,128)S(1)} %collective-permute-done.3.p1, ...), custom_call_target="tpu_custom_call" | custom-call | flops 400000000 | bytes 2000000 | tf_op jit(solution)/shard_map/factor1_kernel/pallas_call | solution.py:261
  37.7 6.0 %collective-permute-done.6.message = f32[384,128]{1,0:T(8,128)S(1)} collective-permute-done((f32[384,128]{1,0:T(8,128)S(1)}, f32[384,128]{1,0:T(8,128)S(1)}, u32[]{:S(2)}, u32[]{:S(2)}) %collective-permute-start.6) | collective-permute-done | bytes 196640 | tf_op jit(solution)/shard_map/ppermute | solution.py:275
  43.7 3.3 %second_kernel.1 = (f32[256,128]{1,0:T(8,128)S(1)}, f32[256,128]{1,0:T(8,128)S(1)}) custom-call(s32[19]{0:T(128)S(1)} %pad_add_fusion.scalars, f32[256,128]{1,0:T(8,128)S(1)} %get-tuple-element.26.after.low_ref, f32[384,128]{1,0:T(8,128)S(1)} %collective-permute-done.6.message, bf16[4,128,512]{2,1,0:T(8,128)(2,1)S(1)} %get-tuple-element.28.a0, ...), custom_call_target="tpu_custom_call" | custom-call | flops 400000000 | bytes 2000000 | tf_op jit(solution)/shard_map/second_kernel/pallas_call | solution.py:261
  47.0 0.1 collective-permute-start.7
  47.1 8.2 %collective-permute-start.11 = (f32[128,128]{1,0:T(8,128)S(1)}, f32[128,128]{1,0:T(8,128)S(1)}, u32[]{:S(2)}, u32[]{:S(2)}) collective-permute-start(f32[128,128]{1,0:T(8,128)S(1)} %get-tuple-element.35), channel_id=1, source_target_pairs={{0,240},{16,0},{32,16},{48,32},{64,48},{80,64},{96,80},{112,96},{1... | collective-permute-start | bytes 196616 | tf_op jit(solution)/shard_map/ppermute | solution.py:275
  55.2 2.8 %factor2_kernel.1 = (bf16[4,128,512]{2,1,0:T(8,128)(2,1)S(1)}, bf16[4,256,256]{2,1,0:T(8,128)(2,1)S(1)}) custom-call(s32[19]{0:T(128)S(1)} %pad_add_fusion.scalars, f32[256,128]{1,0:T(8,128)S(1)} %get-tuple-element.32.after.low_ref, f32[2,128,128]{2,1,0:T(8,128)S(1)} %get-tuple-element.34.p0, f32[2,128,128]{2,1,0:T(8,128)S(1)} %collective-permute-done.8.p1, ...), custom_call_target="tpu_custom_call" | custom-call | flops 400000000 | bytes 2000000 | tf_op jit(solution)/shard_map/factor2_kernel/pallas_call | solution.py:261
  58.0 0.0 collective-permute-done.11.after1.up
  58.0 0.0 collective-permute-done.12.after2.down
  58.0 0.5 collective-permute-done.7.top_ref
  58.5 1.4 %third_kernel.1 = (f32[256,128]{1,0:T(8,128)S(1)}, f32[256,128]{1,0:T(8,128)S(1)}) custom-call(f32[256,128]{1,0:T(8,128)S(1)} %get-tuple-element.32.after.low_ref, f32[256,128]{1,0:T(8,128)S(1)} %collective-permute-done.7.top_ref, f32[128,128]{1,0:T(8,128)S(1)} %collective-permute-done.11.after1.up, f32[3,128,128]{2,1,0:T(8,128)S(1)} %collective-permute-done.12.after2.down, ...), custom_call_target="tpu_custom_call" | custom-call | flops 400000000 | bytes 2000000 | tf_op jit(solution)/shard_map/third_kernel/pallas_call | solution.py:261
  59.9 6.6 %collective-permute-start.14 = (f32[256,128]{1,0:T(8,128)S(1)}, f32[256,128]{1,0:T(8,128)S(1)}, u32[]{:S(2)}, u32[]{:S(2)}) collective-permute-start(f32[256,128]{1,0:T(8,128)S(1)} %get-tuple-element.40.top_ref), channel_id=1, source_target_pairs={{0,240},{16,0},{32,16},{48,32},{64,48},{80,64},{96,80},{112,96},{1... | collective-permute-start | bytes 393224 | tf_op jit(solution)/shard_map/ppermute | solution.py:275
  66.5 0.0 collective-permute-start.13
  66.5 2.8 %factor3_kernel.1 = (bf16[4,128,512]{2,1,0:T(8,128)(2,1)S(1)}, bf16[4,256,256]{2,1,0:T(8,128)(2,1)S(1)}) custom-call(s32[19]{0:T(128)S(1)} %pad_add_fusion.scalars, f32[256,128]{1,0:T(8,128)S(1)} %get-tuple-element.39.after.low_ref, f32[2,128,128]{2,1,0:T(8,128)S(1)} %get-tuple-element.34.p0, f32[2,128,128]{2,1,0:T(8,128)S(1)} %collective-permute-done.8.p1, ...), custom_call_target="tpu_custom_call" | custom-call | flops 400000000 | bytes 2000000 | tf_op jit(solution)/shard_map/factor3_kernel/pallas_call | solution.py:261
  69.3 2.2 %factor4_kernel.1 = (bf16[4,128,512]{2,1,0:T(8,128)(2,1)S(1)}, bf16[4,256,256]{2,1,0:T(8,128)(2,1)S(1)}) custom-call(f32[256,128]{1,0:T(8,128)S(1)} %get-tuple-element.39.after.low_ref, f32[3,128,128]{2,1,0:T(8,128)S(1)} %collective-permute-done.12.after2.down, f32[128,128]{1,0:T(8,128)S(1)} %collective-permute-done.11.after1.up), custom_call_target="tpu_custom_call" | custom-call | flops 400000000 | bytes 2000000 | tf_op jit(solution)/shard_map/factor4_kernel/pallas_call | solution.py:261
  71.5 0.0 collective-permute-done.14.below_ref
  71.5 5.4 %collective-permute-done.13.above_ref = f32[256,128]{1,0:T(8,128)S(1)} collective-permute-done((f32[256,128]{1,0:T(8,128)S(1)}, f32[256,128]{1,0:T(8,128)S(1)}, u32[]{:S(2)}, u32[]{:S(2)}) %collective-permute-start.13) | collective-permute-done | bytes 131104 | tf_op jit(solution)/shard_map/ppermute | solution.py:275
  76.9 3.1 %fourth_kernel.1 = f32[512,128]{1,0:T(8,128)} custom-call(s32[19]{0:T(128)S(1)} %pad_add_fusion.scalars, f32[256,128]{1,0:T(8,128)S(1)} %get-tuple-element.39.after.low_ref, f32[256,128]{1,0:T(8,128)S(1)} %get-tuple-element.40.top_ref, f32[256,128]{1,0:T(8,128)S(1)} %collective-permute-done.13.above_ref, f32[256,128]{1,0:T(8,128)S(1)} %collective-permute-done.14.below_ref, ...), custom_call_target="tpu_custom_call" | custom-call | flops 400000000 | bytes 2000000 | tf_op jit(solution)/shard_map/fourth_kernel/pallas_call | solution.py:261
  (1 shorter events, 0.0 us)
Async XLA Ops:
  0.0 6.2 %collective-permute-start.2 = (f32[128,128]{1,0:T(8,128)}, f32[128,128]{1,0:T(8,128)S(1)}, u32[]{:S(2)}, u32[]{:S(2)}) collective-permute-start(f32[128,128]{1,0:T(8,128)} %bitcast.5), channel_id=1, source_target_pairs={{0,12},{1,13},{2,14},{3,15},{4,0},{5,1},{6,2},{7,3},{8,4},{9,5},{1... | collective-permute-start | bytes 196616 | tf_op jit(solution)/shard_map/ppermute | solution.py:275
  1.8 6.6 %collective-permute-start.1 = (f32[128,128]{1,0:T(8,128)}, f32[128,128]{1,0:T(8,128)S(1)}, u32[]{:S(2)}, u32[]{:S(2)}) collective-permute-start(f32[128,128]{1,0:T(8,128)} %bitcast.6), channel_id=1, source_target_pairs={{0,8},{1,9},{2,10},{3,11},{4,12},{5,13},{6,14},{7,15},{8,0},{9,1},... | collective-permute-start | bytes 196616 | tf_op jit(solution)/shard_map/ppermute | solution.py:275
  3.4 6.2 %collective-permute-start = (f32[128,128]{1,0:T(8,128)}, f32[128,128]{1,0:T(8,128)S(1)}, u32[]{:S(2)}, u32[]{:S(2)}) collective-permute-start(f32[128,128]{1,0:T(8,128)} %bitcast.7), channel_id=1, source_target_pairs={{0,4},{1,5},{2,6},{3,7},{4,8},{5,9},{6,10},{7,11},{8,12},{9,13},{1... | collective-permute-start | bytes 196616 | tf_op jit(solution)/shard_map/ppermute | solution.py:275
  9.6 0.8 %copy-start.1 = (f32[1,128,128]{2,1,0:T(8,128)S(1)}, f32[1,128,128]{2,1,0:T(8,128)}, u32[]{:S(2)}) copy-start(f32[1,128,128]{2,1,0:T(8,128)} %param.4) | copy-start | bytes 196612
  10.4 14.8 %copy-start = (f32[512,128]{1,0:T(8,128)S(1)}, f32[512,128]{1,0:T(8,128)}, u32[]{:S(2)}) copy-start(f32[512,128]{1,0:T(8,128)} %x_ref.1) | copy-start | bytes 786436
  10.4 9.3 %collective-permute-start.5 = (f32[2,128,128]{2,1,0:T(8,128)S(1)}, f32[2,128,128]{2,1,0:T(8,128)S(1)}, u32[]{:S(2)}, u32[]{:S(2)}) collective-permute-start(f32[2,128,128]{2,1,0:T(8,128)S(1)} %get-tuple-element.25.p0), channel_id=1, source_target_pairs={{0,3},{1,0},{2,1},{3,2},{4,7},{5,4},{6,5},{7,6},{8,11},{9,8},{10,9... | collective-permute-start | bytes 393224 | tf_op jit(solution)/shard_map/ppermute | solution.py:279
  13.3 7.4 %collective-permute-start.4 = (f32[2,128,128]{2,1,0:T(8,128)S(1)}, f32[2,128,128]{2,1,0:T(8,128)S(1)}, u32[]{:S(2)}, u32[]{:S(2)}) collective-permute-start(f32[2,128,128]{2,1,0:T(8,128)S(1)} %get-tuple-element.25.p0), channel_id=1, source_target_pairs={{0,2},{1,3},{2,0},{3,1},{4,6},{5,7},{6,4},{7,5},{8,10},{9,11},{10,... | collective-permute-start | bytes 393224 | tf_op jit(solution)/shard_map/ppermute | solution.py:279
  14.1 11.1 %collective-permute-start.3 = (f32[2,128,128]{2,1,0:T(8,128)S(1)}, f32[2,128,128]{2,1,0:T(8,128)S(1)}, u32[]{:S(2)}, u32[]{:S(2)}) collective-permute-start(f32[2,128,128]{2,1,0:T(8,128)S(1)} %get-tuple-element.25.p0), channel_id=1, source_target_pairs={{0,1},{1,2},{2,3},{3,0},{4,5},{5,6},{6,7},{7,4},{8,9},{9,10},{10,1... | collective-permute-start | bytes 393224 | tf_op jit(solution)/shard_map/ppermute | solution.py:279
  15.0 0.7 copy-start.2
  15.9 18.3 %collective-permute-start.10 = (f32[2,128,128]{2,1,0:T(8,128)S(1)}, f32[2,128,128]{2,1,0:T(8,128)S(1)}, u32[]{:S(2)}, u32[]{:S(2)}) collective-permute-start(f32[2,128,128]{2,1,0:T(8,128)S(1)} %get-tuple-element.34.p0), channel_id=1, source_target_pairs={{0,3},{1,0},{2,1},{3,2},{4,7},{5,4},{6,5},{7,6},{8,11},{9,8},{10,9... | collective-permute-start | bytes 393224 | tf_op jit(solution)/shard_map/ppermute | solution.py:279
  18.3 15.9 %collective-permute-start.9 = (f32[2,128,128]{2,1,0:T(8,128)S(1)}, f32[2,128,128]{2,1,0:T(8,128)S(1)}, u32[]{:S(2)}, u32[]{:S(2)}) collective-permute-start(f32[2,128,128]{2,1,0:T(8,128)S(1)} %get-tuple-element.34.p0), channel_id=1, source_target_pairs={{0,2},{1,3},{2,0},{3,1},{4,6},{5,7},{6,4},{7,5},{8,10},{9,11},{10,... | collective-permute-start | bytes 393224 | tf_op jit(solution)/shard_map/ppermute | solution.py:279
  19.8 14.4 %collective-permute-start.8 = (f32[2,128,128]{2,1,0:T(8,128)S(1)}, f32[2,128,128]{2,1,0:T(8,128)S(1)}, u32[]{:S(2)}, u32[]{:S(2)}) collective-permute-start(f32[2,128,128]{2,1,0:T(8,128)S(1)} %get-tuple-element.34.p0), channel_id=1, source_target_pairs={{0,1},{1,2},{2,3},{3,0},{4,5},{5,6},{6,7},{7,4},{8,9},{9,10},{10,1... | collective-permute-start | bytes 393224 | tf_op jit(solution)/shard_map/ppermute | solution.py:279
  28.9 14.8 %collective-permute-start.6 = (f32[384,128]{1,0:T(8,128)S(1)}, f32[384,128]{1,0:T(8,128)S(1)}, u32[]{:S(2)}, u32[]{:S(2)}) collective-permute-start(f32[384,128]{1,0:T(8,128)S(1)} %get-tuple-element.27), channel_id=1, source_target_pairs={{0,240},{16,0},{32,16},{48,32},{64,48},{80,64},{96,80},{112,96},{1... | collective-permute-start | bytes 589832 | tf_op jit(solution)/shard_map/ppermute | solution.py:275
  34.8 23.2 %collective-permute-start.12 = (f32[3,128,128]{2,1,0:T(8,128)S(1)}, f32[3,128,128]{2,1,0:T(8,128)S(1)}, u32[]{:S(2)}, u32[]{:S(2)}) collective-permute-start(f32[3,128,128]{2,1,0:T(8,128)S(1)} %get-tuple-element.36), channel_id=1, source_target_pairs={{0,16},{16,32},{32,48},{48,64},{64,80},{80,96},{96,112},{112,128},... | collective-permute-start | bytes 589832 | tf_op jit(solution)/shard_map/ppermute | solution.py:275
  47.0 11.5 %collective-permute-start.7 = (f32[256,128]{1,0:T(8,128)S(1)}, f32[256,128]{1,0:T(8,128)S(1)}, u32[]{:S(2)}, u32[]{:S(2)}) collective-permute-start(f32[256,128]{1,0:T(8,128)S(1)} %get-tuple-element.33), channel_id=1, source_target_pairs={{0,16},{16,32},{32,48},{48,64},{64,80},{80,96},{96,112},{112,128},... | collective-permute-start | bytes 393224 | tf_op jit(solution)/shard_map/ppermute | solution.py:275
  47.1 10.9 %collective-permute-start.11 = (f32[128,128]{1,0:T(8,128)S(1)}, f32[128,128]{1,0:T(8,128)S(1)}, u32[]{:S(2)}, u32[]{:S(2)}) collective-permute-start(f32[128,128]{1,0:T(8,128)S(1)} %get-tuple-element.35), channel_id=1, source_target_pairs={{0,240},{16,0},{32,16},{48,32},{64,48},{80,64},{96,80},{112,96},{1... | collective-permute-start | bytes 196616 | tf_op jit(solution)/shard_map/ppermute | solution.py:275
  59.9 11.6 %collective-permute-start.14 = (f32[256,128]{1,0:T(8,128)S(1)}, f32[256,128]{1,0:T(8,128)S(1)}, u32[]{:S(2)}, u32[]{:S(2)}) collective-permute-start(f32[256,128]{1,0:T(8,128)S(1)} %get-tuple-element.40.top_ref), channel_id=1, source_target_pairs={{0,240},{16,0},{32,16},{48,32},{64,48},{80,64},{96,80},{112,96},{1... | collective-permute-start | bytes 393224 | tf_op jit(solution)/shard_map/ppermute | solution.py:275
  66.5 10.4 %collective-permute-start.13 = (f32[256,128]{1,0:T(8,128)S(1)}, f32[256,128]{1,0:T(8,128)S(1)}, u32[]{:S(2)}, u32[]{:S(2)}) collective-permute-start(f32[256,128]{1,0:T(8,128)S(1)} %get-tuple-element.39.after.low_ref), channel_id=1, source_target_pairs={{0,16},{16,32},{32,48},{48,64},{64,80},{80,96},{96,112},{112,128},... | collective-permute-start | bytes 393224 | tf_op jit(solution)/shard_map/ppermute | solution.py:275

commit v5 on v4

--- a/solution.py
+++ b/solution.py
@@ -113,21 +113,18 @@
     return [(*a, *split(r.T)) for a, r in zip(products, reflectors)]
 
 
-def stored_factors(packed, a_ref, v_ref):
-    for at, (ah, al, vh, vl) in enumerate(factors(packed)):
-        a_ref[at, :, : 2 * W] = ah
-        a_ref[at, :, 2 * W :] = al
-        v_ref[at, :, :W] = vh
-        v_ref[at, :, W:] = vl
-
-
-def loaded(a_ref, v_ref, at):
-    a, v = a_ref[at], v_ref[at]
-    return a[:, : 2 * W], a[:, 2 * W :], v[:, :W], v[:, W:]
+def whole(factor):
+    ah, al, vh, vl = factor
+    return jnp.concatenate(split(dot3((vh, vl), (ah, al))), axis=1)
+
+
+def stored_wholes(packed, g_ref):
+    for at, factor in enumerate(factors(packed)):
+        g_ref[at] = whole(factor)
 
 
 def slot_of(scalars, level, half):
-    return scalars[3 + 2 * level + half]
+    return scalars[2 + 2 * level + half]
 
 
 def gathered(scalars, pieces, held, at):
@@ -139,26 +136,34 @@
     return held[2 * (level % 2) + slot_of(scalars, level, half)]
 
 
-def applied(x, factor):
+def twice(factor):
     ah, al, vh, vl = factor
-    x_parts = split(x)
-    z_parts = split(dot3((ah, al), x_parts))
-    return x - dot3((vh, vl), z_parts)
-
-
-def across(top, low, factor):
-    middle = applied(jnp.concatenate([top[W:], low[:W]], axis=0), factor)
+
+    def update(x):
+        return x - dot3((vh, vl), split(dot3((ah, al), split(x))))
+
+    return update
+
+
+def once(g_ref, at):
+    g = g_ref[at]
+
+    def update(x):
+        xh, xl = split(x)
+        wide = mm(g[:, : 2 * W], jnp.concatenate([xh, xl], axis=1))
+        return x - (wide[:, :W] + (wide[:, W:] + mm(g[:, 2 * W :], xh)))
+
+    return update
+
+
+def across(top, low, update):
+    middle = update(jnp.concatenate([top[W:], low[:W]], axis=0))
     return jnp.concatenate([top[:W], middle[:W]], axis=0), jnp.concatenate([middle[W:], low[W:]], axis=0)
 
 
-def across_below(last, low, below, factor):
-    new_low, new_below = across(low, jnp.where(last, 0.0, below), factor)
+def across_below(last, low, below, update):
+    new_low, new_below = across(low, jnp.where(last, 0.0, below), update)
     return new_low, jnp.where(last, below, new_below)
-
-
-def across_above(first, above, top, factor):
-    new_above, new_top = across(above, top, factor)
-    return new_above, jnp.where(first, top, new_top)
 
 
 def order_kernel(plane, p0, p1, p2, p3, near, far, held):
@@ -168,86 +173,83 @@
     far[...] = held[2:4]
 
 
-def first_kernel(scalars, x_ref, p0, p1, p2, p3, message, low_ref, a0, v0, held):
+def first_kernel(scalars, x_ref, p0, p1, p2, p3, message, low_ref, held):
     pieces = (p0, p1, p2, p3)
     gathered(scalars, pieces, held, 1)
     message[2 * W :] = block_of(scalars, held, 2, 0)
     gathered(scalars, pieces, held, 0)
-    stored_factors([block_of(scalars, held, level, half) for level in (0, 1) for half in (0, 1)], a0, v0)
-    top = applied(x_ref[: 2 * W], loaded(a0, v0, 0))
-    low = applied(x_ref[2 * W :], loaded(a0, v0, 1))
-    top, low = across(top, low, loaded(a0, v0, 2))
+    found = factors([block_of(scalars, held, level, half) for level, half in ((0, 0), (0, 1), (1, 0))])
+    top = twice(found[0])(x_ref[: 2 * W])
+    low = twice(found[1])(x_ref[2 * W :])
+    top, low = across(top, low, twice(found[2]))
     message[: 2 * W] = top
     low_ref[...] = low
 
 
-def factor1_kernel(scalars, after, p0, p1, p2, p3, a1, v1, held):
-    gathered(scalars, (p0, p1, p2, p3), held, 1)
-    stored_factors([block_of(scalars, held, level, half) for level, half in ((2, 1), (3, 0), (3, 1))], a1, v1)
-
-
-def second_kernel(scalars, low_ref, message, a0, v0, a1, v1, low_out, below_out):
+def factor1_kernel(scalars, after, p0, p1, p2, p3, far, g1, sent, held):
+    sent[...] = far[...]
+    pieces = (p0, p1, p2, p3)
+    gathered(scalars, pieces, held, 0)
+    early = block_of(scalars, held, 1, 1)
+    gathered(scalars, pieces, held, 1)
+    late = [block_of(scalars, held, level, half) for level, half in ((2, 1), (3, 0), (3, 1))]
+    stored_wholes([*late, early], g1)
+
+
+def second_kernel(scalars, low_ref, message, g1, low_out, below_out):
     last = scalars[1] == 1
     (foreign,) = factors([message[2 * W :]])
-    low, below = across_below(last, low_ref[...], message[: 2 * W], loaded(a0, v0, 3))
-    low = applied(low, loaded(a1, v1, 0))
-    below = applied(below, foreign)
-    low, below = across_below(last, low, below, loaded(a1, v1, 2))
+    low, below = across_below(last, low_ref[...], message[: 2 * W], once(g1, 3))
+    low = once(g1, 0)(low)
+    below = twice(foreign)(below)
+    low, below = across_below(last, low, below, once(g1, 2))
     low_out[...] = low
     below_out[...] = below
 
 
-def choose_kernel(scalars, after, p0, p1, p2, p3, down, up, held):
-    pieces = (p0, p1, p2, p3)
-    gathered(scalars, pieces, held, 1)
-    down[1] = block_of(scalars, held, 6, 1)
-    down[2] = block_of(scalars, held, 7, 1)
+def choose_kernel(scalars, after, p0, p1, p2, p3, up, held):
+    gathered(scalars, (p0, p1, p2, p3), held, 1)
     up[...] = block_of(scalars, held, 6, 0)
-    gathered(scalars, pieces, held, 0)
-    down[0] = block_of(scalars, held, 5, 1)
-
-
-def factor2_kernel(scalars, after, p0, p1, p2, p3, a2, v2, held):
+
+
+def factor2_kernel(scalars, after, p0, p1, p2, p3, g2, held):
     gathered(scalars, (p0, p1, p2, p3), held, 0)
-    stored_factors([block_of(scalars, held, level, half) for level in (4, 5) for half in (0, 1)], a2, v2)
-
-
-def third_kernel(low_ref, top_ref, after1, after2, a1, v1, a2, v2, low_out, top_out):
-    top, low = across(top_ref[...], low_ref[...], loaded(a1, v1, 1))
-    top = applied(top, loaded(a2, v2, 0))
-    low = applied(low, loaded(a2, v2, 1))
-    top, low = across(top, low, loaded(a2, v2, 2))
+    stored_wholes([block_of(scalars, held, level, half) for level in (4, 5) for half in (0, 1)], g2)
+
+
+def third_kernel(low_ref, top_ref, after, g1, g2, low_out, top_out):
+    top, low = across(top_ref[...], low_ref[...], once(g1, 1))
+    top = once(g2, 0)(top)
+    low = once(g2, 1)(low)
+    top, low = across(top, low, once(g2, 2))
     low_out[...] = low
     top_out[...] = top
 
 
-def factor3_kernel(scalars, after, p0, p1, p2, p3, a3, v3, held):
+def factor3_kernel(scalars, after, up, p0, p1, p2, p3, g3, held):
     gathered(scalars, (p0, p1, p2, p3), held, 1)
-    stored_factors([block_of(scalars, held, level, half) for level in (6, 7) for half in (0, 1)], a3, v3)
-
-
-def factor4_kernel(after, down, up, a4, v4):
-    stored_factors([down[0], down[1], down[2], up[...]], a4, v4)
-
-
-def fourth_kernel(scalars, low_ref, top_ref, above_ref, below_ref, a2, v2, a3, v3, a4, v4, out_ref):
+    own = [block_of(scalars, held, level, half) for level, half in ((6, 1), (7, 0), (7, 1))]
+    stored_wholes([*own, up[...]], g3)
+
+
+def fourth_kernel(scalars, low_ref, below_ref, g2, g3, low_out, below_out):
     last = scalars[1] == 1
-    first = scalars[2] == 1
-    low, below = across_below(last, low_ref[...], below_ref[...], loaded(a2, v2, 3))
-    above, top = across_above(first, above_ref[...], top_ref[...], loaded(a4, v4, 0))
-    above = applied(above, loaded(a4, v4, 1))
-    top = applied(top, loaded(a3, v3, 0))
-    low = applied(low, loaded(a3, v3, 1))
-    below = applied(below, loaded(a4, v4, 3))
-    _, top = across_above(first, above, top, loaded(a4, v4, 2))
-    low, _ = across_below(last, low, below, loaded(a3, v3, 3))
-    top, low = across(top, low, loaded(a3, v3, 2))
+    low, below = across_below(last, low_ref[...], below_ref[...], once(g2, 3))
+    low = once(g3, 0)(low)
+    below = once(g3, 3)(below)
+    low, below = across_below(last, low, below, once(g3, 2))
+    low_out[...] = low
+    below_out[...] = below
+
+
+def last_kernel(low_ref, top_ref, g3, out_ref):
+    top, low = across(top_ref[...], low_ref[...], once(g3, 1))
     out_ref[: 2 * W] = top
     out_ref[2 * W :] = low
 
 
-def factor_shapes(count):
-    return [jax.ShapeDtypeStruct((count, W, 4 * W), BF16), jax.ShapeDtypeStruct((count, 2 * W, 2 * W), BF16)]
+def wholes(count):
+    return jax.ShapeDtypeStruct((count, 2 * W, 4 * W), BF16)
 
 
 def rows_shape(*shape):
@@ -283,7 +285,7 @@
     column = lax.axis_index("cols")
     row = lax.axis_index("rows")
     plane, place = column // 4, column % 4
-    edges = jnp.stack([place, row == lax.axis_size("rows") - 1, row == 0]).astype(jnp.int32)
+    edges = jnp.stack([place, row == lax.axis_size("rows") - 1]).astype(jnp.int32)
     scalars = jnp.concatenate([edges, slot_block.reshape(-1)])
     packed = wy_packed[0]
     half = rows_shape(2 * W, W)
@@ -292,26 +294,21 @@
     pair = rows_shape(2, W, W)
     near, far = call(order_kernel, (plane.reshape(1), *planes), [pair, pair], HELD)
     near = along_x(near)
+    message, low = call(first_kernel, (scalars, eigvecs, *near), [rows_shape(3 * W, W), half], HELD)
+    message = shifted(message, "rows", -1)
+    g1, far = call(factor1_kernel, (scalars, low, *near, far), [wholes(4), pair], HELD)
     far = along_x(far)
-    message, low, a0, v0 = call(
-        first_kernel, (scalars, eigvecs, *near), [rows_shape(3 * W, W), half, *factor_shapes(4)], HELD
-    )
-    message = shifted(message, "rows", -1)
-    a1, v1 = call(factor1_kernel, (scalars, low, *near), factor_shapes(3), HELD)
-    down, up = call(choose_kernel, (scalars, low, *far), [rows_shape(3, W, W), rows_shape(W, W)], HELD)
-    down = shifted(down, "rows", 1)
+    low, below = call(second_kernel, (scalars, low, message, g1), [half, half])
+    top = shifted(below, "rows", 1)
+    (up,) = call(choose_kernel, (scalars, low, *far), [rows_shape(W, W)], HELD)
+    (g2,) = call(factor2_kernel, (scalars, up, *far), [wholes(4)], HELD)
     up = shifted(up, "rows", -1)
-    low, below = call(second_kernel, (scalars, low, message, a0, v0, a1, v1), [half, half])
+    low, top = call(third_kernel, (low, top, up, g1, g2), [half, half], smem=0)
+    below = shifted(top, "rows", -1)
+    (g3,) = call(factor3_kernel, (scalars, low, up, *far), [wholes(4)], HELD)
+    low, below = call(fourth_kernel, (scalars, low, below, g2, g3), [half, half])
     top = shifted(below, "rows", 1)
-    a2, v2 = call(factor2_kernel, (scalars, low, *far), factor_shapes(4), HELD)
-    low, own = call(third_kernel, (low, top, up, down, a1, v1, a2, v2), [half, half], smem=0)
-    above = shifted(low, "rows", 1)
-    below = shifted(own, "rows", -1)
-    a3, v3 = call(factor3_kernel, (scalars, low, *far), factor_shapes(4), HELD)
-    a4, v4 = call(factor4_kernel, (low, down, up), factor_shapes(4), smem=0)
-    return call(
-        fourth_kernel, (scalars, low, own, above, below, a2, v2, a3, v3, a4, v4), [rows_shape(*eigvecs.shape)]
-    )[0]
+    return call(last_kernel, (low, top, g3), [rows_shape(*eigvecs.shape)], smem=0)[0]
 
 
 def solution(mesh):

time: 80.1 us -> 80.2 us (level)
  the two profiles are of different devices: /device:TPU:32 before, /device:TPU:36 now
where the time goes in v5:
time: 80.2 us; the launch traced here: 80.1 us
  starting transfers between devices  35.8 us (45%)
  waiting for transfers between devices  23.2 us (29%)
  Pallas kernels  19.2 us (24%)
  local copies, waits for them, and re-layouts  1.68 us (2%)
    ppermute x8, starting transfers between devices, shifted(): lax.ppermute(value, axis, [(i, (i + steps) % count) for i in range(count)])  26.6 us
    pallas_call x10, Pallas kernels, call(): pl.pallas_call(kernel, out_shape=tuple(shapes), in_specs=[pl.BlockSpec(me...  19.2 us
    ppermute x8, waiting for transfers between devices, shifted(): lax.ppermute(value, axis, [(i, (i + steps) % count) for i in range(count)])  18.1 us
    ppermute x6, starting transfers between devices, along_x(): lax.ppermute(value, 'cols', [(i, i // 4 * 4 + (i + k) % 4) for i in range...  9.2 us
    ppermute x6, waiting for transfers between devices, along_x(): lax.ppermute(value, 'cols', [(i, i // 4 * 4 + (i + k) % 4) for i in range...  5.08 us
  transfers between devices with their start and end apart: 14, of which 8 were waited for; matrix products, arithmetic and copies ran while one was open for 0% of the time, Pallas kernels for 16%

profile of v5, /device:TPU:36, one launch (start us, length us, event | category | flops | bytes accessed | tf_op | source)
XLA Modules:
  0.0 80.1 jit_solution(12335266859241752670)
XLA Ops:
  0.0 0.1 collective-permute-start.2
  0.1 3.3 %collective-permute-start.1 = (f32[128,128]{1,0:T(8,128)}, f32[128,128]{1,0:T(8,128)S(1)}, u32[]{:S(2)}, u32[]{:S(2)}) collective-permute-start(f32[128,128]{1,0:T(8,128)} %bitcast.5), channel_id=1, source_target_pairs={{0,8},{1,9},{2,10},{3,11},{4,12},{5,13},{6,14},{7,15},{8,0},{9,1},... | collective-permute-start | bytes 196616 | tf_op jit(solution)/shard_map/ppermute | solution.py:277
  3.4 2.8 %collective-permute-start = (f32[128,128]{1,0:T(8,128)}, f32[128,128]{1,0:T(8,128)S(1)}, u32[]{:S(2)}, u32[]{:S(2)}) collective-permute-start(f32[128,128]{1,0:T(8,128)} %bitcast.6), channel_id=1, source_target_pairs={{0,4},{1,5},{2,6},{3,7},{4,8},{5,9},{6,10},{7,11},{8,12},{9,13},{1... | collective-permute-start | bytes 196616 | tf_op jit(solution)/shard_map/ppermute | solution.py:277
  6.2 0.0 collective-permute-done.2.p3
  6.2 2.2 %collective-permute-done.1.p2 = f32[128,128]{1,0:T(8,128)S(1)} collective-permute-done((f32[128,128]{1,0:T(8,128)}, f32[128,128]{1,0:T(8,128)S(1)}, u32[]{:S(2)}, u32[]{:S(2)}) %collective-permute-start.1) | collective-permute-done | bytes 65568 | tf_op jit(solution)/shard_map/ppermute | solution.py:277
  8.4 1.2 %collective-permute-done.p1 = f32[128,128]{1,0:T(8,128)S(1)} collective-permute-done((f32[128,128]{1,0:T(8,128)}, f32[128,128]{1,0:T(8,128)S(1)}, u32[]{:S(2)}, u32[]{:S(2)}) %collective-permute-start) | collective-permute-done | bytes 65568 | tf_op jit(solution)/shard_map/ppermute | solution.py:277
  9.6 0.0 copy-start.1
  9.6 0.8 %copy-done.1 = f32[1,128,128]{2,1,0:T(8,128)S(1)} copy-done((f32[1,128,128]{2,1,0:T(8,128)S(1)}, f32[1,128,128]{2,1,0:T(8,128)}, u32[]{:S(2)}) %copy-start.1) | copy-done | bytes 65560
  10.4 0.0 copy-start
  10.4 0.6 collective-permute-start.5
  11.1 2.7 %collective-permute-start.4 = (f32[2,128,128]{2,1,0:T(8,128)S(1)}, f32[2,128,128]{2,1,0:T(8,128)S(1)}, u32[]{:S(2)}, u32[]{:S(2)}) collective-permute-start(f32[2,128,128]{2,1,0:T(8,128)S(1)} %get-tuple-element.17.p0), channel_id=1, source_target_pairs={{0,2},{1,3},{2,0},{3,1},{4,6},{5,7},{6,4},{7,5},{8,10},{9,11},{10,... | collective-permute-start | bytes 393224 | tf_op jit(solution)/shard_map/ppermute | solution.py:281
  13.8 0.0 collective-permute-start.3
  13.8 0.0 copy-start.2
  13.8 0.7 copy-done.2
  14.5 0.1 copy.5
  14.6 0.1 reshape.6
  14.6 0.1 pad_add_fusion.scalars
  14.7 1.9 %collective-permute-done.5.p3 = f32[2,128,128]{2,1,0:T(8,128)S(1)} collective-permute-done((f32[2,128,128]{2,1,0:T(8,128)S(1)}, f32[2,128,128]{2,1,0:T(8,128)S(1)}, u32[]{:S(2)}, u32[]{:S(2)}) %collective-permute-start.5) | collective-permute-done | bytes 131104 | tf_op jit(solution)/shard_map/ppermute | solution.py:281
  16.6 1.9 %collective-permute-done.4.p2 = f32[2,128,128]{2,1,0:T(8,128)S(1)} collective-permute-done((f32[2,128,128]{2,1,0:T(8,128)S(1)}, f32[2,128,128]{2,1,0:T(8,128)S(1)}, u32[]{:S(2)}, u32[]{:S(2)}) %collective-permute-start.4) | collective-permute-done | bytes 131104 | tf_op jit(solution)/shard_map/ppermute | solution.py:281
  18.5 1.3 %collective-permute-done.3.p1 = f32[2,128,128]{2,1,0:T(8,128)S(1)} collective-permute-done((f32[2,128,128]{2,1,0:T(8,128)S(1)}, f32[2,128,128]{2,1,0:T(8,128)S(1)}, u32[]{:S(2)}, u32[]{:S(2)}) %collective-permute-start.3) | collective-permute-done | bytes 131104 | tf_op jit(solution)/shard_map/ppermute | solution.py:281
  19.8 0.0 copy-done
  19.8 3.4 %first_kernel.1 = (f32[384,128]{1,0:T(8,128)S(1)}, f32[256,128]{1,0:T(8,128)S(1)}) custom-call(s32[18]{0:T(128)S(1)} %pad_add_fusion.scalars, f32[512,128]{1,0:T(8,128)S(1)} %copy-done, f32[2,128,128]{2,1,0:T(8,128)S(1)} %get-tuple-element.17.p0, f32[2,128,128]{2,1,0:T(8,128)S(1)} %collective-permute-done.3.p1, ...), custom_call_target="tpu_custom_call" | custom-call | flops 400000000 | bytes 2000000 | tf_op jit(solution)/shard_map/first_kernel/pallas_call | solution.py:263
  23.2 6.9 %collective-permute-start.6 = (f32[384,128]{1,0:T(8,128)S(1)}, f32[384,128]{1,0:T(8,128)S(1)}, u32[]{:S(2)}, u32[]{:S(2)}) collective-permute-start(f32[384,128]{1,0:T(8,128)S(1)} %get-tuple-element.19), channel_id=1, source_target_pairs={{0,240},{16,0},{32,16},{48,32},{64,48},{80,64},{96,80},{112,96},{1... | collective-permute-start | bytes 589832 | tf_op jit(solution)/shard_map/ppermute | solution.py:277
  30.1 3.2 %factor1_kernel.1 = (bf16[4,256,512]{2,1,0:T(8,128)(2,1)S(1)}, f32[2,128,128]{2,1,0:T(8,128)S(1)}) custom-call(s32[18]{0:T(128)S(1)} %pad_add_fusion.scalars, f32[256,128]{1,0:T(8,128)S(1)} %get-tuple-element.18.after.low_ref, f32[2,128,128]{2,1,0:T(8,128)S(1)} %get-tuple-element.17.p0, f32[2,128,128]{2,1,0:T(8,128)S(1)} %collective-permute-done.3.p1, ...), custom_call_target="tpu_custom_call" | custom-call | flops 400000000 | bytes 2000000 | tf_op jit(solution)/shard_map/factor1_kernel/pallas_call | solution.py:263
  33.3 0.1 collective-permute-start.10
  33.4 3.2 %collective-permute-start.9 = (f32[2,128,128]{2,1,0:T(8,128)S(1)}, f32[2,128,128]{2,1,0:T(8,128)S(1)}, u32[]{:S(2)}, u32[]{:S(2)}) collective-permute-start(f32[2,128,128]{2,1,0:T(8,128)S(1)} %get-tuple-element.24.p0), channel_id=1, source_target_pairs={{0,2},{1,3},{2,0},{3,1},{4,6},{5,7},{6,4},{7,5},{8,10},{9,11},{10,... | collective-permute-start | bytes 393224 | tf_op jit(solution)/shard_map/ppermute | solution.py:281
  36.6 2.5 %collective-permute-start.8 = (f32[2,128,128]{2,1,0:T(8,128)S(1)}, f32[2,128,128]{2,1,0:T(8,128)S(1)}, u32[]{:S(2)}, u32[]{:S(2)}) collective-permute-start(f32[2,128,128]{2,1,0:T(8,128)S(1)} %get-tuple-element.24.p0), channel_id=1, source_target_pairs={{0,1},{1,2},{2,3},{3,0},{4,5},{5,6},{6,7},{7,4},{8,9},{9,10},{10,1... | collective-permute-start | bytes 393224 | tf_op jit(solution)/shard_map/ppermute | solution.py:281
  39.2 0.0 collective-permute-done.6.message
  39.2 2.8 %second_kernel.1 = (f32[256,128]{1,0:T(8,128)S(1)}, f32[256,128]{1,0:T(8,128)S(1)}) custom-call(s32[18]{0:T(128)S(1)} %pad_add_fusion.scalars, f32[256,128]{1,0:T(8,128)S(1)} %get-tuple-element.18.after.low_ref, f32[384,128]{1,0:T(8,128)S(1)} %collective-permute-done.6.message, bf16[4,256,512]{2,1,0:T(8,128)(2,1)S(1)} %get-tuple-element.21.g1), custom_call_target="tpu_custom_call" | custom-call | flops 400000000 | bytes 2000000 | tf_op jit(solution)/shard_map/second_kernel/pallas_call | solution.py:263
  42.0 0.1 collective-permute-start.7
  42.1 0.0 collective-permute-done.10.p3
  42.1 0.0 collective-permute-done.9.p2
  42.1 0.0 collective-permute-done.8.p1
  42.1 0.6 choose_kernel.1.after
  42.7 7.8 %collective-permute-start.11 = (f32[128,128]{1,0:T(8,128)S(1)}, f32[128,128]{1,0:T(8,128)S(1)}, u32[]{:S(2)}, u32[]{:S(2)}) collective-permute-start(f32[128,128]{1,0:T(8,128)S(1)} %choose_kernel.1.after), channel_id=1, source_target_pairs={{0,240},{16,0},{32,16},{48,32},{64,48},{80,64},{96,80},{112,96},{1... | collective-permute-start | bytes 196616 | tf_op jit(solution)/shard_map/ppermute | solution.py:277
  50.5 3.2 %factor2_kernel.1.g2 = bf16[4,256,512]{2,1,0:T(8,128)(2,1)S(1)} custom-call(s32[18]{0:T(128)S(1)} %pad_add_fusion.scalars, f32[128,128]{1,0:T(8,128)S(1)} %choose_kernel.1.after, f32[2,128,128]{2,1,0:T(8,128)S(1)} %get-tuple-element.24.p0, f32[2,128,128]{2,1,0:T(8,128)S(1)} %collective-permute-done.8.p1, f32[2,128,128]{2,1,0:T(8,128)S(1)} %collective-permute-done.9.p2, ...), custom_call_target="tpu_custom_call" | custom-call | flops 400000000 | bytes 2000000 | tf_op jit(solution)/shard_map/factor2_kernel/pallas_call | solution.py:263
  53.7 0.0 collective-permute-done.11.after.up
  53.7 1.0 %collective-permute-done.7.top_ref = f32[256,128]{1,0:T(8,128)S(1)} collective-permute-done((f32[256,128]{1,0:T(8,128)S(1)}, f32[256,128]{1,0:T(8,128)S(1)}, u32[]{:S(2)}, u32[]{:S(2)}) %collective-permute-start.7) | collective-permute-done | bytes 131104 | tf_op jit(solution)/shard_map/ppermute | solution.py:277
  54.7 0.7 third_kernel.1
  55.4 5.6 %collective-permute-start.12 = (f32[256,128]{1,0:T(8,128)S(1)}, f32[256,128]{1,0:T(8,128)S(1)}, u32[]{:S(2)}, u32[]{:S(2)}) collective-permute-start(f32[256,128]{1,0:T(8,128)S(1)} %get-tuple-element.26), channel_id=1, source_target_pairs={{0,240},{16,0},{32,16},{48,32},{64,48},{80,64},{96,80},{112,96},{1... | collective-permute-start | bytes 393224 | tf_op jit(solution)/shard_map/ppermute | solution.py:277
  61.0 3.2 %factor3_kernel.1.g3 = bf16[4,256,512]{2,1,0:T(8,128)(2,1)S(1)} custom-call(s32[18]{0:T(128)S(1)} %pad_add_fusion.scalars, f32[256,128]{1,0:T(8,128)S(1)} %get-tuple-element.25.after.low_ref, f32[128,128]{1,0:T(8,128)S(1)} %collective-permute-done.11.after.up, f32[2,128,128]{2,1,0:T(8,128)S(1)} %get-tuple-element.24.p0, ...), custom_call_target="tpu_custom_call" | custom-call | flops 400000000 | bytes 2000000 | tf_op jit(solution)/shard_map/factor3_kernel/pallas_call | solution.py:263
  64.2 3.1 %collective-permute-done.12.below_ref = f32[256,128]{1,0:T(8,128)S(1)} collective-permute-done((f32[256,128]{1,0:T(8,128)S(1)}, f32[256,128]{1,0:T(8,128)S(1)}, u32[]{:S(2)}, u32[]{:S(2)}) %collective-permute-start.12) | collective-permute-done | bytes 131104 | tf_op jit(solution)/shard_map/ppermute | solution.py:277
  67.2 1.2 %fourth_kernel.1 = (f32[256,128]{1,0:T(8,128)S(1)}, f32[256,128]{1,0:T(8,128)S(1)}) custom-call(s32[18]{0:T(128)S(1)} %pad_add_fusion.scalars, f32[256,128]{1,0:T(8,128)S(1)} %get-tuple-element.25.after.low_ref, f32[256,128]{1,0:T(8,128)S(1)} %collective-permute-done.12.below_ref, bf16[4,256,512]{2,1,0:T(8,128)(2,1)S(1)} %factor2_kernel.1.g2, ...), custom_call_target="tpu_custom_call" | custom-call | flops 400000000 | bytes 2000000 | tf_op jit(solution)/shard_map/fourth_kernel/pallas_call | solution.py:263
  68.4 0.1 collective-permute-start.13
  68.5 10.7 %collective-permute-done.13.top_ref = f32[256,128]{1,0:T(8,128)S(1)} collective-permute-done((f32[256,128]{1,0:T(8,128)S(1)}, f32[256,128]{1,0:T(8,128)S(1)}, u32[]{:S(2)}, u32[]{:S(2)}) %collective-permute-start.13) | collective-permute-done | bytes 131104 | tf_op jit(solution)/shard_map/ppermute | solution.py:277
  79.2 0.9 %last_kernel.1 = f32[512,128]{1,0:T(8,128)} custom-call(f32[256,128]{1,0:T(8,128)S(1)} %get-tuple-element.27.low_ref, f32[256,128]{1,0:T(8,128)S(1)} %collective-permute-done.13.top_ref, bf16[4,256,512]{2,1,0:T(8,128)(2,1)S(1)} %factor3_kernel.1.g3), custom_call_target="tpu_custom_call" | custom-call | flops 400000000 | bytes 2000000 | tf_op jit(solution)/shard_map/last_kernel/pallas_call | solution.py:263
  (1 shorter events, 0.0 us)
Async XLA Ops:
  0.0 6.2 %collective-permute-start.2 = (f32[128,128]{1,0:T(8,128)}, f32[128,128]{1,0:T(8,128)S(1)}, u32[]{:S(2)}, u32[]{:S(2)}) collective-permute-start(f32[128,128]{1,0:T(8,128)} %bitcast.4), channel_id=1, source_target_pairs={{0,12},{1,13},{2,14},{3,15},{4,0},{5,1},{6,2},{7,3},{8,4},{9,5},{1... | collective-permute-start | bytes 196616 | tf_op jit(solution)/shard_map/ppermute | solution.py:277
  0.1 8.3 %collective-permute-start.1 = (f32[128,128]{1,0:T(8,128)}, f32[128,128]{1,0:T(8,128)S(1)}, u32[]{:S(2)}, u32[]{:S(2)}) collective-permute-start(f32[128,128]{1,0:T(8,128)} %bitcast.5), channel_id=1, source_target_pairs={{0,8},{1,9},{2,10},{3,11},{4,12},{5,13},{6,14},{7,15},{8,0},{9,1},... | collective-permute-start | bytes 196616 | tf_op jit(solution)/shard_map/ppermute | solution.py:277
  3.4 6.2 %collective-permute-start = (f32[128,128]{1,0:T(8,128)}, f32[128,128]{1,0:T(8,128)S(1)}, u32[]{:S(2)}, u32[]{:S(2)}) collective-permute-start(f32[128,128]{1,0:T(8,128)} %bitcast.6), channel_id=1, source_target_pairs={{0,4},{1,5},{2,6},{3,7},{4,8},{5,9},{6,10},{7,11},{8,12},{9,13},{1... | collective-permute-start | bytes 196616 | tf_op jit(solution)/shard_map/ppermute | solution.py:277
  9.6 0.8 %copy-start.1 = (f32[1,128,128]{2,1,0:T(8,128)S(1)}, f32[1,128,128]{2,1,0:T(8,128)}, u32[]{:S(2)}) copy-start(f32[1,128,128]{2,1,0:T(8,128)} %param.4) | copy-start | bytes 196612
  10.4 9.4 %copy-start = (f32[512,128]{1,0:T(8,128)S(1)}, f32[512,128]{1,0:T(8,128)}, u32[]{:S(2)}) copy-start(f32[512,128]{1,0:T(8,128)} %x_ref.1) | copy-start | bytes 786436
  10.4 6.2 %collective-permute-start.5 = (f32[2,128,128]{2,1,0:T(8,128)S(1)}, f32[2,128,128]{2,1,0:T(8,128)S(1)}, u32[]{:S(2)}, u32[]{:S(2)}) collective-permute-start(f32[2,128,128]{2,1,0:T(8,128)S(1)} %get-tuple-element.17.p0), channel_id=1, source_target_pairs={{0,3},{1,0},{2,1},{3,2},{4,7},{5,4},{6,5},{7,6},{8,11},{9,8},{10,9... | collective-permute-start | bytes 393224 | tf_op jit(solution)/shard_map/ppermute | solution.py:281
  11.1 7.4 %collective-permute-start.4 = (f32[2,128,128]{2,1,0:T(8,128)S(1)}, f32[2,128,128]{2,1,0:T(8,128)S(1)}, u32[]{:S(2)}, u32[]{:S(2)}) collective-permute-start(f32[2,128,128]{2,1,0:T(8,128)S(1)} %get-tuple-element.17.p0), channel_id=1, source_target_pairs={{0,2},{1,3},{2,0},{3,1},{4,6},{5,7},{6,4},{7,5},{8,10},{9,11},{10,... | collective-permute-start | bytes 393224 | tf_op jit(solution)/shard_map/ppermute | solution.py:281
  13.8 6.0 %collective-permute-start.3 = (f32[2,128,128]{2,1,0:T(8,128)S(1)}, f32[2,128,128]{2,1,0:T(8,128)S(1)}, u32[]{:S(2)}, u32[]{:S(2)}) collective-permute-start(f32[2,128,128]{2,1,0:T(8,128)S(1)} %get-tuple-element.17.p0), channel_id=1, source_target_pairs={{0,1},{1,2},{2,3},{3,0},{4,5},{5,6},{6,7},{7,4},{8,9},{9,10},{10,1... | collective-permute-start | bytes 393224 | tf_op jit(solution)/shard_map/ppermute | solution.py:281
  13.8 0.7 copy-start.2
  23.2 16.0 %collective-permute-start.6 = (f32[384,128]{1,0:T(8,128)S(1)}, f32[384,128]{1,0:T(8,128)S(1)}, u32[]{:S(2)}, u32[]{:S(2)}) collective-permute-start(f32[384,128]{1,0:T(8,128)S(1)} %get-tuple-element.19), channel_id=1, source_target_pairs={{0,240},{16,0},{32,16},{48,32},{64,48},{80,64},{96,80},{112,96},{1... | collective-permute-start | bytes 589832 | tf_op jit(solution)/shard_map/ppermute | solution.py:277
  33.3 8.8 %collective-permute-start.10 = (f32[2,128,128]{2,1,0:T(8,128)S(1)}, f32[2,128,128]{2,1,0:T(8,128)S(1)}, u32[]{:S(2)}, u32[]{:S(2)}) collective-permute-start(f32[2,128,128]{2,1,0:T(8,128)S(1)} %get-tuple-element.24.p0), channel_id=1, source_target_pairs={{0,3},{1,0},{2,1},{3,2},{4,7},{5,4},{6,5},{7,6},{8,11},{9,8},{10,9... | collective-permute-start | bytes 393224 | tf_op jit(solution)/shard_map/ppermute | solution.py:281
  33.4 8.7 %collective-permute-start.9 = (f32[2,128,128]{2,1,0:T(8,128)S(1)}, f32[2,128,128]{2,1,0:T(8,128)S(1)}, u32[]{:S(2)}, u32[]{:S(2)}) collective-permute-start(f32[2,128,128]{2,1,0:T(8,128)S(1)} %get-tuple-element.24.p0), channel_id=1, source_target_pairs={{0,2},{1,3},{2,0},{3,1},{4,6},{5,7},{6,4},{7,5},{8,10},{9,11},{10,... | collective-permute-start | bytes 393224 | tf_op jit(solution)/shard_map/ppermute | solution.py:281
  36.6 5.5 %collective-permute-start.8 = (f32[2,128,128]{2,1,0:T(8,128)S(1)}, f32[2,128,128]{2,1,0:T(8,128)S(1)}, u32[]{:S(2)}, u32[]{:S(2)}) collective-permute-start(f32[2,128,128]{2,1,0:T(8,128)S(1)} %get-tuple-element.24.p0), channel_id=1, source_target_pairs={{0,1},{1,2},{2,3},{3,0},{4,5},{5,6},{6,7},{7,4},{8,9},{9,10},{10,1... | collective-permute-start | bytes 393224 | tf_op jit(solution)/shard_map/ppermute | solution.py:281
  42.0 12.7 %collective-permute-start.7 = (f32[256,128]{1,0:T(8,128)S(1)}, f32[256,128]{1,0:T(8,128)S(1)}, u32[]{:S(2)}, u32[]{:S(2)}) collective-permute-start(f32[256,128]{1,0:T(8,128)S(1)} %get-tuple-element.23), channel_id=1, source_target_pairs={{0,16},{16,32},{32,48},{48,64},{64,80},{80,96},{96,112},{112,128},... | collective-permute-start | bytes 393224 | tf_op jit(solution)/shard_map/ppermute | solution.py:277
  42.7 11.0 %collective-permute-start.11 = (f32[128,128]{1,0:T(8,128)S(1)}, f32[128,128]{1,0:T(8,128)S(1)}, u32[]{:S(2)}, u32[]{:S(2)}) collective-permute-start(f32[128,128]{1,0:T(8,128)S(1)} %choose_kernel.1.after), channel_id=1, source_target_pairs={{0,240},{16,0},{32,16},{48,32},{64,48},{80,64},{96,80},{112,96},{1... | collective-permute-start | bytes 196616 | tf_op jit(solution)/shard_map/ppermute | solution.py:277
  55.4 11.8 %collective-permute-start.12 = (f32[256,128]{1,0:T(8,128)S(1)}, f32[256,128]{1,0:T(8,128)S(1)}, u32[]{:S(2)}, u32[]{:S(2)}) collective-permute-start(f32[256,128]{1,0:T(8,128)S(1)} %get-tuple-element.26), channel_id=1, source_target_pairs={{0,240},{16,0},{32,16},{48,32},{64,48},{80,64},{96,80},{112,96},{1... | collective-permute-start | bytes 393224 | tf_op jit(solution)/shard_map/ppermute | solution.py:277
  68.4 10.8 %collective-permute-start.13 = (f32[256,128]{1,0:T(8,128)S(1)}, f32[256,128]{1,0:T(8,128)S(1)}, u32[]{:S(2)}, u32[]{:S(2)}) collective-permute-start(f32[256,128]{1,0:T(8,128)S(1)} %get-tuple-element.28), channel_id=1, source_target_pairs={{0,16},{16,32},{32,48},{48,64},{64,80},{80,96},{96,112},{112,128},... | collective-permute-start | bytes 393224 | tf_op jit(solution)/shard_map/ppermute | solution.py:277

commit v6 on v5

--- a/solution.py
+++ b/solution.py
@@ -124,7 +124,7 @@
 
 
 def slot_of(scalars, level, half):
-    return scalars[2 + 2 * level + half]
+    return scalars[3 + 2 * level + half]
 
 
 def gathered(scalars, pieces, held, at):
@@ -162,8 +162,7 @@
 
 
 def across_below(last, low, below, update):
-    new_low, new_below = across(low, jnp.where(last, 0.0, below), update)
-    return new_low, jnp.where(last, below, new_below)
+    return across(low, jnp.where(last, 0.0, below), update)
 
 
 def order_kernel(plane, p0, p1, p2, p3, near, far, held):
@@ -193,57 +192,60 @@
     early = block_of(scalars, held, 1, 1)
     gathered(scalars, pieces, held, 1)
     late = [block_of(scalars, held, level, half) for level, half in ((2, 1), (3, 0), (3, 1))]
-    stored_wholes([*late, early], g1)
-
-
-def second_kernel(scalars, low_ref, message, g1, low_out, below_out):
+    stored_wholes([*late, early, block_of(scalars, held, 2, 0)], g1)
+
+
+def second_kernel(scalars, low_ref, own, message, g1, low_out, below_out, top_out):
     last = scalars[1] == 1
     (foreign,) = factors([message[2 * W :]])
     low, below = across_below(last, low_ref[...], message[: 2 * W], once(g1, 3))
     low = once(g1, 0)(low)
     below = twice(foreign)(below)
+    top_out[...] = once(g1, 4)(own[: 2 * W])
     low, below = across_below(last, low, below, once(g1, 2))
     low_out[...] = low
     below_out[...] = below
 
 
-def choose_kernel(scalars, after, p0, p1, p2, p3, up, held):
-    gathered(scalars, (p0, p1, p2, p3), held, 1)
+def factor2_kernel(scalars, after, p0, p1, p2, p3, g2, up, held):
+    pieces = (p0, p1, p2, p3)
+    gathered(scalars, pieces, held, 1)
     up[...] = block_of(scalars, held, 6, 0)
-
-
-def factor2_kernel(scalars, after, p0, p1, p2, p3, g2, held):
-    gathered(scalars, (p0, p1, p2, p3), held, 0)
+    gathered(scalars, pieces, held, 0)
     stored_wholes([block_of(scalars, held, level, half) for level in (4, 5) for half in (0, 1)], g2)
 
 
-def third_kernel(low_ref, top_ref, after, g1, g2, low_out, top_out):
-    top, low = across(top_ref[...], low_ref[...], once(g1, 1))
+def third_kernel(scalars, low_ref, mine, top_ref, up, g1, g2, low_out, message):
+    message[2 * W :] = up[...]
+    top = jnp.where(scalars[2] == 1, mine[...], top_ref[...])
+    top, low = across(top, low_ref[...], once(g1, 1))
     top = once(g2, 0)(top)
     low = once(g2, 1)(low)
     top, low = across(top, low, once(g2, 2))
     low_out[...] = low
-    top_out[...] = top
-
-
-def factor3_kernel(scalars, after, up, p0, p1, p2, p3, g3, held):
+    message[: 2 * W] = top
+
+
+def factor3_kernel(scalars, after, p0, p1, p2, p3, g3, held):
     gathered(scalars, (p0, p1, p2, p3), held, 1)
-    own = [block_of(scalars, held, level, half) for level, half in ((6, 1), (7, 0), (7, 1))]
-    stored_wholes([*own, up[...]], g3)
-
-
-def fourth_kernel(scalars, low_ref, below_ref, g2, g3, low_out, below_out):
+    stored_wholes([block_of(scalars, held, level, half) for level, half in ((6, 1), (7, 0), (7, 1), (6, 0))], g3)
+
+
+def fourth_kernel(scalars, low_ref, own, message, g2, g3, low_out, below_out, top_out):
     last = scalars[1] == 1
-    low, below = across_below(last, low_ref[...], below_ref[...], once(g2, 3))
+    (foreign,) = factors([message[2 * W :]])
+    low, below = across_below(last, low_ref[...], message[: 2 * W], once(g2, 3))
     low = once(g3, 0)(low)
-    below = once(g3, 3)(below)
+    below = twice(foreign)(below)
+    top_out[...] = once(g3, 3)(own[: 2 * W])
     low, below = across_below(last, low, below, once(g3, 2))
     low_out[...] = low
     below_out[...] = below
 
 
-def last_kernel(low_ref, top_ref, g3, out_ref):
-    top, low = across(top_ref[...], low_ref[...], once(g3, 1))
+def last_kernel(scalars, low_ref, mine, top_ref, g3, out_ref):
+    top = jnp.where(scalars[2] == 1, mine[...], top_ref[...])
+    top, low = across(top, low_ref[...], once(g3, 1))
     out_ref[: 2 * W] = top
     out_ref[2 * W :] = low
 
@@ -277,6 +279,11 @@
     return lax.ppermute(value, axis, [(i, (i + steps) % count) for i in range(count)])
 
 
+def to_neighbour(value, steps):
+    count = lax.axis_size("rows")
+    return lax.ppermute(value, "rows", [(i, i + steps) for i in range(count) if 0 <= i + steps < count])
+
+
 def along_x(value):
     return [value] + [lax.ppermute(value, "cols", [(i, (i // 4) * 4 + (i + k) % 4) for i in range(16)]) for k in (1, 2, 3)]
 
@@ -285,7 +292,7 @@
     column = lax.axis_index("cols")
     row = lax.axis_index("rows")
     plane, place = column // 4, column % 4
-    edges = jnp.stack([place, row == lax.axis_size("rows") - 1]).astype(jnp.int32)
+    edges = jnp.stack([place, row == lax.axis_size("rows") - 1, row == 0]).astype(jnp.int32)
     scalars = jnp.concatenate([edges, slot_block.reshape(-1)])
     packed = wy_packed[0]
     half = rows_shape(2 * W, W)
@@ -294,21 +301,20 @@
     pair = rows_shape(2, W, W)
     near, far = call(order_kernel, (plane.reshape(1), *planes), [pair, pair], HELD)
     near = along_x(near)
-    message, low = call(first_kernel, (scalars, eigvecs, *near), [rows_shape(3 * W, W), half], HELD)
-    message = shifted(message, "rows", -1)
-    g1, far = call(factor1_kernel, (scalars, low, *near, far), [wholes(4), pair], HELD)
+    three = rows_shape(3 * W, W)
+    own, low = call(first_kernel, (scalars, eigvecs, *near), [three, half], HELD)
+    message = to_neighbour(own, -1)
+    g1, far = call(factor1_kernel, (scalars, low, *near, far), [wholes(5), pair], HELD)
     far = along_x(far)
-    low, below = call(second_kernel, (scalars, low, message, g1), [half, half])
-    top = shifted(below, "rows", 1)
-    (up,) = call(choose_kernel, (scalars, low, *far), [rows_shape(W, W)], HELD)
-    (g2,) = call(factor2_kernel, (scalars, up, *far), [wholes(4)], HELD)
-    up = shifted(up, "rows", -1)
-    low, top = call(third_kernel, (low, top, up, g1, g2), [half, half], smem=0)
-    below = shifted(top, "rows", -1)
-    (g3,) = call(factor3_kernel, (scalars, low, up, *far), [wholes(4)], HELD)
-    low, below = call(fourth_kernel, (scalars, low, below, g2, g3), [half, half])
-    top = shifted(below, "rows", 1)
-    return call(last_kernel, (low, top, g3), [rows_shape(*eigvecs.shape)], smem=0)[0]
+    low, below, mine = call(second_kernel, (scalars, low, own, message, g1), [half, half, half])
+    top = to_neighbour(below, 1)
+    g2, up = call(factor2_kernel, (scalars, low, *far), [wholes(4), rows_shape(W, W)], HELD)
+    low, own = call(third_kernel, (scalars, low, mine, top, up, g1, g2), [half, three])
+    message = to_neighbour(own, -1)
+    (g3,) = call(factor3_kernel, (scalars, low, *far), [wholes(4)], HELD)
+    low, below, mine = call(fourth_kernel, (scalars, low, own, message, g2, g3), [half, half, half])
+    top = to_neighbour(below, 1)
+    return call(last_kernel, (scalars, low, mine, top, g3), [rows_shape(*eigvecs.shape)])[0]
 
 
 def solution(mesh):

time: 80.2 us -> 79.5 us (level)
  the two profiles are of different devices: /device:TPU:36 before, /device:TPU:56 now
where the time goes in v6:
time: 79.5 us; the launch traced here: 78.4 us
  waiting for transfers between devices  29.8 us (37%)
  starting transfers between devices  25.7 us (32%)
  Pallas kernels  21.7 us (27%)
  local copies, waits for them, and re-layouts  1.01 us (1%)
    pallas_call x9, Pallas kernels, call(): pl.pallas_call(kernel, out_shape=tuple(shapes), in_specs=[pl.BlockSpec(me...  21.7 us
    ppermute x4, waiting for transfers between devices, to_neighbour(): lax.ppermute(value, 'rows', [(i, i + steps) for i in range(count) if 0 <=...  18.6 us
    ppermute x4, starting transfers between devices, to_neighbour(): lax.ppermute(value, 'rows', [(i, i + steps) for i in range(count) if 0 <=...  12.9 us
    ppermute x6, waiting for transfers between devices, along_x(): lax.ppermute(value, 'cols', [(i, i // 4 * 4 + (i + k) % 4) for i in range...  7.83 us
    ppermute x6, starting transfers between devices, along_x(): lax.ppermute(value, 'cols', [(i, i // 4 * 4 + (i + k) % 4) for i in range...  6.62 us
    ppermute x3, starting transfers between devices, shifted(): lax.ppermute(value, axis, [(i, (i + steps) % count) for i in range(count)])  6.2 us
    ppermute x3, waiting for transfers between devices, shifted(): lax.ppermute(value, axis, [(i, (i + steps) % count) for i in range(count)])  3.36 us
  transfers between devices with their start and end apart: 13, of which 9 were waited for; matrix products, arithmetic and copies ran while one was open for 0% of the time, Pallas kernels for 16%

profile of v6, /device:TPU:56, one launch (start us, length us, event | category | flops | bytes accessed | tf_op | source)
XLA Modules:
  0.0 78.4 jit_solution(16885675853943180378)
XLA Ops:
  0.0 0.0 copy-start
  0.0 0.1 collective-permute-start.2
  0.1 3.3 %collective-permute-start.1 = (f32[128,128]{1,0:T(8,128)}, f32[128,128]{1,0:T(8,128)S(1)}, u32[]{:S(2)}, u32[]{:S(2)}) collective-permute-start(f32[128,128]{1,0:T(8,128)} %bitcast.6), channel_id=1, source_target_pairs={{0,8},{1,9},{2,10},{3,11},{4,12},{5,13},{6,14},{7,15},{8,0},{9,1},... | collective-permute-start | bytes 196616 | tf_op jit(solution)/shard_map/ppermute | solution.py:279
  3.4 2.8 %collective-permute-start = (f32[128,128]{1,0:T(8,128)}, f32[128,128]{1,0:T(8,128)S(1)}, u32[]{:S(2)}, u32[]{:S(2)}) collective-permute-start(f32[128,128]{1,0:T(8,128)} %bitcast.7), channel_id=1, source_target_pairs={{0,4},{1,5},{2,6},{3,7},{4,8},{5,9},{6,10},{7,11},{8,12},{9,13},{1... | collective-permute-start | bytes 196616 | tf_op jit(solution)/shard_map/ppermute | solution.py:279
  6.2 0.0 collective-permute-done.2.p3
  6.2 2.2 %collective-permute-done.1.p2 = f32[128,128]{1,0:T(8,128)S(1)} collective-permute-done((f32[128,128]{1,0:T(8,128)}, f32[128,128]{1,0:T(8,128)S(1)}, u32[]{:S(2)}, u32[]{:S(2)}) %collective-permute-start.1) | collective-permute-done | bytes 65568 | tf_op jit(solution)/shard_map/ppermute | solution.py:279
  8.4 1.2 %collective-permute-done.p1 = f32[128,128]{1,0:T(8,128)S(1)} collective-permute-done((f32[128,128]{1,0:T(8,128)}, f32[128,128]{1,0:T(8,128)S(1)}, u32[]{:S(2)}, u32[]{:S(2)}) %collective-permute-start) | collective-permute-done | bytes 65568 | tf_op jit(solution)/shard_map/ppermute | solution.py:279
  9.6 0.0 copy-start.1
  9.6 0.8 %copy-done.1 = f32[1,128,128]{2,1,0:T(8,128)S(1)} copy-done((f32[1,128,128]{2,1,0:T(8,128)S(1)}, f32[1,128,128]{2,1,0:T(8,128)}, u32[]{:S(2)}) %copy-start.1) | copy-done | bytes 65560
  10.4 0.0 copy-start.2
  10.5 2.8 %collective-permute-start.5 = (f32[2,128,128]{2,1,0:T(8,128)S(1)}, f32[2,128,128]{2,1,0:T(8,128)S(1)}, u32[]{:S(2)}, u32[]{:S(2)}) collective-permute-start(f32[2,128,128]{2,1,0:T(8,128)S(1)} %get-tuple-element.21.p0), channel_id=1, source_target_pairs={{0,3},{1,0},{2,1},{3,2},{4,7},{5,4},{6,5},{7,6},{8,11},{9,8},{10,9... | collective-permute-start | bytes 393224 | tf_op jit(solution)/shard_map/ppermute | solution.py:288
  13.3 0.8 %collective-permute-start.4 = (f32[2,128,128]{2,1,0:T(8,128)S(1)}, f32[2,128,128]{2,1,0:T(8,128)S(1)}, u32[]{:S(2)}, u32[]{:S(2)}) collective-permute-start(f32[2,128,128]{2,1,0:T(8,128)S(1)} %get-tuple-element.21.p0), channel_id=1, source_target_pairs={{0,2},{1,3},{2,0},{3,1},{4,6},{5,7},{6,4},{7,5},{8,10},{9,11},{10,... | collective-permute-start | bytes 393224 | tf_op jit(solution)/shard_map/ppermute | solution.py:288
  14.1 0.9 %collective-permute-start.3 = (f32[2,128,128]{2,1,0:T(8,128)S(1)}, f32[2,128,128]{2,1,0:T(8,128)S(1)}, u32[]{:S(2)}, u32[]{:S(2)}) collective-permute-start(f32[2,128,128]{2,1,0:T(8,128)S(1)} %get-tuple-element.21.p0), channel_id=1, source_target_pairs={{0,1},{1,2},{2,3},{3,0},{4,5},{5,6},{6,7},{7,4},{8,9},{9,10},{10,1... | collective-permute-start | bytes 393224 | tf_op jit(solution)/shard_map/ppermute | solution.py:288
  15.0 0.0 copy-done.2
  15.0 0.1 copy.5
  15.1 0.1 reshape.6
  15.1 0.1 pad_add_fusion.scalars
  15.2 3.1 %collective-permute-done.5.p3 = f32[2,128,128]{2,1,0:T(8,128)S(1)} collective-permute-done((f32[2,128,128]{2,1,0:T(8,128)S(1)}, f32[2,128,128]{2,1,0:T(8,128)S(1)}, u32[]{:S(2)}, u32[]{:S(2)}) %collective-permute-start.5) | collective-permute-done | bytes 131104 | tf_op jit(solution)/shard_map/ppermute | solution.py:288
  18.3 2.3 %collective-permute-done.4.p2 = f32[2,128,128]{2,1,0:T(8,128)S(1)} collective-permute-done((f32[2,128,128]{2,1,0:T(8,128)S(1)}, f32[2,128,128]{2,1,0:T(8,128)S(1)}, u32[]{:S(2)}, u32[]{:S(2)}) %collective-permute-start.4) | collective-permute-done | bytes 131104 | tf_op jit(solution)/shard_map/ppermute | solution.py:288
  20.7 1.3 %collective-permute-done.3.p1 = f32[2,128,128]{2,1,0:T(8,128)S(1)} collective-permute-done((f32[2,128,128]{2,1,0:T(8,128)S(1)}, f32[2,128,128]{2,1,0:T(8,128)S(1)}, u32[]{:S(2)}, u32[]{:S(2)}) %collective-permute-start.3) | collective-permute-done | bytes 131104 | tf_op jit(solution)/shard_map/ppermute | solution.py:288
  22.0 0.0 copy-done
  22.0 3.4 %first_kernel.1 = (f32[384,128]{1,0:T(8,128)S(1)}, f32[256,128]{1,0:T(8,128)S(1)}) custom-call(s32[19]{0:T(128)S(1)} %pad_add_fusion.scalars, f32[512,128]{1,0:T(8,128)S(1)} %copy-done, f32[2,128,128]{2,1,0:T(8,128)S(1)} %get-tuple-element.21.p0, f32[2,128,128]{2,1,0:T(8,128)S(1)} %collective-permute-done.3.p1, ...), custom_call_target="tpu_custom_call" | custom-call | flops 400000000 | bytes 2000000 | tf_op jit(solution)/shard_map/first_kernel/pallas_call | solution.py:265
  25.4 6.9 %collective-permute-start.6 = (f32[384,128]{1,0:T(8,128)S(1)}, f32[384,128]{1,0:T(8,128)S(1)}, u32[]{:S(2)}, u32[]{:S(2)}) collective-permute-start(f32[384,128]{1,0:T(8,128)S(1)} %get-tuple-element.23.own), channel_id=1, source_target_pairs={{16,0},{32,16},{48,32},{64,48},{80,64},{96,80},{112,96},{128,112},... | collective-permute-start | bytes 589832 | tf_op jit(solution)/shard_map/ppermute | solution.py:284
  32.3 3.7 %factor1_kernel.1 = (bf16[5,256,512]{2,1,0:T(8,128)(2,1)S(1)}, f32[2,128,128]{2,1,0:T(8,128)S(1)}) custom-call(s32[19]{0:T(128)S(1)} %pad_add_fusion.scalars, f32[256,128]{1,0:T(8,128)S(1)} %get-tuple-element.22.after.low_ref, f32[2,128,128]{2,1,0:T(8,128)S(1)} %get-tuple-element.21.p0, f32[2,128,128]{2,1,0:T(8,128)S(1)} %collective-permute-done.3.p1, ...), custom_call_target="tpu_custom_call" | custom-call | flops 400000000 | bytes 2000000 | tf_op jit(solution)/shard_map/factor1_kernel/pallas_call | solution.py:265
  36.0 0.1 collective-permute-start.10
  36.0 0.5 collective-permute-start.9
  36.5 1.6 %collective-permute-start.8 = (f32[2,128,128]{2,1,0:T(8,128)S(1)}, f32[2,128,128]{2,1,0:T(8,128)S(1)}, u32[]{:S(2)}, u32[]{:S(2)}) collective-permute-start(f32[2,128,128]{2,1,0:T(8,128)S(1)} %get-tuple-element.29.p0), channel_id=1, source_target_pairs={{0,1},{1,2},{2,3},{3,0},{4,5},{5,6},{6,7},{7,4},{8,9},{9,10},{10,1... | collective-permute-start | bytes 393224 | tf_op jit(solution)/shard_map/ppermute | solution.py:288
  38.1 0.0 collective-permute-done.6.message
  38.1 2.8 %second_kernel.1 = (f32[256,128]{1,0:T(8,128)S(1)}, f32[256,128]{1,0:T(8,128)S(1)}, f32[256,128]{1,0:T(8,128)S(1)}) custom-call(s32[19]{0:T(128)S(1)} %pad_add_fusion.scalars, f32[256,128]{1,0:T(8,128)S(1)} %get-tuple-element.22.after.low_ref, f32[384,128]{1,0:T(8,128)S(1)} %get-tuple-element.23.own, f32[384,128]{1,0:T(8,128)S(1)} %collective-permute-done.6.message, ...), custom_call_target="tpu_custom_call" | custom-call | flops 400000000 | bytes 2000000 | tf_op jit(solution)/shard_map/second_kernel/pallas_call | solution.py:265
  40.8 2.1 %collective-permute-start.7 = (f32[256,128]{1,0:T(8,128)S(1)}, f32[256,128]{1,0:T(8,128)S(1)}, u32[]{:S(2)}, u32[]{:S(2)}) collective-permute-start(f32[256,128]{1,0:T(8,128)S(1)} %get-tuple-element.28), channel_id=1, source_target_pairs={{0,16},{16,32},{32,48},{48,64},{64,80},{80,96},{96,112},{112,128},... | collective-permute-start | bytes 393224 | tf_op jit(solution)/shard_map/ppermute | solution.py:284
  43.0 0.0 collective-permute-done.10.p3
  43.0 0.0 collective-permute-done.9.p2
  43.0 1.0 %collective-permute-done.8.p1 = f32[2,128,128]{2,1,0:T(8,128)S(1)} collective-permute-done((f32[2,128,128]{2,1,0:T(8,128)S(1)}, f32[2,128,128]{2,1,0:T(8,128)S(1)}, u32[]{:S(2)}, u32[]{:S(2)}) %collective-permute-start.8) | collective-permute-done | bytes 131104 | tf_op jit(solution)/shard_map/ppermute | solution.py:288
  44.0 3.2 %factor2_kernel.1 = (bf16[4,256,512]{2,1,0:T(8,128)(2,1)S(1)}, f32[128,128]{1,0:T(8,128)S(1)}) custom-call(s32[19]{0:T(128)S(1)} %pad_add_fusion.scalars, f32[256,128]{1,0:T(8,128)S(1)} %get-tuple-element.26.after.low_ref, f32[2,128,128]{2,1,0:T(8,128)S(1)} %get-tuple-element.29.p0, f32[2,128,128]{2,1,0:T(8,128)S(1)} %collective-permute-done.8.p1, ...), custom_call_target="tpu_custom_call" | custom-call | flops 400000000 | bytes 2000000 | tf_op jit(solution)/shard_map/factor2_kernel/pallas_call | solution.py:265
  47.3 6.1 %collective-permute-done.7.top_ref = f32[256,128]{1,0:T(8,128)S(1)} collective-permute-done((f32[256,128]{1,0:T(8,128)S(1)}, f32[256,128]{1,0:T(8,128)S(1)}, u32[]{:S(2)}, u32[]{:S(2)}) %collective-permute-start.7) | collective-permute-done | bytes 131104 | tf_op jit(solution)/shard_map/ppermute | solution.py:284
  53.3 1.2 %third_kernel.1 = (f32[256,128]{1,0:T(8,128)S(1)}, f32[384,128]{1,0:T(8,128)S(1)}) custom-call(s32[19]{0:T(128)S(1)} %pad_add_fusion.scalars, f32[256,128]{1,0:T(8,128)S(1)} %get-tuple-element.26.after.low_ref, f32[256,128]{1,0:T(8,128)S(1)} %get-tuple-element.27.mine, f32[256,128]{1,0:T(8,128)S(1)} %collective-permute-done.7.top_ref, ...), custom_call_target="tpu_custom_call" | custom-call | flops 400000000 | bytes 2000000 | tf_op jit(solution)/shard_map/third_kernel/pallas_call | solution.py:265
  54.5 1.9 %collective-permute-start.11 = (f32[384,128]{1,0:T(8,128)S(1)}, f32[384,128]{1,0:T(8,128)S(1)}, u32[]{:S(2)}, u32[]{:S(2)}) collective-permute-start(f32[384,128]{1,0:T(8,128)S(1)} %get-tuple-element.33.own), channel_id=1, source_target_pairs={{16,0},{32,16},{48,32},{64,48},{80,64},{96,80},{112,96},{128,112},... | collective-permute-start | bytes 589832 | tf_op jit(solution)/shard_map/ppermute | solution.py:284
  56.5 3.2 %factor3_kernel.1.g3 = bf16[4,256,512]{2,1,0:T(8,128)(2,1)S(1)} custom-call(s32[19]{0:T(128)S(1)} %pad_add_fusion.scalars, f32[256,128]{1,0:T(8,128)S(1)} %get-tuple-element.32.after.low_ref, f32[2,128,128]{2,1,0:T(8,128)S(1)} %get-tuple-element.29.p0, f32[2,128,128]{2,1,0:T(8,128)S(1)} %collective-permute-done.8.p1, ...), custom_call_target="tpu_custom_call" | custom-call | flops 400000000 | bytes 2000000 | tf_op jit(solution)/shard_map/factor3_kernel/pallas_call | solution.py:265
  59.7 2.1 %collective-permute-done.11.message = f32[384,128]{1,0:T(8,128)S(1)} collective-permute-done((f32[384,128]{1,0:T(8,128)S(1)}, f32[384,128]{1,0:T(8,128)S(1)}, u32[]{:S(2)}, u32[]{:S(2)}) %collective-permute-start.11) | collective-permute-done | bytes 196640 | tf_op jit(solution)/shard_map/ppermute | solution.py:284
  61.7 2.8 %fourth_kernel.1 = (f32[256,128]{1,0:T(8,128)S(1)}, f32[256,128]{1,0:T(8,128)S(1)}, f32[256,128]{1,0:T(8,128)S(1)}) custom-call(s32[19]{0:T(128)S(1)} %pad_add_fusion.scalars, f32[256,128]{1,0:T(8,128)S(1)} %get-tuple-element.32.after.low_ref, f32[384,128]{1,0:T(8,128)S(1)} %get-tuple-element.33.own, f32[384,128]{1,0:T(8,128)S(1)} %collective-permute-done.11.message, ...), custom_call_target="tpu_custom_call" | custom-call | flops 400000000 | bytes 2000000 | tf_op jit(solution)/shard_map/fourth_kernel/pallas_call | solution.py:265
  64.5 1.9 %collective-permute-start.12 = (f32[256,128]{1,0:T(8,128)S(1)}, f32[256,128]{1,0:T(8,128)S(1)}, u32[]{:S(2)}, u32[]{:S(2)}) collective-permute-start(f32[256,128]{1,0:T(8,128)S(1)} %get-tuple-element.36), channel_id=1, source_target_pairs={{0,16},{16,32},{32,48},{48,64},{64,80},{80,96},{96,112},{112,128},... | collective-permute-start | bytes 393224 | tf_op jit(solution)/shard_map/ppermute | solution.py:284
  66.4 10.5 %collective-permute-done.12.top_ref = f32[256,128]{1,0:T(8,128)S(1)} collective-permute-done((f32[256,128]{1,0:T(8,128)S(1)}, f32[256,128]{1,0:T(8,128)S(1)}, u32[]{:S(2)}, u32[]{:S(2)}) %collective-permute-start.12) | collective-permute-done | bytes 131104 | tf_op jit(solution)/shard_map/ppermute | solution.py:284
  76.9 1.5 %last_kernel.1 = f32[512,128]{1,0:T(8,128)} custom-call(s32[19]{0:T(128)S(1)} %pad_add_fusion.scalars, f32[256,128]{1,0:T(8,128)S(1)} %get-tuple-element.34.low_ref, f32[256,128]{1,0:T(8,128)S(1)} %get-tuple-element.35.mine, f32[256,128]{1,0:T(8,128)S(1)} %collective-permute-done.12.top_ref, bf16[4,256,512]{2,1,0:T(8,128)(2,1)S(1)} %factor3_kernel.1.g3), custom_call_target="tpu_custom_call" | custom-call | flops 400000000 | bytes 2000000 | tf_op jit(solution)/shard_map/last_kernel/pallas_call | solution.py:265
  (1 shorter events, 0.0 us)
Async XLA Ops:
  0.0 22.0 %copy-start = (f32[512,128]{1,0:T(8,128)S(1)}, f32[512,128]{1,0:T(8,128)}, u32[]{:S(2)}) copy-start(f32[512,128]{1,0:T(8,128)} %x_ref.1) | copy-start | bytes 786436
  0.0 6.2 %collective-permute-start.2 = (f32[128,128]{1,0:T(8,128)}, f32[128,128]{1,0:T(8,128)S(1)}, u32[]{:S(2)}, u32[]{:S(2)}) collective-permute-start(f32[128,128]{1,0:T(8,128)} %bitcast.5), channel_id=1, source_target_pairs={{0,12},{1,13},{2,14},{3,15},{4,0},{5,1},{6,2},{7,3},{8,4},{9,5},{1... | collective-permute-start | bytes 196616 | tf_op jit(solution)/shard_map/ppermute | solution.py:279
  0.1 8.3 %collective-permute-start.1 = (f32[128,128]{1,0:T(8,128)}, f32[128,128]{1,0:T(8,128)S(1)}, u32[]{:S(2)}, u32[]{:S(2)}) collective-permute-start(f32[128,128]{1,0:T(8,128)} %bitcast.6), channel_id=1, source_target_pairs={{0,8},{1,9},{2,10},{3,11},{4,12},{5,13},{6,14},{7,15},{8,0},{9,1},... | collective-permute-start | bytes 196616 | tf_op jit(solution)/shard_map/ppermute | solution.py:279
  3.4 6.2 %collective-permute-start = (f32[128,128]{1,0:T(8,128)}, f32[128,128]{1,0:T(8,128)S(1)}, u32[]{:S(2)}, u32[]{:S(2)}) collective-permute-start(f32[128,128]{1,0:T(8,128)} %bitcast.7), channel_id=1, source_target_pairs={{0,4},{1,5},{2,6},{3,7},{4,8},{5,9},{6,10},{7,11},{8,12},{9,13},{1... | collective-permute-start | bytes 196616 | tf_op jit(solution)/shard_map/ppermute | solution.py:279
  9.6 0.8 %copy-start.1 = (f32[1,128,128]{2,1,0:T(8,128)S(1)}, f32[1,128,128]{2,1,0:T(8,128)}, u32[]{:S(2)}) copy-start(f32[1,128,128]{2,1,0:T(8,128)} %param.4) | copy-start | bytes 196612
  10.4 4.6 %copy-start.2 = (s32[1,8,2]{1,2,0:T(2,128)S(1)}, s32[1,8,2]{1,2,0:T(2,128)}, u32[]{:S(2)}) copy-start(s32[1,8,2]{1,2,0:T(2,128)} %param.5) | copy-start | bytes 196
  10.5 7.9 %collective-permute-start.5 = (f32[2,128,128]{2,1,0:T(8,128)S(1)}, f32[2,128,128]{2,1,0:T(8,128)S(1)}, u32[]{:S(2)}, u32[]{:S(2)}) collective-permute-start(f32[2,128,128]{2,1,0:T(8,128)S(1)} %get-tuple-element.21.p0), channel_id=1, source_target_pairs={{0,3},{1,0},{2,1},{3,2},{4,7},{5,4},{6,5},{7,6},{8,11},{9,8},{10,9... | collective-permute-start | bytes 393224 | tf_op jit(solution)/shard_map/ppermute | solution.py:288
  13.3 7.4 %collective-permute-start.4 = (f32[2,128,128]{2,1,0:T(8,128)S(1)}, f32[2,128,128]{2,1,0:T(8,128)S(1)}, u32[]{:S(2)}, u32[]{:S(2)}) collective-permute-start(f32[2,128,128]{2,1,0:T(8,128)S(1)} %get-tuple-element.21.p0), channel_id=1, source_target_pairs={{0,2},{1,3},{2,0},{3,1},{4,6},{5,7},{6,4},{7,5},{8,10},{9,11},{10,... | collective-permute-start | bytes 393224 | tf_op jit(solution)/shard_map/ppermute | solution.py:288
  14.1 7.9 %collective-permute-start.3 = (f32[2,128,128]{2,1,0:T(8,128)S(1)}, f32[2,128,128]{2,1,0:T(8,128)S(1)}, u32[]{:S(2)}, u32[]{:S(2)}) collective-permute-start(f32[2,128,128]{2,1,0:T(8,128)S(1)} %get-tuple-element.21.p0), channel_id=1, source_target_pairs={{0,1},{1,2},{2,3},{3,0},{4,5},{5,6},{6,7},{7,4},{8,9},{9,10},{10,1... | collective-permute-start | bytes 393224 | tf_op jit(solution)/shard_map/ppermute | solution.py:288
  25.4 12.7 %collective-permute-start.6 = (f32[384,128]{1,0:T(8,128)S(1)}, f32[384,128]{1,0:T(8,128)S(1)}, u32[]{:S(2)}, u32[]{:S(2)}) collective-permute-start(f32[384,128]{1,0:T(8,128)S(1)} %get-tuple-element.23.own), channel_id=1, source_target_pairs={{16,0},{32,16},{48,32},{64,48},{80,64},{96,80},{112,96},{128,112},... | collective-permute-start | bytes 589832 | tf_op jit(solution)/shard_map/ppermute | solution.py:284
  36.0 7.0 %collective-permute-start.10 = (f32[2,128,128]{2,1,0:T(8,128)S(1)}, f32[2,128,128]{2,1,0:T(8,128)S(1)}, u32[]{:S(2)}, u32[]{:S(2)}) collective-permute-start(f32[2,128,128]{2,1,0:T(8,128)S(1)} %get-tuple-element.29.p0), channel_id=1, source_target_pairs={{0,3},{1,0},{2,1},{3,2},{4,7},{5,4},{6,5},{7,6},{8,11},{9,8},{10,9... | collective-permute-start | bytes 393224 | tf_op jit(solution)/shard_map/ppermute | solution.py:288
  36.0 6.9 %collective-permute-start.9 = (f32[2,128,128]{2,1,0:T(8,128)S(1)}, f32[2,128,128]{2,1,0:T(8,128)S(1)}, u32[]{:S(2)}, u32[]{:S(2)}) collective-permute-start(f32[2,128,128]{2,1,0:T(8,128)S(1)} %get-tuple-element.29.p0), channel_id=1, source_target_pairs={{0,2},{1,3},{2,0},{3,1},{4,6},{5,7},{6,4},{7,5},{8,10},{9,11},{10,... | collective-permute-start | bytes 393224 | tf_op jit(solution)/shard_map/ppermute | solution.py:288
  36.5 7.5 %collective-permute-start.8 = (f32[2,128,128]{2,1,0:T(8,128)S(1)}, f32[2,128,128]{2,1,0:T(8,128)S(1)}, u32[]{:S(2)}, u32[]{:S(2)}) collective-permute-start(f32[2,128,128]{2,1,0:T(8,128)S(1)} %get-tuple-element.29.p0), channel_id=1, source_target_pairs={{0,1},{1,2},{2,3},{3,0},{4,5},{5,6},{6,7},{7,4},{8,9},{9,10},{10,1... | collective-permute-start | bytes 393224 | tf_op jit(solution)/shard_map/ppermute | solution.py:288
  40.8 12.5 %collective-permute-start.7 = (f32[256,128]{1,0:T(8,128)S(1)}, f32[256,128]{1,0:T(8,128)S(1)}, u32[]{:S(2)}, u32[]{:S(2)}) collective-permute-start(f32[256,128]{1,0:T(8,128)S(1)} %get-tuple-element.28), channel_id=1, source_target_pairs={{0,16},{16,32},{32,48},{48,64},{64,80},{80,96},{96,112},{112,128},... | collective-permute-start | bytes 393224 | tf_op jit(solution)/shard_map/ppermute | solution.py:284
  54.5 7.2 %collective-permute-start.11 = (f32[384,128]{1,0:T(8,128)S(1)}, f32[384,128]{1,0:T(8,128)S(1)}, u32[]{:S(2)}, u32[]{:S(2)}) collective-permute-start(f32[384,128]{1,0:T(8,128)S(1)} %get-tuple-element.33.own), channel_id=1, source_target_pairs={{16,0},{32,16},{48,32},{64,48},{80,64},{96,80},{112,96},{128,112},... | collective-permute-start | bytes 589832 | tf_op jit(solution)/shard_map/ppermute | solution.py:284
  64.5 12.4 %collective-permute-start.12 = (f32[256,128]{1,0:T(8,128)S(1)}, f32[256,128]{1,0:T(8,128)S(1)}, u32[]{:S(2)}, u32[]{:S(2)}) collective-permute-start(f32[256,128]{1,0:T(8,128)S(1)} %get-tuple-element.36), channel_id=1, source_target_pairs={{0,16},{16,32},{32,48},{48,64},{64,80},{80,96},{96,112},{112,128},... | collective-permute-start | bytes 393224 | tf_op jit(solution)/shard_map/ppermute | solution.py:284

commit v7 on v6

--- a/solution.py
+++ b/solution.py
@@ -165,6 +165,11 @@
     return across(low, jnp.where(last, 0.0, below), update)
 
 
+def across_above(first, above, top, update):
+    new_above, new_top = across(above, top, update)
+    return new_above, jnp.where(first, top, new_top)
+
+
 def order_kernel(plane, p0, p1, p2, p3, near, far, held):
     for k, piece in enumerate((p0, p1, p2, p3)):
         held[(plane[0] + 4 - k) % 4] = piece[...]
@@ -207,11 +212,14 @@
     below_out[...] = below
 
 
-def factor2_kernel(scalars, after, p0, p1, p2, p3, g2, up, held):
+def factor2_kernel(scalars, after, p0, p1, p2, p3, g2, up, down, held):
     pieces = (p0, p1, p2, p3)
     gathered(scalars, pieces, held, 1)
     up[...] = block_of(scalars, held, 6, 0)
+    down[1] = block_of(scalars, held, 6, 1)
+    down[2] = block_of(scalars, held, 7, 1)
     gathered(scalars, pieces, held, 0)
+    down[0] = block_of(scalars, held, 5, 1)
     stored_wholes([block_of(scalars, held, level, half) for level in (4, 5) for half in (0, 1)], g2)
 
 
@@ -228,24 +236,26 @@
 
 def factor3_kernel(scalars, after, p0, p1, p2, p3, g3, held):
     gathered(scalars, (p0, p1, p2, p3), held, 1)
-    stored_wholes([block_of(scalars, held, level, half) for level, half in ((6, 1), (7, 0), (7, 1), (6, 0))], g3)
-
-
-def fourth_kernel(scalars, low_ref, own, message, g2, g3, low_out, below_out, top_out):
+    stored_wholes([block_of(scalars, held, level, half) for level, half in ((6, 0), (6, 1), (7, 0), (7, 1))], g3)
+
+
+def factor4_kernel(after, down, g4):
+    stored_wholes([down[0], down[1], down[2]], g4)
+
+
+def fourth_kernel(scalars, low_ref, own, above_ref, message, g2, g3, g4, out_ref):
     last = scalars[1] == 1
+    first = scalars[2] == 1
     (foreign,) = factors([message[2 * W :]])
     low, below = across_below(last, low_ref[...], message[: 2 * W], once(g2, 3))
-    low = once(g3, 0)(low)
+    above, top = across_above(first, above_ref[...], own[: 2 * W], once(g4, 0))
+    above = once(g4, 1)(above)
+    top = once(g3, 0)(top)
+    low = once(g3, 1)(low)
+    _, top = across_above(first, above, top, once(g4, 2))
     below = twice(foreign)(below)
-    top_out[...] = once(g3, 3)(own[: 2 * W])
-    low, below = across_below(last, low, below, once(g3, 2))
-    low_out[...] = low
-    below_out[...] = below
-
-
-def last_kernel(scalars, low_ref, mine, top_ref, g3, out_ref):
-    top = jnp.where(scalars[2] == 1, mine[...], top_ref[...])
-    top, low = across(top, low_ref[...], once(g3, 1))
+    low, _ = across_below(last, low, below, once(g3, 3))
+    top, low = across(top, low, once(g3, 2))
     out_ref[: 2 * W] = top
     out_ref[2 * W :] = low
 
@@ -285,7 +295,8 @@
 
 
 def along_x(value):
-    return [value] + [lax.ppermute(value, "cols", [(i, (i // 4) * 4 + (i + k) % 4) for i in range(16)]) for k in (1, 2, 3)]
+    found = {k: lax.ppermute(value, "cols", [(i, (i // 4) * 4 + (i + k) % 4) for i in range(16)]) for k in (1, 3, 2)}
+    return [value, found[1], found[2], found[3]]
 
 
 def per_device(eigvecs, wy_packed, slot_block):
@@ -308,13 +319,17 @@
     far = along_x(far)
     low, below, mine = call(second_kernel, (scalars, low, own, message, g1), [half, half, half])
     top = to_neighbour(below, 1)
-    g2, up = call(factor2_kernel, (scalars, low, *far), [wholes(4), rows_shape(W, W)], HELD)
+    blocks = [wholes(4), rows_shape(W, W), rows_shape(3, W, W)]
+    g2, up, down = call(factor2_kernel, (scalars, low, *far), blocks, HELD)
+    down = to_neighbour(down, 1)
     low, own = call(third_kernel, (scalars, low, mine, top, up, g1, g2), [half, three])
+    above = to_neighbour(low, 1)
     message = to_neighbour(own, -1)
     (g3,) = call(factor3_kernel, (scalars, low, *far), [wholes(4)], HELD)
-    low, below, mine = call(fourth_kernel, (scalars, low, own, message, g2, g3), [half, half, half])
-    top = to_neighbour(below, 1)
-    return call(last_kernel, (scalars, low, mine, top, g3), [rows_shape(*eigvecs.shape)])[0]
+    (g4,) = call(factor4_kernel, (low, down), [wholes(3)], smem=0)
+    return call(
+        fourth_kernel, (scalars, low, own, above, message, g2, g3, g4), [rows_shape(*eigvecs.shape)]
+    )[0]
 
 
 def solution(mesh):

time: 79.5 us -> 76.3 us (0.960)
  waiting for transfers between devices: 29.8 us -> 20.3 us
  starting transfers between devices: 25.7 us -> 30 us
  Pallas kernels: 21.7 us -> 23.8 us
    ppermute x4 -> x5, waiting for transfers between devices: 18.6 us -> 9.12 us  [to_neighbour(): lax.ppermute(value, 'rows', [(i, i + steps) for i in range(count) if 0 <=...]
    ppermute x4 -> x5, starting transfers between devices: 12.9 us -> 17.2 us  [to_neighbour(): lax.ppermute(value, 'rows', [(i, i + steps) for i in range(count) if 0 <=...]
    pallas_call x9, Pallas kernels: 21.7 us -> 23.8 us  [call(): pl.pallas_call(kernel, out_shape=tuple(shapes), in_specs=[pl.BlockSpec(me...]
  transfers between devices with their start and end apart: 13 -> 14, of which waited for: 9 -> 8; matrix products, arithmetic and copies ran while one was open for 0% -> 0% of each run, Pallas kernels for 16% -> 22%
where the time goes in v7:
time: 76.3 us; the launch traced here: 75.3 us
  starting transfers between devices  30 us (39%)
  Pallas kernels  23.8 us (31%)
  waiting for transfers between devices  20.3 us (27%)
  local copies, waits for them, and re-layouts  1.01 us (1%)
    pallas_call x9, Pallas kernels, call(): pl.pallas_call(kernel, out_shape=tuple(shapes), in_specs=[pl.BlockSpec(me...  23.8 us
    ppermute x5, starting transfers between devices, to_neighbour(): lax.ppermute(value, 'rows', [(i, i + steps) for i in range(count) if 0 <=...  17.2 us
    ppermute x5, waiting for transfers between devices, to_neighbour(): lax.ppermute(value, 'rows', [(i, i + steps) for i in range(count) if 0 <=...  9.12 us
    ppermute x6, waiting for transfers between devices, along_x(): lax.ppermute(value, 'cols', [(i, i // 4 * 4 + (i + k) % 4) for i in range...  7.83 us
    ppermute x6, starting transfers between devices, along_x(): lax.ppermute(value, 'cols', [(i, i // 4 * 4 + (i + k) % 4) for i in range...  6.62 us
    ppermute x3, starting transfers between devices, shifted(): lax.ppermute(value, axis, [(i, (i + steps) % count) for i in range(count)])  6.2 us
    ppermute x3, waiting for transfers between devices, shifted(): lax.ppermute(value, axis, [(i, (i + steps) % count) for i in range(count)])  3.36 us
  transfers between devices with their start and end apart: 14, of which 8 were waited for; matrix products, arithmetic and copies ran while one was open for 0% of the time, Pallas kernels for 22%

profile of v7, /device:TPU:56, one launch (start us, length us, event | category | flops | bytes accessed | tf_op | source)
XLA Modules:
  0.0 75.3 jit_solution(16242927545362297290)
XLA Ops:
  0.0 0.0 copy-start
  0.0 0.1 collective-permute-start.2
  0.1 3.3 %collective-permute-start.1 = (f32[128,128]{1,0:T(8,128)}, f32[128,128]{1,0:T(8,128)S(1)}, u32[]{:S(2)}, u32[]{:S(2)}) collective-permute-start(f32[128,128]{1,0:T(8,128)} %bitcast.6), channel_id=1, source_target_pairs={{0,8},{1,9},{2,10},{3,11},{4,12},{5,13},{6,14},{7,15},{8,0},{9,1},... | collective-permute-start | bytes 196616 | tf_op jit(solution)/shard_map/ppermute | solution.py:289
  3.4 2.8 %collective-permute-start = (f32[128,128]{1,0:T(8,128)}, f32[128,128]{1,0:T(8,128)S(1)}, u32[]{:S(2)}, u32[]{:S(2)}) collective-permute-start(f32[128,128]{1,0:T(8,128)} %bitcast.7), channel_id=1, source_target_pairs={{0,4},{1,5},{2,6},{3,7},{4,8},{5,9},{6,10},{7,11},{8,12},{9,13},{1... | collective-permute-start | bytes 196616 | tf_op jit(solution)/shard_map/ppermute | solution.py:289
  6.2 0.0 collective-permute-done.2.p3
  6.2 2.2 %collective-permute-done.1.p2 = f32[128,128]{1,0:T(8,128)S(1)} collective-permute-done((f32[128,128]{1,0:T(8,128)}, f32[128,128]{1,0:T(8,128)S(1)}, u32[]{:S(2)}, u32[]{:S(2)}) %collective-permute-start.1) | collective-permute-done | bytes 65568 | tf_op jit(solution)/shard_map/ppermute | solution.py:289
  8.4 1.2 %collective-permute-done.p1 = f32[128,128]{1,0:T(8,128)S(1)} collective-permute-done((f32[128,128]{1,0:T(8,128)}, f32[128,128]{1,0:T(8,128)S(1)}, u32[]{:S(2)}, u32[]{:S(2)}) %collective-permute-start) | collective-permute-done | bytes 65568 | tf_op jit(solution)/shard_map/ppermute | solution.py:289
  9.6 0.0 copy-start.1
  9.6 0.8 %copy-done.1 = f32[1,128,128]{2,1,0:T(8,128)S(1)} copy-done((f32[1,128,128]{2,1,0:T(8,128)S(1)}, f32[1,128,128]{2,1,0:T(8,128)}, u32[]{:S(2)}) %copy-start.1) | copy-done | bytes 65560
  10.4 0.0 copy-start.2
  10.5 2.8 %collective-permute-start.5 = (f32[2,128,128]{2,1,0:T(8,128)S(1)}, f32[2,128,128]{2,1,0:T(8,128)S(1)}, u32[]{:S(2)}, u32[]{:S(2)}) collective-permute-start(f32[2,128,128]{2,1,0:T(8,128)S(1)} %get-tuple-element.19.p0), channel_id=1, source_target_pairs={{0,3},{1,0},{2,1},{3,2},{4,7},{5,4},{6,5},{7,6},{8,11},{9,8},{10,9... | collective-permute-start | bytes 393224 | tf_op jit(solution)/shard_map/ppermute | solution.py:298
  13.3 0.8 %collective-permute-start.4 = (f32[2,128,128]{2,1,0:T(8,128)S(1)}, f32[2,128,128]{2,1,0:T(8,128)S(1)}, u32[]{:S(2)}, u32[]{:S(2)}) collective-permute-start(f32[2,128,128]{2,1,0:T(8,128)S(1)} %get-tuple-element.19.p0), channel_id=1, source_target_pairs={{0,2},{1,3},{2,0},{3,1},{4,6},{5,7},{6,4},{7,5},{8,10},{9,11},{10,... | collective-permute-start | bytes 393224 | tf_op jit(solution)/shard_map/ppermute | solution.py:298
  14.1 0.9 %collective-permute-start.3 = (f32[2,128,128]{2,1,0:T(8,128)S(1)}, f32[2,128,128]{2,1,0:T(8,128)S(1)}, u32[]{:S(2)}, u32[]{:S(2)}) collective-permute-start(f32[2,128,128]{2,1,0:T(8,128)S(1)} %get-tuple-element.19.p0), channel_id=1, source_target_pairs={{0,1},{1,2},{2,3},{3,0},{4,5},{5,6},{6,7},{7,4},{8,9},{9,10},{10,1... | collective-permute-start | bytes 393224 | tf_op jit(solution)/shard_map/ppermute | solution.py:298
  15.0 0.0 copy-done.2
  15.0 0.1 copy.5
  15.1 0.1 reshape.6
  15.1 0.1 pad_add_fusion.scalars
  15.2 3.1 %collective-permute-done.5.p3 = f32[2,128,128]{2,1,0:T(8,128)S(1)} collective-permute-done((f32[2,128,128]{2,1,0:T(8,128)S(1)}, f32[2,128,128]{2,1,0:T(8,128)S(1)}, u32[]{:S(2)}, u32[]{:S(2)}) %collective-permute-start.5) | collective-permute-done | bytes 131104 | tf_op jit(solution)/shard_map/ppermute | solution.py:298
  18.3 2.3 %collective-permute-done.4.p2 = f32[2,128,128]{2,1,0:T(8,128)S(1)} collective-permute-done((f32[2,128,128]{2,1,0:T(8,128)S(1)}, f32[2,128,128]{2,1,0:T(8,128)S(1)}, u32[]{:S(2)}, u32[]{:S(2)}) %collective-permute-start.4) | collective-permute-done | bytes 131104 | tf_op jit(solution)/shard_map/ppermute | solution.py:298
  20.7 1.3 %collective-permute-done.3.p1 = f32[2,128,128]{2,1,0:T(8,128)S(1)} collective-permute-done((f32[2,128,128]{2,1,0:T(8,128)S(1)}, f32[2,128,128]{2,1,0:T(8,128)S(1)}, u32[]{:S(2)}, u32[]{:S(2)}) %collective-permute-start.3) | collective-permute-done | bytes 131104 | tf_op jit(solution)/shard_map/ppermute | solution.py:298
  22.0 0.0 copy-done
  22.0 3.4 %first_kernel.1 = (f32[384,128]{1,0:T(8,128)S(1)}, f32[256,128]{1,0:T(8,128)S(1)}) custom-call(s32[19]{0:T(128)S(1)} %pad_add_fusion.scalars, f32[512,128]{1,0:T(8,128)S(1)} %copy-done, f32[2,128,128]{2,1,0:T(8,128)S(1)} %get-tuple-element.19.p0, f32[2,128,128]{2,1,0:T(8,128)S(1)} %collective-permute-done.3.p1, ...), custom_call_target="tpu_custom_call" | custom-call | flops 400000000 | bytes 2000000 | tf_op jit(solution)/shard_map/first_kernel/pallas_call | solution.py:275
  25.4 6.9 %collective-permute-start.6 = (f32[384,128]{1,0:T(8,128)S(1)}, f32[384,128]{1,0:T(8,128)S(1)}, u32[]{:S(2)}, u32[]{:S(2)}) collective-permute-start(f32[384,128]{1,0:T(8,128)S(1)} %get-tuple-element.21.own), channel_id=1, source_target_pairs={{16,0},{32,16},{48,32},{64,48},{80,64},{96,80},{112,96},{128,112},... | collective-permute-start | bytes 589832 | tf_op jit(solution)/shard_map/ppermute | solution.py:294
  32.3 3.7 %factor1_kernel.1 = (bf16[5,256,512]{2,1,0:T(8,128)(2,1)S(1)}, f32[2,128,128]{2,1,0:T(8,128)S(1)}) custom-call(s32[19]{0:T(128)S(1)} %pad_add_fusion.scalars, f32[256,128]{1,0:T(8,128)S(1)} %get-tuple-element.20.after.low_ref, f32[2,128,128]{2,1,0:T(8,128)S(1)} %get-tuple-element.19.p0, f32[2,128,128]{2,1,0:T(8,128)S(1)} %collective-permute-done.3.p1, ...), custom_call_target="tpu_custom_call" | custom-call | flops 400000000 | bytes 2000000 | tf_op jit(solution)/shard_map/factor1_kernel/pallas_call | solution.py:275
  36.0 0.1 collective-permute-start.10
  36.0 0.5 collective-permute-start.9
  36.5 1.6 %collective-permute-start.8 = (f32[2,128,128]{2,1,0:T(8,128)S(1)}, f32[2,128,128]{2,1,0:T(8,128)S(1)}, u32[]{:S(2)}, u32[]{:S(2)}) collective-permute-start(f32[2,128,128]{2,1,0:T(8,128)S(1)} %get-tuple-element.27.p0), channel_id=1, source_target_pairs={{0,1},{1,2},{2,3},{3,0},{4,5},{5,6},{6,7},{7,4},{8,9},{9,10},{10,1... | collective-permute-start | bytes 393224 | tf_op jit(solution)/shard_map/ppermute | solution.py:298
  38.1 0.0 collective-permute-done.6.message
  38.1 2.8 %second_kernel.1 = (f32[256,128]{1,0:T(8,128)S(1)}, f32[256,128]{1,0:T(8,128)S(1)}, f32[256,128]{1,0:T(8,128)S(1)}) custom-call(s32[19]{0:T(128)S(1)} %pad_add_fusion.scalars, f32[256,128]{1,0:T(8,128)S(1)} %get-tuple-element.20.after.low_ref, f32[384,128]{1,0:T(8,128)S(1)} %get-tuple-element.21.own, f32[384,128]{1,0:T(8,128)S(1)} %collective-permute-done.6.message, ...), custom_call_target="tpu_custom_call" | custom-call | flops 400000000 | bytes 2000000 | tf_op jit(solution)/shard_map/second_kernel/pallas_call | solution.py:275
  40.8 2.1 %collective-permute-start.7 = (f32[256,128]{1,0:T(8,128)S(1)}, f32[256,128]{1,0:T(8,128)S(1)}, u32[]{:S(2)}, u32[]{:S(2)}) collective-permute-start(f32[256,128]{1,0:T(8,128)S(1)} %get-tuple-element.26), channel_id=1, source_target_pairs={{0,16},{16,32},{32,48},{48,64},{64,80},{80,96},{96,112},{112,128},... | collective-permute-start | bytes 393224 | tf_op jit(solution)/shard_map/ppermute | solution.py:294
  43.0 0.0 collective-permute-done.10.p3
  43.0 0.0 collective-permute-done.9.p2
  43.0 1.0 %collective-permute-done.8.p1 = f32[2,128,128]{2,1,0:T(8,128)S(1)} collective-permute-done((f32[2,128,128]{2,1,0:T(8,128)S(1)}, f32[2,128,128]{2,1,0:T(8,128)S(1)}, u32[]{:S(2)}, u32[]{:S(2)}) %collective-permute-start.8) | collective-permute-done | bytes 131104 | tf_op jit(solution)/shard_map/ppermute | solution.py:298
  44.0 3.2 %factor2_kernel.1 = (bf16[4,256,512]{2,1,0:T(8,128)(2,1)S(1)}, f32[128,128]{1,0:T(8,128)S(1)}, f32[3,128,128]{2,1,0:T(8,128)S(1)}) custom-call(s32[19]{0:T(128)S(1)} %pad_add_fusion.scalars, f32[256,128]{1,0:T(8,128)S(1)} %get-tuple-element.24.after.low_ref, f32[2,128,128]{2,1,0:T(8,128)S(1)} %get-tuple-element.27.p0, ...), custom_call_target="tpu_custom_call" | custom-call | flops 400000000 | bytes 2000000 | tf_op jit(solution)/shard_map/factor2_kernel/pallas_call | solution.py:275
  47.3 1.9 %collective-permute-start.13 = (f32[3,128,128]{2,1,0:T(8,128)S(1)}, f32[3,128,128]{2,1,0:T(8,128)S(1)}, u32[]{:S(2)}, u32[]{:S(2)}) collective-permute-start(f32[3,128,128]{2,1,0:T(8,128)S(1)} %get-tuple-element.32), channel_id=1, source_target_pairs={{0,16},{16,32},{32,48},{48,64},{64,80},{80,96},{96,112},{112,128},... | collective-permute-start | bytes 589832 | tf_op jit(solution)/shard_map/ppermute | solution.py:294
  49.2 4.1 %collective-permute-done.7.top_ref = f32[256,128]{1,0:T(8,128)S(1)} collective-permute-done((f32[256,128]{1,0:T(8,128)S(1)}, f32[256,128]{1,0:T(8,128)S(1)}, u32[]{:S(2)}, u32[]{:S(2)}) %collective-permute-start.7) | collective-permute-done | bytes 131104 | tf_op jit(solution)/shard_map/ppermute | solution.py:294
  53.3 1.2 %third_kernel.1 = (f32[256,128]{1,0:T(8,128)S(1)}, f32[384,128]{1,0:T(8,128)S(1)}) custom-call(s32[19]{0:T(128)S(1)} %pad_add_fusion.scalars, f32[256,128]{1,0:T(8,128)S(1)} %get-tuple-element.24.after.low_ref, f32[256,128]{1,0:T(8,128)S(1)} %get-tuple-element.25.mine, f32[256,128]{1,0:T(8,128)S(1)} %collective-permute-done.7.top_ref, ...), custom_call_target="tpu_custom_call" | custom-call | flops 400000000 | bytes 2000000 | tf_op jit(solution)/shard_map/third_kernel/pallas_call | solution.py:275
  54.5 4.3 %collective-permute-start.12 = (f32[384,128]{1,0:T(8,128)S(1)}, f32[384,128]{1,0:T(8,128)S(1)}, u32[]{:S(2)}, u32[]{:S(2)}) collective-permute-start(f32[384,128]{1,0:T(8,128)S(1)} %get-tuple-element.31.own), channel_id=1, source_target_pairs={{16,0},{32,16},{48,32},{64,48},{80,64},{96,80},{112,96},{128,112},... | collective-permute-start | bytes 589832 | tf_op jit(solution)/shard_map/ppermute | solution.py:294
  58.9 1.9 %collective-permute-start.11 = (f32[256,128]{1,0:T(8,128)S(1)}, f32[256,128]{1,0:T(8,128)S(1)}, u32[]{:S(2)}, u32[]{:S(2)}) collective-permute-start(f32[256,128]{1,0:T(8,128)S(1)} %get-tuple-element.30.after.low_ref), channel_id=1, source_target_pairs={{0,16},{16,32},{32,48},{48,64},{64,80},{80,96},{96,112},{112,128},... | collective-permute-start | bytes 393224 | tf_op jit(solution)/shard_map/ppermute | solution.py:294
  60.8 3.2 %factor3_kernel.1.g3 = bf16[4,256,512]{2,1,0:T(8,128)(2,1)S(1)} custom-call(s32[19]{0:T(128)S(1)} %pad_add_fusion.scalars, f32[256,128]{1,0:T(8,128)S(1)} %get-tuple-element.30.after.low_ref, f32[2,128,128]{2,1,0:T(8,128)S(1)} %get-tuple-element.27.p0, f32[2,128,128]{2,1,0:T(8,128)S(1)} %collective-permute-done.8.p1, ...), custom_call_target="tpu_custom_call" | custom-call | flops 400000000 | bytes 2000000 | tf_op jit(solution)/shard_map/factor3_kernel/pallas_call | solution.py:275
  64.0 0.0 collective-permute-done.13.down
  64.0 2.4 %factor4_kernel.1.g4 = bf16[3,256,512]{2,1,0:T(8,128)(2,1)S(1)} custom-call(f32[256,128]{1,0:T(8,128)S(1)} %get-tuple-element.30.after.low_ref, f32[3,128,128]{2,1,0:T(8,128)S(1)} %collective-permute-done.13.down), custom_call_target="tpu_custom_call" | custom-call | flops 400000000 | bytes 2000000 | tf_op jit(solution)/shard_map/factor4_kernel/pallas_call | solution.py:275
  66.4 5.0 %collective-permute-done.11.above_ref = f32[256,128]{1,0:T(8,128)S(1)} collective-permute-done((f32[256,128]{1,0:T(8,128)S(1)}, f32[256,128]{1,0:T(8,128)S(1)}, u32[]{:S(2)}, u32[]{:S(2)}) %collective-permute-start.11) | collective-permute-done | bytes 131104 | tf_op jit(solution)/shard_map/ppermute | solution.py:294
  71.4 0.0 collective-permute-done.12.message
  71.4 3.9 %fourth_kernel.1 = f32[512,128]{1,0:T(8,128)} custom-call(s32[19]{0:T(128)S(1)} %pad_add_fusion.scalars, f32[256,128]{1,0:T(8,128)S(1)} %get-tuple-element.30.after.low_ref, f32[384,128]{1,0:T(8,128)S(1)} %get-tuple-element.31.own, f32[256,128]{1,0:T(8,128)S(1)} %collective-permute-done.11.above_ref, f32[384,128]{1,0:T(8,128)S(1)} %collective-permute-done.12.message, ...), custom_call_target="tpu_custom_call" | custom-call | flops 400000000 | bytes 2000000 | tf_op jit(solution)/shard_map/fourth_kernel/pallas_call | solution.py:275
  (1 shorter events, 0.0 us)
Async XLA Ops:
  0.0 22.0 %copy-start = (f32[512,128]{1,0:T(8,128)S(1)}, f32[512,128]{1,0:T(8,128)}, u32[]{:S(2)}) copy-start(f32[512,128]{1,0:T(8,128)} %x_ref.1) | copy-start | bytes 786436
  0.0 6.2 %collective-permute-start.2 = (f32[128,128]{1,0:T(8,128)}, f32[128,128]{1,0:T(8,128)S(1)}, u32[]{:S(2)}, u32[]{:S(2)}) collective-permute-start(f32[128,128]{1,0:T(8,128)} %bitcast.5), channel_id=1, source_target_pairs={{0,12},{1,13},{2,14},{3,15},{4,0},{5,1},{6,2},{7,3},{8,4},{9,5},{1... | collective-permute-start | bytes 196616 | tf_op jit(solution)/shard_map/ppermute | solution.py:289
  0.1 8.3 %collective-permute-start.1 = (f32[128,128]{1,0:T(8,128)}, f32[128,128]{1,0:T(8,128)S(1)}, u32[]{:S(2)}, u32[]{:S(2)}) collective-permute-start(f32[128,128]{1,0:T(8,128)} %bitcast.6), channel_id=1, source_target_pairs={{0,8},{1,9},{2,10},{3,11},{4,12},{5,13},{6,14},{7,15},{8,0},{9,1},... | collective-permute-start | bytes 196616 | tf_op jit(solution)/shard_map/ppermute | solution.py:289
  3.4 6.2 %collective-permute-start = (f32[128,128]{1,0:T(8,128)}, f32[128,128]{1,0:T(8,128)S(1)}, u32[]{:S(2)}, u32[]{:S(2)}) collective-permute-start(f32[128,128]{1,0:T(8,128)} %bitcast.7), channel_id=1, source_target_pairs={{0,4},{1,5},{2,6},{3,7},{4,8},{5,9},{6,10},{7,11},{8,12},{9,13},{1... | collective-permute-start | bytes 196616 | tf_op jit(solution)/shard_map/ppermute | solution.py:289
  9.6 0.8 %copy-start.1 = (f32[1,128,128]{2,1,0:T(8,128)S(1)}, f32[1,128,128]{2,1,0:T(8,128)}, u32[]{:S(2)}) copy-start(f32[1,128,128]{2,1,0:T(8,128)} %param.4) | copy-start | bytes 196612
  10.4 4.6 %copy-start.2 = (s32[1,8,2]{1,2,0:T(2,128)S(1)}, s32[1,8,2]{1,2,0:T(2,128)}, u32[]{:S(2)}) copy-start(s32[1,8,2]{1,2,0:T(2,128)} %param.5) | copy-start | bytes 196
  10.5 7.9 %collective-permute-start.5 = (f32[2,128,128]{2,1,0:T(8,128)S(1)}, f32[2,128,128]{2,1,0:T(8,128)S(1)}, u32[]{:S(2)}, u32[]{:S(2)}) collective-permute-start(f32[2,128,128]{2,1,0:T(8,128)S(1)} %get-tuple-element.19.p0), channel_id=1, source_target_pairs={{0,3},{1,0},{2,1},{3,2},{4,7},{5,4},{6,5},{7,6},{8,11},{9,8},{10,9... | collective-permute-start | bytes 393224 | tf_op jit(solution)/shard_map/ppermute | solution.py:298
  13.3 7.4 %collective-permute-start.4 = (f32[2,128,128]{2,1,0:T(8,128)S(1)}, f32[2,128,128]{2,1,0:T(8,128)S(1)}, u32[]{:S(2)}, u32[]{:S(2)}) collective-permute-start(f32[2,128,128]{2,1,0:T(8,128)S(1)} %get-tuple-element.19.p0), channel_id=1, source_target_pairs={{0,2},{1,3},{2,0},{3,1},{4,6},{5,7},{6,4},{7,5},{8,10},{9,11},{10,... | collective-permute-start | bytes 393224 | tf_op jit(solution)/shard_map/ppermute | solution.py:298
  14.1 7.9 %collective-permute-start.3 = (f32[2,128,128]{2,1,0:T(8,128)S(1)}, f32[2,128,128]{2,1,0:T(8,128)S(1)}, u32[]{:S(2)}, u32[]{:S(2)}) collective-permute-start(f32[2,128,128]{2,1,0:T(8,128)S(1)} %get-tuple-element.19.p0), channel_id=1, source_target_pairs={{0,1},{1,2},{2,3},{3,0},{4,5},{5,6},{6,7},{7,4},{8,9},{9,10},{10,1... | collective-permute-start | bytes 393224 | tf_op jit(solution)/shard_map/ppermute | solution.py:298
  25.4 12.7 %collective-permute-start.6 = (f32[384,128]{1,0:T(8,128)S(1)}, f32[384,128]{1,0:T(8,128)S(1)}, u32[]{:S(2)}, u32[]{:S(2)}) collective-permute-start(f32[384,128]{1,0:T(8,128)S(1)} %get-tuple-element.21.own), channel_id=1, source_target_pairs={{16,0},{32,16},{48,32},{64,48},{80,64},{96,80},{112,96},{128,112},... | collective-permute-start | bytes 589832 | tf_op jit(solution)/shard_map/ppermute | solution.py:294
  36.0 7.0 %collective-permute-start.10 = (f32[2,128,128]{2,1,0:T(8,128)S(1)}, f32[2,128,128]{2,1,0:T(8,128)S(1)}, u32[]{:S(2)}, u32[]{:S(2)}) collective-permute-start(f32[2,128,128]{2,1,0:T(8,128)S(1)} %get-tuple-element.27.p0), channel_id=1, source_target_pairs={{0,3},{1,0},{2,1},{3,2},{4,7},{5,4},{6,5},{7,6},{8,11},{9,8},{10,9... | collective-permute-start | bytes 393224 | tf_op jit(solution)/shard_map/ppermute | solution.py:298
  36.0 6.9 %collective-permute-start.9 = (f32[2,128,128]{2,1,0:T(8,128)S(1)}, f32[2,128,128]{2,1,0:T(8,128)S(1)}, u32[]{:S(2)}, u32[]{:S(2)}) collective-permute-start(f32[2,128,128]{2,1,0:T(8,128)S(1)} %get-tuple-element.27.p0), channel_id=1, source_target_pairs={{0,2},{1,3},{2,0},{3,1},{4,6},{5,7},{6,4},{7,5},{8,10},{9,11},{10,... | collective-permute-start | bytes 393224 | tf_op jit(solution)/shard_map/ppermute | solution.py:298
  36.5 7.5 %collective-permute-start.8 = (f32[2,128,128]{2,1,0:T(8,128)S(1)}, f32[2,128,128]{2,1,0:T(8,128)S(1)}, u32[]{:S(2)}, u32[]{:S(2)}) collective-permute-start(f32[2,128,128]{2,1,0:T(8,128)S(1)} %get-tuple-element.27.p0), channel_id=1, source_target_pairs={{0,1},{1,2},{2,3},{3,0},{4,5},{5,6},{6,7},{7,4},{8,9},{9,10},{10,1... | collective-permute-start | bytes 393224 | tf_op jit(solution)/shard_map/ppermute | solution.py:298
  40.8 12.5 %collective-permute-start.7 = (f32[256,128]{1,0:T(8,128)S(1)}, f32[256,128]{1,0:T(8,128)S(1)}, u32[]{:S(2)}, u32[]{:S(2)}) collective-permute-start(f32[256,128]{1,0:T(8,128)S(1)} %get-tuple-element.26), channel_id=1, source_target_pairs={{0,16},{16,32},{32,48},{48,64},{64,80},{80,96},{96,112},{112,128},... | collective-permute-start | bytes 393224 | tf_op jit(solution)/shard_map/ppermute | solution.py:294
  47.3 16.7 %collective-permute-start.13 = (f32[3,128,128]{2,1,0:T(8,128)S(1)}, f32[3,128,128]{2,1,0:T(8,128)S(1)}, u32[]{:S(2)}, u32[]{:S(2)}) collective-permute-start(f32[3,128,128]{2,1,0:T(8,128)S(1)} %get-tuple-element.32), channel_id=1, source_target_pairs={{0,16},{16,32},{32,48},{48,64},{64,80},{80,96},{96,112},{112,128},... | collective-permute-start | bytes 589832 | tf_op jit(solution)/shard_map/ppermute | solution.py:294
  54.5 16.8 %collective-permute-start.12 = (f32[384,128]{1,0:T(8,128)S(1)}, f32[384,128]{1,0:T(8,128)S(1)}, u32[]{:S(2)}, u32[]{:S(2)}) collective-permute-start(f32[384,128]{1,0:T(8,128)S(1)} %get-tuple-element.31.own), channel_id=1, source_target_pairs={{16,0},{32,16},{48,32},{64,48},{80,64},{96,80},{112,96},{128,112},... | collective-permute-start | bytes 589832 | tf_op jit(solution)/shard_map/ppermute | solution.py:294
  58.9 12.5 %collective-permute-start.11 = (f32[256,128]{1,0:T(8,128)S(1)}, f32[256,128]{1,0:T(8,128)S(1)}, u32[]{:S(2)}, u32[]{:S(2)}) collective-permute-start(f32[256,128]{1,0:T(8,128)S(1)} %get-tuple-element.30.after.low_ref), channel_id=1, source_target_pairs={{0,16},{16,32},{32,48},{48,64},{64,80},{80,96},{96,112},{112,128},... | collective-permute-start | bytes 393224 | tf_op jit(solution)/shard_map/ppermute | solution.py:294

commit v8 on v7

--- a/solution.py
+++ b/solution.py
@@ -161,13 +161,31 @@
     return jnp.concatenate([top[:W], middle[:W]], axis=0), jnp.concatenate([middle[W:], low[W:]], axis=0)
 
 
-def across_below(last, low, below, update):
-    return across(low, jnp.where(last, 0.0, below), update)
+def joined(g_ref, at):
+    g = g_ref[at]
+    return g[:W, :W].astype(F32) + g[:W, 2 * W : 3 * W].astype(F32)
+
+
+def below_rows(message):
+    return message[:W], message[W : 2 * W], message[2 * W :]
+
+
+def across_below(last, low, near, update):
+    middle = update(jnp.concatenate([low[W:], jnp.where(last, 0.0, near)], axis=0))
+    return jnp.concatenate([low[:W], middle[:W]], axis=0), middle[W:]
+
+
+def carried(settled, quarter, change):
+    return settled + (change - dot3(split(quarter), split(change)))
 
 
 def across_above(first, above, top, update):
     new_above, new_top = across(above, top, update)
     return new_above, jnp.where(first, top, new_top)
+
+
+def keep_kernel(piece, kept):
+    kept[...] = piece[...]
 
 
 def order_kernel(plane, p0, p1, p2, p3, near, far, held):
@@ -177,16 +195,23 @@
     far[...] = held[2:4]
 
 
-def first_kernel(scalars, x_ref, p0, p1, p2, p3, message, low_ref, held):
+def first_kernel(scalars, x_ref, p0, p1, p2, p3, message, low_ref, rest, held):
     pieces = (p0, p1, p2, p3)
     gathered(scalars, pieces, held, 1)
-    message[2 * W :] = block_of(scalars, held, 2, 0)
+    ahead = block_of(scalars, held, 2, 0)
     gathered(scalars, pieces, held, 0)
-    found = factors([block_of(scalars, held, level, half) for level, half in ((0, 0), (0, 1), (1, 0))])
+    found = factors([block_of(scalars, held, level, half) for level, half in ((0, 0), (0, 1), (1, 0))] + [ahead])
+    ah, al, vh, vl = found[3]
+    left = dot3((vh, vl), (ah[:, :W], al[:, :W]))
     top = twice(found[0])(x_ref[: 2 * W])
     low = twice(found[1])(x_ref[2 * W :])
     top, low = across(top, low, twice(found[2]))
-    message[: 2 * W] = top
+    settled = twice(found[3])(top)
+    message[:W] = top[:W]
+    message[W : 2 * W] = settled[:W]
+    message[2 * W :] = left[:W]
+    rest[:W] = settled[W:]
+    rest[W:] = left[W:]
     low_ref[...] = low
 
 
@@ -197,41 +222,47 @@
     early = block_of(scalars, held, 1, 1)
     gathered(scalars, pieces, held, 1)
     late = [block_of(scalars, held, level, half) for level, half in ((2, 1), (3, 0), (3, 1))]
-    stored_wholes([*late, early, block_of(scalars, held, 2, 0)], g1)
-
-
-def second_kernel(scalars, low_ref, own, message, g1, low_out, below_out, top_out):
+    stored_wholes([*late, early], g1)
+
+
+def second_kernel(scalars, low_ref, message, g1, low_out, back):
     last = scalars[1] == 1
-    (foreign,) = factors([message[2 * W :]])
-    low, below = across_below(last, low_ref[...], message[: 2 * W], once(g1, 3))
+    near, settled, quarter = below_rows(message)
+    low, moved = across_below(last, low_ref[...], near, once(g1, 3))
+    change = moved - near
     low = once(g1, 0)(low)
-    below = twice(foreign)(below)
-    top_out[...] = once(g1, 4)(own[: 2 * W])
-    low, below = across_below(last, low, below, once(g1, 2))
+    low, moved = across_below(last, low, carried(settled, quarter, change), once(g1, 2))
     low_out[...] = low
-    below_out[...] = below
-
-
-def factor2_kernel(scalars, after, p0, p1, p2, p3, g2, up, down, held):
+    back[:W] = moved
+    back[W:] = change
+
+
+def choose_kernel(scalars, after, p0, p1, p2, p3, down, held):
     pieces = (p0, p1, p2, p3)
     gathered(scalars, pieces, held, 1)
-    up[...] = block_of(scalars, held, 6, 0)
     down[1] = block_of(scalars, held, 6, 1)
     down[2] = block_of(scalars, held, 7, 1)
     gathered(scalars, pieces, held, 0)
     down[0] = block_of(scalars, held, 5, 1)
+
+
+def factor2_kernel(scalars, after, p0, p1, p2, p3, g2, held):
+    gathered(scalars, (p0, p1, p2, p3), held, 0)
     stored_wholes([block_of(scalars, held, level, half) for level in (4, 5) for half in (0, 1)], g2)
 
 
-def third_kernel(scalars, low_ref, mine, top_ref, up, g1, g2, low_out, message):
-    message[2 * W :] = up[...]
-    top = jnp.where(scalars[2] == 1, mine[...], top_ref[...])
-    top, low = across(top, low_ref[...], once(g1, 1))
+def third_kernel(scalars, low_ref, own, rest, back, g1, g2, g3, low_out, top_out, message):
+    upper = jnp.where(scalars[2] == 1, own[W : 2 * W], back[:W])
+    lower = rest[:W] - dot3(split(rest[W:]), split(back[W:]))
+    top, low = across(jnp.concatenate([upper, lower], axis=0), low_ref[...], once(g1, 1))
     top = once(g2, 0)(top)
     low = once(g2, 1)(low)
     top, low = across(top, low, once(g2, 2))
     low_out[...] = low
-    message[: 2 * W] = top
+    top_out[...] = top
+    message[:W] = top[:W]
+    message[W : 2 * W] = once(g3, 0)(top)[:W]
+    message[2 * W :] = joined(g3, 0)
 
 
 def factor3_kernel(scalars, after, p0, p1, p2, p3, g3, held):
@@ -243,18 +274,17 @@
     stored_wholes([down[0], down[1], down[2]], g4)
 
 
-def fourth_kernel(scalars, low_ref, own, above_ref, message, g2, g3, g4, out_ref):
+def fourth_kernel(scalars, low_ref, top_ref, above_ref, message, g2, g3, g4, out_ref):
     last = scalars[1] == 1
     first = scalars[2] == 1
-    (foreign,) = factors([message[2 * W :]])
-    low, below = across_below(last, low_ref[...], message[: 2 * W], once(g2, 3))
-    above, top = across_above(first, above_ref[...], own[: 2 * W], once(g4, 0))
+    near, settled, quarter = below_rows(message)
+    low, moved = across_below(last, low_ref[...], near, once(g2, 3))
+    above, top = across_above(first, above_ref[...], top_ref[...], once(g4, 0))
     above = once(g4, 1)(above)
     top = once(g3, 0)(top)
     low = once(g3, 1)(low)
     _, top = across_above(first, above, top, once(g4, 2))
-    below = twice(foreign)(below)
-    low, _ = across_below(last, low, below, once(g3, 3))
+    low, _ = across_below(last, low, carried(settled, quarter, moved - near), once(g3, 3))
     top, low = across(top, low, once(g3, 2))
     out_ref[: 2 * W] = top
     out_ref[2 * W :] = low
@@ -308,27 +338,29 @@
     packed = wy_packed[0]
     half = rows_shape(2 * W, W)
 
+    (held,) = call(keep_kernel, (packed,), [rows_shape(W, W)], smem=0)
     planes = [packed] + [shifted(packed, "cols", 4 * k) for k in (1, 2, 3)]
     pair = rows_shape(2, W, W)
-    near, far = call(order_kernel, (plane.reshape(1), *planes), [pair, pair], HELD)
+    near, far = call(order_kernel, (plane.reshape(1), held, *planes[1:]), [pair, pair], HELD)
     near = along_x(near)
     three = rows_shape(3 * W, W)
-    own, low = call(first_kernel, (scalars, eigvecs, *near), [three, half], HELD)
+    three = rows_shape(3 * W, W)
+    own, low, rest = call(first_kernel, (scalars, eigvecs, *near), [three, half, half], HELD)
     message = to_neighbour(own, -1)
-    g1, far = call(factor1_kernel, (scalars, low, *near, far), [wholes(5), pair], HELD)
+    g1, far = call(factor1_kernel, (scalars, low, *near, far), [wholes(4), pair], HELD)
     far = along_x(far)
-    low, below, mine = call(second_kernel, (scalars, low, own, message, g1), [half, half, half])
-    top = to_neighbour(below, 1)
-    blocks = [wholes(4), rows_shape(W, W), rows_shape(3, W, W)]
-    g2, up, down = call(factor2_kernel, (scalars, low, *far), blocks, HELD)
+    low, back = call(second_kernel, (scalars, low, message, g1), [half, half])
+    back = to_neighbour(back, 1)
+    (down,) = call(choose_kernel, (scalars, low, *far), [rows_shape(3, W, W)], HELD)
+    (g2,) = call(factor2_kernel, (scalars, down, *far), [wholes(4)], HELD)
+    (g3,) = call(factor3_kernel, (scalars, down, *far), [wholes(4)], HELD)
     down = to_neighbour(down, 1)
-    low, own = call(third_kernel, (scalars, low, mine, top, up, g1, g2), [half, three])
+    low, top, message = call(third_kernel, (scalars, low, own, rest, back, g1, g2, g3), [half, half, three])
     above = to_neighbour(low, 1)
-    message = to_neighbour(own, -1)
-    (g3,) = call(factor3_kernel, (scalars, low, *far), [wholes(4)], HELD)
+    message = to_neighbour(message, -1)
     (g4,) = call(factor4_kernel, (low, down), [wholes(3)], smem=0)
     return call(
-        fourth_kernel, (scalars, low, own, above, message, g2, g3, g4), [rows_shape(*eigvecs.shape)]
+        fourth_kernel, (scalars, low, top, above, message, g2, g3, g4), [rows_shape(*eigvecs.shape)]
     )[0]
 
 

time: 76.3 us -> 76.8 us (level)
  starting transfers between devices: 30 us -> 36.7 us
  waiting for transfers between devices: 20.3 us -> 16.4 us
  Pallas kernels: 23.8 us -> 21.9 us
    ppermute x6, starting transfers between devices: 6.62 us -> 10.5 us  [along_x(): lax.ppermute(value, 'cols', [(i, i // 4 * 4 + (i + k) % 4) for i in range...]
    ppermute x5, starting transfers between devices: 17.2 us -> 20.9 us  [to_neighbour(): lax.ppermute(value, 'rows', [(i, i + steps) for i in range(count) if 0 <=...]
    ppermute x6, waiting for transfers between devices: 7.83 us -> 5.45 us  [along_x(): lax.ppermute(value, 'cols', [(i, i // 4 * 4 + (i + k) % 4) for i in range...]
    pallas_call x9 -> x11, Pallas kernels: 23.8 us -> 21.9 us  [call(): pl.pallas_call(kernel, out_shape=tuple(shapes), in_specs=[pl.BlockSpec(me...]
    ppermute x5, waiting for transfers between devices: 9.12 us -> 7.39 us  [to_neighbour(): lax.ppermute(value, 'rows', [(i, i + steps) for i in range(count) if 0 <=...]
    ppermute x3, starting transfers between devices: 6.2 us -> 5.3 us  [shifted(): lax.ppermute(value, axis, [(i, (i + steps) % count) for i in range(count)])]
  transfers between devices with their start and end apart: 14 -> 14, of which waited for: 8 -> 7; matrix products, arithmetic and copies ran while one was open for 0% -> 0% of each run, Pallas kernels for 22% -> 20%
where the time goes in v8:
time: 76.8 us; the launch traced here: 76.3 us
  starting transfers between devices  36.7 us (48%)
  Pallas kernels  21.9 us (29%)
  waiting for transfers between devices  16.4 us (21%)
  local copies, waits for them, and re-layouts  1.04 us (1%)
    pallas_call x11, Pallas kernels, call(): pl.pallas_call(kernel, out_shape=tuple(shapes), in_specs=[pl.BlockSpec(me...  21.9 us
    ppermute x5, starting transfers between devices, to_neighbour(): lax.ppermute(value, 'rows', [(i, i + steps) for i in range(count) if 0 <=...  20.9 us
    ppermute x6, starting transfers between devices, along_x(): lax.ppermute(value, 'cols', [(i, i // 4 * 4 + (i + k) % 4) for i in range...  10.5 us
    ppermute x5, waiting for transfers between devices, to_neighbour(): lax.ppermute(value, 'rows', [(i, i + steps) for i in range(count) if 0 <=...  7.39 us
    ppermute x6, waiting for transfers between devices, along_x(): lax.ppermute(value, 'cols', [(i, i // 4 * 4 + (i + k) % 4) for i in range...  5.45 us
    ppermute x3, starting transfers between devices, shifted(): lax.ppermute(value, axis, [(i, (i + steps) % count) for i in range(count)])  5.3 us
    ppermute x3, waiting for transfers between devices, shifted(): lax.ppermute(value, axis, [(i, (i + steps) % count) for i in range(count)])  3.6 us
  transfers between devices with their start and end apart: 14, of which 7 were waited for; matrix products, arithmetic and copies ran while one was open for 0% of the time, Pallas kernels for 20%

profile of v8, /device:TPU:56, one launch (start us, length us, event | category | flops | bytes accessed | tf_op | source)
XLA Modules:
  0.0 76.3 jit_solution(3741720458488002590)
XLA Ops:
  0.0 1.9 %collective-permute-start = (f32[128,128]{1,0:T(8,128)}, f32[128,128]{1,0:T(8,128)S(1)}, u32[]{:S(2)}, u32[]{:S(2)}) collective-permute-start(f32[128,128]{1,0:T(8,128)} %bitcast.5), channel_id=1, source_target_pairs={{0,4},{1,5},{2,6},{3,7},{4,8},{5,9},{6,10},{7,11},{8,12},{9,13},{1... | collective-permute-start | bytes 196616 | tf_op jit(solution)/shard_map/ppermute | solution.py:319
  1.9 1.4 %collective-permute-start.1 = (f32[128,128]{1,0:T(8,128)}, f32[128,128]{1,0:T(8,128)S(1)}, u32[]{:S(2)}, u32[]{:S(2)}) collective-permute-start(f32[128,128]{1,0:T(8,128)} %bitcast.6), channel_id=1, source_target_pairs={{0,8},{1,9},{2,10},{3,11},{4,12},{5,13},{6,14},{7,15},{8,0},{9,1},... | collective-permute-start | bytes 196616 | tf_op jit(solution)/shard_map/ppermute | solution.py:319
  3.3 2.0 %collective-permute-start.2 = (f32[128,128]{1,0:T(8,128)}, f32[128,128]{1,0:T(8,128)S(1)}, u32[]{:S(2)}, u32[]{:S(2)}) collective-permute-start(f32[128,128]{1,0:T(8,128)} %bitcast.7), channel_id=1, source_target_pairs={{0,12},{1,13},{2,14},{3,15},{4,0},{5,1},{6,2},{7,3},{8,4},{9,5},{1... | collective-permute-start | bytes 196616 | tf_op jit(solution)/shard_map/ppermute | solution.py:319
  5.3 0.0 copy-start.1
  5.3 0.9 %copy-done.1 = f32[1,128,128]{2,1,0:T(8,128)S(1)} copy-done((f32[1,128,128]{2,1,0:T(8,128)S(1)}, f32[1,128,128]{2,1,0:T(8,128)}, u32[]{:S(2)}) %copy-start.1) | copy-done | bytes 65560
  6.2 0.0 collective-permute-done.p1
  6.2 2.1 %collective-permute-done.1.p2 = f32[128,128]{1,0:T(8,128)S(1)} collective-permute-done((f32[128,128]{1,0:T(8,128)}, f32[128,128]{1,0:T(8,128)S(1)}, u32[]{:S(2)}, u32[]{:S(2)}) %collective-permute-start.1) | collective-permute-done | bytes 65568 | tf_op jit(solution)/shard_map/ppermute | solution.py:319
  8.3 1.5 %collective-permute-done.2.p3 = f32[128,128]{1,0:T(8,128)S(1)} collective-permute-done((f32[128,128]{1,0:T(8,128)}, f32[128,128]{1,0:T(8,128)S(1)}, u32[]{:S(2)}, u32[]{:S(2)}) %collective-permute-start.2) | collective-permute-done | bytes 65568 | tf_op jit(solution)/shard_map/ppermute | solution.py:319
  9.8 0.0 copy-start
  9.8 0.0 copy-start.2
  9.8 1.6 %collective-permute-start.3 = (f32[2,128,128]{2,1,0:T(8,128)S(1)}, f32[2,128,128]{2,1,0:T(8,128)S(1)}, u32[]{:S(2)}, u32[]{:S(2)}) collective-permute-start(f32[2,128,128]{2,1,0:T(8,128)S(1)} %get-tuple-element.17.p0), channel_id=1, source_target_pairs={{0,1},{1,2},{2,3},{3,0},{4,5},{5,6},{6,7},{7,4},{8,9},{9,10},{10,1... | collective-permute-start | bytes 393224 | tf_op jit(solution)/shard_map/ppermute | solution.py:328
  11.4 2.7 %collective-permute-start.4 = (f32[2,128,128]{2,1,0:T(8,128)S(1)}, f32[2,128,128]{2,1,0:T(8,128)S(1)}, u32[]{:S(2)}, u32[]{:S(2)}) collective-permute-start(f32[2,128,128]{2,1,0:T(8,128)S(1)} %get-tuple-element.17.p0), channel_id=1, source_target_pairs={{0,2},{1,3},{2,0},{3,1},{4,6},{5,7},{6,4},{7,5},{8,10},{9,11},{10,... | collective-permute-start | bytes 393224 | tf_op jit(solution)/shard_map/ppermute | solution.py:328
  14.1 1.4 %collective-permute-start.5 = (f32[2,128,128]{2,1,0:T(8,128)S(1)}, f32[2,128,128]{2,1,0:T(8,128)S(1)}, u32[]{:S(2)}, u32[]{:S(2)}) collective-permute-start(f32[2,128,128]{2,1,0:T(8,128)S(1)} %get-tuple-element.17.p0), channel_id=1, source_target_pairs={{0,3},{1,0},{2,1},{3,2},{4,7},{5,4},{6,5},{7,6},{8,11},{9,8},{10,9... | collective-permute-start | bytes 393224 | tf_op jit(solution)/shard_map/ppermute | solution.py:328
  15.6 0.0 copy-done.2
  15.6 0.1 copy.5
  15.7 0.1 reshape.6
  15.7 0.1 pad_add_fusion.scalars
  15.8 0.7 collective-permute-done.3.p1
  16.5 3.8 %collective-permute-done.4.p2 = f32[2,128,128]{2,1,0:T(8,128)S(1)} collective-permute-done((f32[2,128,128]{2,1,0:T(8,128)S(1)}, f32[2,128,128]{2,1,0:T(8,128)S(1)}, u32[]{:S(2)}, u32[]{:S(2)}) %collective-permute-start.4) | collective-permute-done | bytes 131104 | tf_op jit(solution)/shard_map/ppermute | solution.py:328
  20.3 0.0 collective-permute-done.5.p3
  20.3 0.0 copy-done
  20.3 4.2 %first_kernel.1 = (f32[384,128]{1,0:T(8,128)S(1)}, f32[256,128]{1,0:T(8,128)S(1)}, f32[256,128]{1,0:T(8,128)S(1)}) custom-call(s32[19]{0:T(128)S(1)} %pad_add_fusion.scalars, f32[512,128]{1,0:T(8,128)S(1)} %copy-done, f32[2,128,128]{2,1,0:T(8,128)S(1)} %get-tuple-element.17.p0, f32[2,128,128]{2,1,0:T(8,128)S(1)} %collective-permute-done.3.p1, ...), custom_call_target="tpu_custom_call" | custom-call | flops 400000000 | bytes 2000000 | tf_op jit(solution)/shard_map/first_kernel/pallas_call | solution.py:305
  24.5 6.5 %collective-permute-start.6 = (f32[384,128]{1,0:T(8,128)S(1)}, f32[384,128]{1,0:T(8,128)S(1)}, u32[]{:S(2)}, u32[]{:S(2)}) collective-permute-start(f32[384,128]{1,0:T(8,128)S(1)} %get-tuple-element.19.own), channel_id=1, source_target_pairs={{16,0},{32,16},{48,32},{64,48},{80,64},{96,80},{112,96},{128,112},... | collective-permute-start | bytes 589832 | tf_op jit(solution)/shard_map/ppermute | solution.py:324
  31.0 3.2 %factor1_kernel.1 = (bf16[4,256,512]{2,1,0:T(8,128)(2,1)S(1)}, f32[2,128,128]{2,1,0:T(8,128)S(1)}) custom-call(s32[19]{0:T(128)S(1)} %pad_add_fusion.scalars, f32[256,128]{1,0:T(8,128)S(1)} %get-tuple-element.18.after.low_ref, f32[2,128,128]{2,1,0:T(8,128)S(1)} %get-tuple-element.17.p0, f32[2,128,128]{2,1,0:T(8,128)S(1)} %collective-permute-done.3.p1, ...), custom_call_target="tpu_custom_call" | custom-call | flops 400000000 | bytes 2000000 | tf_op jit(solution)/shard_map/factor1_kernel/pallas_call | solution.py:305
  34.2 1.5 %collective-permute-start.8 = (f32[2,128,128]{2,1,0:T(8,128)S(1)}, f32[2,128,128]{2,1,0:T(8,128)S(1)}, u32[]{:S(2)}, u32[]{:S(2)}) collective-permute-start(f32[2,128,128]{2,1,0:T(8,128)S(1)} %get-tuple-element.25.p0), channel_id=1, source_target_pairs={{0,1},{1,2},{2,3},{3,0},{4,5},{5,6},{6,7},{7,4},{8,9},{9,10},{10,1... | collective-permute-start | bytes 393224 | tf_op jit(solution)/shard_map/ppermute | solution.py:328
  35.8 2.5 %collective-permute-start.9 = (f32[2,128,128]{2,1,0:T(8,128)S(1)}, f32[2,128,128]{2,1,0:T(8,128)S(1)}, u32[]{:S(2)}, u32[]{:S(2)}) collective-permute-start(f32[2,128,128]{2,1,0:T(8,128)S(1)} %get-tuple-element.25.p0), channel_id=1, source_target_pairs={{0,2},{1,3},{2,0},{3,1},{4,6},{5,7},{6,4},{7,5},{8,10},{9,11},{10,... | collective-permute-start | bytes 393224 | tf_op jit(solution)/shard_map/ppermute | solution.py:328
  38.2 0.8 %collective-permute-start.10 = (f32[2,128,128]{2,1,0:T(8,128)S(1)}, f32[2,128,128]{2,1,0:T(8,128)S(1)}, u32[]{:S(2)}, u32[]{:S(2)}) collective-permute-start(f32[2,128,128]{2,1,0:T(8,128)S(1)} %get-tuple-element.25.p0), channel_id=1, source_target_pairs={{0,3},{1,0},{2,1},{3,2},{4,7},{5,4},{6,5},{7,6},{8,11},{9,8},{10,9... | collective-permute-start | bytes 393224 | tf_op jit(solution)/shard_map/ppermute | solution.py:328
  39.0 0.0 collective-permute-done.6.message
  39.0 1.2 %second_kernel.1 = (f32[256,128]{1,0:T(8,128)S(1)}, f32[256,128]{1,0:T(8,128)S(1)}) custom-call(s32[19]{0:T(128)S(1)} %pad_add_fusion.scalars, f32[256,128]{1,0:T(8,128)S(1)} %get-tuple-element.18.after.low_ref, f32[384,128]{1,0:T(8,128)S(1)} %collective-permute-done.6.message, bf16[4,256,512]{2,1,0:T(8,128)(2,1)S(1)} %get-tuple-element.21.g1), custom_call_target="tpu_custom_call" | custom-call | flops 400000000 | bytes 2000000 | tf_op jit(solution)/shard_map/second_kernel/pallas_call | solution.py:305
  40.3 1.9 %collective-permute-start.7 = (f32[256,128]{1,0:T(8,128)S(1)}, f32[256,128]{1,0:T(8,128)S(1)}, u32[]{:S(2)}, u32[]{:S(2)}) collective-permute-start(f32[256,128]{1,0:T(8,128)S(1)} %get-tuple-element.24), channel_id=1, source_target_pairs={{0,16},{16,32},{32,48},{48,64},{64,80},{80,96},{96,112},{112,128},... | collective-permute-start | bytes 393224 | tf_op jit(solution)/shard_map/ppermute | solution.py:324
  42.2 0.0 collective-permute-done.8.p1
  42.2 0.4 collective-permute-done.9.p2
  42.6 0.6 collective-permute-done.10.p3
  43.2 0.6 choose_kernel.1.after
  43.8 3.0 %collective-permute-start.13 = (f32[3,128,128]{2,1,0:T(8,128)S(1)}, f32[3,128,128]{2,1,0:T(8,128)S(1)}, u32[]{:S(2)}, u32[]{:S(2)}) collective-permute-start(f32[3,128,128]{2,1,0:T(8,128)S(1)} %choose_kernel.1.after), channel_id=1, source_target_pairs={{0,16},{16,32},{32,48},{48,64},{64,80},{80,96},{96,112},{112,128},... | collective-permute-start | bytes 589832 | tf_op jit(solution)/shard_map/ppermute | solution.py:324
  46.8 3.2 %factor2_kernel.1.g2 = bf16[4,256,512]{2,1,0:T(8,128)(2,1)S(1)} custom-call(s32[19]{0:T(128)S(1)} %pad_add_fusion.scalars, f32[3,128,128]{2,1,0:T(8,128)S(1)} %choose_kernel.1.after, f32[2,128,128]{2,1,0:T(8,128)S(1)} %get-tuple-element.25.p0, f32[2,128,128]{2,1,0:T(8,128)S(1)} %collective-permute-done.8.p1, f32[2,128,128]{2,1,0:T(8,128)S(1)} %collective-permute-done.9.p2, ...), custom_call_target="tpu_custom_call" | custom-call | flops 400000000 | bytes 2000000 | tf_op jit(solution)/shard_map/factor2_kernel/pallas_call | solution.py:305
  50.0 3.2 %factor3_kernel.1.g3 = bf16[4,256,512]{2,1,0:T(8,128)(2,1)S(1)} custom-call(s32[19]{0:T(128)S(1)} %pad_add_fusion.scalars, f32[3,128,128]{2,1,0:T(8,128)S(1)} %choose_kernel.1.after, f32[2,128,128]{2,1,0:T(8,128)S(1)} %get-tuple-element.25.p0, f32[2,128,128]{2,1,0:T(8,128)S(1)} %collective-permute-done.8.p1, f32[2,128,128]{2,1,0:T(8,128)S(1)} %collective-permute-done.9.p2, ...), custom_call_target="tpu_custom_call" | custom-call | flops 400000000 | bytes 2000000 | tf_op jit(solution)/shard_map/factor3_kernel/pallas_call | solution.py:305
  53.2 0.0 collective-permute-done.7.back
  53.2 1.5 %third_kernel.1 = (f32[256,128]{1,0:T(8,128)S(1)}, f32[256,128]{1,0:T(8,128)S(1)}, f32[384,128]{1,0:T(8,128)S(1)}) custom-call(s32[19]{0:T(128)S(1)} %pad_add_fusion.scalars, f32[256,128]{1,0:T(8,128)S(1)} %get-tuple-element.22.after.low_ref, f32[384,128]{1,0:T(8,128)S(1)} %get-tuple-element.19.own, f32[256,128]{1,0:T(8,128)S(1)} %get-tuple-element.23.rest, ...), custom_call_target="tpu_custom_call" | custom-call | flops 400000000 | bytes 2000000 | tf_op jit(solution)/shard_map/third_kernel/pallas_call | solution.py:305
  54.8 7.5 %collective-permute-start.12 = (f32[384,128]{1,0:T(8,128)S(1)}, f32[384,128]{1,0:T(8,128)S(1)}, u32[]{:S(2)}, u32[]{:S(2)}) collective-permute-start(f32[384,128]{1,0:T(8,128)S(1)} %get-tuple-element.28), channel_id=1, source_target_pairs={{16,0},{32,16},{48,32},{64,48},{80,64},{96,80},{112,96},{128,112},... | collective-permute-start | bytes 589832 | tf_op jit(solution)/shard_map/ppermute | solution.py:324
  62.3 1.9 %collective-permute-start.11 = (f32[256,128]{1,0:T(8,128)S(1)}, f32[256,128]{1,0:T(8,128)S(1)}, u32[]{:S(2)}, u32[]{:S(2)}) collective-permute-start(f32[256,128]{1,0:T(8,128)S(1)} %get-tuple-element.26.after.low_ref), channel_id=1, source_target_pairs={{0,16},{16,32},{32,48},{48,64},{64,80},{80,96},{96,112},{112,128},... | collective-permute-start | bytes 393224 | tf_op jit(solution)/shard_map/ppermute | solution.py:324
  64.2 0.0 collective-permute-done.13.down
  64.2 2.4 %factor4_kernel.1.g4 = bf16[3,256,512]{2,1,0:T(8,128)(2,1)S(1)} custom-call(f32[256,128]{1,0:T(8,128)S(1)} %get-tuple-element.26.after.low_ref, f32[3,128,128]{2,1,0:T(8,128)S(1)} %collective-permute-done.13.down), custom_call_target="tpu_custom_call" | custom-call | flops 400000000 | bytes 2000000 | tf_op jit(solution)/shard_map/factor4_kernel/pallas_call | solution.py:305
  66.6 7.4 %collective-permute-done.11.above_ref = f32[256,128]{1,0:T(8,128)S(1)} collective-permute-done((f32[256,128]{1,0:T(8,128)S(1)}, f32[256,128]{1,0:T(8,128)S(1)}, u32[]{:S(2)}, u32[]{:S(2)}) %collective-permute-start.11) | collective-permute-done | bytes 131104 | tf_op jit(solution)/shard_map/ppermute | solution.py:324
  74.0 0.0 collective-permute-done.12.message
  74.0 2.3 %fourth_kernel.1 = f32[512,128]{1,0:T(8,128)} custom-call(s32[19]{0:T(128)S(1)} %pad_add_fusion.scalars, f32[256,128]{1,0:T(8,128)S(1)} %get-tuple-element.26.after.low_ref, f32[256,128]{1,0:T(8,128)S(1)} %get-tuple-element.27.top_ref, f32[256,128]{1,0:T(8,128)S(1)} %collective-permute-done.11.above_ref, f32[384,128]{1,0:T(8,128)S(1)} %collective-permute-done.12.message, ...), custom_call_target="tpu_custom_call" | custom-call | flops 400000000 | bytes 2000000 | tf_op jit(solution)/shard_map/fourth_kernel/pallas_call | solution.py:305
  (2 shorter events, 0.0 us)
Async XLA Ops:
  0.0 6.2 %collective-permute-start = (f32[128,128]{1,0:T(8,128)}, f32[128,128]{1,0:T(8,128)S(1)}, u32[]{:S(2)}, u32[]{:S(2)}) collective-permute-start(f32[128,128]{1,0:T(8,128)} %bitcast.5), channel_id=1, source_target_pairs={{0,4},{1,5},{2,6},{3,7},{4,8},{5,9},{6,10},{7,11},{8,12},{9,13},{1... | collective-permute-start | bytes 196616 | tf_op jit(solution)/shard_map/ppermute | solution.py:319
  1.9 6.3 %collective-permute-start.1 = (f32[128,128]{1,0:T(8,128)}, f32[128,128]{1,0:T(8,128)S(1)}, u32[]{:S(2)}, u32[]{:S(2)}) collective-permute-start(f32[128,128]{1,0:T(8,128)} %bitcast.6), channel_id=1, source_target_pairs={{0,8},{1,9},{2,10},{3,11},{4,12},{5,13},{6,14},{7,15},{8,0},{9,1},... | collective-permute-start | bytes 196616 | tf_op jit(solution)/shard_map/ppermute | solution.py:319
  3.3 6.5 %collective-permute-start.2 = (f32[128,128]{1,0:T(8,128)}, f32[128,128]{1,0:T(8,128)S(1)}, u32[]{:S(2)}, u32[]{:S(2)}) collective-permute-start(f32[128,128]{1,0:T(8,128)} %bitcast.7), channel_id=1, source_target_pairs={{0,12},{1,13},{2,14},{3,15},{4,0},{5,1},{6,2},{7,3},{8,4},{9,5},{1... | collective-permute-start | bytes 196616 | tf_op jit(solution)/shard_map/ppermute | solution.py:319
  5.3 0.9 %copy-start.1 = (f32[1,128,128]{2,1,0:T(8,128)S(1)}, f32[1,128,128]{2,1,0:T(8,128)}, u32[]{:S(2)}) copy-start(f32[1,128,128]{2,1,0:T(8,128)} %param.4) | copy-start | bytes 196612
  9.8 10.5 %copy-start = (f32[512,128]{1,0:T(8,128)S(1)}, f32[512,128]{1,0:T(8,128)}, u32[]{:S(2)}) copy-start(f32[512,128]{1,0:T(8,128)} %x_ref.1) | copy-start | bytes 786436
  9.8 5.7 %copy-start.2 = (s32[1,8,2]{1,2,0:T(2,128)S(1)}, s32[1,8,2]{1,2,0:T(2,128)}, u32[]{:S(2)}) copy-start(s32[1,8,2]{1,2,0:T(2,128)} %param.5) | copy-start | bytes 196
  9.8 6.7 %collective-permute-start.3 = (f32[2,128,128]{2,1,0:T(8,128)S(1)}, f32[2,128,128]{2,1,0:T(8,128)S(1)}, u32[]{:S(2)}, u32[]{:S(2)}) collective-permute-start(f32[2,128,128]{2,1,0:T(8,128)S(1)} %get-tuple-element.17.p0), channel_id=1, source_target_pairs={{0,1},{1,2},{2,3},{3,0},{4,5},{5,6},{6,7},{7,4},{8,9},{9,10},{10,1... | collective-permute-start | bytes 393224 | tf_op jit(solution)/shard_map/ppermute | solution.py:328
  11.4 8.9 %collective-permute-start.4 = (f32[2,128,128]{2,1,0:T(8,128)S(1)}, f32[2,128,128]{2,1,0:T(8,128)S(1)}, u32[]{:S(2)}, u32[]{:S(2)}) collective-permute-start(f32[2,128,128]{2,1,0:T(8,128)S(1)} %get-tuple-element.17.p0), channel_id=1, source_target_pairs={{0,2},{1,3},{2,0},{3,1},{4,6},{5,7},{6,4},{7,5},{8,10},{9,11},{10,... | collective-permute-start | bytes 393224 | tf_op jit(solution)/shard_map/ppermute | solution.py:328
  14.1 6.1 %collective-permute-start.5 = (f32[2,128,128]{2,1,0:T(8,128)S(1)}, f32[2,128,128]{2,1,0:T(8,128)S(1)}, u32[]{:S(2)}, u32[]{:S(2)}) collective-permute-start(f32[2,128,128]{2,1,0:T(8,128)S(1)} %get-tuple-element.17.p0), channel_id=1, source_target_pairs={{0,3},{1,0},{2,1},{3,2},{4,7},{5,4},{6,5},{7,6},{8,11},{9,8},{10,9... | collective-permute-start | bytes 393224 | tf_op jit(solution)/shard_map/ppermute | solution.py:328
  24.5 14.5 %collective-permute-start.6 = (f32[384,128]{1,0:T(8,128)S(1)}, f32[384,128]{1,0:T(8,128)S(1)}, u32[]{:S(2)}, u32[]{:S(2)}) collective-permute-start(f32[384,128]{1,0:T(8,128)S(1)} %get-tuple-element.19.own), channel_id=1, source_target_pairs={{16,0},{32,16},{48,32},{64,48},{80,64},{96,80},{112,96},{128,112},... | collective-permute-start | bytes 589832 | tf_op jit(solution)/shard_map/ppermute | solution.py:324
  34.2 8.0 %collective-permute-start.8 = (f32[2,128,128]{2,1,0:T(8,128)S(1)}, f32[2,128,128]{2,1,0:T(8,128)S(1)}, u32[]{:S(2)}, u32[]{:S(2)}) collective-permute-start(f32[2,128,128]{2,1,0:T(8,128)S(1)} %get-tuple-element.25.p0), channel_id=1, source_target_pairs={{0,1},{1,2},{2,3},{3,0},{4,5},{5,6},{6,7},{7,4},{8,9},{9,10},{10,1... | collective-permute-start | bytes 393224 | tf_op jit(solution)/shard_map/ppermute | solution.py:328
  35.8 6.8 %collective-permute-start.9 = (f32[2,128,128]{2,1,0:T(8,128)S(1)}, f32[2,128,128]{2,1,0:T(8,128)S(1)}, u32[]{:S(2)}, u32[]{:S(2)}) collective-permute-start(f32[2,128,128]{2,1,0:T(8,128)S(1)} %get-tuple-element.25.p0), channel_id=1, source_target_pairs={{0,2},{1,3},{2,0},{3,1},{4,6},{5,7},{6,4},{7,5},{8,10},{9,11},{10,... | collective-permute-start | bytes 393224 | tf_op jit(solution)/shard_map/ppermute | solution.py:328
  38.2 5.0 %collective-permute-start.10 = (f32[2,128,128]{2,1,0:T(8,128)S(1)}, f32[2,128,128]{2,1,0:T(8,128)S(1)}, u32[]{:S(2)}, u32[]{:S(2)}) collective-permute-start(f32[2,128,128]{2,1,0:T(8,128)S(1)} %get-tuple-element.25.p0), channel_id=1, source_target_pairs={{0,3},{1,0},{2,1},{3,2},{4,7},{5,4},{6,5},{7,6},{8,11},{9,8},{10,9... | collective-permute-start | bytes 393224 | tf_op jit(solution)/shard_map/ppermute | solution.py:328
  40.3 13.0 %collective-permute-start.7 = (f32[256,128]{1,0:T(8,128)S(1)}, f32[256,128]{1,0:T(8,128)S(1)}, u32[]{:S(2)}, u32[]{:S(2)}) collective-permute-start(f32[256,128]{1,0:T(8,128)S(1)} %get-tuple-element.24), channel_id=1, source_target_pairs={{0,16},{16,32},{32,48},{48,64},{64,80},{80,96},{96,112},{112,128},... | collective-permute-start | bytes 393224 | tf_op jit(solution)/shard_map/ppermute | solution.py:324
  43.8 20.4 %collective-permute-start.13 = (f32[3,128,128]{2,1,0:T(8,128)S(1)}, f32[3,128,128]{2,1,0:T(8,128)S(1)}, u32[]{:S(2)}, u32[]{:S(2)}) collective-permute-start(f32[3,128,128]{2,1,0:T(8,128)S(1)} %choose_kernel.1.after), channel_id=1, source_target_pairs={{0,16},{16,32},{32,48},{48,64},{64,80},{80,96},{96,112},{112,128},... | collective-permute-start | bytes 589832 | tf_op jit(solution)/shard_map/ppermute | solution.py:324
  54.8 19.2 %collective-permute-start.12 = (f32[384,128]{1,0:T(8,128)S(1)}, f32[384,128]{1,0:T(8,128)S(1)}, u32[]{:S(2)}, u32[]{:S(2)}) collective-permute-start(f32[384,128]{1,0:T(8,128)S(1)} %get-tuple-element.28), channel_id=1, source_target_pairs={{16,0},{32,16},{48,32},{64,48},{80,64},{96,80},{112,96},{128,112},... | collective-permute-start | bytes 589832 | tf_op jit(solution)/shard_map/ppermute | solution.py:324
  62.3 11.7 %collective-permute-start.11 = (f32[256,128]{1,0:T(8,128)S(1)}, f32[256,128]{1,0:T(8,128)S(1)}, u32[]{:S(2)}, u32[]{:S(2)}) collective-permute-start(f32[256,128]{1,0:T(8,128)S(1)} %get-tuple-element.26.after.low_ref), channel_id=1, source_target_pairs={{0,16},{16,32},{32,48},{48,64},{64,80},{80,96},{96,112},{112,128},... | collective-permute-start | bytes 393224 | tf_op jit(solution)/shard_map/ppermute | solution.py:324

commit v9 on v8

--- a/solution.py
+++ b/solution.py
@@ -124,7 +124,7 @@
 
 
 def slot_of(scalars, level, half):
-    return scalars[3 + 2 * level + half]
+    return scalars[4 + 2 * level + half]
 
 
 def gathered(scalars, pieces, held, at):
@@ -215,8 +215,7 @@
     low_ref[...] = low
 
 
-def factor1_kernel(scalars, after, p0, p1, p2, p3, far, g1, sent, held):
-    sent[...] = far[...]
+def factor1_kernel(scalars, after, p0, p1, p2, p3, g1, held):
     pieces = (p0, p1, p2, p3)
     gathered(scalars, pieces, held, 0)
     early = block_of(scalars, held, 1, 1)
@@ -247,11 +246,14 @@
 
 
 def factor2_kernel(scalars, after, p0, p1, p2, p3, g2, held):
-    gathered(scalars, (p0, p1, p2, p3), held, 0)
-    stored_wholes([block_of(scalars, held, level, half) for level in (4, 5) for half in (0, 1)], g2)
-
-
-def third_kernel(scalars, low_ref, own, rest, back, g1, g2, g3, low_out, top_out, message):
+    pieces = (p0, p1, p2, p3)
+    gathered(scalars, pieces, held, 1)
+    later = block_of(scalars, held, 6, 0)
+    gathered(scalars, pieces, held, 0)
+    stored_wholes([block_of(scalars, held, level, half) for level in (4, 5) for half in (0, 1)] + [later], g2)
+
+
+def third_kernel(scalars, low_ref, own, rest, back, g1, g2, low_out, top_out, far_out, near_out):
     upper = jnp.where(scalars[2] == 1, own[W : 2 * W], back[:W])
     lower = rest[:W] - dot3(split(rest[W:]), split(back[W:]))
     top, low = across(jnp.concatenate([upper, lower], axis=0), low_ref[...], once(g1, 1))
@@ -260,32 +262,36 @@
     top, low = across(top, low, once(g2, 2))
     low_out[...] = low
     top_out[...] = top
-    message[:W] = top[:W]
-    message[W : 2 * W] = once(g3, 0)(top)[:W]
-    message[2 * W :] = joined(g3, 0)
+    settled = once(g2, 4)(top)
+    odd = scalars[3] == 1
+    for at, (up, down) in enumerate(((top[:W], low[:W]), (settled[:W], low[W:]), (joined(g2, 4), top[W:]))):
+        far_out[at * W : (at + 1) * W] = jnp.where(odd, down, up)
+        near_out[at * W : (at + 1) * W] = jnp.where(odd, up, down)
 
 
 def factor3_kernel(scalars, after, p0, p1, p2, p3, g3, held):
     gathered(scalars, (p0, p1, p2, p3), held, 1)
-    stored_wholes([block_of(scalars, held, level, half) for level, half in ((6, 0), (6, 1), (7, 0), (7, 1))], g3)
+    stored_wholes([block_of(scalars, held, level, half) for level, half in ((6, 1), (7, 0), (7, 1))], g3)
 
 
 def factor4_kernel(after, down, g4):
     stored_wholes([down[0], down[1], down[2]], g4)
 
 
-def fourth_kernel(scalars, low_ref, top_ref, above_ref, message, g2, g3, g4, out_ref):
+def fourth_kernel(scalars, low_ref, top_ref, far, near, g2, g3, g4, out_ref):
     last = scalars[1] == 1
     first = scalars[2] == 1
-    near, settled, quarter = below_rows(message)
+    odd = scalars[3] == 1
+    above = jnp.where(odd, near[: 2 * W], far[: 2 * W])
+    near, settled, quarter = below_rows(jnp.where(odd, far[...], near[...]))
     low, moved = across_below(last, low_ref[...], near, once(g2, 3))
-    above, top = across_above(first, above_ref[...], top_ref[...], once(g4, 0))
+    above, top = across_above(first, above, top_ref[...], once(g4, 0))
     above = once(g4, 1)(above)
-    top = once(g3, 0)(top)
-    low = once(g3, 1)(low)
+    top = once(g2, 4)(top)
+    low = once(g3, 0)(low)
     _, top = across_above(first, above, top, once(g4, 2))
-    low, _ = across_below(last, low, carried(settled, quarter, moved - near), once(g3, 3))
-    top, low = across(top, low, once(g3, 2))
+    low, _ = across_below(last, low, carried(settled, quarter, moved - near), once(g3, 2))
+    top, low = across(top, low, once(g3, 1))
     out_ref[: 2 * W] = top
     out_ref[2 * W :] = low
 
@@ -324,6 +330,12 @@
     return lax.ppermute(value, "rows", [(i, i + steps) for i in range(count) if 0 <= i + steps < count])
 
 
+def swapped(value, start):
+    count = lax.axis_size("rows")
+    pairs = [(i, i + 1) for i in range(start, count - 1, 2)]
+    return lax.ppermute(value, "rows", pairs + [(j, i) for i, j in pairs])
+
+
 def along_x(value):
     found = {k: lax.ppermute(value, "cols", [(i, (i // 4) * 4 + (i + k) % 4) for i in range(16)]) for k in (1, 3, 2)}
     return [value, found[1], found[2], found[3]]
@@ -333,7 +345,7 @@
     column = lax.axis_index("cols")
     row = lax.axis_index("rows")
     plane, place = column // 4, column % 4
-    edges = jnp.stack([place, row == lax.axis_size("rows") - 1, row == 0]).astype(jnp.int32)
+    edges = jnp.stack([place, row == lax.axis_size("rows") - 1, row == 0, row % 2]).astype(jnp.int32)
     scalars = jnp.concatenate([edges, slot_block.reshape(-1)])
     packed = wy_packed[0]
     half = rows_shape(2 * W, W)
@@ -343,24 +355,26 @@
     pair = rows_shape(2, W, W)
     near, far = call(order_kernel, (plane.reshape(1), held, *planes[1:]), [pair, pair], HELD)
     near = along_x(near)
+    far = along_x(far)
     three = rows_shape(3 * W, W)
     three = rows_shape(3 * W, W)
     own, low, rest = call(first_kernel, (scalars, eigvecs, *near), [three, half, half], HELD)
     message = to_neighbour(own, -1)
-    g1, far = call(factor1_kernel, (scalars, low, *near, far), [wholes(4), pair], HELD)
-    far = along_x(far)
+    (g1,) = call(factor1_kernel, (scalars, low, *near), [wholes(4)], HELD)
     low, back = call(second_kernel, (scalars, low, message, g1), [half, half])
     back = to_neighbour(back, 1)
     (down,) = call(choose_kernel, (scalars, low, *far), [rows_shape(3, W, W)], HELD)
-    (g2,) = call(factor2_kernel, (scalars, down, *far), [wholes(4)], HELD)
-    (g3,) = call(factor3_kernel, (scalars, down, *far), [wholes(4)], HELD)
+    (g2,) = call(factor2_kernel, (scalars, down, *far), [wholes(5)], HELD)
     down = to_neighbour(down, 1)
-    low, top, message = call(third_kernel, (scalars, low, own, rest, back, g1, g2, g3), [half, half, three])
-    above = to_neighbour(low, 1)
-    message = to_neighbour(message, -1)
+    low, top, far_out, near_out = call(
+        third_kernel, (scalars, low, own, rest, back, g1, g2), [half, half, three, three]
+    )
+    from_far = swapped(far_out, 1)
+    from_near = swapped(near_out, 0)
+    (g3,) = call(factor3_kernel, (scalars, low, *far), [wholes(3)], HELD)
     (g4,) = call(factor4_kernel, (low, down), [wholes(3)], smem=0)
     return call(
-        fourth_kernel, (scalars, low, top, above, message, g2, g3, g4), [rows_shape(*eigvecs.shape)]
+        fourth_kernel, (scalars, low, top, from_far, from_near, g2, g3, g4), [rows_shape(*eigvecs.shape)]
     )[0]
 
 

time: 76.8 us -> 73.1 us (0.952)
  starting transfers between devices: 36.7 us -> 29.3 us
  waiting for transfers between devices: 16.4 us -> 19.5 us
    ppermute x5 -> x3, starting transfers between devices: 20.9 us -> 11.6 us  [to_neighbour(): lax.ppermute(value, 'rows', [(i, i + steps) for i in range(count) if 0 <=...]
    ppermute x0 -> x2, waiting for transfers between devices: none -> 6.59 us  [swapped(): return lax.ppermute(value, 'rows', pairs + [(j, i) for i, j in pairs])]
    ppermute x0 -> x2, starting transfers between devices: none -> 4.9 us  [swapped(): return lax.ppermute(value, 'rows', pairs + [(j, i) for i, j in pairs])]
    ppermute x6, starting transfers between devices: 10.5 us -> 6.62 us  [along_x(): lax.ppermute(value, 'cols', [(i, i // 4 * 4 + (i + k) % 4) for i in range...]
    ppermute x5 -> x3, waiting for transfers between devices: 7.39 us -> 3.61 us  [to_neighbour(): lax.ppermute(value, 'rows', [(i, i + steps) for i in range(count) if 0 <=...]
    ppermute x6, waiting for transfers between devices: 5.45 us -> 6.8 us  [along_x(): lax.ppermute(value, 'cols', [(i, i // 4 * 4 + (i + k) % 4) for i in range...]
    ppermute x3, waiting for transfers between devices: 3.6 us -> 2.47 us  [shifted(): lax.ppermute(value, axis, [(i, (i + steps) % count) for i in range(count)])]
    ppermute x3, starting transfers between devices: 5.3 us -> 6.2 us  [shifted(): lax.ppermute(value, axis, [(i, (i + steps) % count) for i in range(count)])]
  transfers between devices with their start and end apart: 14 -> 14, of which waited for: 7 -> 7; matrix products, arithmetic and copies ran while one was open for 0% -> 0% of each run, Pallas kernels for 20% -> 22%
where the time goes in v9:
time: 73.1 us; the launch traced here: 72.2 us
  starting transfers between devices  29.3 us (40%)
  Pallas kernels  22.1 us (30%)
  waiting for transfers between devices  19.5 us (27%)
  local copies, waits for them, and re-layouts  1.13 us (2%)
    pallas_call x11, Pallas kernels, call(): pl.pallas_call(kernel, out_shape=tuple(shapes), in_specs=[pl.BlockSpec(me...  22.1 us
    ppermute x3, starting transfers between devices, to_neighbour(): lax.ppermute(value, 'rows', [(i, i + steps) for i in range(count) if 0 <=...  11.6 us
    ppermute x6, waiting for transfers between devices, along_x(): lax.ppermute(value, 'cols', [(i, i // 4 * 4 + (i + k) % 4) for i in range...  6.8 us
    ppermute x6, starting transfers between devices, along_x(): lax.ppermute(value, 'cols', [(i, i // 4 * 4 + (i + k) % 4) for i in range...  6.62 us
    ppermute x2, waiting for transfers between devices, swapped(): return lax.ppermute(value, 'rows', pairs + [(j, i) for i, j in pairs])  6.59 us
    ppermute x3, starting transfers between devices, shifted(): lax.ppermute(value, axis, [(i, (i + steps) % count) for i in range(count)])  6.2 us
    ppermute x2, starting transfers between devices, swapped(): return lax.ppermute(value, 'rows', pairs + [(j, i) for i, j in pairs])  4.9 us
    ppermute x3, waiting for transfers between devices, to_neighbour(): lax.ppermute(value, 'rows', [(i, i + steps) for i in range(count) if 0 <=...  3.61 us
  transfers between devices with their start and end apart: 14, of which 7 were waited for; matrix products, arithmetic and copies ran while one was open for 0% of the time, Pallas kernels for 22%

profile of v9, /device:TPU:56, one launch (start us, length us, event | category | flops | bytes accessed | tf_op | source)
XLA Modules:
  0.0 72.2 jit_solution(5201635553988321825)
XLA Ops:
  0.0 0.1 collective-permute-start.2
  0.1 3.3 %collective-permute-start.1 = (f32[128,128]{1,0:T(8,128)}, f32[128,128]{1,0:T(8,128)S(1)}, u32[]{:S(2)}, u32[]{:S(2)}) collective-permute-start(f32[128,128]{1,0:T(8,128)} %bitcast.7), channel_id=1, source_target_pairs={{0,8},{1,9},{2,10},{3,11},{4,12},{5,13},{6,14},{7,15},{8,0},{9,1},... | collective-permute-start | bytes 196616 | tf_op jit(solution)/shard_map/ppermute | solution.py:325
  3.4 2.8 %collective-permute-start = (f32[128,128]{1,0:T(8,128)}, f32[128,128]{1,0:T(8,128)S(1)}, u32[]{:S(2)}, u32[]{:S(2)}) collective-permute-start(f32[128,128]{1,0:T(8,128)} %bitcast.8), channel_id=1, source_target_pairs={{0,4},{1,5},{2,6},{3,7},{4,8},{5,9},{6,10},{7,11},{8,12},{9,13},{1... | collective-permute-start | bytes 196616 | tf_op jit(solution)/shard_map/ppermute | solution.py:325
  6.2 0.0 copy-start.1
  6.2 0.9 %copy-done.1 = f32[1,128,128]{2,1,0:T(8,128)S(1)} copy-done((f32[1,128,128]{2,1,0:T(8,128)S(1)}, f32[1,128,128]{2,1,0:T(8,128)}, u32[]{:S(2)}) %copy-start.1) | copy-done | bytes 65560
  7.1 0.0 copy-start.2
  7.1 0.0 copy-start
  7.1 0.0 collective-permute-done.2.p3
  7.1 1.3 %collective-permute-done.1.p2 = f32[128,128]{1,0:T(8,128)S(1)} collective-permute-done((f32[128,128]{1,0:T(8,128)}, f32[128,128]{1,0:T(8,128)S(1)}, u32[]{:S(2)}, u32[]{:S(2)}) %collective-permute-start.1) | collective-permute-done | bytes 65568 | tf_op jit(solution)/shard_map/ppermute | solution.py:325
  8.4 1.2 %collective-permute-done.p1 = f32[128,128]{1,0:T(8,128)S(1)} collective-permute-done((f32[128,128]{1,0:T(8,128)}, f32[128,128]{1,0:T(8,128)S(1)}, u32[]{:S(2)}, u32[]{:S(2)}) %collective-permute-start) | collective-permute-done | bytes 65568 | tf_op jit(solution)/shard_map/ppermute | solution.py:325
  9.6 2.8 %collective-permute-start.5 = (f32[2,128,128]{2,1,0:T(8,128)S(1)}, f32[2,128,128]{2,1,0:T(8,128)S(1)}, u32[]{:S(2)}, u32[]{:S(2)}) collective-permute-start(f32[2,128,128]{2,1,0:T(8,128)S(1)} %get-tuple-element.16.p0), channel_id=1, source_target_pairs={{0,3},{1,0},{2,1},{3,2},{4,7},{5,4},{6,5},{7,6},{8,11},{9,8},{10,9... | collective-permute-start | bytes 393224 | tf_op jit(solution)/shard_map/ppermute | solution.py:340
  12.4 0.8 %collective-permute-start.4 = (f32[2,128,128]{2,1,0:T(8,128)S(1)}, f32[2,128,128]{2,1,0:T(8,128)S(1)}, u32[]{:S(2)}, u32[]{:S(2)}) collective-permute-start(f32[2,128,128]{2,1,0:T(8,128)S(1)} %get-tuple-element.16.p0), channel_id=1, source_target_pairs={{0,2},{1,3},{2,0},{3,1},{4,6},{5,7},{6,4},{7,5},{8,10},{9,11},{10,... | collective-permute-start | bytes 393224 | tf_op jit(solution)/shard_map/ppermute | solution.py:340
  13.2 0.9 %collective-permute-start.3 = (f32[2,128,128]{2,1,0:T(8,128)S(1)}, f32[2,128,128]{2,1,0:T(8,128)S(1)}, u32[]{:S(2)}, u32[]{:S(2)}) collective-permute-start(f32[2,128,128]{2,1,0:T(8,128)S(1)} %get-tuple-element.16.p0), channel_id=1, source_target_pairs={{0,1},{1,2},{2,3},{3,0},{4,5},{5,6},{6,7},{7,4},{8,9},{9,10},{10,1... | collective-permute-start | bytes 393224 | tf_op jit(solution)/shard_map/ppermute | solution.py:340
  14.1 0.0 copy-done.2
  14.1 0.1 copy.5
  14.2 0.1 reshape.6
  14.3 0.1 concatenate.3.scalars
  14.4 3.1 %collective-permute-done.5.p3 = f32[2,128,128]{2,1,0:T(8,128)S(1)} collective-permute-done((f32[2,128,128]{2,1,0:T(8,128)S(1)}, f32[2,128,128]{2,1,0:T(8,128)S(1)}, u32[]{:S(2)}, u32[]{:S(2)}) %collective-permute-start.5) | collective-permute-done | bytes 131104 | tf_op jit(solution)/shard_map/ppermute | solution.py:340
  17.5 2.3 %collective-permute-done.4.p2 = f32[2,128,128]{2,1,0:T(8,128)S(1)} collective-permute-done((f32[2,128,128]{2,1,0:T(8,128)S(1)}, f32[2,128,128]{2,1,0:T(8,128)S(1)}, u32[]{:S(2)}, u32[]{:S(2)}) %collective-permute-start.4) | collective-permute-done | bytes 131104 | tf_op jit(solution)/shard_map/ppermute | solution.py:340
  19.8 1.3 %collective-permute-done.3.p1 = f32[2,128,128]{2,1,0:T(8,128)S(1)} collective-permute-done((f32[2,128,128]{2,1,0:T(8,128)S(1)}, f32[2,128,128]{2,1,0:T(8,128)S(1)}, u32[]{:S(2)}, u32[]{:S(2)}) %collective-permute-start.3) | collective-permute-done | bytes 131104 | tf_op jit(solution)/shard_map/ppermute | solution.py:340
  21.2 0.0 copy-done
  21.2 4.1 %first_kernel.1 = (f32[384,128]{1,0:T(8,128)S(1)}, f32[256,128]{1,0:T(8,128)S(1)}, f32[256,128]{1,0:T(8,128)S(1)}) custom-call(s32[20]{0:T(128)S(1)} %concatenate.3.scalars, f32[512,128]{1,0:T(8,128)S(1)} %copy-done, f32[2,128,128]{2,1,0:T(8,128)S(1)} %get-tuple-element.16.p0, f32[2,128,128]{2,1,0:T(8,128)S(1)} %collective-permute-done.3.p1, ...), custom_call_target="tpu_custom_call" | custom-call | flops 400000000 | bytes 2000000 | tf_op jit(solution)/shard_map/first_kernel/pallas_call | solution.py:311
  25.3 6.9 %collective-permute-start.6 = (f32[384,128]{1,0:T(8,128)S(1)}, f32[384,128]{1,0:T(8,128)S(1)}, u32[]{:S(2)}, u32[]{:S(2)}) collective-permute-start(f32[384,128]{1,0:T(8,128)S(1)} %get-tuple-element.18.own), channel_id=1, source_target_pairs={{16,0},{32,16},{48,32},{64,48},{80,64},{96,80},{112,96},{128,112},... | collective-permute-start | bytes 589832 | tf_op jit(solution)/shard_map/ppermute | solution.py:330
  32.2 0.1 collective-permute-start.10
  32.3 0.5 collective-permute-start.9
  32.8 1.6 %collective-permute-start.8 = (f32[2,128,128]{2,1,0:T(8,128)S(1)}, f32[2,128,128]{2,1,0:T(8,128)S(1)}, u32[]{:S(2)}, u32[]{:S(2)}) collective-permute-start(f32[2,128,128]{2,1,0:T(8,128)S(1)} %get-tuple-element.22.p0), channel_id=1, source_target_pairs={{0,1},{1,2},{2,3},{3,0},{4,5},{5,6},{6,7},{7,4},{8,9},{9,10},{10,1... | collective-permute-start | bytes 393224 | tf_op jit(solution)/shard_map/ppermute | solution.py:340
  34.3 3.2 %factor1_kernel.1.g1 = bf16[4,256,512]{2,1,0:T(8,128)(2,1)S(1)} custom-call(s32[20]{0:T(128)S(1)} %concatenate.3.scalars, f32[256,128]{1,0:T(8,128)S(1)} %get-tuple-element.17.after.low_ref, f32[2,128,128]{2,1,0:T(8,128)S(1)} %get-tuple-element.16.p0, f32[2,128,128]{2,1,0:T(8,128)S(1)} %collective-permute-done.3.p1, ...), custom_call_target="tpu_custom_call" | custom-call | flops 400000000 | bytes 2000000 | tf_op jit(solution)/shard_map/factor1_kernel/pallas_call | solution.py:311
  37.6 0.0 collective-permute-done.6.message
  37.6 1.3 %second_kernel.1 = (f32[256,128]{1,0:T(8,128)S(1)}, f32[256,128]{1,0:T(8,128)S(1)}) custom-call(s32[20]{0:T(128)S(1)} %concatenate.3.scalars, f32[256,128]{1,0:T(8,128)S(1)} %get-tuple-element.17.after.low_ref, f32[384,128]{1,0:T(8,128)S(1)} %collective-permute-done.6.message, bf16[4,256,512]{2,1,0:T(8,128)(2,1)S(1)} %factor1_kernel.1.g1), custom_call_target="tpu_custom_call" | custom-call | flops 400000000 | bytes 2000000 | tf_op jit(solution)/shard_map/second_kernel/pallas_call | solution.py:311
  38.8 2.6 %collective-permute-start.7 = (f32[256,128]{1,0:T(8,128)S(1)}, f32[256,128]{1,0:T(8,128)S(1)}, u32[]{:S(2)}, u32[]{:S(2)}) collective-permute-start(f32[256,128]{1,0:T(8,128)S(1)} %get-tuple-element.21), channel_id=1, source_target_pairs={{0,16},{16,32},{32,48},{48,64},{64,80},{80,96},{96,112},{112,128},... | collective-permute-start | bytes 393224 | tf_op jit(solution)/shard_map/ppermute | solution.py:330
  41.4 0.0 collective-permute-done.10.p3
  41.4 0.0 collective-permute-done.9.p2
  41.4 0.0 collective-permute-done.8.p1
  41.4 0.6 choose_kernel.1.after
  42.0 2.2 %collective-permute-start.13 = (f32[3,128,128]{2,1,0:T(8,128)S(1)}, f32[3,128,128]{2,1,0:T(8,128)S(1)}, u32[]{:S(2)}, u32[]{:S(2)}) collective-permute-start(f32[3,128,128]{2,1,0:T(8,128)S(1)} %choose_kernel.1.after), channel_id=1, source_target_pairs={{0,16},{16,32},{32,48},{48,64},{64,80},{80,96},{96,112},{112,128},... | collective-permute-start | bytes 589832 | tf_op jit(solution)/shard_map/ppermute | solution.py:330
  44.2 3.7 %factor2_kernel.1.g2 = bf16[5,256,512]{2,1,0:T(8,128)(2,1)S(1)} custom-call(s32[20]{0:T(128)S(1)} %concatenate.3.scalars, f32[3,128,128]{2,1,0:T(8,128)S(1)} %choose_kernel.1.after, f32[2,128,128]{2,1,0:T(8,128)S(1)} %get-tuple-element.22.p0, f32[2,128,128]{2,1,0:T(8,128)S(1)} %collective-permute-done.8.p1, f32[2,128,128]{2,1,0:T(8,128)S(1)} %collective-permute-done.9.p2, ...), custom_call_target="tpu_custom_call" | custom-call | flops 400000000 | bytes 2000000 | tf_op jit(solution)/shard_map/factor2_kernel/pallas_call | solution.py:311
  47.9 3.6 %collective-permute-done.7.back = f32[256,128]{1,0:T(8,128)S(1)} collective-permute-done((f32[256,128]{1,0:T(8,128)S(1)}, f32[256,128]{1,0:T(8,128)S(1)}, u32[]{:S(2)}, u32[]{:S(2)}) %collective-permute-start.7) | collective-permute-done | bytes 131104 | tf_op jit(solution)/shard_map/ppermute | solution.py:330
  51.5 1.5 %third_kernel.1 = (f32[256,128]{1,0:T(8,128)S(1)}, f32[256,128]{1,0:T(8,128)S(1)}, f32[384,128]{1,0:T(8,128)S(1)}, f32[384,128]{1,0:T(8,128)S(1)}) custom-call(s32[20]{0:T(128)S(1)} %concatenate.3.scalars, f32[256,128]{1,0:T(8,128)S(1)} %get-tuple-element.19.after.low_ref, f32[384,128]{1,0:T(8,128)S(1)} %get-tuple-element.18.own, ...), custom_call_target="tpu_custom_call" | custom-call | flops 400000000 | bytes 2000000 | tf_op jit(solution)/shard_map/third_kernel/pallas_call | solution.py:311
  53.0 4.8 %collective-permute-start.11 = (f32[384,128]{1,0:T(8,128)S(1)}, f32[384,128]{1,0:T(8,128)S(1)}, u32[]{:S(2)}, u32[]{:S(2)}) collective-permute-start(f32[384,128]{1,0:T(8,128)S(1)} %get-tuple-element.25), channel_id=1, source_target_pairs={{16,32},{48,64},{80,96},{112,128},{144,160},{176,192},{208,224},{3... | collective-permute-start | bytes 589832 | tf_op jit(solution)/shard_map/ppermute | solution.py:336
  57.8 0.1 collective-permute-start.12
  57.9 2.9 %factor3_kernel.1.g3 = bf16[3,256,512]{2,1,0:T(8,128)(2,1)S(1)} custom-call(s32[20]{0:T(128)S(1)} %concatenate.3.scalars, f32[256,128]{1,0:T(8,128)S(1)} %get-tuple-element.23.after.low_ref, f32[2,128,128]{2,1,0:T(8,128)S(1)} %get-tuple-element.22.p0, f32[2,128,128]{2,1,0:T(8,128)S(1)} %collective-permute-done.8.p1, ...), custom_call_target="tpu_custom_call" | custom-call | flops 400000000 | bytes 2000000 | tf_op jit(solution)/shard_map/factor3_kernel/pallas_call | solution.py:311
  60.8 0.0 collective-permute-done.13.down
  60.9 2.4 %factor4_kernel.1.g4 = bf16[3,256,512]{2,1,0:T(8,128)(2,1)S(1)} custom-call(f32[256,128]{1,0:T(8,128)S(1)} %get-tuple-element.23.after.low_ref, f32[3,128,128]{2,1,0:T(8,128)S(1)} %collective-permute-done.13.down), custom_call_target="tpu_custom_call" | custom-call | flops 400000000 | bytes 2000000 | tf_op jit(solution)/shard_map/factor4_kernel/pallas_call | solution.py:311
  63.2 6.6 %collective-permute-done.11.far = f32[384,128]{1,0:T(8,128)S(1)} collective-permute-done((f32[384,128]{1,0:T(8,128)S(1)}, f32[384,128]{1,0:T(8,128)S(1)}, u32[]{:S(2)}, u32[]{:S(2)}) %collective-permute-start.11) | collective-permute-done | bytes 196640 | tf_op jit(solution)/shard_map/ppermute | solution.py:336
  69.8 0.0 collective-permute-done.12.near
  69.8 2.3 %fourth_kernel.1 = f32[512,128]{1,0:T(8,128)} custom-call(s32[20]{0:T(128)S(1)} %concatenate.3.scalars, f32[256,128]{1,0:T(8,128)S(1)} %get-tuple-element.23.after.low_ref, f32[256,128]{1,0:T(8,128)S(1)} %get-tuple-element.24.top_ref, f32[384,128]{1,0:T(8,128)S(1)} %collective-permute-done.11.far, f32[384,128]{1,0:T(8,128)S(1)} %collective-permute-done.12.near, ...), custom_call_target="tpu_custom_call" | custom-call | flops 400000000 | bytes 2000000 | tf_op jit(solution)/shard_map/fourth_kernel/pallas_call | solution.py:311
  (2 shorter events, 0.0 us)
Async XLA Ops:
  0.0 7.1 %collective-permute-start.2 = (f32[128,128]{1,0:T(8,128)}, f32[128,128]{1,0:T(8,128)S(1)}, u32[]{:S(2)}, u32[]{:S(2)}) collective-permute-start(f32[128,128]{1,0:T(8,128)} %bitcast.6), channel_id=1, source_target_pairs={{0,12},{1,13},{2,14},{3,15},{4,0},{5,1},{6,2},{7,3},{8,4},{9,5},{1... | collective-permute-start | bytes 196616 | tf_op jit(solution)/shard_map/ppermute | solution.py:325
  0.1 8.3 %collective-permute-start.1 = (f32[128,128]{1,0:T(8,128)}, f32[128,128]{1,0:T(8,128)S(1)}, u32[]{:S(2)}, u32[]{:S(2)}) collective-permute-start(f32[128,128]{1,0:T(8,128)} %bitcast.7), channel_id=1, source_target_pairs={{0,8},{1,9},{2,10},{3,11},{4,12},{5,13},{6,14},{7,15},{8,0},{9,1},... | collective-permute-start | bytes 196616 | tf_op jit(solution)/shard_map/ppermute | solution.py:325
  3.4 6.2 %collective-permute-start = (f32[128,128]{1,0:T(8,128)}, f32[128,128]{1,0:T(8,128)S(1)}, u32[]{:S(2)}, u32[]{:S(2)}) collective-permute-start(f32[128,128]{1,0:T(8,128)} %bitcast.8), channel_id=1, source_target_pairs={{0,4},{1,5},{2,6},{3,7},{4,8},{5,9},{6,10},{7,11},{8,12},{9,13},{1... | collective-permute-start | bytes 196616 | tf_op jit(solution)/shard_map/ppermute | solution.py:325
  6.2 0.9 %copy-start.1 = (f32[1,128,128]{2,1,0:T(8,128)S(1)}, f32[1,128,128]{2,1,0:T(8,128)}, u32[]{:S(2)}) copy-start(f32[1,128,128]{2,1,0:T(8,128)} %param.4) | copy-start | bytes 196612
  7.1 7.1 %copy-start.2 = (s32[1,8,2]{1,2,0:T(2,128)S(1)}, s32[1,8,2]{1,2,0:T(2,128)}, u32[]{:S(2)}) copy-start(s32[1,8,2]{1,2,0:T(2,128)} %param.5) | copy-start | bytes 196
  7.1 14.1 %copy-start = (f32[512,128]{1,0:T(8,128)S(1)}, f32[512,128]{1,0:T(8,128)}, u32[]{:S(2)}) copy-start(f32[512,128]{1,0:T(8,128)} %x_ref.1) | copy-start | bytes 786436
  9.6 7.9 %collective-permute-start.5 = (f32[2,128,128]{2,1,0:T(8,128)S(1)}, f32[2,128,128]{2,1,0:T(8,128)S(1)}, u32[]{:S(2)}, u32[]{:S(2)}) collective-permute-start(f32[2,128,128]{2,1,0:T(8,128)S(1)} %get-tuple-element.16.p0), channel_id=1, source_target_pairs={{0,3},{1,0},{2,1},{3,2},{4,7},{5,4},{6,5},{7,6},{8,11},{9,8},{10,9... | collective-permute-start | bytes 393224 | tf_op jit(solution)/shard_map/ppermute | solution.py:340
  12.4 7.4 %collective-permute-start.4 = (f32[2,128,128]{2,1,0:T(8,128)S(1)}, f32[2,128,128]{2,1,0:T(8,128)S(1)}, u32[]{:S(2)}, u32[]{:S(2)}) collective-permute-start(f32[2,128,128]{2,1,0:T(8,128)S(1)} %get-tuple-element.16.p0), channel_id=1, source_target_pairs={{0,2},{1,3},{2,0},{3,1},{4,6},{5,7},{6,4},{7,5},{8,10},{9,11},{10,... | collective-permute-start | bytes 393224 | tf_op jit(solution)/shard_map/ppermute | solution.py:340
  13.2 7.9 %collective-permute-start.3 = (f32[2,128,128]{2,1,0:T(8,128)S(1)}, f32[2,128,128]{2,1,0:T(8,128)S(1)}, u32[]{:S(2)}, u32[]{:S(2)}) collective-permute-start(f32[2,128,128]{2,1,0:T(8,128)S(1)} %get-tuple-element.16.p0), channel_id=1, source_target_pairs={{0,1},{1,2},{2,3},{3,0},{4,5},{5,6},{6,7},{7,4},{8,9},{9,10},{10,1... | collective-permute-start | bytes 393224 | tf_op jit(solution)/shard_map/ppermute | solution.py:340
  25.3 12.2 %collective-permute-start.6 = (f32[384,128]{1,0:T(8,128)S(1)}, f32[384,128]{1,0:T(8,128)S(1)}, u32[]{:S(2)}, u32[]{:S(2)}) collective-permute-start(f32[384,128]{1,0:T(8,128)S(1)} %get-tuple-element.18.own), channel_id=1, source_target_pairs={{16,0},{32,16},{48,32},{64,48},{80,64},{96,80},{112,96},{128,112},... | collective-permute-start | bytes 589832 | tf_op jit(solution)/shard_map/ppermute | solution.py:330
  32.2 9.2 %collective-permute-start.10 = (f32[2,128,128]{2,1,0:T(8,128)S(1)}, f32[2,128,128]{2,1,0:T(8,128)S(1)}, u32[]{:S(2)}, u32[]{:S(2)}) collective-permute-start(f32[2,128,128]{2,1,0:T(8,128)S(1)} %get-tuple-element.22.p0), channel_id=1, source_target_pairs={{0,3},{1,0},{2,1},{3,2},{4,7},{5,4},{6,5},{7,6},{8,11},{9,8},{10,9... | collective-permute-start | bytes 393224 | tf_op jit(solution)/shard_map/ppermute | solution.py:340
  32.3 9.1 %collective-permute-start.9 = (f32[2,128,128]{2,1,0:T(8,128)S(1)}, f32[2,128,128]{2,1,0:T(8,128)S(1)}, u32[]{:S(2)}, u32[]{:S(2)}) collective-permute-start(f32[2,128,128]{2,1,0:T(8,128)S(1)} %get-tuple-element.22.p0), channel_id=1, source_target_pairs={{0,2},{1,3},{2,0},{3,1},{4,6},{5,7},{6,4},{7,5},{8,10},{9,11},{10,... | collective-permute-start | bytes 393224 | tf_op jit(solution)/shard_map/ppermute | solution.py:340
  32.8 8.6 %collective-permute-start.8 = (f32[2,128,128]{2,1,0:T(8,128)S(1)}, f32[2,128,128]{2,1,0:T(8,128)S(1)}, u32[]{:S(2)}, u32[]{:S(2)}) collective-permute-start(f32[2,128,128]{2,1,0:T(8,128)S(1)} %get-tuple-element.22.p0), channel_id=1, source_target_pairs={{0,1},{1,2},{2,3},{3,0},{4,5},{5,6},{6,7},{7,4},{8,9},{9,10},{10,1... | collective-permute-start | bytes 393224 | tf_op jit(solution)/shard_map/ppermute | solution.py:340
  38.8 12.6 %collective-permute-start.7 = (f32[256,128]{1,0:T(8,128)S(1)}, f32[256,128]{1,0:T(8,128)S(1)}, u32[]{:S(2)}, u32[]{:S(2)}) collective-permute-start(f32[256,128]{1,0:T(8,128)S(1)} %get-tuple-element.21), channel_id=1, source_target_pairs={{0,16},{16,32},{32,48},{48,64},{64,80},{80,96},{96,112},{112,128},... | collective-permute-start | bytes 393224 | tf_op jit(solution)/shard_map/ppermute | solution.py:330
  42.0 18.8 %collective-permute-start.13 = (f32[3,128,128]{2,1,0:T(8,128)S(1)}, f32[3,128,128]{2,1,0:T(8,128)S(1)}, u32[]{:S(2)}, u32[]{:S(2)}) collective-permute-start(f32[3,128,128]{2,1,0:T(8,128)S(1)} %choose_kernel.1.after), channel_id=1, source_target_pairs={{0,16},{16,32},{32,48},{48,64},{64,80},{80,96},{96,112},{112,128},... | collective-permute-start | bytes 589832 | tf_op jit(solution)/shard_map/ppermute | solution.py:330
  53.0 16.8 %collective-permute-start.11 = (f32[384,128]{1,0:T(8,128)S(1)}, f32[384,128]{1,0:T(8,128)S(1)}, u32[]{:S(2)}, u32[]{:S(2)}) collective-permute-start(f32[384,128]{1,0:T(8,128)S(1)} %get-tuple-element.25), channel_id=1, source_target_pairs={{16,32},{48,64},{80,96},{112,128},{144,160},{176,192},{208,224},{3... | collective-permute-start | bytes 589832 | tf_op jit(solution)/shard_map/ppermute | solution.py:336
  57.8 12.0 %collective-permute-start.12 = (f32[384,128]{1,0:T(8,128)S(1)}, f32[384,128]{1,0:T(8,128)S(1)}, u32[]{:S(2)}, u32[]{:S(2)}) collective-permute-start(f32[384,128]{1,0:T(8,128)S(1)} %get-tuple-element.26), channel_id=1, source_target_pairs={{0,16},{32,48},{64,80},{96,112},{128,144},{160,176},{192,208},{224... | collective-permute-start | bytes 589832 | tf_op jit(solution)/shard_map/ppermute | solution.py:336

commit v10 on v9

--- a/solution.py
+++ b/solution.py
@@ -360,11 +360,11 @@
     three = rows_shape(3 * W, W)
     own, low, rest = call(first_kernel, (scalars, eigvecs, *near), [three, half, half], HELD)
     message = to_neighbour(own, -1)
-    (g1,) = call(factor1_kernel, (scalars, low, *near), [wholes(4)], HELD)
+    (down,) = call(choose_kernel, (scalars, low, *far), [rows_shape(3, W, W)], HELD)
+    (g1,) = call(factor1_kernel, (scalars, down, *near), [wholes(4)], HELD)
     low, back = call(second_kernel, (scalars, low, message, g1), [half, half])
     back = to_neighbour(back, 1)
-    (down,) = call(choose_kernel, (scalars, low, *far), [rows_shape(3, W, W)], HELD)
-    (g2,) = call(factor2_kernel, (scalars, down, *far), [wholes(5)], HELD)
+    (g2,) = call(factor2_kernel, (scalars, low, *far), [wholes(5)], HELD)
     down = to_neighbour(down, 1)
     low, top, far_out, near_out = call(
         third_kernel, (scalars, low, own, rest, back, g1, g2), [half, half, three, three]

time: 73.1 us -> 72 us (0.985)
  the two profiles are of different devices: /device:TPU:56 before, /device:TPU:33 now
where the time goes in v10:
time: 72 us; the launch traced here: 71.8 us
  starting transfers between devices  27.1 us (38%)
  Pallas kernels  22.1 us (31%)
  waiting for transfers between devices  21.2 us (29%)
  local copies, waits for them, and re-layouts  1.13 us (2%)
    pallas_call x11, Pallas kernels, call(): pl.pallas_call(kernel, out_shape=tuple(shapes), in_specs=[pl.BlockSpec(me...  22.1 us
    ppermute x3, starting transfers between devices, to_neighbour(): lax.ppermute(value, 'rows', [(i, i + steps) for i in range(count) if 0 <=...  12.3 us
    ppermute x2, waiting for transfers between devices, swapped(): return lax.ppermute(value, 'rows', pairs + [(j, i) for i, j in pairs])  7.27 us
    ppermute x6, starting transfers between devices, along_x(): lax.ppermute(value, 'cols', [(i, i // 4 * 4 + (i + k) % 4) for i in range...  7 us
    ppermute x3, waiting for transfers between devices, to_neighbour(): lax.ppermute(value, 'rows', [(i, i + steps) for i in range(count) if 0 <=...  5.86 us
    ppermute x3, starting transfers between devices, shifted(): lax.ppermute(value, axis, [(i, (i + steps) % count) for i in range(count)])  5.36 us
    ppermute x6, waiting for transfers between devices, along_x(): lax.ppermute(value, 'cols', [(i, i // 4 * 4 + (i + k) % 4) for i in range...  5.35 us
    ppermute x3, waiting for transfers between devices, shifted(): lax.ppermute(value, axis, [(i, (i + steps) % count) for i in range(count)])  2.76 us
  transfers between devices with their start and end apart: 14, of which 5 were waited for; matrix products, arithmetic and copies ran while one was open for 0% of the time, Pallas kernels for 26%

profile of v10, /device:TPU:33, one launch (start us, length us, event | category | flops | bytes accessed | tf_op | source)
XLA Modules:
  0.0 71.8 jit_solution(9138640818258073235)
XLA Ops:
  0.0 0.0 collective-permute-start.2
  0.0 3.0 %collective-permute-start.1 = (f32[128,128]{1,0:T(8,128)}, f32[128,128]{1,0:T(8,128)S(1)}, u32[]{:S(2)}, u32[]{:S(2)}) collective-permute-start(f32[128,128]{1,0:T(8,128)} %bitcast.7), channel_id=1, source_target_pairs={{0,8},{1,9},{2,10},{3,11},{4,12},{5,13},{6,14},{7,15},{8,0},{9,1},... | collective-permute-start | bytes 196616 | tf_op jit(solution)/shard_map/ppermute | solution.py:325
  3.0 2.4 %collective-permute-start = (f32[128,128]{1,0:T(8,128)}, f32[128,128]{1,0:T(8,128)S(1)}, u32[]{:S(2)}, u32[]{:S(2)}) collective-permute-start(f32[128,128]{1,0:T(8,128)} %bitcast.8), channel_id=1, source_target_pairs={{0,4},{1,5},{2,6},{3,7},{4,8},{5,9},{6,10},{7,11},{8,12},{9,13},{1... | collective-permute-start | bytes 196616 | tf_op jit(solution)/shard_map/ppermute | solution.py:325
  5.4 0.0 copy-start.1
  5.4 0.9 %copy-done.1 = f32[1,128,128]{2,1,0:T(8,128)S(1)} copy-done((f32[1,128,128]{2,1,0:T(8,128)S(1)}, f32[1,128,128]{2,1,0:T(8,128)}, u32[]{:S(2)}) %copy-start.1) | copy-done | bytes 65560
  6.2 0.0 copy-start.2
  6.2 0.0 copy-start
  6.2 0.0 collective-permute-done.2.p3
  6.3 0.0 collective-permute-done.1.p2
  6.3 2.8 %collective-permute-done.p1 = f32[128,128]{1,0:T(8,128)S(1)} collective-permute-done((f32[128,128]{1,0:T(8,128)}, f32[128,128]{1,0:T(8,128)S(1)}, u32[]{:S(2)}, u32[]{:S(2)}) %collective-permute-start) | collective-permute-done | bytes 65568 | tf_op jit(solution)/shard_map/ppermute | solution.py:325
  9.1 2.6 %collective-permute-start.5 = (f32[2,128,128]{2,1,0:T(8,128)S(1)}, f32[2,128,128]{2,1,0:T(8,128)S(1)}, u32[]{:S(2)}, u32[]{:S(2)}) collective-permute-start(f32[2,128,128]{2,1,0:T(8,128)S(1)} %get-tuple-element.16.p0), channel_id=1, source_target_pairs={{0,3},{1,0},{2,1},{3,2},{4,7},{5,4},{6,5},{7,6},{8,11},{9,8},{10,9... | collective-permute-start | bytes 393224 | tf_op jit(solution)/shard_map/ppermute | solution.py:340
  11.6 0.5 collective-permute-start.4
  12.1 0.6 collective-permute-start.3
  12.8 0.0 copy-done.2
  12.8 0.1 copy.5
  12.8 0.1 reshape.6
  12.9 0.1 concatenate.3.scalars
  13.0 2.1 %collective-permute-start.9 = (f32[2,128,128]{2,1,0:T(8,128)S(1)}, f32[2,128,128]{2,1,0:T(8,128)S(1)}, u32[]{:S(2)}, u32[]{:S(2)}) collective-permute-start(f32[2,128,128]{2,1,0:T(8,128)S(1)} %get-tuple-element.19.p0), channel_id=1, source_target_pairs={{0,3},{1,0},{2,1},{3,2},{4,7},{5,4},{6,5},{7,6},{8,11},{9,8},{10,9... | collective-permute-start | bytes 393224 | tf_op jit(solution)/shard_map/ppermute | solution.py:340
  15.1 1.2 %collective-permute-start.8 = (f32[2,128,128]{2,1,0:T(8,128)S(1)}, f32[2,128,128]{2,1,0:T(8,128)S(1)}, u32[]{:S(2)}, u32[]{:S(2)}) collective-permute-start(f32[2,128,128]{2,1,0:T(8,128)S(1)} %get-tuple-element.19.p0), channel_id=1, source_target_pairs={{0,2},{1,3},{2,0},{3,1},{4,6},{5,7},{6,4},{7,5},{8,10},{9,11},{10,... | collective-permute-start | bytes 393224 | tf_op jit(solution)/shard_map/ppermute | solution.py:340
  16.3 0.0 collective-permute-done.5.p3
  16.3 0.0 collective-permute-start.7
  16.3 0.7 %collective-permute-done.4.p2 = f32[2,128,128]{2,1,0:T(8,128)S(1)} collective-permute-done((f32[2,128,128]{2,1,0:T(8,128)S(1)}, f32[2,128,128]{2,1,0:T(8,128)S(1)}, u32[]{:S(2)}, u32[]{:S(2)}) %collective-permute-start.4) | collective-permute-done | bytes 131104 | tf_op jit(solution)/shard_map/ppermute | solution.py:340
  17.1 4.6 %collective-permute-done.3.p1 = f32[2,128,128]{2,1,0:T(8,128)S(1)} collective-permute-done((f32[2,128,128]{2,1,0:T(8,128)S(1)}, f32[2,128,128]{2,1,0:T(8,128)S(1)}, u32[]{:S(2)}, u32[]{:S(2)}) %collective-permute-start.3) | collective-permute-done | bytes 131104 | tf_op jit(solution)/shard_map/ppermute | solution.py:340
  21.7 0.0 copy-done
  21.7 4.1 %first_kernel.1 = (f32[384,128]{1,0:T(8,128)S(1)}, f32[256,128]{1,0:T(8,128)S(1)}, f32[256,128]{1,0:T(8,128)S(1)}) custom-call(s32[20]{0:T(128)S(1)} %concatenate.3.scalars, f32[512,128]{1,0:T(8,128)S(1)} %copy-done, f32[2,128,128]{2,1,0:T(8,128)S(1)} %get-tuple-element.16.p0, f32[2,128,128]{2,1,0:T(8,128)S(1)} %collective-permute-done.3.p1, ...), custom_call_target="tpu_custom_call" | custom-call | flops 400000000 | bytes 2000000 | tf_op jit(solution)/shard_map/first_kernel/pallas_call | solution.py:311
  25.8 4.7 %collective-permute-start.6 = (f32[384,128]{1,0:T(8,128)S(1)}, f32[384,128]{1,0:T(8,128)S(1)}, u32[]{:S(2)}, u32[]{:S(2)}) collective-permute-start(f32[384,128]{1,0:T(8,128)S(1)} %get-tuple-element.18.own), channel_id=1, source_target_pairs={{16,0},{32,16},{48,32},{64,48},{80,64},{96,80},{112,96},{128,112},... | collective-permute-start | bytes 589832 | tf_op jit(solution)/shard_map/ppermute | solution.py:330
  30.5 0.0 collective-permute-done.9.p3
  30.5 0.0 collective-permute-done.8.p2
  30.5 0.0 collective-permute-done.7.p1
  30.5 0.6 choose_kernel.1.after
  31.1 3.2 %factor1_kernel.1.g1 = bf16[4,256,512]{2,1,0:T(8,128)(2,1)S(1)} custom-call(s32[20]{0:T(128)S(1)} %concatenate.3.scalars, f32[3,128,128]{2,1,0:T(8,128)S(1)} %choose_kernel.1.after, f32[2,128,128]{2,1,0:T(8,128)S(1)} %get-tuple-element.16.p0, f32[2,128,128]{2,1,0:T(8,128)S(1)} %collective-permute-done.3.p1, f32[2,128,128]{2,1,0:T(8,128)S(1)} %collective-permute-done.4.p2, ...), custom_call_target="tpu_custom_call" | custom-call | flops 400000000 | bytes 2000000 | tf_op jit(solution)/shard_map/factor1_kernel/pallas_call | solution.py:311
  34.4 5.9 %collective-permute-done.6.message = f32[384,128]{1,0:T(8,128)S(1)} collective-permute-done((f32[384,128]{1,0:T(8,128)S(1)}, f32[384,128]{1,0:T(8,128)S(1)}, u32[]{:S(2)}, u32[]{:S(2)}) %collective-permute-start.6) | collective-permute-done | bytes 196640 | tf_op jit(solution)/shard_map/ppermute | solution.py:330
  40.2 1.3 %second_kernel.1 = (f32[256,128]{1,0:T(8,128)S(1)}, f32[256,128]{1,0:T(8,128)S(1)}) custom-call(s32[20]{0:T(128)S(1)} %concatenate.3.scalars, f32[256,128]{1,0:T(8,128)S(1)} %get-tuple-element.17.after.low_ref, f32[384,128]{1,0:T(8,128)S(1)} %collective-permute-done.6.message, bf16[4,256,512]{2,1,0:T(8,128)(2,1)S(1)} %factor1_kernel.1.g1), custom_call_target="tpu_custom_call" | custom-call | flops 400000000 | bytes 2000000 | tf_op jit(solution)/shard_map/second_kernel/pallas_call | solution.py:311
  41.5 1.9 %collective-permute-start.10 = (f32[256,128]{1,0:T(8,128)S(1)}, f32[256,128]{1,0:T(8,128)S(1)}, u32[]{:S(2)}, u32[]{:S(2)}) collective-permute-start(f32[256,128]{1,0:T(8,128)S(1)} %get-tuple-element.22), channel_id=1, source_target_pairs={{0,16},{16,32},{32,48},{48,64},{64,80},{80,96},{96,112},{112,128},... | collective-permute-start | bytes 393224 | tf_op jit(solution)/shard_map/ppermute | solution.py:330
  43.4 5.7 %collective-permute-start.13 = (f32[3,128,128]{2,1,0:T(8,128)S(1)}, f32[3,128,128]{2,1,0:T(8,128)S(1)}, u32[]{:S(2)}, u32[]{:S(2)}) collective-permute-start(f32[3,128,128]{2,1,0:T(8,128)S(1)} %choose_kernel.1.after), channel_id=1, source_target_pairs={{0,16},{16,32},{32,48},{48,64},{64,80},{80,96},{96,112},{112,128},... | collective-permute-start | bytes 589832 | tf_op jit(solution)/shard_map/ppermute | solution.py:330
  49.1 3.7 %factor2_kernel.1.g2 = bf16[5,256,512]{2,1,0:T(8,128)(2,1)S(1)} custom-call(s32[20]{0:T(128)S(1)} %concatenate.3.scalars, f32[256,128]{1,0:T(8,128)S(1)} %get-tuple-element.20.after.low_ref, f32[2,128,128]{2,1,0:T(8,128)S(1)} %get-tuple-element.19.p0, f32[2,128,128]{2,1,0:T(8,128)S(1)} %collective-permute-done.7.p1, ...), custom_call_target="tpu_custom_call" | custom-call | flops 400000000 | bytes 2000000 | tf_op jit(solution)/shard_map/factor2_kernel/pallas_call | solution.py:311
  52.8 0.0 collective-permute-done.10.back
  52.8 1.5 %third_kernel.1 = (f32[256,128]{1,0:T(8,128)S(1)}, f32[256,128]{1,0:T(8,128)S(1)}, f32[384,128]{1,0:T(8,128)S(1)}, f32[384,128]{1,0:T(8,128)S(1)}) custom-call(s32[20]{0:T(128)S(1)} %concatenate.3.scalars, f32[256,128]{1,0:T(8,128)S(1)} %get-tuple-element.20.after.low_ref, f32[384,128]{1,0:T(8,128)S(1)} %get-tuple-element.18.own, ...), custom_call_target="tpu_custom_call" | custom-call | flops 400000000 | bytes 2000000 | tf_op jit(solution)/shard_map/third_kernel/pallas_call | solution.py:311
  54.3 2.4 %collective-permute-start.11 = (f32[384,128]{1,0:T(8,128)S(1)}, f32[384,128]{1,0:T(8,128)S(1)}, u32[]{:S(2)}, u32[]{:S(2)}) collective-permute-start(f32[384,128]{1,0:T(8,128)S(1)} %get-tuple-element.25), channel_id=1, source_target_pairs={{16,32},{48,64},{80,96},{112,128},{144,160},{176,192},{208,224},{3... | collective-permute-start | bytes 589832 | tf_op jit(solution)/shard_map/ppermute | solution.py:336
  56.7 0.1 collective-permute-start.12
  56.8 2.9 %factor3_kernel.1.g3 = bf16[3,256,512]{2,1,0:T(8,128)(2,1)S(1)} custom-call(s32[20]{0:T(128)S(1)} %concatenate.3.scalars, f32[256,128]{1,0:T(8,128)S(1)} %get-tuple-element.23.after.low_ref, f32[2,128,128]{2,1,0:T(8,128)S(1)} %get-tuple-element.19.p0, f32[2,128,128]{2,1,0:T(8,128)S(1)} %collective-permute-done.7.p1, ...), custom_call_target="tpu_custom_call" | custom-call | flops 400000000 | bytes 2000000 | tf_op jit(solution)/shard_map/factor3_kernel/pallas_call | solution.py:311
  59.8 0.0 collective-permute-done.13.down
  59.8 2.4 %factor4_kernel.1.g4 = bf16[3,256,512]{2,1,0:T(8,128)(2,1)S(1)} custom-call(f32[256,128]{1,0:T(8,128)S(1)} %get-tuple-element.23.after.low_ref, f32[3,128,128]{2,1,0:T(8,128)S(1)} %collective-permute-done.13.down), custom_call_target="tpu_custom_call" | custom-call | flops 400000000 | bytes 2000000 | tf_op jit(solution)/shard_map/factor4_kernel/pallas_call | solution.py:311
  62.2 7.3 %collective-permute-done.11.far = f32[384,128]{1,0:T(8,128)S(1)} collective-permute-done((f32[384,128]{1,0:T(8,128)S(1)}, f32[384,128]{1,0:T(8,128)S(1)}, u32[]{:S(2)}, u32[]{:S(2)}) %collective-permute-start.11) | collective-permute-done | bytes 196640 | tf_op jit(solution)/shard_map/ppermute | solution.py:336
  69.4 0.0 collective-permute-done.12.near
  69.4 2.3 %fourth_kernel.1 = f32[512,128]{1,0:T(8,128)} custom-call(s32[20]{0:T(128)S(1)} %concatenate.3.scalars, f32[256,128]{1,0:T(8,128)S(1)} %get-tuple-element.23.after.low_ref, f32[256,128]{1,0:T(8,128)S(1)} %get-tuple-element.24.top_ref, f32[384,128]{1,0:T(8,128)S(1)} %collective-permute-done.11.far, f32[384,128]{1,0:T(8,128)S(1)} %collective-permute-done.12.near, ...), custom_call_target="tpu_custom_call" | custom-call | flops 400000000 | bytes 2000000 | tf_op jit(solution)/shard_map/fourth_kernel/pallas_call | solution.py:311
  (2 shorter events, 0.0 us)
Async XLA Ops:
  0.0 6.2 %collective-permute-start.2 = (f32[128,128]{1,0:T(8,128)}, f32[128,128]{1,0:T(8,128)S(1)}, u32[]{:S(2)}, u32[]{:S(2)}) collective-permute-start(f32[128,128]{1,0:T(8,128)} %bitcast.6), channel_id=1, source_target_pairs={{0,12},{1,13},{2,14},{3,15},{4,0},{5,1},{6,2},{7,3},{8,4},{9,5},{1... | collective-permute-start | bytes 196616 | tf_op jit(solution)/shard_map/ppermute | solution.py:325
  0.0 6.3 %collective-permute-start.1 = (f32[128,128]{1,0:T(8,128)}, f32[128,128]{1,0:T(8,128)S(1)}, u32[]{:S(2)}, u32[]{:S(2)}) collective-permute-start(f32[128,128]{1,0:T(8,128)} %bitcast.7), channel_id=1, source_target_pairs={{0,8},{1,9},{2,10},{3,11},{4,12},{5,13},{6,14},{7,15},{8,0},{9,1},... | collective-permute-start | bytes 196616 | tf_op jit(solution)/shard_map/ppermute | solution.py:325
  3.0 6.0 %collective-permute-start = (f32[128,128]{1,0:T(8,128)}, f32[128,128]{1,0:T(8,128)S(1)}, u32[]{:S(2)}, u32[]{:S(2)}) collective-permute-start(f32[128,128]{1,0:T(8,128)} %bitcast.8), channel_id=1, source_target_pairs={{0,4},{1,5},{2,6},{3,7},{4,8},{5,9},{6,10},{7,11},{8,12},{9,13},{1... | collective-permute-start | bytes 196616 | tf_op jit(solution)/shard_map/ppermute | solution.py:325
  5.4 0.9 %copy-start.1 = (f32[1,128,128]{2,1,0:T(8,128)S(1)}, f32[1,128,128]{2,1,0:T(8,128)}, u32[]{:S(2)}) copy-start(f32[1,128,128]{2,1,0:T(8,128)} %param.4) | copy-start | bytes 196612
  6.2 6.5 %copy-start.2 = (s32[1,8,2]{1,2,0:T(2,128)S(1)}, s32[1,8,2]{1,2,0:T(2,128)}, u32[]{:S(2)}) copy-start(s32[1,8,2]{1,2,0:T(2,128)} %param.5) | copy-start | bytes 196
  6.2 15.4 %copy-start = (f32[512,128]{1,0:T(8,128)S(1)}, f32[512,128]{1,0:T(8,128)}, u32[]{:S(2)}) copy-start(f32[512,128]{1,0:T(8,128)} %x_ref.1) | copy-start | bytes 786436
  9.1 7.3 %collective-permute-start.5 = (f32[2,128,128]{2,1,0:T(8,128)S(1)}, f32[2,128,128]{2,1,0:T(8,128)S(1)}, u32[]{:S(2)}, u32[]{:S(2)}) collective-permute-start(f32[2,128,128]{2,1,0:T(8,128)S(1)} %get-tuple-element.16.p0), channel_id=1, source_target_pairs={{0,3},{1,0},{2,1},{3,2},{4,7},{5,4},{6,5},{7,6},{8,11},{9,8},{10,9... | collective-permute-start | bytes 393224 | tf_op jit(solution)/shard_map/ppermute | solution.py:340
  11.6 5.4 %collective-permute-start.4 = (f32[2,128,128]{2,1,0:T(8,128)S(1)}, f32[2,128,128]{2,1,0:T(8,128)S(1)}, u32[]{:S(2)}, u32[]{:S(2)}) collective-permute-start(f32[2,128,128]{2,1,0:T(8,128)S(1)} %get-tuple-element.16.p0), channel_id=1, source_target_pairs={{0,2},{1,3},{2,0},{3,1},{4,6},{5,7},{6,4},{7,5},{8,10},{9,11},{10,... | collective-permute-start | bytes 393224 | tf_op jit(solution)/shard_map/ppermute | solution.py:340
  12.1 9.5 %collective-permute-start.3 = (f32[2,128,128]{2,1,0:T(8,128)S(1)}, f32[2,128,128]{2,1,0:T(8,128)S(1)}, u32[]{:S(2)}, u32[]{:S(2)}) collective-permute-start(f32[2,128,128]{2,1,0:T(8,128)S(1)} %get-tuple-element.16.p0), channel_id=1, source_target_pairs={{0,1},{1,2},{2,3},{3,0},{4,5},{5,6},{6,7},{7,4},{8,9},{9,10},{10,1... | collective-permute-start | bytes 393224 | tf_op jit(solution)/shard_map/ppermute | solution.py:340
  13.0 17.5 %collective-permute-start.9 = (f32[2,128,128]{2,1,0:T(8,128)S(1)}, f32[2,128,128]{2,1,0:T(8,128)S(1)}, u32[]{:S(2)}, u32[]{:S(2)}) collective-permute-start(f32[2,128,128]{2,1,0:T(8,128)S(1)} %get-tuple-element.19.p0), channel_id=1, source_target_pairs={{0,3},{1,0},{2,1},{3,2},{4,7},{5,4},{6,5},{7,6},{8,11},{9,8},{10,9... | collective-permute-start | bytes 393224 | tf_op jit(solution)/shard_map/ppermute | solution.py:340
  15.1 15.4 %collective-permute-start.8 = (f32[2,128,128]{2,1,0:T(8,128)S(1)}, f32[2,128,128]{2,1,0:T(8,128)S(1)}, u32[]{:S(2)}, u32[]{:S(2)}) collective-permute-start(f32[2,128,128]{2,1,0:T(8,128)S(1)} %get-tuple-element.19.p0), channel_id=1, source_target_pairs={{0,2},{1,3},{2,0},{3,1},{4,6},{5,7},{6,4},{7,5},{8,10},{9,11},{10,... | collective-permute-start | bytes 393224 | tf_op jit(solution)/shard_map/ppermute | solution.py:340
  16.3 14.2 %collective-permute-start.7 = (f32[2,128,128]{2,1,0:T(8,128)S(1)}, f32[2,128,128]{2,1,0:T(8,128)S(1)}, u32[]{:S(2)}, u32[]{:S(2)}) collective-permute-start(f32[2,128,128]{2,1,0:T(8,128)S(1)} %get-tuple-element.19.p0), channel_id=1, source_target_pairs={{0,1},{1,2},{2,3},{3,0},{4,5},{5,6},{6,7},{7,4},{8,9},{9,10},{10,1... | collective-permute-start | bytes 393224 | tf_op jit(solution)/shard_map/ppermute | solution.py:340
  25.8 14.4 %collective-permute-start.6 = (f32[384,128]{1,0:T(8,128)S(1)}, f32[384,128]{1,0:T(8,128)S(1)}, u32[]{:S(2)}, u32[]{:S(2)}) collective-permute-start(f32[384,128]{1,0:T(8,128)S(1)} %get-tuple-element.18.own), channel_id=1, source_target_pairs={{16,0},{32,16},{48,32},{64,48},{80,64},{96,80},{112,96},{128,112},... | collective-permute-start | bytes 589832 | tf_op jit(solution)/shard_map/ppermute | solution.py:330
  41.5 11.3 %collective-permute-start.10 = (f32[256,128]{1,0:T(8,128)S(1)}, f32[256,128]{1,0:T(8,128)S(1)}, u32[]{:S(2)}, u32[]{:S(2)}) collective-permute-start(f32[256,128]{1,0:T(8,128)S(1)} %get-tuple-element.22), channel_id=1, source_target_pairs={{0,16},{16,32},{32,48},{48,64},{64,80},{80,96},{96,112},{112,128},... | collective-permute-start | bytes 393224 | tf_op jit(solution)/shard_map/ppermute | solution.py:330
  43.4 16.4 %collective-permute-start.13 = (f32[3,128,128]{2,1,0:T(8,128)S(1)}, f32[3,128,128]{2,1,0:T(8,128)S(1)}, u32[]{:S(2)}, u32[]{:S(2)}) collective-permute-start(f32[3,128,128]{2,1,0:T(8,128)S(1)} %choose_kernel.1.after), channel_id=1, source_target_pairs={{0,16},{16,32},{32,48},{48,64},{64,80},{80,96},{96,112},{112,128},... | collective-permute-start | bytes 589832 | tf_op jit(solution)/shard_map/ppermute | solution.py:330
  54.3 15.1 %collective-permute-start.11 = (f32[384,128]{1,0:T(8,128)S(1)}, f32[384,128]{1,0:T(8,128)S(1)}, u32[]{:S(2)}, u32[]{:S(2)}) collective-permute-start(f32[384,128]{1,0:T(8,128)S(1)} %get-tuple-element.25), channel_id=1, source_target_pairs={{16,32},{48,64},{80,96},{112,128},{144,160},{176,192},{208,224},{3... | collective-permute-start | bytes 589832 | tf_op jit(solution)/shard_map/ppermute | solution.py:336
  56.7 12.7 %collective-permute-start.12 = (f32[384,128]{1,0:T(8,128)S(1)}, f32[384,128]{1,0:T(8,128)S(1)}, u32[]{:S(2)}, u32[]{:S(2)}) collective-permute-start(f32[384,128]{1,0:T(8,128)S(1)} %get-tuple-element.26), channel_id=1, source_target_pairs={{0,16},{32,48},{64,80},{96,112},{128,144},{160,176},{192,208},{224... | collective-permute-start | bytes 589832 | tf_op jit(solution)/shard_map/ppermute | solution.py:336

commit v11 on v10

--- a/solution.py
+++ b/solution.py
@@ -337,7 +337,7 @@
 
 
 def along_x(value):
-    found = {k: lax.ppermute(value, "cols", [(i, (i // 4) * 4 + (i + k) % 4) for i in range(16)]) for k in (1, 3, 2)}
+    found = {k: lax.ppermute(value, "cols", [(i, (i // 4) * 4 + (i + k) % 4) for i in range(16)]) for k in (3, 2, 1)}
     return [value, found[1], found[2], found[3]]
 
 

time: 72 us -> 72 us (level)
  no operation moved by 1% of the time
where the time goes in v11:
time: 72 us; the launch traced here: 71.8 us
  starting transfers between devices  27.1 us (38%)
  Pallas kernels  22.1 us (31%)
  waiting for transfers between devices  21.2 us (29%)
  local copies, waits for them, and re-layouts  1.13 us (2%)
    pallas_call x11, Pallas kernels, call(): pl.pallas_call(kernel, out_shape=tuple(shapes), in_specs=[pl.BlockSpec(me...  22.1 us
    ppermute x3, starting transfers between devices, to_neighbour(): lax.ppermute(value, 'rows', [(i, i + steps) for i in range(count) if 0 <=...  12.3 us
    ppermute x2, waiting for transfers between devices, swapped(): return lax.ppermute(value, 'rows', pairs + [(j, i) for i, j in pairs])  7.28 us
    ppermute x6, starting transfers between devices, along_x(): lax.ppermute(value, 'cols', [(i, i // 4 * 4 + (i + k) % 4) for i in range...  7 us
    ppermute x3, waiting for transfers between devices, to_neighbour(): lax.ppermute(value, 'rows', [(i, i + steps) for i in range(count) if 0 <=...  5.86 us
    ppermute x3, starting transfers between devices, shifted(): lax.ppermute(value, axis, [(i, (i + steps) % count) for i in range(count)])  5.36 us
    ppermute x6, waiting for transfers between devices, along_x(): lax.ppermute(value, 'cols', [(i, i // 4 * 4 + (i + k) % 4) for i in range...  5.35 us
    ppermute x3, waiting for transfers between devices, shifted(): lax.ppermute(value, axis, [(i, (i + steps) % count) for i in range(count)])  2.76 us
  transfers between devices with their start and end apart: 14, of which 5 were waited for; matrix products, arithmetic and copies ran while one was open for 0% of the time, Pallas kernels for 26%

profile of v11, /device:TPU:33, one launch (start us, length us, event | category | flops | bytes accessed | tf_op | source)
XLA Modules:
  0.0 71.8 jit_solution(9138640818258073235)
XLA Ops:
  0.0 0.0 collective-permute-start.2
  0.0 3.0 %collective-permute-start.1 = (f32[128,128]{1,0:T(8,128)}, f32[128,128]{1,0:T(8,128)S(1)}, u32[]{:S(2)}, u32[]{:S(2)}) collective-permute-start(f32[128,128]{1,0:T(8,128)} %bitcast.7), channel_id=1, source_target_pairs={{0,8},{1,9},{2,10},{3,11},{4,12},{5,13},{6,14},{7,15},{8,0},{9,1},... | collective-permute-start | bytes 196616 | tf_op jit(solution)/shard_map/ppermute | solution.py:325
  3.0 2.4 %collective-permute-start = (f32[128,128]{1,0:T(8,128)}, f32[128,128]{1,0:T(8,128)S(1)}, u32[]{:S(2)}, u32[]{:S(2)}) collective-permute-start(f32[128,128]{1,0:T(8,128)} %bitcast.8), channel_id=1, source_target_pairs={{0,4},{1,5},{2,6},{3,7},{4,8},{5,9},{6,10},{7,11},{8,12},{9,13},{1... | collective-permute-start | bytes 196616 | tf_op jit(solution)/shard_map/ppermute | solution.py:325
  5.4 0.0 copy-start.1
  5.4 0.9 %copy-done.1 = f32[1,128,128]{2,1,0:T(8,128)S(1)} copy-done((f32[1,128,128]{2,1,0:T(8,128)S(1)}, f32[1,128,128]{2,1,0:T(8,128)}, u32[]{:S(2)}) %copy-start.1) | copy-done | bytes 65560
  6.2 0.0 copy-start.2
  6.2 0.0 copy-start
  6.2 0.0 collective-permute-done.2.p3
  6.3 0.0 collective-permute-done.1.p2
  6.3 2.8 %collective-permute-done.p1 = f32[128,128]{1,0:T(8,128)S(1)} collective-permute-done((f32[128,128]{1,0:T(8,128)}, f32[128,128]{1,0:T(8,128)S(1)}, u32[]{:S(2)}, u32[]{:S(2)}) %collective-permute-start) | collective-permute-done | bytes 65568 | tf_op jit(solution)/shard_map/ppermute | solution.py:325
  9.1 2.6 %collective-permute-start.5 = (f32[2,128,128]{2,1,0:T(8,128)S(1)}, f32[2,128,128]{2,1,0:T(8,128)S(1)}, u32[]{:S(2)}, u32[]{:S(2)}) collective-permute-start(f32[2,128,128]{2,1,0:T(8,128)S(1)} %get-tuple-element.16.p0), channel_id=1, source_target_pairs={{0,3},{1,0},{2,1},{3,2},{4,7},{5,4},{6,5},{7,6},{8,11},{9,8},{10,9... | collective-permute-start | bytes 393224 | tf_op jit(solution)/shard_map/ppermute | solution.py:340
  11.6 0.5 collective-permute-start.4
  12.1 0.6 collective-permute-start.3
  12.8 0.0 copy-done.2
  12.8 0.1 copy.5
  12.8 0.1 reshape.6
  12.9 0.1 concatenate.3.scalars
  13.0 2.1 %collective-permute-start.9 = (f32[2,128,128]{2,1,0:T(8,128)S(1)}, f32[2,128,128]{2,1,0:T(8,128)S(1)}, u32[]{:S(2)}, u32[]{:S(2)}) collective-permute-start(f32[2,128,128]{2,1,0:T(8,128)S(1)} %get-tuple-element.19.p0), channel_id=1, source_target_pairs={{0,3},{1,0},{2,1},{3,2},{4,7},{5,4},{6,5},{7,6},{8,11},{9,8},{10,9... | collective-permute-start | bytes 393224 | tf_op jit(solution)/shard_map/ppermute | solution.py:340
  15.1 1.2 %collective-permute-start.8 = (f32[2,128,128]{2,1,0:T(8,128)S(1)}, f32[2,128,128]{2,1,0:T(8,128)S(1)}, u32[]{:S(2)}, u32[]{:S(2)}) collective-permute-start(f32[2,128,128]{2,1,0:T(8,128)S(1)} %get-tuple-element.19.p0), channel_id=1, source_target_pairs={{0,2},{1,3},{2,0},{3,1},{4,6},{5,7},{6,4},{7,5},{8,10},{9,11},{10,... | collective-permute-start | bytes 393224 | tf_op jit(solution)/shard_map/ppermute | solution.py:340
  16.3 0.0 collective-permute-done.5.p3
  16.3 0.0 collective-permute-start.7
  16.3 0.7 %collective-permute-done.4.p2 = f32[2,128,128]{2,1,0:T(8,128)S(1)} collective-permute-done((f32[2,128,128]{2,1,0:T(8,128)S(1)}, f32[2,128,128]{2,1,0:T(8,128)S(1)}, u32[]{:S(2)}, u32[]{:S(2)}) %collective-permute-start.4) | collective-permute-done | bytes 131104 | tf_op jit(solution)/shard_map/ppermute | solution.py:340
  17.1 4.6 %collective-permute-done.3.p1 = f32[2,128,128]{2,1,0:T(8,128)S(1)} collective-permute-done((f32[2,128,128]{2,1,0:T(8,128)S(1)}, f32[2,128,128]{2,1,0:T(8,128)S(1)}, u32[]{:S(2)}, u32[]{:S(2)}) %collective-permute-start.3) | collective-permute-done | bytes 131104 | tf_op jit(solution)/shard_map/ppermute | solution.py:340
  21.7 0.0 copy-done
  21.7 4.1 %first_kernel.1 = (f32[384,128]{1,0:T(8,128)S(1)}, f32[256,128]{1,0:T(8,128)S(1)}, f32[256,128]{1,0:T(8,128)S(1)}) custom-call(s32[20]{0:T(128)S(1)} %concatenate.3.scalars, f32[512,128]{1,0:T(8,128)S(1)} %copy-done, f32[2,128,128]{2,1,0:T(8,128)S(1)} %get-tuple-element.16.p0, f32[2,128,128]{2,1,0:T(8,128)S(1)} %collective-permute-done.3.p1, ...), custom_call_target="tpu_custom_call" | custom-call | flops 400000000 | bytes 2000000 | tf_op jit(solution)/shard_map/first_kernel/pallas_call | solution.py:311
  25.8 4.7 %collective-permute-start.6 = (f32[384,128]{1,0:T(8,128)S(1)}, f32[384,128]{1,0:T(8,128)S(1)}, u32[]{:S(2)}, u32[]{:S(2)}) collective-permute-start(f32[384,128]{1,0:T(8,128)S(1)} %get-tuple-element.18.own), channel_id=1, source_target_pairs={{16,0},{32,16},{48,32},{64,48},{80,64},{96,80},{112,96},{128,112},... | collective-permute-start | bytes 589832 | tf_op jit(solution)/shard_map/ppermute | solution.py:330
  30.5 0.0 collective-permute-done.9.p3
  30.5 0.0 collective-permute-done.8.p2
  30.5 0.0 collective-permute-done.7.p1
  30.5 0.6 choose_kernel.1.after
  31.1 3.2 %factor1_kernel.1.g1 = bf16[4,256,512]{2,1,0:T(8,128)(2,1)S(1)} custom-call(s32[20]{0:T(128)S(1)} %concatenate.3.scalars, f32[3,128,128]{2,1,0:T(8,128)S(1)} %choose_kernel.1.after, f32[2,128,128]{2,1,0:T(8,128)S(1)} %get-tuple-element.16.p0, f32[2,128,128]{2,1,0:T(8,128)S(1)} %collective-permute-done.3.p1, f32[2,128,128]{2,1,0:T(8,128)S(1)} %collective-permute-done.4.p2, ...), custom_call_target="tpu_custom_call" | custom-call | flops 400000000 | bytes 2000000 | tf_op jit(solution)/shard_map/factor1_kernel/pallas_call | solution.py:311
  34.4 5.9 %collective-permute-done.6.message = f32[384,128]{1,0:T(8,128)S(1)} collective-permute-done((f32[384,128]{1,0:T(8,128)S(1)}, f32[384,128]{1,0:T(8,128)S(1)}, u32[]{:S(2)}, u32[]{:S(2)}) %collective-permute-start.6) | collective-permute-done | bytes 196640 | tf_op jit(solution)/shard_map/ppermute | solution.py:330
  40.2 1.3 %second_kernel.1 = (f32[256,128]{1,0:T(8,128)S(1)}, f32[256,128]{1,0:T(8,128)S(1)}) custom-call(s32[20]{0:T(128)S(1)} %concatenate.3.scalars, f32[256,128]{1,0:T(8,128)S(1)} %get-tuple-element.17.after.low_ref, f32[384,128]{1,0:T(8,128)S(1)} %collective-permute-done.6.message, bf16[4,256,512]{2,1,0:T(8,128)(2,1)S(1)} %factor1_kernel.1.g1), custom_call_target="tpu_custom_call" | custom-call | flops 400000000 | bytes 2000000 | tf_op jit(solution)/shard_map/second_kernel/pallas_call | solution.py:311
  41.5 1.9 %collective-permute-start.10 = (f32[256,128]{1,0:T(8,128)S(1)}, f32[256,128]{1,0:T(8,128)S(1)}, u32[]{:S(2)}, u32[]{:S(2)}) collective-permute-start(f32[256,128]{1,0:T(8,128)S(1)} %get-tuple-element.22), channel_id=1, source_target_pairs={{0,16},{16,32},{32,48},{48,64},{64,80},{80,96},{96,112},{112,128},... | collective-permute-start | bytes 393224 | tf_op jit(solution)/shard_map/ppermute | solution.py:330
  43.4 5.7 %collective-permute-start.13 = (f32[3,128,128]{2,1,0:T(8,128)S(1)}, f32[3,128,128]{2,1,0:T(8,128)S(1)}, u32[]{:S(2)}, u32[]{:S(2)}) collective-permute-start(f32[3,128,128]{2,1,0:T(8,128)S(1)} %choose_kernel.1.after), channel_id=1, source_target_pairs={{0,16},{16,32},{32,48},{48,64},{64,80},{80,96},{96,112},{112,128},... | collective-permute-start | bytes 589832 | tf_op jit(solution)/shard_map/ppermute | solution.py:330
  49.1 3.7 %factor2_kernel.1.g2 = bf16[5,256,512]{2,1,0:T(8,128)(2,1)S(1)} custom-call(s32[20]{0:T(128)S(1)} %concatenate.3.scalars, f32[256,128]{1,0:T(8,128)S(1)} %get-tuple-element.20.after.low_ref, f32[2,128,128]{2,1,0:T(8,128)S(1)} %get-tuple-element.19.p0, f32[2,128,128]{2,1,0:T(8,128)S(1)} %collective-permute-done.7.p1, ...), custom_call_target="tpu_custom_call" | custom-call | flops 400000000 | bytes 2000000 | tf_op jit(solution)/shard_map/factor2_kernel/pallas_call | solution.py:311
  52.8 0.0 collective-permute-done.10.back
  52.8 1.5 %third_kernel.1 = (f32[256,128]{1,0:T(8,128)S(1)}, f32[256,128]{1,0:T(8,128)S(1)}, f32[384,128]{1,0:T(8,128)S(1)}, f32[384,128]{1,0:T(8,128)S(1)}) custom-call(s32[20]{0:T(128)S(1)} %concatenate.3.scalars, f32[256,128]{1,0:T(8,128)S(1)} %get-tuple-element.20.after.low_ref, f32[384,128]{1,0:T(8,128)S(1)} %get-tuple-element.18.own, ...), custom_call_target="tpu_custom_call" | custom-call | flops 400000000 | bytes 2000000 | tf_op jit(solution)/shard_map/third_kernel/pallas_call | solution.py:311
  54.3 2.4 %collective-permute-start.11 = (f32[384,128]{1,0:T(8,128)S(1)}, f32[384,128]{1,0:T(8,128)S(1)}, u32[]{:S(2)}, u32[]{:S(2)}) collective-permute-start(f32[384,128]{1,0:T(8,128)S(1)} %get-tuple-element.25), channel_id=1, source_target_pairs={{16,32},{48,64},{80,96},{112,128},{144,160},{176,192},{208,224},{3... | collective-permute-start | bytes 589832 | tf_op jit(solution)/shard_map/ppermute | solution.py:336
  56.7 0.1 collective-permute-start.12
  56.8 2.9 %factor3_kernel.1.g3 = bf16[3,256,512]{2,1,0:T(8,128)(2,1)S(1)} custom-call(s32[20]{0:T(128)S(1)} %concatenate.3.scalars, f32[256,128]{1,0:T(8,128)S(1)} %get-tuple-element.23.after.low_ref, f32[2,128,128]{2,1,0:T(8,128)S(1)} %get-tuple-element.19.p0, f32[2,128,128]{2,1,0:T(8,128)S(1)} %collective-permute-done.7.p1, ...), custom_call_target="tpu_custom_call" | custom-call | flops 400000000 | bytes 2000000 | tf_op jit(solution)/shard_map/factor3_kernel/pallas_call | solution.py:311
  59.8 0.0 collective-permute-done.13.down
  59.8 2.4 %factor4_kernel.1.g4 = bf16[3,256,512]{2,1,0:T(8,128)(2,1)S(1)} custom-call(f32[256,128]{1,0:T(8,128)S(1)} %get-tuple-element.23.after.low_ref, f32[3,128,128]{2,1,0:T(8,128)S(1)} %collective-permute-done.13.down), custom_call_target="tpu_custom_call" | custom-call | flops 400000000 | bytes 2000000 | tf_op jit(solution)/shard_map/factor4_kernel/pallas_call | solution.py:311
  62.2 7.3 %collective-permute-done.11.far = f32[384,128]{1,0:T(8,128)S(1)} collective-permute-done((f32[384,128]{1,0:T(8,128)S(1)}, f32[384,128]{1,0:T(8,128)S(1)}, u32[]{:S(2)}, u32[]{:S(2)}) %collective-permute-start.11) | collective-permute-done | bytes 196640 | tf_op jit(solution)/shard_map/ppermute | solution.py:336
  69.4 0.0 collective-permute-done.12.near
  69.4 2.3 %fourth_kernel.1 = f32[512,128]{1,0:T(8,128)} custom-call(s32[20]{0:T(128)S(1)} %concatenate.3.scalars, f32[256,128]{1,0:T(8,128)S(1)} %get-tuple-element.23.after.low_ref, f32[256,128]{1,0:T(8,128)S(1)} %get-tuple-element.24.top_ref, f32[384,128]{1,0:T(8,128)S(1)} %collective-permute-done.11.far, f32[384,128]{1,0:T(8,128)S(1)} %collective-permute-done.12.near, ...), custom_call_target="tpu_custom_call" | custom-call | flops 400000000 | bytes 2000000 | tf_op jit(solution)/shard_map/fourth_kernel/pallas_call | solution.py:311
  (2 shorter events, 0.0 us)
Async XLA Ops:
  0.0 6.2 %collective-permute-start.2 = (f32[128,128]{1,0:T(8,128)}, f32[128,128]{1,0:T(8,128)S(1)}, u32[]{:S(2)}, u32[]{:S(2)}) collective-permute-start(f32[128,128]{1,0:T(8,128)} %bitcast.6), channel_id=1, source_target_pairs={{0,12},{1,13},{2,14},{3,15},{4,0},{5,1},{6,2},{7,3},{8,4},{9,5},{1... | collective-permute-start | bytes 196616 | tf_op jit(solution)/shard_map/ppermute | solution.py:325
  0.0 6.3 %collective-permute-start.1 = (f32[128,128]{1,0:T(8,128)}, f32[128,128]{1,0:T(8,128)S(1)}, u32[]{:S(2)}, u32[]{:S(2)}) collective-permute-start(f32[128,128]{1,0:T(8,128)} %bitcast.7), channel_id=1, source_target_pairs={{0,8},{1,9},{2,10},{3,11},{4,12},{5,13},{6,14},{7,15},{8,0},{9,1},... | collective-permute-start | bytes 196616 | tf_op jit(solution)/shard_map/ppermute | solution.py:325
  3.0 6.0 %collective-permute-start = (f32[128,128]{1,0:T(8,128)}, f32[128,128]{1,0:T(8,128)S(1)}, u32[]{:S(2)}, u32[]{:S(2)}) collective-permute-start(f32[128,128]{1,0:T(8,128)} %bitcast.8), channel_id=1, source_target_pairs={{0,4},{1,5},{2,6},{3,7},{4,8},{5,9},{6,10},{7,11},{8,12},{9,13},{1... | collective-permute-start | bytes 196616 | tf_op jit(solution)/shard_map/ppermute | solution.py:325
  5.4 0.9 %copy-start.1 = (f32[1,128,128]{2,1,0:T(8,128)S(1)}, f32[1,128,128]{2,1,0:T(8,128)}, u32[]{:S(2)}) copy-start(f32[1,128,128]{2,1,0:T(8,128)} %param.4) | copy-start | bytes 196612
  6.2 6.5 %copy-start.2 = (s32[1,8,2]{1,2,0:T(2,128)S(1)}, s32[1,8,2]{1,2,0:T(2,128)}, u32[]{:S(2)}) copy-start(s32[1,8,2]{1,2,0:T(2,128)} %param.5) | copy-start | bytes 196
  6.2 15.4 %copy-start = (f32[512,128]{1,0:T(8,128)S(1)}, f32[512,128]{1,0:T(8,128)}, u32[]{:S(2)}) copy-start(f32[512,128]{1,0:T(8,128)} %x_ref.1) | copy-start | bytes 786436
  9.1 7.3 %collective-permute-start.5 = (f32[2,128,128]{2,1,0:T(8,128)S(1)}, f32[2,128,128]{2,1,0:T(8,128)S(1)}, u32[]{:S(2)}, u32[]{:S(2)}) collective-permute-start(f32[2,128,128]{2,1,0:T(8,128)S(1)} %get-tuple-element.16.p0), channel_id=1, source_target_pairs={{0,3},{1,0},{2,1},{3,2},{4,7},{5,4},{6,5},{7,6},{8,11},{9,8},{10,9... | collective-permute-start | bytes 393224 | tf_op jit(solution)/shard_map/ppermute | solution.py:340
  11.6 5.4 %collective-permute-start.4 = (f32[2,128,128]{2,1,0:T(8,128)S(1)}, f32[2,128,128]{2,1,0:T(8,128)S(1)}, u32[]{:S(2)}, u32[]{:S(2)}) collective-permute-start(f32[2,128,128]{2,1,0:T(8,128)S(1)} %get-tuple-element.16.p0), channel_id=1, source_target_pairs={{0,2},{1,3},{2,0},{3,1},{4,6},{5,7},{6,4},{7,5},{8,10},{9,11},{10,... | collective-permute-start | bytes 393224 | tf_op jit(solution)/shard_map/ppermute | solution.py:340
  12.1 9.5 %collective-permute-start.3 = (f32[2,128,128]{2,1,0:T(8,128)S(1)}, f32[2,128,128]{2,1,0:T(8,128)S(1)}, u32[]{:S(2)}, u32[]{:S(2)}) collective-permute-start(f32[2,128,128]{2,1,0:T(8,128)S(1)} %get-tuple-element.16.p0), channel_id=1, source_target_pairs={{0,1},{1,2},{2,3},{3,0},{4,5},{5,6},{6,7},{7,4},{8,9},{9,10},{10,1... | collective-permute-start | bytes 393224 | tf_op jit(solution)/shard_map/ppermute | solution.py:340
  13.0 17.5 %collective-permute-start.9 = (f32[2,128,128]{2,1,0:T(8,128)S(1)}, f32[2,128,128]{2,1,0:T(8,128)S(1)}, u32[]{:S(2)}, u32[]{:S(2)}) collective-permute-start(f32[2,128,128]{2,1,0:T(8,128)S(1)} %get-tuple-element.19.p0), channel_id=1, source_target_pairs={{0,3},{1,0},{2,1},{3,2},{4,7},{5,4},{6,5},{7,6},{8,11},{9,8},{10,9... | collective-permute-start | bytes 393224 | tf_op jit(solution)/shard_map/ppermute | solution.py:340
  15.1 15.4 %collective-permute-start.8 = (f32[2,128,128]{2,1,0:T(8,128)S(1)}, f32[2,128,128]{2,1,0:T(8,128)S(1)}, u32[]{:S(2)}, u32[]{:S(2)}) collective-permute-start(f32[2,128,128]{2,1,0:T(8,128)S(1)} %get-tuple-element.19.p0), channel_id=1, source_target_pairs={{0,2},{1,3},{2,0},{3,1},{4,6},{5,7},{6,4},{7,5},{8,10},{9,11},{10,... | collective-permute-start | bytes 393224 | tf_op jit(solution)/shard_map/ppermute | solution.py:340
  16.3 14.2 %collective-permute-start.7 = (f32[2,128,128]{2,1,0:T(8,128)S(1)}, f32[2,128,128]{2,1,0:T(8,128)S(1)}, u32[]{:S(2)}, u32[]{:S(2)}) collective-permute-start(f32[2,128,128]{2,1,0:T(8,128)S(1)} %get-tuple-element.19.p0), channel_id=1, source_target_pairs={{0,1},{1,2},{2,3},{3,0},{4,5},{5,6},{6,7},{7,4},{8,9},{9,10},{10,1... | collective-permute-start | bytes 393224 | tf_op jit(solution)/shard_map/ppermute | solution.py:340
  25.8 14.4 %collective-permute-start.6 = (f32[384,128]{1,0:T(8,128)S(1)}, f32[384,128]{1,0:T(8,128)S(1)}, u32[]{:S(2)}, u32[]{:S(2)}) collective-permute-start(f32[384,128]{1,0:T(8,128)S(1)} %get-tuple-element.18.own), channel_id=1, source_target_pairs={{16,0},{32,16},{48,32},{64,48},{80,64},{96,80},{112,96},{128,112},... | collective-permute-start | bytes 589832 | tf_op jit(solution)/shard_map/ppermute | solution.py:330
  41.5 11.3 %collective-permute-start.10 = (f32[256,128]{1,0:T(8,128)S(1)}, f32[256,128]{1,0:T(8,128)S(1)}, u32[]{:S(2)}, u32[]{:S(2)}) collective-permute-start(f32[256,128]{1,0:T(8,128)S(1)} %get-tuple-element.22), channel_id=1, source_target_pairs={{0,16},{16,32},{32,48},{48,64},{64,80},{80,96},{96,112},{112,128},... | collective-permute-start | bytes 393224 | tf_op jit(solution)/shard_map/ppermute | solution.py:330
  43.4 16.4 %collective-permute-start.13 = (f32[3,128,128]{2,1,0:T(8,128)S(1)}, f32[3,128,128]{2,1,0:T(8,128)S(1)}, u32[]{:S(2)}, u32[]{:S(2)}) collective-permute-start(f32[3,128,128]{2,1,0:T(8,128)S(1)} %choose_kernel.1.after), channel_id=1, source_target_pairs={{0,16},{16,32},{32,48},{48,64},{64,80},{80,96},{96,112},{112,128},... | collective-permute-start | bytes 589832 | tf_op jit(solution)/shard_map/ppermute | solution.py:330
  54.3 15.1 %collective-permute-start.11 = (f32[384,128]{1,0:T(8,128)S(1)}, f32[384,128]{1,0:T(8,128)S(1)}, u32[]{:S(2)}, u32[]{:S(2)}) collective-permute-start(f32[384,128]{1,0:T(8,128)S(1)} %get-tuple-element.25), channel_id=1, source_target_pairs={{16,32},{48,64},{80,96},{112,128},{144,160},{176,192},{208,224},{3... | collective-permute-start | bytes 589832 | tf_op jit(solution)/shard_map/ppermute | solution.py:336
  56.7 12.7 %collective-permute-start.12 = (f32[384,128]{1,0:T(8,128)S(1)}, f32[384,128]{1,0:T(8,128)S(1)}, u32[]{:S(2)}, u32[]{:S(2)}) collective-permute-start(f32[384,128]{1,0:T(8,128)S(1)} %get-tuple-element.26), channel_id=1, source_target_pairs={{0,16},{32,48},{64,80},{96,112},{128,144},{160,176},{192,208},{224... | collective-permute-start | bytes 589832 | tf_op jit(solution)/shard_map/ppermute | solution.py:336

commit v12 on v11

--- a/solution.py
+++ b/solution.py
@@ -253,7 +253,7 @@
     stored_wholes([block_of(scalars, held, level, half) for level in (4, 5) for half in (0, 1)] + [later], g2)
 
 
-def third_kernel(scalars, low_ref, own, rest, back, g1, g2, low_out, top_out, far_out, near_out):
+def third_kernel(scalars, low_ref, own, rest, back, after, g1, g2, low_out, top_out, far_out, near_out):
     upper = jnp.where(scalars[2] == 1, own[W : 2 * W], back[:W])
     lower = rest[:W] - dot3(split(rest[W:]), split(back[W:]))
     top, low = across(jnp.concatenate([upper, lower], axis=0), low_ref[...], once(g1, 1))
@@ -367,7 +367,7 @@
     (g2,) = call(factor2_kernel, (scalars, low, *far), [wholes(5)], HELD)
     down = to_neighbour(down, 1)
     low, top, far_out, near_out = call(
-        third_kernel, (scalars, low, own, rest, back, g1, g2), [half, half, three, three]
+        third_kernel, (scalars, low, own, rest, back, down, g1, g2), [half, half, three, three]
     )
     from_far = swapped(far_out, 1)
     from_near = swapped(near_out, 0)

time: 72 us -> 70.3 us (0.976)
  the two profiles are of different devices: /device:TPU:33 before, /device:TPU:88 now
where the time goes in v12:
time: 70.3 us; the launch traced here: 70 us
  starting transfers between devices  27.8 us (40%)
  Pallas kernels  22.1 us (31%)
  waiting for transfers between devices  18.8 us (27%)
  local copies, waits for them, and re-layouts  1.16 us (2%)
    pallas_call x11, Pallas kernels, call(): pl.pallas_call(kernel, out_shape=tuple(shapes), in_specs=[pl.BlockSpec(me...  22.1 us
    ppermute x3, starting transfers between devices, to_neighbour(): lax.ppermute(value, 'rows', [(i, i + steps) for i in range(count) if 0 <=...  10.9 us
    ppermute x6, starting transfers between devices, along_x(): lax.ppermute(value, 'cols', [(i, i // 4 * 4 + (i + k) % 4) for i in range...  8.4 us
    ppermute x6, waiting for transfers between devices, along_x(): lax.ppermute(value, 'cols', [(i, i // 4 * 4 + (i + k) % 4) for i in range...  5.5 us
    ppermute x3, waiting for transfers between devices, shifted(): lax.ppermute(value, axis, [(i, (i + steps) % count) for i in range(count)])  4.6 us
    ppermute x2, waiting for transfers between devices, swapped(): return lax.ppermute(value, 'rows', pairs + [(j, i) for i, j in pairs])  4.59 us
    ppermute x3, starting transfers between devices, shifted(): lax.ppermute(value, axis, [(i, (i + steps) % count) for i in range(count)])  4.28 us
    ppermute x2, starting transfers between devices, swapped(): return lax.ppermute(value, 'rows', pairs + [(j, i) for i, j in pairs])  4.23 us
  transfers between devices with their start and end apart: 14, of which 7 were waited for; matrix products, arithmetic and copies ran while one was open for 0% of the time, Pallas kernels for 26%

profile of v12, /device:TPU:88, one launch (start us, length us, event | category | flops | bytes accessed | tf_op | source)
XLA Modules:
  0.0 70.0 jit_solution(5052127614430751214)
XLA Ops:
  0.0 0.1 collective-permute-start.2
  0.1 4.2 %collective-permute-start.1 = (f32[128,128]{1,0:T(8,128)}, f32[128,128]{1,0:T(8,128)S(1)}, u32[]{:S(2)}, u32[]{:S(2)}) collective-permute-start(f32[128,128]{1,0:T(8,128)} %bitcast.7), channel_id=1, source_target_pairs={{0,8},{1,9},{2,10},{3,11},{4,12},{5,13},{6,14},{7,15},{8,0},{9,1},... | collective-permute-start | bytes 196616 | tf_op jit(solution)/shard_map/ppermute | solution.py:325
  4.3 0.0 collective-permute-start
  4.3 0.0 copy-start.1
  4.3 0.9 %copy-done.1 = f32[1,128,128]{2,1,0:T(8,128)S(1)} copy-done((f32[1,128,128]{2,1,0:T(8,128)S(1)}, f32[1,128,128]{2,1,0:T(8,128)}, u32[]{:S(2)}) %copy-start.1) | copy-done | bytes 65560
  5.2 0.0 copy-start.2
  5.2 0.0 copy-start
  5.2 0.0 collective-permute-done.2.p3
  5.2 3.2 %collective-permute-done.1.p2 = f32[128,128]{1,0:T(8,128)S(1)} collective-permute-done((f32[128,128]{1,0:T(8,128)}, f32[128,128]{1,0:T(8,128)S(1)}, u32[]{:S(2)}, u32[]{:S(2)}) %collective-permute-start.1) | collective-permute-done | bytes 65568 | tf_op jit(solution)/shard_map/ppermute | solution.py:325
  8.4 1.4 %collective-permute-done.p1 = f32[128,128]{1,0:T(8,128)S(1)} collective-permute-done((f32[128,128]{1,0:T(8,128)}, f32[128,128]{1,0:T(8,128)S(1)}, u32[]{:S(2)}, u32[]{:S(2)}) %collective-permute-start) | collective-permute-done | bytes 65568 | tf_op jit(solution)/shard_map/ppermute | solution.py:325
  9.9 2.8 %collective-permute-start.5 = (f32[2,128,128]{2,1,0:T(8,128)S(1)}, f32[2,128,128]{2,1,0:T(8,128)S(1)}, u32[]{:S(2)}, u32[]{:S(2)}) collective-permute-start(f32[2,128,128]{2,1,0:T(8,128)S(1)} %get-tuple-element.16.p0), channel_id=1, source_target_pairs={{0,3},{1,0},{2,1},{3,2},{4,7},{5,4},{6,5},{7,6},{8,11},{9,8},{10,9... | collective-permute-start | bytes 393224 | tf_op jit(solution)/shard_map/ppermute | solution.py:340
  12.7 0.8 %collective-permute-start.4 = (f32[2,128,128]{2,1,0:T(8,128)S(1)}, f32[2,128,128]{2,1,0:T(8,128)S(1)}, u32[]{:S(2)}, u32[]{:S(2)}) collective-permute-start(f32[2,128,128]{2,1,0:T(8,128)S(1)} %get-tuple-element.16.p0), channel_id=1, source_target_pairs={{0,2},{1,3},{2,0},{3,1},{4,6},{5,7},{6,4},{7,5},{8,10},{9,11},{10,... | collective-permute-start | bytes 393224 | tf_op jit(solution)/shard_map/ppermute | solution.py:340
  13.5 0.9 %collective-permute-start.3 = (f32[2,128,128]{2,1,0:T(8,128)S(1)}, f32[2,128,128]{2,1,0:T(8,128)S(1)}, u32[]{:S(2)}, u32[]{:S(2)}) collective-permute-start(f32[2,128,128]{2,1,0:T(8,128)S(1)} %get-tuple-element.16.p0), channel_id=1, source_target_pairs={{0,1},{1,2},{2,3},{3,0},{4,5},{5,6},{6,7},{7,4},{8,9},{9,10},{10,1... | collective-permute-start | bytes 393224 | tf_op jit(solution)/shard_map/ppermute | solution.py:340
  14.4 0.0 copy-done.2
  14.4 0.1 copy.5
  14.5 0.1 reshape.6
  14.5 0.1 concatenate.3.scalars
  14.6 2.4 %collective-permute-start.9 = (f32[2,128,128]{2,1,0:T(8,128)S(1)}, f32[2,128,128]{2,1,0:T(8,128)S(1)}, u32[]{:S(2)}, u32[]{:S(2)}) collective-permute-start(f32[2,128,128]{2,1,0:T(8,128)S(1)} %get-tuple-element.19.p0), channel_id=1, source_target_pairs={{0,3},{1,0},{2,1},{3,2},{4,7},{5,4},{6,5},{7,6},{8,11},{9,8},{10,9... | collective-permute-start | bytes 393224 | tf_op jit(solution)/shard_map/ppermute | solution.py:340
  17.0 1.5 %collective-permute-start.8 = (f32[2,128,128]{2,1,0:T(8,128)S(1)}, f32[2,128,128]{2,1,0:T(8,128)S(1)}, u32[]{:S(2)}, u32[]{:S(2)}) collective-permute-start(f32[2,128,128]{2,1,0:T(8,128)S(1)} %get-tuple-element.19.p0), channel_id=1, source_target_pairs={{0,2},{1,3},{2,0},{3,1},{4,6},{5,7},{6,4},{7,5},{8,10},{9,11},{10,... | collective-permute-start | bytes 393224 | tf_op jit(solution)/shard_map/ppermute | solution.py:340
  18.5 0.7 %collective-permute-done.5.p3 = f32[2,128,128]{2,1,0:T(8,128)S(1)} collective-permute-done((f32[2,128,128]{2,1,0:T(8,128)S(1)}, f32[2,128,128]{2,1,0:T(8,128)S(1)}, u32[]{:S(2)}, u32[]{:S(2)}) %collective-permute-start.5) | collective-permute-done | bytes 131104 | tf_op jit(solution)/shard_map/ppermute | solution.py:340
  19.2 0.0 collective-permute-start.7
  19.3 1.4 %collective-permute-done.4.p2 = f32[2,128,128]{2,1,0:T(8,128)S(1)} collective-permute-done((f32[2,128,128]{2,1,0:T(8,128)S(1)}, f32[2,128,128]{2,1,0:T(8,128)S(1)}, u32[]{:S(2)}, u32[]{:S(2)}) %collective-permute-start.4) | collective-permute-done | bytes 131104 | tf_op jit(solution)/shard_map/ppermute | solution.py:340
  20.7 3.3 %collective-permute-done.3.p1 = f32[2,128,128]{2,1,0:T(8,128)S(1)} collective-permute-done((f32[2,128,128]{2,1,0:T(8,128)S(1)}, f32[2,128,128]{2,1,0:T(8,128)S(1)}, u32[]{:S(2)}, u32[]{:S(2)}) %collective-permute-start.3) | collective-permute-done | bytes 131104 | tf_op jit(solution)/shard_map/ppermute | solution.py:340
  24.0 0.0 copy-done
  24.0 4.1 %first_kernel.1 = (f32[384,128]{1,0:T(8,128)S(1)}, f32[256,128]{1,0:T(8,128)S(1)}, f32[256,128]{1,0:T(8,128)S(1)}) custom-call(s32[20]{0:T(128)S(1)} %concatenate.3.scalars, f32[512,128]{1,0:T(8,128)S(1)} %copy-done, f32[2,128,128]{2,1,0:T(8,128)S(1)} %get-tuple-element.16.p0, f32[2,128,128]{2,1,0:T(8,128)S(1)} %collective-permute-done.3.p1, ...), custom_call_target="tpu_custom_call" | custom-call | flops 400000000 | bytes 2000000 | tf_op jit(solution)/shard_map/first_kernel/pallas_call | solution.py:311
  28.2 5.7 %collective-permute-start.6 = (f32[384,128]{1,0:T(8,128)S(1)}, f32[384,128]{1,0:T(8,128)S(1)}, u32[]{:S(2)}, u32[]{:S(2)}) collective-permute-start(f32[384,128]{1,0:T(8,128)S(1)} %get-tuple-element.18.own), channel_id=1, source_target_pairs={{16,0},{32,16},{48,32},{64,48},{80,64},{96,80},{112,96},{128,112},... | collective-permute-start | bytes 589832 | tf_op jit(solution)/shard_map/ppermute | solution.py:330
  33.8 0.0 collective-permute-done.9.p3
  33.9 0.0 collective-permute-done.8.p2
  33.9 0.0 collective-permute-done.7.p1
  33.9 0.6 choose_kernel.1.after
  34.5 1.9 %collective-permute-start.11 = (f32[3,128,128]{2,1,0:T(8,128)S(1)}, f32[3,128,128]{2,1,0:T(8,128)S(1)}, u32[]{:S(2)}, u32[]{:S(2)}) collective-permute-start(f32[3,128,128]{2,1,0:T(8,128)S(1)} %choose_kernel.1.after), channel_id=1, source_target_pairs={{0,16},{16,32},{32,48},{48,64},{64,80},{80,96},{96,112},{112,128},... | collective-permute-start | bytes 589832 | tf_op jit(solution)/shard_map/ppermute | solution.py:330
  36.4 3.2 %factor1_kernel.1.g1 = bf16[4,256,512]{2,1,0:T(8,128)(2,1)S(1)} custom-call(s32[20]{0:T(128)S(1)} %concatenate.3.scalars, f32[3,128,128]{2,1,0:T(8,128)S(1)} %choose_kernel.1.after, f32[2,128,128]{2,1,0:T(8,128)S(1)} %get-tuple-element.16.p0, f32[2,128,128]{2,1,0:T(8,128)S(1)} %collective-permute-done.3.p1, f32[2,128,128]{2,1,0:T(8,128)S(1)} %collective-permute-done.4.p2, ...), custom_call_target="tpu_custom_call" | custom-call | flops 400000000 | bytes 2000000 | tf_op jit(solution)/shard_map/factor1_kernel/pallas_call | solution.py:311
  39.7 0.0 collective-permute-done.6.message
  39.7 1.3 %second_kernel.1 = (f32[256,128]{1,0:T(8,128)S(1)}, f32[256,128]{1,0:T(8,128)S(1)}) custom-call(s32[20]{0:T(128)S(1)} %concatenate.3.scalars, f32[256,128]{1,0:T(8,128)S(1)} %get-tuple-element.17.after.low_ref, f32[384,128]{1,0:T(8,128)S(1)} %collective-permute-done.6.message, bf16[4,256,512]{2,1,0:T(8,128)(2,1)S(1)} %factor1_kernel.1.g1), custom_call_target="tpu_custom_call" | custom-call | flops 400000000 | bytes 2000000 | tf_op jit(solution)/shard_map/second_kernel/pallas_call | solution.py:311
  40.9 3.3 %collective-permute-start.10 = (f32[256,128]{1,0:T(8,128)S(1)}, f32[256,128]{1,0:T(8,128)S(1)}, u32[]{:S(2)}, u32[]{:S(2)}) collective-permute-start(f32[256,128]{1,0:T(8,128)S(1)} %get-tuple-element.22), channel_id=1, source_target_pairs={{0,16},{16,32},{32,48},{48,64},{64,80},{80,96},{96,112},{112,128},... | collective-permute-start | bytes 393224 | tf_op jit(solution)/shard_map/ppermute | solution.py:330
  44.3 3.7 %factor2_kernel.1.g2 = bf16[5,256,512]{2,1,0:T(8,128)(2,1)S(1)} custom-call(s32[20]{0:T(128)S(1)} %concatenate.3.scalars, f32[256,128]{1,0:T(8,128)S(1)} %get-tuple-element.20.after.low_ref, f32[2,128,128]{2,1,0:T(8,128)S(1)} %get-tuple-element.19.p0, f32[2,128,128]{2,1,0:T(8,128)S(1)} %collective-permute-done.7.p1, ...), custom_call_target="tpu_custom_call" | custom-call | flops 400000000 | bytes 2000000 | tf_op jit(solution)/shard_map/factor2_kernel/pallas_call | solution.py:311
  47.9 0.0 collective-permute-done.11.after.down
  47.9 4.1 %collective-permute-done.10.back = f32[256,128]{1,0:T(8,128)S(1)} collective-permute-done((f32[256,128]{1,0:T(8,128)S(1)}, f32[256,128]{1,0:T(8,128)S(1)}, u32[]{:S(2)}, u32[]{:S(2)}) %collective-permute-start.10) | collective-permute-done | bytes 131104 | tf_op jit(solution)/shard_map/ppermute | solution.py:330
  52.0 1.5 %third_kernel.1 = (f32[256,128]{1,0:T(8,128)S(1)}, f32[256,128]{1,0:T(8,128)S(1)}, f32[384,128]{1,0:T(8,128)S(1)}, f32[384,128]{1,0:T(8,128)S(1)}) custom-call(s32[20]{0:T(128)S(1)} %concatenate.3.scalars, f32[256,128]{1,0:T(8,128)S(1)} %get-tuple-element.20.after.low_ref, f32[384,128]{1,0:T(8,128)S(1)} %get-tuple-element.18.own, ...), custom_call_target="tpu_custom_call" | custom-call | flops 400000000 | bytes 2000000 | tf_op jit(solution)/shard_map/third_kernel/pallas_call | solution.py:311
  53.5 3.1 %collective-permute-start.12 = (f32[384,128]{1,0:T(8,128)S(1)}, f32[384,128]{1,0:T(8,128)S(1)}, u32[]{:S(2)}, u32[]{:S(2)}) collective-permute-start(f32[384,128]{1,0:T(8,128)S(1)} %get-tuple-element.25), channel_id=1, source_target_pairs={{16,32},{48,64},{80,96},{112,128},{144,160},{176,192},{208,224},{3... | collective-permute-start | bytes 589832 | tf_op jit(solution)/shard_map/ppermute | solution.py:336
  56.7 1.1 %collective-permute-start.13 = (f32[384,128]{1,0:T(8,128)S(1)}, f32[384,128]{1,0:T(8,128)S(1)}, u32[]{:S(2)}, u32[]{:S(2)}) collective-permute-start(f32[384,128]{1,0:T(8,128)S(1)} %get-tuple-element.26), channel_id=1, source_target_pairs={{0,16},{32,48},{64,80},{96,112},{128,144},{160,176},{192,208},{224... | collective-permute-start | bytes 589832 | tf_op jit(solution)/shard_map/ppermute | solution.py:336
  57.8 2.9 %factor3_kernel.1.g3 = bf16[3,256,512]{2,1,0:T(8,128)(2,1)S(1)} custom-call(s32[20]{0:T(128)S(1)} %concatenate.3.scalars, f32[256,128]{1,0:T(8,128)S(1)} %get-tuple-element.23.after.low_ref, f32[2,128,128]{2,1,0:T(8,128)S(1)} %get-tuple-element.19.p0, f32[2,128,128]{2,1,0:T(8,128)S(1)} %collective-permute-done.7.p1, ...), custom_call_target="tpu_custom_call" | custom-call | flops 400000000 | bytes 2000000 | tf_op jit(solution)/shard_map/factor3_kernel/pallas_call | solution.py:311
  60.7 2.4 %factor4_kernel.1.g4 = bf16[3,256,512]{2,1,0:T(8,128)(2,1)S(1)} custom-call(f32[256,128]{1,0:T(8,128)S(1)} %get-tuple-element.23.after.low_ref, f32[3,128,128]{2,1,0:T(8,128)S(1)} %collective-permute-done.11.after.down), custom_call_target="tpu_custom_call" | custom-call | flops 400000000 | bytes 2000000 | tf_op jit(solution)/shard_map/factor4_kernel/pallas_call | solution.py:311
  63.1 4.6 %collective-permute-done.12.far = f32[384,128]{1,0:T(8,128)S(1)} collective-permute-done((f32[384,128]{1,0:T(8,128)S(1)}, f32[384,128]{1,0:T(8,128)S(1)}, u32[]{:S(2)}, u32[]{:S(2)}) %collective-permute-start.12) | collective-permute-done | bytes 196640 | tf_op jit(solution)/shard_map/ppermute | solution.py:336
  67.7 0.0 collective-permute-done.13.near
  67.7 2.3 %fourth_kernel.1 = f32[512,128]{1,0:T(8,128)} custom-call(s32[20]{0:T(128)S(1)} %concatenate.3.scalars, f32[256,128]{1,0:T(8,128)S(1)} %get-tuple-element.23.after.low_ref, f32[256,128]{1,0:T(8,128)S(1)} %get-tuple-element.24.top_ref, f32[384,128]{1,0:T(8,128)S(1)} %collective-permute-done.12.far, f32[384,128]{1,0:T(8,128)S(1)} %collective-permute-done.13.near, ...), custom_call_target="tpu_custom_call" | custom-call | flops 400000000 | bytes 2000000 | tf_op jit(solution)/shard_map/fourth_kernel/pallas_call | solution.py:311
  (2 shorter events, 0.0 us)
Async XLA Ops:
  0.0 5.2 %collective-permute-start.2 = (f32[128,128]{1,0:T(8,128)}, f32[128,128]{1,0:T(8,128)S(1)}, u32[]{:S(2)}, u32[]{:S(2)}) collective-permute-start(f32[128,128]{1,0:T(8,128)} %bitcast.6), channel_id=1, source_target_pairs={{0,12},{1,13},{2,14},{3,15},{4,0},{5,1},{6,2},{7,3},{8,4},{9,5},{1... | collective-permute-start | bytes 196616 | tf_op jit(solution)/shard_map/ppermute | solution.py:325
  0.1 8.3 %collective-permute-start.1 = (f32[128,128]{1,0:T(8,128)}, f32[128,128]{1,0:T(8,128)S(1)}, u32[]{:S(2)}, u32[]{:S(2)}) collective-permute-start(f32[128,128]{1,0:T(8,128)} %bitcast.7), channel_id=1, source_target_pairs={{0,8},{1,9},{2,10},{3,11},{4,12},{5,13},{6,14},{7,15},{8,0},{9,1},... | collective-permute-start | bytes 196616 | tf_op jit(solution)/shard_map/ppermute | solution.py:325
  4.3 5.5 %collective-permute-start = (f32[128,128]{1,0:T(8,128)}, f32[128,128]{1,0:T(8,128)S(1)}, u32[]{:S(2)}, u32[]{:S(2)}) collective-permute-start(f32[128,128]{1,0:T(8,128)} %bitcast.8), channel_id=1, source_target_pairs={{0,4},{1,5},{2,6},{3,7},{4,8},{5,9},{6,10},{7,11},{8,12},{9,13},{1... | collective-permute-start | bytes 196616 | tf_op jit(solution)/shard_map/ppermute | solution.py:325
  4.3 0.9 %copy-start.1 = (f32[1,128,128]{2,1,0:T(8,128)S(1)}, f32[1,128,128]{2,1,0:T(8,128)}, u32[]{:S(2)}) copy-start(f32[1,128,128]{2,1,0:T(8,128)} %param.4) | copy-start | bytes 196612
  5.2 9.2 %copy-start.2 = (s32[1,8,2]{1,2,0:T(2,128)S(1)}, s32[1,8,2]{1,2,0:T(2,128)}, u32[]{:S(2)}) copy-start(s32[1,8,2]{1,2,0:T(2,128)} %param.5) | copy-start | bytes 196
  5.2 18.8 %copy-start = (f32[512,128]{1,0:T(8,128)S(1)}, f32[512,128]{1,0:T(8,128)}, u32[]{:S(2)}) copy-start(f32[512,128]{1,0:T(8,128)} %x_ref.1) | copy-start | bytes 786436
  9.9 9.4 %collective-permute-start.5 = (f32[2,128,128]{2,1,0:T(8,128)S(1)}, f32[2,128,128]{2,1,0:T(8,128)S(1)}, u32[]{:S(2)}, u32[]{:S(2)}) collective-permute-start(f32[2,128,128]{2,1,0:T(8,128)S(1)} %get-tuple-element.16.p0), channel_id=1, source_target_pairs={{0,3},{1,0},{2,1},{3,2},{4,7},{5,4},{6,5},{7,6},{8,11},{9,8},{10,9... | collective-permute-start | bytes 393224 | tf_op jit(solution)/shard_map/ppermute | solution.py:340
  12.7 8.0 %collective-permute-start.4 = (f32[2,128,128]{2,1,0:T(8,128)S(1)}, f32[2,128,128]{2,1,0:T(8,128)S(1)}, u32[]{:S(2)}, u32[]{:S(2)}) collective-permute-start(f32[2,128,128]{2,1,0:T(8,128)S(1)} %get-tuple-element.16.p0), channel_id=1, source_target_pairs={{0,2},{1,3},{2,0},{3,1},{4,6},{5,7},{6,4},{7,5},{8,10},{9,11},{10,... | collective-permute-start | bytes 393224 | tf_op jit(solution)/shard_map/ppermute | solution.py:340
  13.5 10.5 %collective-permute-start.3 = (f32[2,128,128]{2,1,0:T(8,128)S(1)}, f32[2,128,128]{2,1,0:T(8,128)S(1)}, u32[]{:S(2)}, u32[]{:S(2)}) collective-permute-start(f32[2,128,128]{2,1,0:T(8,128)S(1)} %get-tuple-element.16.p0), channel_id=1, source_target_pairs={{0,1},{1,2},{2,3},{3,0},{4,5},{5,6},{6,7},{7,4},{8,9},{9,10},{10,1... | collective-permute-start | bytes 393224 | tf_op jit(solution)/shard_map/ppermute | solution.py:340
  14.6 19.2 %collective-permute-start.9 = (f32[2,128,128]{2,1,0:T(8,128)S(1)}, f32[2,128,128]{2,1,0:T(8,128)S(1)}, u32[]{:S(2)}, u32[]{:S(2)}) collective-permute-start(f32[2,128,128]{2,1,0:T(8,128)S(1)} %get-tuple-element.19.p0), channel_id=1, source_target_pairs={{0,3},{1,0},{2,1},{3,2},{4,7},{5,4},{6,5},{7,6},{8,11},{9,8},{10,9... | collective-permute-start | bytes 393224 | tf_op jit(solution)/shard_map/ppermute | solution.py:340
  17.0 16.9 %collective-permute-start.8 = (f32[2,128,128]{2,1,0:T(8,128)S(1)}, f32[2,128,128]{2,1,0:T(8,128)S(1)}, u32[]{:S(2)}, u32[]{:S(2)}) collective-permute-start(f32[2,128,128]{2,1,0:T(8,128)S(1)} %get-tuple-element.19.p0), channel_id=1, source_target_pairs={{0,2},{1,3},{2,0},{3,1},{4,6},{5,7},{6,4},{7,5},{8,10},{9,11},{10,... | collective-permute-start | bytes 393224 | tf_op jit(solution)/shard_map/ppermute | solution.py:340
  19.2 14.6 %collective-permute-start.7 = (f32[2,128,128]{2,1,0:T(8,128)S(1)}, f32[2,128,128]{2,1,0:T(8,128)S(1)}, u32[]{:S(2)}, u32[]{:S(2)}) collective-permute-start(f32[2,128,128]{2,1,0:T(8,128)S(1)} %get-tuple-element.19.p0), channel_id=1, source_target_pairs={{0,1},{1,2},{2,3},{3,0},{4,5},{5,6},{6,7},{7,4},{8,9},{9,10},{10,1... | collective-permute-start | bytes 393224 | tf_op jit(solution)/shard_map/ppermute | solution.py:340
  28.2 11.5 %collective-permute-start.6 = (f32[384,128]{1,0:T(8,128)S(1)}, f32[384,128]{1,0:T(8,128)S(1)}, u32[]{:S(2)}, u32[]{:S(2)}) collective-permute-start(f32[384,128]{1,0:T(8,128)S(1)} %get-tuple-element.18.own), channel_id=1, source_target_pairs={{16,0},{32,16},{48,32},{64,48},{80,64},{96,80},{112,96},{128,112},... | collective-permute-start | bytes 589832 | tf_op jit(solution)/shard_map/ppermute | solution.py:330
  34.5 13.4 %collective-permute-start.11 = (f32[3,128,128]{2,1,0:T(8,128)S(1)}, f32[3,128,128]{2,1,0:T(8,128)S(1)}, u32[]{:S(2)}, u32[]{:S(2)}) collective-permute-start(f32[3,128,128]{2,1,0:T(8,128)S(1)} %choose_kernel.1.after), channel_id=1, source_target_pairs={{0,16},{16,32},{32,48},{48,64},{64,80},{80,96},{96,112},{112,128},... | collective-permute-start | bytes 589832 | tf_op jit(solution)/shard_map/ppermute | solution.py:330
  40.9 11.1 %collective-permute-start.10 = (f32[256,128]{1,0:T(8,128)S(1)}, f32[256,128]{1,0:T(8,128)S(1)}, u32[]{:S(2)}, u32[]{:S(2)}) collective-permute-start(f32[256,128]{1,0:T(8,128)S(1)} %get-tuple-element.22), channel_id=1, source_target_pairs={{0,16},{16,32},{32,48},{48,64},{64,80},{80,96},{96,112},{112,128},... | collective-permute-start | bytes 393224 | tf_op jit(solution)/shard_map/ppermute | solution.py:330
  53.5 14.2 %collective-permute-start.12 = (f32[384,128]{1,0:T(8,128)S(1)}, f32[384,128]{1,0:T(8,128)S(1)}, u32[]{:S(2)}, u32[]{:S(2)}) collective-permute-start(f32[384,128]{1,0:T(8,128)S(1)} %get-tuple-element.25), channel_id=1, source_target_pairs={{16,32},{48,64},{80,96},{112,128},{144,160},{176,192},{208,224},{3... | collective-permute-start | bytes 589832 | tf_op jit(solution)/shard_map/ppermute | solution.py:336
  56.7 11.0 %collective-permute-start.13 = (f32[384,128]{1,0:T(8,128)S(1)}, f32[384,128]{1,0:T(8,128)S(1)}, u32[]{:S(2)}, u32[]{:S(2)}) collective-permute-start(f32[384,128]{1,0:T(8,128)S(1)} %get-tuple-element.26), channel_id=1, source_target_pairs={{0,16},{32,48},{64,80},{96,112},{128,144},{160,176},{192,208},{224... | collective-permute-start | bytes 589832 | tf_op jit(solution)/shard_map/ppermute | solution.py:336

commit v13 on v12

--- a/solution.py
+++ b/solution.py
@@ -245,6 +245,11 @@
     down[0] = block_of(scalars, held, 5, 1)
 
 
+def choose2_kernel(scalars, after, p0, p1, p2, p3, up, held):
+    gathered(scalars, (p0, p1, p2, p3), held, 1)
+    up[...] = block_of(scalars, held, 6, 0)
+
+
 def factor2_kernel(scalars, after, p0, p1, p2, p3, g2, held):
     pieces = (p0, p1, p2, p3)
     gathered(scalars, pieces, held, 1)
@@ -253,7 +258,7 @@
     stored_wholes([block_of(scalars, held, level, half) for level in (4, 5) for half in (0, 1)] + [later], g2)
 
 
-def third_kernel(scalars, low_ref, own, rest, back, after, g1, g2, low_out, top_out, far_out, near_out):
+def third_kernel(scalars, low_ref, own, rest, back, after, after2, g1, g2, low_out, top_out, far_out, near_out):
     upper = jnp.where(scalars[2] == 1, own[W : 2 * W], back[:W])
     lower = rest[:W] - dot3(split(rest[W:]), split(back[W:]))
     top, low = across(jnp.concatenate([upper, lower], axis=0), low_ref[...], once(g1, 1))
@@ -264,7 +269,7 @@
     top_out[...] = top
     settled = once(g2, 4)(top)
     odd = scalars[3] == 1
-    for at, (up, down) in enumerate(((top[:W], low[:W]), (settled[:W], low[W:]), (joined(g2, 4), top[W:]))):
+    for at, (up, down) in enumerate(((top[:W], low[:W]), (settled[:W], low[W:]))):
         far_out[at * W : (at + 1) * W] = jnp.where(odd, down, up)
         near_out[at * W : (at + 1) * W] = jnp.where(odd, up, down)
 
@@ -274,16 +279,17 @@
     stored_wholes([block_of(scalars, held, level, half) for level, half in ((6, 1), (7, 0), (7, 1))], g3)
 
 
-def factor4_kernel(after, down, g4):
-    stored_wholes([down[0], down[1], down[2]], g4)
+def factor4_kernel(after, down, up, g4):
+    stored_wholes([down[0], down[1], down[2], up[...]], g4)
 
 
 def fourth_kernel(scalars, low_ref, top_ref, far, near, g2, g3, g4, out_ref):
     last = scalars[1] == 1
     first = scalars[2] == 1
     odd = scalars[3] == 1
-    above = jnp.where(odd, near[: 2 * W], far[: 2 * W])
-    near, settled, quarter = below_rows(jnp.where(odd, far[...], near[...]))
+    above = jnp.where(odd, near[...], far[...])
+    below = jnp.where(odd, far[...], near[...])
+    near, settled, quarter = below[:W], below[W:], joined(g4, 3)
     low, moved = across_below(last, low_ref[...], near, once(g2, 3))
     above, top = across_above(first, above, top_ref[...], once(g4, 0))
     above = once(g4, 1)(above)
@@ -364,15 +370,17 @@
     (g1,) = call(factor1_kernel, (scalars, down, *near), [wholes(4)], HELD)
     low, back = call(second_kernel, (scalars, low, message, g1), [half, half])
     back = to_neighbour(back, 1)
-    (g2,) = call(factor2_kernel, (scalars, low, *far), [wholes(5)], HELD)
+    (up,) = call(choose2_kernel, (scalars, low, *far), [rows_shape(W, W)], HELD)
+    (g2,) = call(factor2_kernel, (scalars, up, *far), [wholes(5)], HELD)
+    up = to_neighbour(up, -1)
     down = to_neighbour(down, 1)
     low, top, far_out, near_out = call(
-        third_kernel, (scalars, low, own, rest, back, down, g1, g2), [half, half, three, three]
+        third_kernel, (scalars, low, own, rest, back, down, up, g1, g2), [half, half, half, half]
     )
     from_far = swapped(far_out, 1)
     from_near = swapped(near_out, 0)
     (g3,) = call(factor3_kernel, (scalars, low, *far), [wholes(3)], HELD)
-    (g4,) = call(factor4_kernel, (low, down), [wholes(3)], smem=0)
+    (g4,) = call(factor4_kernel, (low, down, up), [wholes(4)], smem=0)
     return call(
         fourth_kernel, (scalars, low, top, from_far, from_near, g2, g3, g4), [rows_shape(*eigvecs.shape)]
     )[0]

time: 70.3 us -> 73.3 us (1.043)
  the two profiles are of different devices: /device:TPU:88 before, /device:TPU:56 now
where the time goes in v13:
time: 73.3 us; the launch traced here: 73.1 us
  starting transfers between devices  39.1 us (53%)
  Pallas kernels  22.9 us (31%)
  waiting for transfers between devices  9.67 us (13%)
  local copies, waits for them, and re-layouts  1.13 us (2%)
    pallas_call x12, Pallas kernels, call(): pl.pallas_call(kernel, out_shape=tuple(shapes), in_specs=[pl.BlockSpec(me...  22.9 us
    ppermute x4, starting transfers between devices, to_neighbour(): lax.ppermute(value, 'rows', [(i, i + steps) for i in range(count) if 0 <=...  17.9 us
    ppermute x6, starting transfers between devices, along_x(): lax.ppermute(value, 'cols', [(i, i // 4 * 4 + (i + k) % 4) for i in range...  8.4 us
    ppermute x2, starting transfers between devices, swapped(): return lax.ppermute(value, 'rows', pairs + [(j, i) for i, j in pairs])  6.61 us
    ppermute x3, starting transfers between devices, shifted(): lax.ppermute(value, axis, [(i, (i + steps) % count) for i in range(count)])  6.2 us
    ppermute x6, waiting for transfers between devices, along_x(): lax.ppermute(value, 'cols', [(i, i // 4 * 4 + (i + k) % 4) for i in range...  5.5 us
    ppermute x3, waiting for transfers between devices, shifted(): lax.ppermute(value, axis, [(i, (i + steps) % count) for i in range(count)])  2.47 us
    ppermute x2, waiting for transfers between devices, swapped(): return lax.ppermute(value, 'rows', pairs + [(j, i) for i, j in pairs])  1.68 us
  transfers between devices with their start and end apart: 15, of which 5 were waited for; matrix products, arithmetic and copies ran while one was open for 0% of the time, Pallas kernels for 26%

profile of v13, /device:TPU:56, one launch (start us, length us, event | category | flops | bytes accessed | tf_op | source)
XLA Modules:
  0.0 73.1 jit_solution(15638933991498060890)
XLA Ops:
  0.0 0.1 collective-permute-start.2
  0.1 3.3 %collective-permute-start.1 = (f32[128,128]{1,0:T(8,128)}, f32[128,128]{1,0:T(8,128)S(1)}, u32[]{:S(2)}, u32[]{:S(2)}) collective-permute-start(f32[128,128]{1,0:T(8,128)} %bitcast.7), channel_id=1, source_target_pairs={{0,8},{1,9},{2,10},{3,11},{4,12},{5,13},{6,14},{7,15},{8,0},{9,1},... | collective-permute-start | bytes 196616 | tf_op jit(solution)/shard_map/ppermute | solution.py:331
  3.4 2.8 %collective-permute-start = (f32[128,128]{1,0:T(8,128)}, f32[128,128]{1,0:T(8,128)S(1)}, u32[]{:S(2)}, u32[]{:S(2)}) collective-permute-start(f32[128,128]{1,0:T(8,128)} %bitcast.8), channel_id=1, source_target_pairs={{0,4},{1,5},{2,6},{3,7},{4,8},{5,9},{6,10},{7,11},{8,12},{9,13},{1... | collective-permute-start | bytes 196616 | tf_op jit(solution)/shard_map/ppermute | solution.py:331
  6.2 0.0 copy-start.1
  6.2 0.9 %copy-done.1 = f32[1,128,128]{2,1,0:T(8,128)S(1)} copy-done((f32[1,128,128]{2,1,0:T(8,128)S(1)}, f32[1,128,128]{2,1,0:T(8,128)}, u32[]{:S(2)}) %copy-start.1) | copy-done | bytes 65560
  7.1 0.0 copy-start.2
  7.1 0.0 copy-start
  7.1 0.0 collective-permute-done.2.p3
  7.1 1.3 %collective-permute-done.1.p2 = f32[128,128]{1,0:T(8,128)S(1)} collective-permute-done((f32[128,128]{1,0:T(8,128)}, f32[128,128]{1,0:T(8,128)S(1)}, u32[]{:S(2)}, u32[]{:S(2)}) %collective-permute-start.1) | collective-permute-done | bytes 65568 | tf_op jit(solution)/shard_map/ppermute | solution.py:331
  8.4 1.2 %collective-permute-done.p1 = f32[128,128]{1,0:T(8,128)S(1)} collective-permute-done((f32[128,128]{1,0:T(8,128)}, f32[128,128]{1,0:T(8,128)S(1)}, u32[]{:S(2)}, u32[]{:S(2)}) %collective-permute-start) | collective-permute-done | bytes 65568 | tf_op jit(solution)/shard_map/ppermute | solution.py:331
  9.6 2.8 %collective-permute-start.5 = (f32[2,128,128]{2,1,0:T(8,128)S(1)}, f32[2,128,128]{2,1,0:T(8,128)S(1)}, u32[]{:S(2)}, u32[]{:S(2)}) collective-permute-start(f32[2,128,128]{2,1,0:T(8,128)S(1)} %get-tuple-element.16.p0), channel_id=1, source_target_pairs={{0,3},{1,0},{2,1},{3,2},{4,7},{5,4},{6,5},{7,6},{8,11},{9,8},{10,9... | collective-permute-start | bytes 393224 | tf_op jit(solution)/shard_map/ppermute | solution.py:346
  12.4 0.8 %collective-permute-start.4 = (f32[2,128,128]{2,1,0:T(8,128)S(1)}, f32[2,128,128]{2,1,0:T(8,128)S(1)}, u32[]{:S(2)}, u32[]{:S(2)}) collective-permute-start(f32[2,128,128]{2,1,0:T(8,128)S(1)} %get-tuple-element.16.p0), channel_id=1, source_target_pairs={{0,2},{1,3},{2,0},{3,1},{4,6},{5,7},{6,4},{7,5},{8,10},{9,11},{10,... | collective-permute-start | bytes 393224 | tf_op jit(solution)/shard_map/ppermute | solution.py:346
  13.2 0.9 %collective-permute-start.3 = (f32[2,128,128]{2,1,0:T(8,128)S(1)}, f32[2,128,128]{2,1,0:T(8,128)S(1)}, u32[]{:S(2)}, u32[]{:S(2)}) collective-permute-start(f32[2,128,128]{2,1,0:T(8,128)S(1)} %get-tuple-element.16.p0), channel_id=1, source_target_pairs={{0,1},{1,2},{2,3},{3,0},{4,5},{5,6},{6,7},{7,4},{8,9},{9,10},{10,1... | collective-permute-start | bytes 393224 | tf_op jit(solution)/shard_map/ppermute | solution.py:346
  14.1 0.0 copy-done.2
  14.1 0.1 copy.5
  14.2 0.1 reshape.6
  14.3 0.1 concatenate.3.scalars
  14.4 2.4 %collective-permute-start.9 = (f32[2,128,128]{2,1,0:T(8,128)S(1)}, f32[2,128,128]{2,1,0:T(8,128)S(1)}, u32[]{:S(2)}, u32[]{:S(2)}) collective-permute-start(f32[2,128,128]{2,1,0:T(8,128)S(1)} %get-tuple-element.19.p0), channel_id=1, source_target_pairs={{0,3},{1,0},{2,1},{3,2},{4,7},{5,4},{6,5},{7,6},{8,11},{9,8},{10,9... | collective-permute-start | bytes 393224 | tf_op jit(solution)/shard_map/ppermute | solution.py:346
  16.7 1.5 %collective-permute-start.8 = (f32[2,128,128]{2,1,0:T(8,128)S(1)}, f32[2,128,128]{2,1,0:T(8,128)S(1)}, u32[]{:S(2)}, u32[]{:S(2)}) collective-permute-start(f32[2,128,128]{2,1,0:T(8,128)S(1)} %get-tuple-element.19.p0), channel_id=1, source_target_pairs={{0,2},{1,3},{2,0},{3,1},{4,6},{5,7},{6,4},{7,5},{8,10},{9,11},{10,... | collective-permute-start | bytes 393224 | tf_op jit(solution)/shard_map/ppermute | solution.py:346
  18.3 0.0 collective-permute-done.5.p3
  18.3 0.0 collective-permute-start.7
  18.3 2.2 %collective-permute-done.4.p2 = f32[2,128,128]{2,1,0:T(8,128)S(1)} collective-permute-done((f32[2,128,128]{2,1,0:T(8,128)S(1)}, f32[2,128,128]{2,1,0:T(8,128)S(1)}, u32[]{:S(2)}, u32[]{:S(2)}) %collective-permute-start.4) | collective-permute-done | bytes 131104 | tf_op jit(solution)/shard_map/ppermute | solution.py:346
  20.4 3.3 %collective-permute-done.3.p1 = f32[2,128,128]{2,1,0:T(8,128)S(1)} collective-permute-done((f32[2,128,128]{2,1,0:T(8,128)S(1)}, f32[2,128,128]{2,1,0:T(8,128)S(1)}, u32[]{:S(2)}, u32[]{:S(2)}) %collective-permute-start.3) | collective-permute-done | bytes 131104 | tf_op jit(solution)/shard_map/ppermute | solution.py:346
  23.8 0.0 copy-done
  23.8 4.1 %first_kernel.1 = (f32[384,128]{1,0:T(8,128)S(1)}, f32[256,128]{1,0:T(8,128)S(1)}, f32[256,128]{1,0:T(8,128)S(1)}) custom-call(s32[20]{0:T(128)S(1)} %concatenate.3.scalars, f32[512,128]{1,0:T(8,128)S(1)} %copy-done, f32[2,128,128]{2,1,0:T(8,128)S(1)} %get-tuple-element.16.p0, f32[2,128,128]{2,1,0:T(8,128)S(1)} %collective-permute-done.3.p1, ...), custom_call_target="tpu_custom_call" | custom-call | flops 400000000 | bytes 2000000 | tf_op jit(solution)/shard_map/first_kernel/pallas_call | solution.py:317
  27.9 5.5 %collective-permute-start.6 = (f32[384,128]{1,0:T(8,128)S(1)}, f32[384,128]{1,0:T(8,128)S(1)}, u32[]{:S(2)}, u32[]{:S(2)}) collective-permute-start(f32[384,128]{1,0:T(8,128)S(1)} %get-tuple-element.18.own), channel_id=1, source_target_pairs={{16,0},{32,16},{48,32},{64,48},{80,64},{96,80},{112,96},{128,112},... | collective-permute-start | bytes 589832 | tf_op jit(solution)/shard_map/ppermute | solution.py:336
  33.4 0.0 collective-permute-done.9.p3
  33.4 0.0 collective-permute-done.8.p2
  33.4 0.0 collective-permute-done.7.p1
  33.4 0.6 choose_kernel.1.after
  34.0 1.9 %collective-permute-start.11 = (f32[3,128,128]{2,1,0:T(8,128)S(1)}, f32[3,128,128]{2,1,0:T(8,128)S(1)}, u32[]{:S(2)}, u32[]{:S(2)}) collective-permute-start(f32[3,128,128]{2,1,0:T(8,128)S(1)} %choose_kernel.1.after), channel_id=1, source_target_pairs={{0,16},{16,32},{32,48},{48,64},{64,80},{80,96},{96,112},{112,128},... | collective-permute-start | bytes 589832 | tf_op jit(solution)/shard_map/ppermute | solution.py:336
  36.0 3.2 %factor1_kernel.1.g1 = bf16[4,256,512]{2,1,0:T(8,128)(2,1)S(1)} custom-call(s32[20]{0:T(128)S(1)} %concatenate.3.scalars, f32[3,128,128]{2,1,0:T(8,128)S(1)} %choose_kernel.1.after, f32[2,128,128]{2,1,0:T(8,128)S(1)} %get-tuple-element.16.p0, f32[2,128,128]{2,1,0:T(8,128)S(1)} %collective-permute-done.3.p1, f32[2,128,128]{2,1,0:T(8,128)S(1)} %collective-permute-done.4.p2, ...), custom_call_target="tpu_custom_call" | custom-call | flops 400000000 | bytes 2000000 | tf_op jit(solution)/shard_map/factor1_kernel/pallas_call | solution.py:317
  39.2 0.0 collective-permute-done.6.message
  39.2 1.3 %second_kernel.1 = (f32[256,128]{1,0:T(8,128)S(1)}, f32[256,128]{1,0:T(8,128)S(1)}) custom-call(s32[20]{0:T(128)S(1)} %concatenate.3.scalars, f32[256,128]{1,0:T(8,128)S(1)} %get-tuple-element.17.after.low_ref, f32[384,128]{1,0:T(8,128)S(1)} %collective-permute-done.6.message, bf16[4,256,512]{2,1,0:T(8,128)(2,1)S(1)} %factor1_kernel.1.g1), custom_call_target="tpu_custom_call" | custom-call | flops 400000000 | bytes 2000000 | tf_op jit(solution)/shard_map/second_kernel/pallas_call | solution.py:317
  40.5 3.1 %collective-permute-start.10 = (f32[256,128]{1,0:T(8,128)S(1)}, f32[256,128]{1,0:T(8,128)S(1)}, u32[]{:S(2)}, u32[]{:S(2)}) collective-permute-start(f32[256,128]{1,0:T(8,128)S(1)} %get-tuple-element.22), channel_id=1, source_target_pairs={{0,16},{16,32},{32,48},{48,64},{64,80},{80,96},{96,112},{112,128},... | collective-permute-start | bytes 393224 | tf_op jit(solution)/shard_map/ppermute | solution.py:336
  43.6 0.6 choose2_kernel.1.after
  44.2 7.4 %collective-permute-start.12 = (f32[128,128]{1,0:T(8,128)S(1)}, f32[128,128]{1,0:T(8,128)S(1)}, u32[]{:S(2)}, u32[]{:S(2)}) collective-permute-start(f32[128,128]{1,0:T(8,128)S(1)} %choose2_kernel.1.after), channel_id=1, source_target_pairs={{16,0},{32,16},{48,32},{64,48},{80,64},{96,80},{112,96},{128,112},... | collective-permute-start | bytes 196616 | tf_op jit(solution)/shard_map/ppermute | solution.py:336
  51.6 3.7 %factor2_kernel.1.g2 = bf16[5,256,512]{2,1,0:T(8,128)(2,1)S(1)} custom-call(s32[20]{0:T(128)S(1)} %concatenate.3.scalars, f32[128,128]{1,0:T(8,128)S(1)} %choose2_kernel.1.after, f32[2,128,128]{2,1,0:T(8,128)S(1)} %get-tuple-element.19.p0, f32[2,128,128]{2,1,0:T(8,128)S(1)} %collective-permute-done.7.p1, f32[2,128,128]{2,1,0:T(8,128)S(1)} %collective-permute-done.8.p2, ...), custom_call_target="tpu_custom_call" | custom-call | flops 400000000 | bytes 2000000 | tf_op jit(solution)/shard_map/factor2_kernel/pallas_call | solution.py:317
  55.3 0.0 collective-permute-done.11.after.down
  55.3 0.0 collective-permute-done.12.after2.up
  55.3 0.0 collective-permute-done.10.back
  55.3 1.5 %third_kernel.1 = (f32[256,128]{1,0:T(8,128)S(1)}, f32[256,128]{1,0:T(8,128)S(1)}, f32[256,128]{1,0:T(8,128)S(1)}, f32[256,128]{1,0:T(8,128)S(1)}) custom-call(s32[20]{0:T(128)S(1)} %concatenate.3.scalars, f32[256,128]{1,0:T(8,128)S(1)} %get-tuple-element.20.after.low_ref, f32[384,128]{1,0:T(8,128)S(1)} %get-tuple-element.18.own, ...), custom_call_target="tpu_custom_call" | custom-call | flops 400000000 | bytes 2000000 | tf_op jit(solution)/shard_map/third_kernel/pallas_call | solution.py:317
  56.8 6.5 %collective-permute-start.13 = (f32[256,128]{1,0:T(8,128)S(1)}, f32[256,128]{1,0:T(8,128)S(1)}, u32[]{:S(2)}, u32[]{:S(2)}) collective-permute-start(f32[256,128]{1,0:T(8,128)S(1)} %get-tuple-element.25), channel_id=1, source_target_pairs={{16,32},{48,64},{80,96},{112,128},{144,160},{176,192},{208,224},{3... | collective-permute-start | bytes 393224 | tf_op jit(solution)/shard_map/ppermute | solution.py:342
  63.4 0.1 collective-permute-start.14
  63.5 2.9 %factor3_kernel.1.g3 = bf16[3,256,512]{2,1,0:T(8,128)(2,1)S(1)} custom-call(s32[20]{0:T(128)S(1)} %concatenate.3.scalars, f32[256,128]{1,0:T(8,128)S(1)} %get-tuple-element.23.after.low_ref, f32[2,128,128]{2,1,0:T(8,128)S(1)} %get-tuple-element.19.p0, f32[2,128,128]{2,1,0:T(8,128)S(1)} %collective-permute-done.7.p1, ...), custom_call_target="tpu_custom_call" | custom-call | flops 400000000 | bytes 2000000 | tf_op jit(solution)/shard_map/factor3_kernel/pallas_call | solution.py:317
  66.4 2.6 %factor4_kernel.1.g4 = bf16[4,256,512]{2,1,0:T(8,128)(2,1)S(1)} custom-call(f32[256,128]{1,0:T(8,128)S(1)} %get-tuple-element.23.after.low_ref, f32[3,128,128]{2,1,0:T(8,128)S(1)} %collective-permute-done.11.after.down, f32[128,128]{1,0:T(8,128)S(1)} %collective-permute-done.12.after2.up), custom_call_target="tpu_custom_call" | custom-call | flops 400000000 | bytes 2000000 | tf_op jit(solution)/shard_map/factor4_kernel/pallas_call | solution.py:317
  69.1 1.7 %collective-permute-done.13.far = f32[256,128]{1,0:T(8,128)S(1)} collective-permute-done((f32[256,128]{1,0:T(8,128)S(1)}, f32[256,128]{1,0:T(8,128)S(1)}, u32[]{:S(2)}, u32[]{:S(2)}) %collective-permute-start.13) | collective-permute-done | bytes 131104 | tf_op jit(solution)/shard_map/ppermute | solution.py:342
  70.7 0.0 collective-permute-done.14.near
  70.7 2.3 %fourth_kernel.1 = f32[512,128]{1,0:T(8,128)} custom-call(s32[20]{0:T(128)S(1)} %concatenate.3.scalars, f32[256,128]{1,0:T(8,128)S(1)} %get-tuple-element.23.after.low_ref, f32[256,128]{1,0:T(8,128)S(1)} %get-tuple-element.24.top_ref, f32[256,128]{1,0:T(8,128)S(1)} %collective-permute-done.13.far, f32[256,128]{1,0:T(8,128)S(1)} %collective-permute-done.14.near, ...), custom_call_target="tpu_custom_call" | custom-call | flops 400000000 | bytes 2000000 | tf_op jit(solution)/shard_map/fourth_kernel/pallas_call | solution.py:317
  (2 shorter events, 0.0 us)
Async XLA Ops:
  0.0 7.1 %collective-permute-start.2 = (f32[128,128]{1,0:T(8,128)}, f32[128,128]{1,0:T(8,128)S(1)}, u32[]{:S(2)}, u32[]{:S(2)}) collective-permute-start(f32[128,128]{1,0:T(8,128)} %bitcast.6), channel_id=1, source_target_pairs={{0,12},{1,13},{2,14},{3,15},{4,0},{5,1},{6,2},{7,3},{8,4},{9,5},{1... | collective-permute-start | bytes 196616 | tf_op jit(solution)/shard_map/ppermute | solution.py:331
  0.1 8.3 %collective-permute-start.1 = (f32[128,128]{1,0:T(8,128)}, f32[128,128]{1,0:T(8,128)S(1)}, u32[]{:S(2)}, u32[]{:S(2)}) collective-permute-start(f32[128,128]{1,0:T(8,128)} %bitcast.7), channel_id=1, source_target_pairs={{0,8},{1,9},{2,10},{3,11},{4,12},{5,13},{6,14},{7,15},{8,0},{9,1},... | collective-permute-start | bytes 196616 | tf_op jit(solution)/shard_map/ppermute | solution.py:331
  3.4 6.2 %collective-permute-start = (f32[128,128]{1,0:T(8,128)}, f32[128,128]{1,0:T(8,128)S(1)}, u32[]{:S(2)}, u32[]{:S(2)}) collective-permute-start(f32[128,128]{1,0:T(8,128)} %bitcast.8), channel_id=1, source_target_pairs={{0,4},{1,5},{2,6},{3,7},{4,8},{5,9},{6,10},{7,11},{8,12},{9,13},{1... | collective-permute-start | bytes 196616 | tf_op jit(solution)/shard_map/ppermute | solution.py:331
  6.2 0.9 %copy-start.1 = (f32[1,128,128]{2,1,0:T(8,128)S(1)}, f32[1,128,128]{2,1,0:T(8,128)}, u32[]{:S(2)}) copy-start(f32[1,128,128]{2,1,0:T(8,128)} %param.4) | copy-start | bytes 196612
  7.1 7.1 %copy-start.2 = (s32[1,8,2]{1,2,0:T(2,128)S(1)}, s32[1,8,2]{1,2,0:T(2,128)}, u32[]{:S(2)}) copy-start(s32[1,8,2]{1,2,0:T(2,128)} %param.5) | copy-start | bytes 196
  7.1 16.7 %copy-start = (f32[512,128]{1,0:T(8,128)S(1)}, f32[512,128]{1,0:T(8,128)}, u32[]{:S(2)}) copy-start(f32[512,128]{1,0:T(8,128)} %x_ref.1) | copy-start | bytes 786436
  9.6 8.7 %collective-permute-start.5 = (f32[2,128,128]{2,1,0:T(8,128)S(1)}, f32[2,128,128]{2,1,0:T(8,128)S(1)}, u32[]{:S(2)}, u32[]{:S(2)}) collective-permute-start(f32[2,128,128]{2,1,0:T(8,128)S(1)} %get-tuple-element.16.p0), channel_id=1, source_target_pairs={{0,3},{1,0},{2,1},{3,2},{4,7},{5,4},{6,5},{7,6},{8,11},{9,8},{10,9... | collective-permute-start | bytes 393224 | tf_op jit(solution)/shard_map/ppermute | solution.py:346
  12.4 8.0 %collective-permute-start.4 = (f32[2,128,128]{2,1,0:T(8,128)S(1)}, f32[2,128,128]{2,1,0:T(8,128)S(1)}, u32[]{:S(2)}, u32[]{:S(2)}) collective-permute-start(f32[2,128,128]{2,1,0:T(8,128)S(1)} %get-tuple-element.16.p0), channel_id=1, source_target_pairs={{0,2},{1,3},{2,0},{3,1},{4,6},{5,7},{6,4},{7,5},{8,10},{9,11},{10,... | collective-permute-start | bytes 393224 | tf_op jit(solution)/shard_map/ppermute | solution.py:346
  13.2 10.5 %collective-permute-start.3 = (f32[2,128,128]{2,1,0:T(8,128)S(1)}, f32[2,128,128]{2,1,0:T(8,128)S(1)}, u32[]{:S(2)}, u32[]{:S(2)}) collective-permute-start(f32[2,128,128]{2,1,0:T(8,128)S(1)} %get-tuple-element.16.p0), channel_id=1, source_target_pairs={{0,1},{1,2},{2,3},{3,0},{4,5},{5,6},{6,7},{7,4},{8,9},{9,10},{10,1... | collective-permute-start | bytes 393224 | tf_op jit(solution)/shard_map/ppermute | solution.py:346
  14.4 19.0 %collective-permute-start.9 = (f32[2,128,128]{2,1,0:T(8,128)S(1)}, f32[2,128,128]{2,1,0:T(8,128)S(1)}, u32[]{:S(2)}, u32[]{:S(2)}) collective-permute-start(f32[2,128,128]{2,1,0:T(8,128)S(1)} %get-tuple-element.19.p0), channel_id=1, source_target_pairs={{0,3},{1,0},{2,1},{3,2},{4,7},{5,4},{6,5},{7,6},{8,11},{9,8},{10,9... | collective-permute-start | bytes 393224 | tf_op jit(solution)/shard_map/ppermute | solution.py:346
  16.7 16.7 %collective-permute-start.8 = (f32[2,128,128]{2,1,0:T(8,128)S(1)}, f32[2,128,128]{2,1,0:T(8,128)S(1)}, u32[]{:S(2)}, u32[]{:S(2)}) collective-permute-start(f32[2,128,128]{2,1,0:T(8,128)S(1)} %get-tuple-element.19.p0), channel_id=1, source_target_pairs={{0,2},{1,3},{2,0},{3,1},{4,6},{5,7},{6,4},{7,5},{8,10},{9,11},{10,... | collective-permute-start | bytes 393224 | tf_op jit(solution)/shard_map/ppermute | solution.py:346
  18.3 15.2 %collective-permute-start.7 = (f32[2,128,128]{2,1,0:T(8,128)S(1)}, f32[2,128,128]{2,1,0:T(8,128)S(1)}, u32[]{:S(2)}, u32[]{:S(2)}) collective-permute-start(f32[2,128,128]{2,1,0:T(8,128)S(1)} %get-tuple-element.19.p0), channel_id=1, source_target_pairs={{0,1},{1,2},{2,3},{3,0},{4,5},{5,6},{6,7},{7,4},{8,9},{9,10},{10,1... | collective-permute-start | bytes 393224 | tf_op jit(solution)/shard_map/ppermute | solution.py:346
  27.9 11.3 %collective-permute-start.6 = (f32[384,128]{1,0:T(8,128)S(1)}, f32[384,128]{1,0:T(8,128)S(1)}, u32[]{:S(2)}, u32[]{:S(2)}) collective-permute-start(f32[384,128]{1,0:T(8,128)S(1)} %get-tuple-element.18.own), channel_id=1, source_target_pairs={{16,0},{32,16},{48,32},{64,48},{80,64},{96,80},{112,96},{128,112},... | collective-permute-start | bytes 589832 | tf_op jit(solution)/shard_map/ppermute | solution.py:336
  34.0 21.2 %collective-permute-start.11 = (f32[3,128,128]{2,1,0:T(8,128)S(1)}, f32[3,128,128]{2,1,0:T(8,128)S(1)}, u32[]{:S(2)}, u32[]{:S(2)}) collective-permute-start(f32[3,128,128]{2,1,0:T(8,128)S(1)} %choose_kernel.1.after), channel_id=1, source_target_pairs={{0,16},{16,32},{32,48},{48,64},{64,80},{80,96},{96,112},{112,128},... | collective-permute-start | bytes 589832 | tf_op jit(solution)/shard_map/ppermute | solution.py:336
  40.5 14.8 %collective-permute-start.10 = (f32[256,128]{1,0:T(8,128)S(1)}, f32[256,128]{1,0:T(8,128)S(1)}, u32[]{:S(2)}, u32[]{:S(2)}) collective-permute-start(f32[256,128]{1,0:T(8,128)S(1)} %get-tuple-element.22), channel_id=1, source_target_pairs={{0,16},{16,32},{32,48},{48,64},{64,80},{80,96},{96,112},{112,128},... | collective-permute-start | bytes 393224 | tf_op jit(solution)/shard_map/ppermute | solution.py:336
  44.2 11.1 %collective-permute-start.12 = (f32[128,128]{1,0:T(8,128)S(1)}, f32[128,128]{1,0:T(8,128)S(1)}, u32[]{:S(2)}, u32[]{:S(2)}) collective-permute-start(f32[128,128]{1,0:T(8,128)S(1)} %choose2_kernel.1.after), channel_id=1, source_target_pairs={{16,0},{32,16},{48,32},{64,48},{80,64},{96,80},{112,96},{128,112},... | collective-permute-start | bytes 196616 | tf_op jit(solution)/shard_map/ppermute | solution.py:336
  56.8 13.9 %collective-permute-start.13 = (f32[256,128]{1,0:T(8,128)S(1)}, f32[256,128]{1,0:T(8,128)S(1)}, u32[]{:S(2)}, u32[]{:S(2)}) collective-permute-start(f32[256,128]{1,0:T(8,128)S(1)} %get-tuple-element.25), channel_id=1, source_target_pairs={{16,32},{48,64},{80,96},{112,128},{144,160},{176,192},{208,224},{3... | collective-permute-start | bytes 393224 | tf_op jit(solution)/shard_map/ppermute | solution.py:342
  63.4 7.4 %collective-permute-start.14 = (f32[256,128]{1,0:T(8,128)S(1)}, f32[256,128]{1,0:T(8,128)S(1)}, u32[]{:S(2)}, u32[]{:S(2)}) collective-permute-start(f32[256,128]{1,0:T(8,128)S(1)} %get-tuple-element.26), channel_id=1, source_target_pairs={{0,16},{32,48},{64,80},{96,112},{128,144},{160,176},{192,208},{224... | collective-permute-start | bytes 393224 | tf_op jit(solution)/shard_map/ppermute | solution.py:342

commit v14 on v12

--- a/solution.py
+++ b/solution.py
@@ -360,8 +360,8 @@
     three = rows_shape(3 * W, W)
     own, low, rest = call(first_kernel, (scalars, eigvecs, *near), [three, half, half], HELD)
     message = to_neighbour(own, -1)
-    (down,) = call(choose_kernel, (scalars, low, *far), [rows_shape(3, W, W)], HELD)
-    (g1,) = call(factor1_kernel, (scalars, down, *near), [wholes(4)], HELD)
+    (g1,) = call(factor1_kernel, (scalars, low, *near), [wholes(4)], HELD)
+    (down,) = call(choose_kernel, (scalars, g1, *far), [rows_shape(3, W, W)], HELD)
     low, back = call(second_kernel, (scalars, low, message, g1), [half, half])
     back = to_neighbour(back, 1)
     (g2,) = call(factor2_kernel, (scalars, low, *far), [wholes(5)], HELD)

time: 70.3 us -> 72 us (1.024)
  the two profiles are of different devices: /device:TPU:88 before, /device:TPU:56 now
where the time goes in v14:
time: 72 us; the launch traced here: 71.7 us
  starting transfers between devices  27.6 us (38%)
  Pallas kernels  22.1 us (31%)
  waiting for transfers between devices  20.7 us (29%)
  local copies, waits for them, and re-layouts  1.13 us (2%)
    pallas_call x11, Pallas kernels, call(): pl.pallas_call(kernel, out_shape=tuple(shapes), in_specs=[pl.BlockSpec(me...  22.1 us
    ppermute x3, starting transfers between devices, to_neighbour(): lax.ppermute(value, 'rows', [(i, i + steps) for i in range(count) if 0 <=...  10.7 us
    ppermute x6, starting transfers between devices, along_x(): lax.ppermute(value, 'cols', [(i, i // 4 * 4 + (i + k) % 4) for i in range...  8.4 us
    ppermute x3, waiting for transfers between devices, to_neighbour(): lax.ppermute(value, 'rows', [(i, i + steps) for i in range(count) if 0 <=...  6.53 us
    ppermute x2, waiting for transfers between devices, swapped(): return lax.ppermute(value, 'rows', pairs + [(j, i) for i, j in pairs])  6.22 us
    ppermute x3, starting transfers between devices, shifted(): lax.ppermute(value, axis, [(i, (i + steps) % count) for i in range(count)])  6.2 us
    ppermute x6, waiting for transfers between devices, along_x(): lax.ppermute(value, 'cols', [(i, i // 4 * 4 + (i + k) % 4) for i in range...  5.5 us
    ppermute x3, waiting for transfers between devices, shifted(): lax.ppermute(value, axis, [(i, (i + steps) % count) for i in range(count)])  2.47 us
  transfers between devices with their start and end apart: 14, of which 7 were waited for; matrix products, arithmetic and copies ran while one was open for 0% of the time, Pallas kernels for 25%

profile of v14, /device:TPU:56, one launch (start us, length us, event | category | flops | bytes accessed | tf_op | source)
XLA Modules:
  0.0 71.7 jit_solution(17589197968248366506)
XLA Ops:
  0.0 0.1 collective-permute-start.2
  0.1 3.3 %collective-permute-start.1 = (f32[128,128]{1,0:T(8,128)}, f32[128,128]{1,0:T(8,128)S(1)}, u32[]{:S(2)}, u32[]{:S(2)}) collective-permute-start(f32[128,128]{1,0:T(8,128)} %bitcast.7), channel_id=1, source_target_pairs={{0,8},{1,9},{2,10},{3,11},{4,12},{5,13},{6,14},{7,15},{8,0},{9,1},... | collective-permute-start | bytes 196616 | tf_op jit(solution)/shard_map/ppermute | solution.py:325
  3.4 2.8 %collective-permute-start = (f32[128,128]{1,0:T(8,128)}, f32[128,128]{1,0:T(8,128)S(1)}, u32[]{:S(2)}, u32[]{:S(2)}) collective-permute-start(f32[128,128]{1,0:T(8,128)} %bitcast.8), channel_id=1, source_target_pairs={{0,4},{1,5},{2,6},{3,7},{4,8},{5,9},{6,10},{7,11},{8,12},{9,13},{1... | collective-permute-start | bytes 196616 | tf_op jit(solution)/shard_map/ppermute | solution.py:325
  6.2 0.0 copy-start.1
  6.2 0.9 %copy-done.1 = f32[1,128,128]{2,1,0:T(8,128)S(1)} copy-done((f32[1,128,128]{2,1,0:T(8,128)S(1)}, f32[1,128,128]{2,1,0:T(8,128)}, u32[]{:S(2)}) %copy-start.1) | copy-done | bytes 65560
  7.1 0.0 copy-start.2
  7.1 0.0 copy-start
  7.1 0.0 collective-permute-done.2.p3
  7.1 1.3 %collective-permute-done.1.p2 = f32[128,128]{1,0:T(8,128)S(1)} collective-permute-done((f32[128,128]{1,0:T(8,128)}, f32[128,128]{1,0:T(8,128)S(1)}, u32[]{:S(2)}, u32[]{:S(2)}) %collective-permute-start.1) | collective-permute-done | bytes 65568 | tf_op jit(solution)/shard_map/ppermute | solution.py:325
  8.4 1.2 %collective-permute-done.p1 = f32[128,128]{1,0:T(8,128)S(1)} collective-permute-done((f32[128,128]{1,0:T(8,128)}, f32[128,128]{1,0:T(8,128)S(1)}, u32[]{:S(2)}, u32[]{:S(2)}) %collective-permute-start) | collective-permute-done | bytes 65568 | tf_op jit(solution)/shard_map/ppermute | solution.py:325
  9.6 2.8 %collective-permute-start.5 = (f32[2,128,128]{2,1,0:T(8,128)S(1)}, f32[2,128,128]{2,1,0:T(8,128)S(1)}, u32[]{:S(2)}, u32[]{:S(2)}) collective-permute-start(f32[2,128,128]{2,1,0:T(8,128)S(1)} %get-tuple-element.16.p0), channel_id=1, source_target_pairs={{0,3},{1,0},{2,1},{3,2},{4,7},{5,4},{6,5},{7,6},{8,11},{9,8},{10,9... | collective-permute-start | bytes 393224 | tf_op jit(solution)/shard_map/ppermute | solution.py:340
  12.4 0.8 %collective-permute-start.4 = (f32[2,128,128]{2,1,0:T(8,128)S(1)}, f32[2,128,128]{2,1,0:T(8,128)S(1)}, u32[]{:S(2)}, u32[]{:S(2)}) collective-permute-start(f32[2,128,128]{2,1,0:T(8,128)S(1)} %get-tuple-element.16.p0), channel_id=1, source_target_pairs={{0,2},{1,3},{2,0},{3,1},{4,6},{5,7},{6,4},{7,5},{8,10},{9,11},{10,... | collective-permute-start | bytes 393224 | tf_op jit(solution)/shard_map/ppermute | solution.py:340
  13.2 0.9 %collective-permute-start.3 = (f32[2,128,128]{2,1,0:T(8,128)S(1)}, f32[2,128,128]{2,1,0:T(8,128)S(1)}, u32[]{:S(2)}, u32[]{:S(2)}) collective-permute-start(f32[2,128,128]{2,1,0:T(8,128)S(1)} %get-tuple-element.16.p0), channel_id=1, source_target_pairs={{0,1},{1,2},{2,3},{3,0},{4,5},{5,6},{6,7},{7,4},{8,9},{9,10},{10,1... | collective-permute-start | bytes 393224 | tf_op jit(solution)/shard_map/ppermute | solution.py:340
  14.1 0.0 copy-done.2
  14.1 0.1 copy.5
  14.2 0.1 reshape.6
  14.3 0.1 concatenate.3.scalars
  14.4 2.4 %collective-permute-start.10 = (f32[2,128,128]{2,1,0:T(8,128)S(1)}, f32[2,128,128]{2,1,0:T(8,128)S(1)}, u32[]{:S(2)}, u32[]{:S(2)}) collective-permute-start(f32[2,128,128]{2,1,0:T(8,128)S(1)} %get-tuple-element.22.p0), channel_id=1, source_target_pairs={{0,3},{1,0},{2,1},{3,2},{4,7},{5,4},{6,5},{7,6},{8,11},{9,8},{10,9... | collective-permute-start | bytes 393224 | tf_op jit(solution)/shard_map/ppermute | solution.py:340
  16.7 1.5 %collective-permute-start.9 = (f32[2,128,128]{2,1,0:T(8,128)S(1)}, f32[2,128,128]{2,1,0:T(8,128)S(1)}, u32[]{:S(2)}, u32[]{:S(2)}) collective-permute-start(f32[2,128,128]{2,1,0:T(8,128)S(1)} %get-tuple-element.22.p0), channel_id=1, source_target_pairs={{0,2},{1,3},{2,0},{3,1},{4,6},{5,7},{6,4},{7,5},{8,10},{9,11},{10,... | collective-permute-start | bytes 393224 | tf_op jit(solution)/shard_map/ppermute | solution.py:340
  18.3 0.0 collective-permute-done.5.p3
  18.3 0.0 collective-permute-start.8
  18.3 2.2 %collective-permute-done.4.p2 = f32[2,128,128]{2,1,0:T(8,128)S(1)} collective-permute-done((f32[2,128,128]{2,1,0:T(8,128)S(1)}, f32[2,128,128]{2,1,0:T(8,128)S(1)}, u32[]{:S(2)}, u32[]{:S(2)}) %collective-permute-start.4) | collective-permute-done | bytes 131104 | tf_op jit(solution)/shard_map/ppermute | solution.py:340
  20.4 3.3 %collective-permute-done.3.p1 = f32[2,128,128]{2,1,0:T(8,128)S(1)} collective-permute-done((f32[2,128,128]{2,1,0:T(8,128)S(1)}, f32[2,128,128]{2,1,0:T(8,128)S(1)}, u32[]{:S(2)}, u32[]{:S(2)}) %collective-permute-start.3) | collective-permute-done | bytes 131104 | tf_op jit(solution)/shard_map/ppermute | solution.py:340
  23.8 0.0 copy-done
  23.8 4.1 %first_kernel.1 = (f32[384,128]{1,0:T(8,128)S(1)}, f32[256,128]{1,0:T(8,128)S(1)}, f32[256,128]{1,0:T(8,128)S(1)}) custom-call(s32[20]{0:T(128)S(1)} %concatenate.3.scalars, f32[512,128]{1,0:T(8,128)S(1)} %copy-done, f32[2,128,128]{2,1,0:T(8,128)S(1)} %get-tuple-element.16.p0, f32[2,128,128]{2,1,0:T(8,128)S(1)} %collective-permute-done.3.p1, ...), custom_call_target="tpu_custom_call" | custom-call | flops 400000000 | bytes 2000000 | tf_op jit(solution)/shard_map/first_kernel/pallas_call | solution.py:311
  27.9 5.5 %collective-permute-start.6 = (f32[384,128]{1,0:T(8,128)S(1)}, f32[384,128]{1,0:T(8,128)S(1)}, u32[]{:S(2)}, u32[]{:S(2)}) collective-permute-start(f32[384,128]{1,0:T(8,128)S(1)} %get-tuple-element.18.own), channel_id=1, source_target_pairs={{16,0},{32,16},{48,32},{64,48},{80,64},{96,80},{112,96},{128,112},... | collective-permute-start | bytes 589832 | tf_op jit(solution)/shard_map/ppermute | solution.py:330
  33.4 3.2 %factor1_kernel.1.g1.after = bf16[4,256,512]{2,1,0:T(8,128)(2,1)S(1)} custom-call(s32[20]{0:T(128)S(1)} %concatenate.3.scalars, f32[256,128]{1,0:T(8,128)S(1)} %get-tuple-element.17.after.low_ref, f32[2,128,128]{2,1,0:T(8,128)S(1)} %get-tuple-element.16.p0, f32[2,128,128]{2,1,0:T(8,128)S(1)} %collective-permute-done.3.p1, ...), custom_call_target="tpu_custom_call" | custom-call | flops 400000000 | bytes 2000000 | tf_op jit(solution)/shard_map/factor1_kernel/pallas_call | solution.py:311
  36.6 0.0 collective-permute-done.10.p3
  36.6 0.0 collective-permute-done.9.p2
  36.6 0.0 collective-permute-done.8.p1
  36.7 0.6 choose_kernel.1
  37.3 1.9 %collective-permute-start.11 = (f32[3,128,128]{2,1,0:T(8,128)S(1)}, f32[3,128,128]{2,1,0:T(8,128)S(1)}, u32[]{:S(2)}, u32[]{:S(2)}) collective-permute-start(f32[3,128,128]{2,1,0:T(8,128)S(1)} %choose_kernel.1), channel_id=1, source_target_pairs={{0,16},{16,32},{32,48},{48,64},{64,80},{80,96},{96,112},{112,128},... | collective-permute-start | bytes 589832 | tf_op jit(solution)/shard_map/ppermute | solution.py:330
  39.2 0.0 collective-permute-done.6.message
  39.2 1.3 %second_kernel.1 = (f32[256,128]{1,0:T(8,128)S(1)}, f32[256,128]{1,0:T(8,128)S(1)}) custom-call(s32[20]{0:T(128)S(1)} %concatenate.3.scalars, f32[256,128]{1,0:T(8,128)S(1)} %get-tuple-element.17.after.low_ref, f32[384,128]{1,0:T(8,128)S(1)} %collective-permute-done.6.message, bf16[4,256,512]{2,1,0:T(8,128)(2,1)S(1)} %factor1_kernel.1.g1.after), custom_call_target="tpu_custom_call" | custom-call | flops 400000000 | bytes 2000000 | tf_op jit(solution)/shard_map/second_kernel/pallas_call | solution.py:311
  40.5 3.3 %collective-permute-start.7 = (f32[256,128]{1,0:T(8,128)S(1)}, f32[256,128]{1,0:T(8,128)S(1)}, u32[]{:S(2)}, u32[]{:S(2)}) collective-permute-start(f32[256,128]{1,0:T(8,128)S(1)} %get-tuple-element.21), channel_id=1, source_target_pairs={{0,16},{16,32},{32,48},{48,64},{64,80},{80,96},{96,112},{112,128},... | collective-permute-start | bytes 393224 | tf_op jit(solution)/shard_map/ppermute | solution.py:330
  43.8 3.7 %factor2_kernel.1.g2 = bf16[5,256,512]{2,1,0:T(8,128)(2,1)S(1)} custom-call(s32[20]{0:T(128)S(1)} %concatenate.3.scalars, f32[256,128]{1,0:T(8,128)S(1)} %get-tuple-element.19.after.low_ref, f32[2,128,128]{2,1,0:T(8,128)S(1)} %get-tuple-element.22.p0, f32[2,128,128]{2,1,0:T(8,128)S(1)} %collective-permute-done.8.p1, ...), custom_call_target="tpu_custom_call" | custom-call | flops 400000000 | bytes 2000000 | tf_op jit(solution)/shard_map/factor2_kernel/pallas_call | solution.py:311
  47.5 3.7 %collective-permute-done.11.after.down = f32[3,128,128]{2,1,0:T(8,128)S(1)} collective-permute-done((f32[3,128,128]{2,1,0:T(8,128)S(1)}, f32[3,128,128]{2,1,0:T(8,128)S(1)}, u32[]{:S(2)}, u32[]{:S(2)}) %collective-permute-start.11) | collective-permute-done | bytes 196640 | tf_op jit(solution)/shard_map/ppermute | solution.py:330
  51.2 2.8 %collective-permute-done.7.back = f32[256,128]{1,0:T(8,128)S(1)} collective-permute-done((f32[256,128]{1,0:T(8,128)S(1)}, f32[256,128]{1,0:T(8,128)S(1)}, u32[]{:S(2)}, u32[]{:S(2)}) %collective-permute-start.7) | collective-permute-done | bytes 131104 | tf_op jit(solution)/shard_map/ppermute | solution.py:330
  54.0 1.5 %third_kernel.1 = (f32[256,128]{1,0:T(8,128)S(1)}, f32[256,128]{1,0:T(8,128)S(1)}, f32[384,128]{1,0:T(8,128)S(1)}, f32[384,128]{1,0:T(8,128)S(1)}) custom-call(s32[20]{0:T(128)S(1)} %concatenate.3.scalars, f32[256,128]{1,0:T(8,128)S(1)} %get-tuple-element.19.after.low_ref, f32[384,128]{1,0:T(8,128)S(1)} %get-tuple-element.18.own, ...), custom_call_target="tpu_custom_call" | custom-call | flops 400000000 | bytes 2000000 | tf_op jit(solution)/shard_map/third_kernel/pallas_call | solution.py:311
  55.5 1.9 %collective-permute-start.12 = (f32[384,128]{1,0:T(8,128)S(1)}, f32[384,128]{1,0:T(8,128)S(1)}, u32[]{:S(2)}, u32[]{:S(2)}) collective-permute-start(f32[384,128]{1,0:T(8,128)S(1)} %get-tuple-element.25), channel_id=1, source_target_pairs={{16,32},{48,64},{80,96},{112,128},{144,160},{176,192},{208,224},{3... | collective-permute-start | bytes 589832 | tf_op jit(solution)/shard_map/ppermute | solution.py:336
  57.4 0.4 collective-permute-start.13
  57.8 2.9 %factor3_kernel.1.g3 = bf16[3,256,512]{2,1,0:T(8,128)(2,1)S(1)} custom-call(s32[20]{0:T(128)S(1)} %concatenate.3.scalars, f32[256,128]{1,0:T(8,128)S(1)} %get-tuple-element.23.after.low_ref, f32[2,128,128]{2,1,0:T(8,128)S(1)} %get-tuple-element.22.p0, f32[2,128,128]{2,1,0:T(8,128)S(1)} %collective-permute-done.8.p1, ...), custom_call_target="tpu_custom_call" | custom-call | flops 400000000 | bytes 2000000 | tf_op jit(solution)/shard_map/factor3_kernel/pallas_call | solution.py:311
  60.8 2.4 %factor4_kernel.1.g4 = bf16[3,256,512]{2,1,0:T(8,128)(2,1)S(1)} custom-call(f32[256,128]{1,0:T(8,128)S(1)} %get-tuple-element.23.after.low_ref, f32[3,128,128]{2,1,0:T(8,128)S(1)} %collective-permute-done.11.after.down), custom_call_target="tpu_custom_call" | custom-call | flops 400000000 | bytes 2000000 | tf_op jit(solution)/shard_map/factor4_kernel/pallas_call | solution.py:311
  63.2 6.2 %collective-permute-done.12.far = f32[384,128]{1,0:T(8,128)S(1)} collective-permute-done((f32[384,128]{1,0:T(8,128)S(1)}, f32[384,128]{1,0:T(8,128)S(1)}, u32[]{:S(2)}, u32[]{:S(2)}) %collective-permute-start.12) | collective-permute-done | bytes 196640 | tf_op jit(solution)/shard_map/ppermute | solution.py:336
  69.4 0.0 collective-permute-done.13.near
  69.4 2.3 %fourth_kernel.1 = f32[512,128]{1,0:T(8,128)} custom-call(s32[20]{0:T(128)S(1)} %concatenate.3.scalars, f32[256,128]{1,0:T(8,128)S(1)} %get-tuple-element.23.after.low_ref, f32[256,128]{1,0:T(8,128)S(1)} %get-tuple-element.24.top_ref, f32[384,128]{1,0:T(8,128)S(1)} %collective-permute-done.12.far, f32[384,128]{1,0:T(8,128)S(1)} %collective-permute-done.13.near, ...), custom_call_target="tpu_custom_call" | custom-call | flops 400000000 | bytes 2000000 | tf_op jit(solution)/shard_map/fourth_kernel/pallas_call | solution.py:311
  (2 shorter events, 0.0 us)
Async XLA Ops:
  0.0 7.1 %collective-permute-start.2 = (f32[128,128]{1,0:T(8,128)}, f32[128,128]{1,0:T(8,128)S(1)}, u32[]{:S(2)}, u32[]{:S(2)}) collective-permute-start(f32[128,128]{1,0:T(8,128)} %bitcast.6), channel_id=1, source_target_pairs={{0,12},{1,13},{2,14},{3,15},{4,0},{5,1},{6,2},{7,3},{8,4},{9,5},{1... | collective-permute-start | bytes 196616 | tf_op jit(solution)/shard_map/ppermute | solution.py:325
  0.1 8.3 %collective-permute-start.1 = (f32[128,128]{1,0:T(8,128)}, f32[128,128]{1,0:T(8,128)S(1)}, u32[]{:S(2)}, u32[]{:S(2)}) collective-permute-start(f32[128,128]{1,0:T(8,128)} %bitcast.7), channel_id=1, source_target_pairs={{0,8},{1,9},{2,10},{3,11},{4,12},{5,13},{6,14},{7,15},{8,0},{9,1},... | collective-permute-start | bytes 196616 | tf_op jit(solution)/shard_map/ppermute | solution.py:325
  3.4 6.2 %collective-permute-start = (f32[128,128]{1,0:T(8,128)}, f32[128,128]{1,0:T(8,128)S(1)}, u32[]{:S(2)}, u32[]{:S(2)}) collective-permute-start(f32[128,128]{1,0:T(8,128)} %bitcast.8), channel_id=1, source_target_pairs={{0,4},{1,5},{2,6},{3,7},{4,8},{5,9},{6,10},{7,11},{8,12},{9,13},{1... | collective-permute-start | bytes 196616 | tf_op jit(solution)/shard_map/ppermute | solution.py:325
  6.2 0.9 %copy-start.1 = (f32[1,128,128]{2,1,0:T(8,128)S(1)}, f32[1,128,128]{2,1,0:T(8,128)}, u32[]{:S(2)}) copy-start(f32[1,128,128]{2,1,0:T(8,128)} %param.4) | copy-start | bytes 196612
  7.1 7.1 %copy-start.2 = (s32[1,8,2]{1,2,0:T(2,128)S(1)}, s32[1,8,2]{1,2,0:T(2,128)}, u32[]{:S(2)}) copy-start(s32[1,8,2]{1,2,0:T(2,128)} %param.5) | copy-start | bytes 196
  7.1 16.7 %copy-start = (f32[512,128]{1,0:T(8,128)S(1)}, f32[512,128]{1,0:T(8,128)}, u32[]{:S(2)}) copy-start(f32[512,128]{1,0:T(8,128)} %x_ref.1) | copy-start | bytes 786436
  9.6 8.7 %collective-permute-start.5 = (f32[2,128,128]{2,1,0:T(8,128)S(1)}, f32[2,128,128]{2,1,0:T(8,128)S(1)}, u32[]{:S(2)}, u32[]{:S(2)}) collective-permute-start(f32[2,128,128]{2,1,0:T(8,128)S(1)} %get-tuple-element.16.p0), channel_id=1, source_target_pairs={{0,3},{1,0},{2,1},{3,2},{4,7},{5,4},{6,5},{7,6},{8,11},{9,8},{10,9... | collective-permute-start | bytes 393224 | tf_op jit(solution)/shard_map/ppermute | solution.py:340
  12.4 8.0 %collective-permute-start.4 = (f32[2,128,128]{2,1,0:T(8,128)S(1)}, f32[2,128,128]{2,1,0:T(8,128)S(1)}, u32[]{:S(2)}, u32[]{:S(2)}) collective-permute-start(f32[2,128,128]{2,1,0:T(8,128)S(1)} %get-tuple-element.16.p0), channel_id=1, source_target_pairs={{0,2},{1,3},{2,0},{3,1},{4,6},{5,7},{6,4},{7,5},{8,10},{9,11},{10,... | collective-permute-start | bytes 393224 | tf_op jit(solution)/shard_map/ppermute | solution.py:340
  13.2 10.5 %collective-permute-start.3 = (f32[2,128,128]{2,1,0:T(8,128)S(1)}, f32[2,128,128]{2,1,0:T(8,128)S(1)}, u32[]{:S(2)}, u32[]{:S(2)}) collective-permute-start(f32[2,128,128]{2,1,0:T(8,128)S(1)} %get-tuple-element.16.p0), channel_id=1, source_target_pairs={{0,1},{1,2},{2,3},{3,0},{4,5},{5,6},{6,7},{7,4},{8,9},{9,10},{10,1... | collective-permute-start | bytes 393224 | tf_op jit(solution)/shard_map/ppermute | solution.py:340
  14.4 22.2 %collective-permute-start.10 = (f32[2,128,128]{2,1,0:T(8,128)S(1)}, f32[2,128,128]{2,1,0:T(8,128)S(1)}, u32[]{:S(2)}, u32[]{:S(2)}) collective-permute-start(f32[2,128,128]{2,1,0:T(8,128)S(1)} %get-tuple-element.22.p0), channel_id=1, source_target_pairs={{0,3},{1,0},{2,1},{3,2},{4,7},{5,4},{6,5},{7,6},{8,11},{9,8},{10,9... | collective-permute-start | bytes 393224 | tf_op jit(solution)/shard_map/ppermute | solution.py:340
  16.7 19.9 %collective-permute-start.9 = (f32[2,128,128]{2,1,0:T(8,128)S(1)}, f32[2,128,128]{2,1,0:T(8,128)S(1)}, u32[]{:S(2)}, u32[]{:S(2)}) collective-permute-start(f32[2,128,128]{2,1,0:T(8,128)S(1)} %get-tuple-element.22.p0), channel_id=1, source_target_pairs={{0,2},{1,3},{2,0},{3,1},{4,6},{5,7},{6,4},{7,5},{8,10},{9,11},{10,... | collective-permute-start | bytes 393224 | tf_op jit(solution)/shard_map/ppermute | solution.py:340
  18.3 18.4 %collective-permute-start.8 = (f32[2,128,128]{2,1,0:T(8,128)S(1)}, f32[2,128,128]{2,1,0:T(8,128)S(1)}, u32[]{:S(2)}, u32[]{:S(2)}) collective-permute-start(f32[2,128,128]{2,1,0:T(8,128)S(1)} %get-tuple-element.22.p0), channel_id=1, source_target_pairs={{0,1},{1,2},{2,3},{3,0},{4,5},{5,6},{6,7},{7,4},{8,9},{9,10},{10,1... | collective-permute-start | bytes 393224 | tf_op jit(solution)/shard_map/ppermute | solution.py:340
  27.9 11.3 %collective-permute-start.6 = (f32[384,128]{1,0:T(8,128)S(1)}, f32[384,128]{1,0:T(8,128)S(1)}, u32[]{:S(2)}, u32[]{:S(2)}) collective-permute-start(f32[384,128]{1,0:T(8,128)S(1)} %get-tuple-element.18.own), channel_id=1, source_target_pairs={{16,0},{32,16},{48,32},{64,48},{80,64},{96,80},{112,96},{128,112},... | collective-permute-start | bytes 589832 | tf_op jit(solution)/shard_map/ppermute | solution.py:330
  37.3 13.9 %collective-permute-start.11 = (f32[3,128,128]{2,1,0:T(8,128)S(1)}, f32[3,128,128]{2,1,0:T(8,128)S(1)}, u32[]{:S(2)}, u32[]{:S(2)}) collective-permute-start(f32[3,128,128]{2,1,0:T(8,128)S(1)} %choose_kernel.1), channel_id=1, source_target_pairs={{0,16},{16,32},{32,48},{48,64},{64,80},{80,96},{96,112},{112,128},... | collective-permute-start | bytes 589832 | tf_op jit(solution)/shard_map/ppermute | solution.py:330
  40.5 13.5 %collective-permute-start.7 = (f32[256,128]{1,0:T(8,128)S(1)}, f32[256,128]{1,0:T(8,128)S(1)}, u32[]{:S(2)}, u32[]{:S(2)}) collective-permute-start(f32[256,128]{1,0:T(8,128)S(1)} %get-tuple-element.21), channel_id=1, source_target_pairs={{0,16},{16,32},{32,48},{48,64},{64,80},{80,96},{96,112},{112,128},... | collective-permute-start | bytes 393224 | tf_op jit(solution)/shard_map/ppermute | solution.py:330
  55.5 13.9 %collective-permute-start.12 = (f32[384,128]{1,0:T(8,128)S(1)}, f32[384,128]{1,0:T(8,128)S(1)}, u32[]{:S(2)}, u32[]{:S(2)}) collective-permute-start(f32[384,128]{1,0:T(8,128)S(1)} %get-tuple-element.25), channel_id=1, source_target_pairs={{16,32},{48,64},{80,96},{112,128},{144,160},{176,192},{208,224},{3... | collective-permute-start | bytes 589832 | tf_op jit(solution)/shard_map/ppermute | solution.py:336
  57.4 12.0 %collective-permute-start.13 = (f32[384,128]{1,0:T(8,128)S(1)}, f32[384,128]{1,0:T(8,128)S(1)}, u32[]{:S(2)}, u32[]{:S(2)}) collective-permute-start(f32[384,128]{1,0:T(8,128)S(1)} %get-tuple-element.26), channel_id=1, source_target_pairs={{0,16},{32,48},{64,80},{96,112},{128,144},{160,176},{192,208},{224... | collective-permute-start | bytes 589832 | tf_op jit(solution)/shard_map/ppermute | solution.py:336

commit v15 on v12

--- a/solution.py
+++ b/solution.py
@@ -188,6 +188,10 @@
     kept[...] = piece[...]
 
 
+def pass_kernel(after, value, passed):
+    passed[...] = value[...]
+
+
 def order_kernel(plane, p0, p1, p2, p3, near, far, held):
     for k, piece in enumerate((p0, p1, p2, p3)):
         held[(plane[0] + 4 - k) % 4] = piece[...]
@@ -355,6 +359,7 @@
     pair = rows_shape(2, W, W)
     near, far = call(order_kernel, (plane.reshape(1), held, *planes[1:]), [pair, pair], HELD)
     near = along_x(near)
+    (far,) = call(pass_kernel, (near[3], far), [pair], smem=0)
     far = along_x(far)
     three = rows_shape(3 * W, W)
     three = rows_shape(3 * W, W)

time: 70.3 us -> 69.6 us (0.990)
  the two profiles are of different devices: /device:TPU:88 before, /device:TPU:56 now
where the time goes in v15:
time: 69.6 us; the launch traced here: 69.4 us
  starting transfers between devices  32.7 us (47%)
  Pallas kernels  22.1 us (32%)
  waiting for transfers between devices  13.3 us (19%)
  local copies, waits for them, and re-layouts  1.13 us (2%)
    pallas_call x12, Pallas kernels, call(): pl.pallas_call(kernel, out_shape=tuple(shapes), in_specs=[pl.BlockSpec(me...  22.1 us
    ppermute x3, starting transfers between devices, to_neighbour(): lax.ppermute(value, 'rows', [(i, i + steps) for i in range(count) if 0 <=...  12.5 us
    ppermute x6, starting transfers between devices, along_x(): lax.ppermute(value, 'cols', [(i, i // 4 * 4 + (i + k) % 4) for i in range...  9.21 us
    ppermute x3, starting transfers between devices, shifted(): lax.ppermute(value, axis, [(i, (i + steps) % count) for i in range(count)])  6.2 us
    ppermute x2, starting transfers between devices, swapped(): return lax.ppermute(value, 'rows', pairs + [(j, i) for i, j in pairs])  4.77 us
    ppermute x2, waiting for transfers between devices, swapped(): return lax.ppermute(value, 'rows', pairs + [(j, i) for i, j in pairs])  4.6 us
    ppermute x6, waiting for transfers between devices, along_x(): lax.ppermute(value, 'cols', [(i, i // 4 * 4 + (i + k) % 4) for i in range...  3.13 us
    ppermute x3, waiting for transfers between devices, to_neighbour(): lax.ppermute(value, 'rows', [(i, i + steps) for i in range(count) if 0 <=...  3.07 us
  transfers between devices with their start and end apart: 14, of which 5 were waited for; matrix products, arithmetic and copies ran while one was open for 0% of the time, Pallas kernels for 26%

profile of v15, /device:TPU:56, one launch (start us, length us, event | category | flops | bytes accessed | tf_op | source)
XLA Modules:
  0.0 69.4 jit_solution(1420238789355168970)
XLA Ops:
  0.0 0.1 collective-permute-start.2
  0.1 3.3 %collective-permute-start.1 = (f32[128,128]{1,0:T(8,128)}, f32[128,128]{1,0:T(8,128)S(1)}, u32[]{:S(2)}, u32[]{:S(2)}) collective-permute-start(f32[128,128]{1,0:T(8,128)} %bitcast.7), channel_id=1, source_target_pairs={{0,8},{1,9},{2,10},{3,11},{4,12},{5,13},{6,14},{7,15},{8,0},{9,1},... | collective-permute-start | bytes 196616 | tf_op jit(solution)/shard_map/ppermute | solution.py:329
  3.4 2.8 %collective-permute-start = (f32[128,128]{1,0:T(8,128)}, f32[128,128]{1,0:T(8,128)S(1)}, u32[]{:S(2)}, u32[]{:S(2)}) collective-permute-start(f32[128,128]{1,0:T(8,128)} %bitcast.8), channel_id=1, source_target_pairs={{0,4},{1,5},{2,6},{3,7},{4,8},{5,9},{6,10},{7,11},{8,12},{9,13},{1... | collective-permute-start | bytes 196616 | tf_op jit(solution)/shard_map/ppermute | solution.py:329
  6.2 0.0 copy-start.1
  6.2 0.9 %copy-done.1 = f32[1,128,128]{2,1,0:T(8,128)S(1)} copy-done((f32[1,128,128]{2,1,0:T(8,128)S(1)}, f32[1,128,128]{2,1,0:T(8,128)}, u32[]{:S(2)}) %copy-start.1) | copy-done | bytes 65560
  7.1 0.0 copy-start.2
  7.1 0.0 collective-permute-done.2.p3
  7.1 1.3 %collective-permute-done.1.p2 = f32[128,128]{1,0:T(8,128)S(1)} collective-permute-done((f32[128,128]{1,0:T(8,128)}, f32[128,128]{1,0:T(8,128)S(1)}, u32[]{:S(2)}, u32[]{:S(2)}) %collective-permute-start.1) | collective-permute-done | bytes 65568 | tf_op jit(solution)/shard_map/ppermute | solution.py:329
  8.4 1.2 %collective-permute-done.p1 = f32[128,128]{1,0:T(8,128)S(1)} collective-permute-done((f32[128,128]{1,0:T(8,128)}, f32[128,128]{1,0:T(8,128)S(1)}, u32[]{:S(2)}, u32[]{:S(2)}) %collective-permute-start) | collective-permute-done | bytes 65568 | tf_op jit(solution)/shard_map/ppermute | solution.py:329
  9.6 0.0 copy-start
  9.6 2.8 %collective-permute-start.5 = (f32[2,128,128]{2,1,0:T(8,128)S(1)}, f32[2,128,128]{2,1,0:T(8,128)S(1)}, u32[]{:S(2)}, u32[]{:S(2)}) collective-permute-start(f32[2,128,128]{2,1,0:T(8,128)S(1)} %get-tuple-element.16.p0), channel_id=1, source_target_pairs={{0,3},{1,0},{2,1},{3,2},{4,7},{5,4},{6,5},{7,6},{8,11},{9,8},{10,9... | collective-permute-start | bytes 393224 | tf_op jit(solution)/shard_map/ppermute | solution.py:344
  12.4 0.8 %collective-permute-start.4 = (f32[2,128,128]{2,1,0:T(8,128)S(1)}, f32[2,128,128]{2,1,0:T(8,128)S(1)}, u32[]{:S(2)}, u32[]{:S(2)}) collective-permute-start(f32[2,128,128]{2,1,0:T(8,128)S(1)} %get-tuple-element.16.p0), channel_id=1, source_target_pairs={{0,2},{1,3},{2,0},{3,1},{4,6},{5,7},{6,4},{7,5},{8,10},{9,11},{10,... | collective-permute-start | bytes 393224 | tf_op jit(solution)/shard_map/ppermute | solution.py:344
  13.2 0.9 %collective-permute-start.3 = (f32[2,128,128]{2,1,0:T(8,128)S(1)}, f32[2,128,128]{2,1,0:T(8,128)S(1)}, u32[]{:S(2)}, u32[]{:S(2)}) collective-permute-start(f32[2,128,128]{2,1,0:T(8,128)S(1)} %get-tuple-element.16.p0), channel_id=1, source_target_pairs={{0,1},{1,2},{2,3},{3,0},{4,5},{5,6},{6,7},{7,4},{8,9},{9,10},{10,1... | collective-permute-start | bytes 393224 | tf_op jit(solution)/shard_map/ppermute | solution.py:344
  14.1 0.0 copy-done.2
  14.1 0.1 copy.5
  14.2 0.1 reshape.6
  14.3 0.1 concatenate.3.scalars
  14.4 3.1 %collective-permute-done.5.p3.after = f32[2,128,128]{2,1,0:T(8,128)S(1)} collective-permute-done((f32[2,128,128]{2,1,0:T(8,128)S(1)}, f32[2,128,128]{2,1,0:T(8,128)S(1)}, u32[]{:S(2)}, u32[]{:S(2)}) %collective-permute-start.5) | collective-permute-done | bytes 131104 | tf_op jit(solution)/shard_map/ppermute | solution.py:344
  17.5 3.7 %collective-permute-start.9 = (f32[2,128,128]{2,1,0:T(8,128)S(1)}, f32[2,128,128]{2,1,0:T(8,128)S(1)}, u32[]{:S(2)}, u32[]{:S(2)}) collective-permute-start(f32[2,128,128]{2,1,0:T(8,128)S(1)} %pass_kernel.1.p0), channel_id=1, source_target_pairs={{0,3},{1,0},{2,1},{3,2},{4,7},{5,4},{6,5},{7,6},{8,11},{9,8},{10,9... | collective-permute-start | bytes 393224 | tf_op jit(solution)/shard_map/ppermute | solution.py:344
  21.3 0.0 collective-permute-start.8
  21.3 1.0 %collective-permute-start.7 = (f32[2,128,128]{2,1,0:T(8,128)S(1)}, f32[2,128,128]{2,1,0:T(8,128)S(1)}, u32[]{:S(2)}, u32[]{:S(2)}) collective-permute-start(f32[2,128,128]{2,1,0:T(8,128)S(1)} %pass_kernel.1.p0), channel_id=1, source_target_pairs={{0,1},{1,2},{2,3},{3,0},{4,5},{5,6},{6,7},{7,4},{8,9},{9,10},{10,1... | collective-permute-start | bytes 393224 | tf_op jit(solution)/shard_map/ppermute | solution.py:344
  22.2 0.0 collective-permute-done.4.p2
  22.2 0.0 collective-permute-done.3.p1
  22.2 0.0 copy-done
  22.2 4.1 %first_kernel.1 = (f32[384,128]{1,0:T(8,128)S(1)}, f32[256,128]{1,0:T(8,128)S(1)}, f32[256,128]{1,0:T(8,128)S(1)}) custom-call(s32[20]{0:T(128)S(1)} %concatenate.3.scalars, f32[512,128]{1,0:T(8,128)S(1)} %copy-done, f32[2,128,128]{2,1,0:T(8,128)S(1)} %get-tuple-element.16.p0, f32[2,128,128]{2,1,0:T(8,128)S(1)} %collective-permute-done.3.p1, ...), custom_call_target="tpu_custom_call" | custom-call | flops 400000000 | bytes 2000000 | tf_op jit(solution)/shard_map/first_kernel/pallas_call | solution.py:315
  26.4 5.8 %collective-permute-start.6 = (f32[384,128]{1,0:T(8,128)S(1)}, f32[384,128]{1,0:T(8,128)S(1)}, u32[]{:S(2)}, u32[]{:S(2)}) collective-permute-start(f32[384,128]{1,0:T(8,128)S(1)} %get-tuple-element.18.own), channel_id=1, source_target_pairs={{16,0},{32,16},{48,32},{64,48},{80,64},{96,80},{112,96},{128,112},... | collective-permute-start | bytes 589832 | tf_op jit(solution)/shard_map/ppermute | solution.py:334
  32.2 0.0 collective-permute-done.9.p3
  32.2 0.0 collective-permute-done.8.p2
  32.2 0.0 collective-permute-done.7.p1
  32.2 0.6 choose_kernel.1.after
  32.9 1.9 %collective-permute-start.11 = (f32[3,128,128]{2,1,0:T(8,128)S(1)}, f32[3,128,128]{2,1,0:T(8,128)S(1)}, u32[]{:S(2)}, u32[]{:S(2)}) collective-permute-start(f32[3,128,128]{2,1,0:T(8,128)S(1)} %choose_kernel.1.after), channel_id=1, source_target_pairs={{0,16},{16,32},{32,48},{48,64},{64,80},{80,96},{96,112},{112,128},... | collective-permute-start | bytes 589832 | tf_op jit(solution)/shard_map/ppermute | solution.py:334
  34.8 3.2 %factor1_kernel.1.g1 = bf16[4,256,512]{2,1,0:T(8,128)(2,1)S(1)} custom-call(s32[20]{0:T(128)S(1)} %concatenate.3.scalars, f32[3,128,128]{2,1,0:T(8,128)S(1)} %choose_kernel.1.after, f32[2,128,128]{2,1,0:T(8,128)S(1)} %get-tuple-element.16.p0, f32[2,128,128]{2,1,0:T(8,128)S(1)} %collective-permute-done.3.p1, f32[2,128,128]{2,1,0:T(8,128)S(1)} %collective-permute-done.4.p2, ...), custom_call_target="tpu_custom_call" | custom-call | flops 400000000 | bytes 2000000 | tf_op jit(solution)/shard_map/factor1_kernel/pallas_call | solution.py:315
  38.0 0.0 collective-permute-done.6.message
  38.0 1.3 %second_kernel.1 = (f32[256,128]{1,0:T(8,128)S(1)}, f32[256,128]{1,0:T(8,128)S(1)}) custom-call(s32[20]{0:T(128)S(1)} %concatenate.3.scalars, f32[256,128]{1,0:T(8,128)S(1)} %get-tuple-element.17.after.low_ref, f32[384,128]{1,0:T(8,128)S(1)} %collective-permute-done.6.message, bf16[4,256,512]{2,1,0:T(8,128)(2,1)S(1)} %factor1_kernel.1.g1), custom_call_target="tpu_custom_call" | custom-call | flops 400000000 | bytes 2000000 | tf_op jit(solution)/shard_map/second_kernel/pallas_call | solution.py:315
  39.3 4.8 %collective-permute-start.10 = (f32[256,128]{1,0:T(8,128)S(1)}, f32[256,128]{1,0:T(8,128)S(1)}, u32[]{:S(2)}, u32[]{:S(2)}) collective-permute-start(f32[256,128]{1,0:T(8,128)S(1)} %get-tuple-element.22), channel_id=1, source_target_pairs={{0,16},{16,32},{32,48},{48,64},{64,80},{80,96},{96,112},{112,128},... | collective-permute-start | bytes 393224 | tf_op jit(solution)/shard_map/ppermute | solution.py:334
  44.1 3.7 %factor2_kernel.1.g2 = bf16[5,256,512]{2,1,0:T(8,128)(2,1)S(1)} custom-call(s32[20]{0:T(128)S(1)} %concatenate.3.scalars, f32[256,128]{1,0:T(8,128)S(1)} %get-tuple-element.20.after.low_ref, f32[2,128,128]{2,1,0:T(8,128)S(1)} %pass_kernel.1.p0, f32[2,128,128]{2,1,0:T(8,128)S(1)} %collective-permute-done.7.p1, f32[2,128,128]{2,1,0:T(8,128)S(1)} %collective-permute-done.8.p2, ...), custom_call_target="tpu_custom_call" | custom-call | flops 400000000 | bytes 2000000 | tf_op jit(solution)/shard_map/factor2_kernel/pallas_call | solution.py:315
  47.8 0.0 collective-permute-done.11.after.down
  47.8 3.1 %collective-permute-done.10.back = f32[256,128]{1,0:T(8,128)S(1)} collective-permute-done((f32[256,128]{1,0:T(8,128)S(1)}, f32[256,128]{1,0:T(8,128)S(1)}, u32[]{:S(2)}, u32[]{:S(2)}) %collective-permute-start.10) | collective-permute-done | bytes 131104 | tf_op jit(solution)/shard_map/ppermute | solution.py:334
  50.8 1.5 %third_kernel.1 = (f32[256,128]{1,0:T(8,128)S(1)}, f32[256,128]{1,0:T(8,128)S(1)}, f32[384,128]{1,0:T(8,128)S(1)}, f32[384,128]{1,0:T(8,128)S(1)}) custom-call(s32[20]{0:T(128)S(1)} %concatenate.3.scalars, f32[256,128]{1,0:T(8,128)S(1)} %get-tuple-element.20.after.low_ref, f32[384,128]{1,0:T(8,128)S(1)} %get-tuple-element.18.own, ...), custom_call_target="tpu_custom_call" | custom-call | flops 400000000 | bytes 2000000 | tf_op jit(solution)/shard_map/third_kernel/pallas_call | solution.py:315
  52.4 2.7 %collective-permute-start.12 = (f32[384,128]{1,0:T(8,128)S(1)}, f32[384,128]{1,0:T(8,128)S(1)}, u32[]{:S(2)}, u32[]{:S(2)}) collective-permute-start(f32[384,128]{1,0:T(8,128)S(1)} %get-tuple-element.25), channel_id=1, source_target_pairs={{16,32},{48,64},{80,96},{112,128},{144,160},{176,192},{208,224},{3... | collective-permute-start | bytes 589832 | tf_op jit(solution)/shard_map/ppermute | solution.py:340
  55.1 2.1 %collective-permute-start.13 = (f32[384,128]{1,0:T(8,128)S(1)}, f32[384,128]{1,0:T(8,128)S(1)}, u32[]{:S(2)}, u32[]{:S(2)}) collective-permute-start(f32[384,128]{1,0:T(8,128)S(1)} %get-tuple-element.26), channel_id=1, source_target_pairs={{0,16},{32,48},{64,80},{96,112},{128,144},{160,176},{192,208},{224... | collective-permute-start | bytes 589832 | tf_op jit(solution)/shard_map/ppermute | solution.py:340
  57.1 2.9 %factor3_kernel.1.g3 = bf16[3,256,512]{2,1,0:T(8,128)(2,1)S(1)} custom-call(s32[20]{0:T(128)S(1)} %concatenate.3.scalars, f32[256,128]{1,0:T(8,128)S(1)} %get-tuple-element.23.after.low_ref, f32[2,128,128]{2,1,0:T(8,128)S(1)} %pass_kernel.1.p0, f32[2,128,128]{2,1,0:T(8,128)S(1)} %collective-permute-done.7.p1, f32[2,128,128]{2,1,0:T(8,128)S(1)} %collective-permute-done.8.p2, ...), custom_call_target="tpu_custom_call" | custom-call | flops 400000000 | bytes 2000000 | tf_op jit(solution)/shard_map/factor3_kernel/pallas_call | solution.py:315
  60.1 2.4 %factor4_kernel.1.g4 = bf16[3,256,512]{2,1,0:T(8,128)(2,1)S(1)} custom-call(f32[256,128]{1,0:T(8,128)S(1)} %get-tuple-element.23.after.low_ref, f32[3,128,128]{2,1,0:T(8,128)S(1)} %collective-permute-done.11.after.down), custom_call_target="tpu_custom_call" | custom-call | flops 400000000 | bytes 2000000 | tf_op jit(solution)/shard_map/factor4_kernel/pallas_call | solution.py:315
  62.5 4.6 %collective-permute-done.12.far = f32[384,128]{1,0:T(8,128)S(1)} collective-permute-done((f32[384,128]{1,0:T(8,128)S(1)}, f32[384,128]{1,0:T(8,128)S(1)}, u32[]{:S(2)}, u32[]{:S(2)}) %collective-permute-start.12) | collective-permute-done | bytes 196640 | tf_op jit(solution)/shard_map/ppermute | solution.py:340
  67.1 0.0 collective-permute-done.13.near
  67.1 2.3 %fourth_kernel.1 = f32[512,128]{1,0:T(8,128)} custom-call(s32[20]{0:T(128)S(1)} %concatenate.3.scalars, f32[256,128]{1,0:T(8,128)S(1)} %get-tuple-element.23.after.low_ref, f32[256,128]{1,0:T(8,128)S(1)} %get-tuple-element.24.top_ref, f32[384,128]{1,0:T(8,128)S(1)} %collective-permute-done.12.far, f32[384,128]{1,0:T(8,128)S(1)} %collective-permute-done.13.near, ...), custom_call_target="tpu_custom_call" | custom-call | flops 400000000 | bytes 2000000 | tf_op jit(solution)/shard_map/fourth_kernel/pallas_call | solution.py:315
  (3 shorter events, 0.1 us)
Async XLA Ops:
  0.0 7.1 %collective-permute-start.2 = (f32[128,128]{1,0:T(8,128)}, f32[128,128]{1,0:T(8,128)S(1)}, u32[]{:S(2)}, u32[]{:S(2)}) collective-permute-start(f32[128,128]{1,0:T(8,128)} %bitcast.6), channel_id=1, source_target_pairs={{0,12},{1,13},{2,14},{3,15},{4,0},{5,1},{6,2},{7,3},{8,4},{9,5},{1... | collective-permute-start | bytes 196616 | tf_op jit(solution)/shard_map/ppermute | solution.py:329
  0.1 8.3 %collective-permute-start.1 = (f32[128,128]{1,0:T(8,128)}, f32[128,128]{1,0:T(8,128)S(1)}, u32[]{:S(2)}, u32[]{:S(2)}) collective-permute-start(f32[128,128]{1,0:T(8,128)} %bitcast.7), channel_id=1, source_target_pairs={{0,8},{1,9},{2,10},{3,11},{4,12},{5,13},{6,14},{7,15},{8,0},{9,1},... | collective-permute-start | bytes 196616 | tf_op jit(solution)/shard_map/ppermute | solution.py:329
  3.4 6.2 %collective-permute-start = (f32[128,128]{1,0:T(8,128)}, f32[128,128]{1,0:T(8,128)S(1)}, u32[]{:S(2)}, u32[]{:S(2)}) collective-permute-start(f32[128,128]{1,0:T(8,128)} %bitcast.8), channel_id=1, source_target_pairs={{0,4},{1,5},{2,6},{3,7},{4,8},{5,9},{6,10},{7,11},{8,12},{9,13},{1... | collective-permute-start | bytes 196616 | tf_op jit(solution)/shard_map/ppermute | solution.py:329
  6.2 0.9 %copy-start.1 = (f32[1,128,128]{2,1,0:T(8,128)S(1)}, f32[1,128,128]{2,1,0:T(8,128)}, u32[]{:S(2)}) copy-start(f32[1,128,128]{2,1,0:T(8,128)} %param.4) | copy-start | bytes 196612
  7.1 7.1 %copy-start.2 = (s32[1,8,2]{1,2,0:T(2,128)S(1)}, s32[1,8,2]{1,2,0:T(2,128)}, u32[]{:S(2)}) copy-start(s32[1,8,2]{1,2,0:T(2,128)} %param.5) | copy-start | bytes 196
  9.6 12.7 %copy-start = (f32[512,128]{1,0:T(8,128)S(1)}, f32[512,128]{1,0:T(8,128)}, u32[]{:S(2)}) copy-start(f32[512,128]{1,0:T(8,128)} %x_ref.1) | copy-start | bytes 786436
  9.6 7.9 %collective-permute-start.5 = (f32[2,128,128]{2,1,0:T(8,128)S(1)}, f32[2,128,128]{2,1,0:T(8,128)S(1)}, u32[]{:S(2)}, u32[]{:S(2)}) collective-permute-start(f32[2,128,128]{2,1,0:T(8,128)S(1)} %get-tuple-element.16.p0), channel_id=1, source_target_pairs={{0,3},{1,0},{2,1},{3,2},{4,7},{5,4},{6,5},{7,6},{8,11},{9,8},{10,9... | collective-permute-start | bytes 393224 | tf_op jit(solution)/shard_map/ppermute | solution.py:344
  12.4 9.8 %collective-permute-start.4 = (f32[2,128,128]{2,1,0:T(8,128)S(1)}, f32[2,128,128]{2,1,0:T(8,128)S(1)}, u32[]{:S(2)}, u32[]{:S(2)}) collective-permute-start(f32[2,128,128]{2,1,0:T(8,128)S(1)} %get-tuple-element.16.p0), channel_id=1, source_target_pairs={{0,2},{1,3},{2,0},{3,1},{4,6},{5,7},{6,4},{7,5},{8,10},{9,11},{10,... | collective-permute-start | bytes 393224 | tf_op jit(solution)/shard_map/ppermute | solution.py:344
  13.2 9.0 %collective-permute-start.3 = (f32[2,128,128]{2,1,0:T(8,128)S(1)}, f32[2,128,128]{2,1,0:T(8,128)S(1)}, u32[]{:S(2)}, u32[]{:S(2)}) collective-permute-start(f32[2,128,128]{2,1,0:T(8,128)S(1)} %get-tuple-element.16.p0), channel_id=1, source_target_pairs={{0,1},{1,2},{2,3},{3,0},{4,5},{5,6},{6,7},{7,4},{8,9},{9,10},{10,1... | collective-permute-start | bytes 393224 | tf_op jit(solution)/shard_map/ppermute | solution.py:344
  17.5 14.7 %collective-permute-start.9 = (f32[2,128,128]{2,1,0:T(8,128)S(1)}, f32[2,128,128]{2,1,0:T(8,128)S(1)}, u32[]{:S(2)}, u32[]{:S(2)}) collective-permute-start(f32[2,128,128]{2,1,0:T(8,128)S(1)} %pass_kernel.1.p0), channel_id=1, source_target_pairs={{0,3},{1,0},{2,1},{3,2},{4,7},{5,4},{6,5},{7,6},{8,11},{9,8},{10,9... | collective-permute-start | bytes 393224 | tf_op jit(solution)/shard_map/ppermute | solution.py:344
  21.3 11.0 %collective-permute-start.8 = (f32[2,128,128]{2,1,0:T(8,128)S(1)}, f32[2,128,128]{2,1,0:T(8,128)S(1)}, u32[]{:S(2)}, u32[]{:S(2)}) collective-permute-start(f32[2,128,128]{2,1,0:T(8,128)S(1)} %pass_kernel.1.p0), channel_id=1, source_target_pairs={{0,2},{1,3},{2,0},{3,1},{4,6},{5,7},{6,4},{7,5},{8,10},{9,11},{10,... | collective-permute-start | bytes 393224 | tf_op jit(solution)/shard_map/ppermute | solution.py:344
  21.3 11.0 %collective-permute-start.7 = (f32[2,128,128]{2,1,0:T(8,128)S(1)}, f32[2,128,128]{2,1,0:T(8,128)S(1)}, u32[]{:S(2)}, u32[]{:S(2)}) collective-permute-start(f32[2,128,128]{2,1,0:T(8,128)S(1)} %pass_kernel.1.p0), channel_id=1, source_target_pairs={{0,1},{1,2},{2,3},{3,0},{4,5},{5,6},{6,7},{7,4},{8,9},{9,10},{10,1... | collective-permute-start | bytes 393224 | tf_op jit(solution)/shard_map/ppermute | solution.py:344
  26.4 11.7 %collective-permute-start.6 = (f32[384,128]{1,0:T(8,128)S(1)}, f32[384,128]{1,0:T(8,128)S(1)}, u32[]{:S(2)}, u32[]{:S(2)}) collective-permute-start(f32[384,128]{1,0:T(8,128)S(1)} %get-tuple-element.18.own), channel_id=1, source_target_pairs={{16,0},{32,16},{48,32},{64,48},{80,64},{96,80},{112,96},{128,112},... | collective-permute-start | bytes 589832 | tf_op jit(solution)/shard_map/ppermute | solution.py:334
  32.9 14.9 %collective-permute-start.11 = (f32[3,128,128]{2,1,0:T(8,128)S(1)}, f32[3,128,128]{2,1,0:T(8,128)S(1)}, u32[]{:S(2)}, u32[]{:S(2)}) collective-permute-start(f32[3,128,128]{2,1,0:T(8,128)S(1)} %choose_kernel.1.after), channel_id=1, source_target_pairs={{0,16},{16,32},{32,48},{48,64},{64,80},{80,96},{96,112},{112,128},... | collective-permute-start | bytes 589832 | tf_op jit(solution)/shard_map/ppermute | solution.py:334
  39.3 11.5 %collective-permute-start.10 = (f32[256,128]{1,0:T(8,128)S(1)}, f32[256,128]{1,0:T(8,128)S(1)}, u32[]{:S(2)}, u32[]{:S(2)}) collective-permute-start(f32[256,128]{1,0:T(8,128)S(1)} %get-tuple-element.22), channel_id=1, source_target_pairs={{0,16},{16,32},{32,48},{48,64},{64,80},{80,96},{96,112},{112,128},... | collective-permute-start | bytes 393224 | tf_op jit(solution)/shard_map/ppermute | solution.py:334
  52.4 14.7 %collective-permute-start.12 = (f32[384,128]{1,0:T(8,128)S(1)}, f32[384,128]{1,0:T(8,128)S(1)}, u32[]{:S(2)}, u32[]{:S(2)}) collective-permute-start(f32[384,128]{1,0:T(8,128)S(1)} %get-tuple-element.25), channel_id=1, source_target_pairs={{16,32},{48,64},{80,96},{112,128},{144,160},{176,192},{208,224},{3... | collective-permute-start | bytes 589832 | tf_op jit(solution)/shard_map/ppermute | solution.py:340
  55.1 12.0 %collective-permute-start.13 = (f32[384,128]{1,0:T(8,128)S(1)}, f32[384,128]{1,0:T(8,128)S(1)}, u32[]{:S(2)}, u32[]{:S(2)}) collective-permute-start(f32[384,128]{1,0:T(8,128)S(1)} %get-tuple-element.26), channel_id=1, source_target_pairs={{0,16},{32,48},{64,80},{96,112},{128,144},{160,176},{192,208},{224... | collective-permute-start | bytes 589832 | tf_op jit(solution)/shard_map/ppermute | solution.py:340
